TPU v7x, 32 devices: a whole 2x2x4 slice. The times are simulated.
32 devices in a mesh: seq: 8 (over y, x, core), tp: 4 (over z).
Axes of the slice: x: 2, y: 2, z: 4, core: 2. Of those that a mesh axis runs over, the one named last changes fastest.
Arguments:
- patches: bfloat16 [16384, 1280], P('seq', 'tp'), may hold values from -6 to 6
- route: int32 [256, 1], P('seq'), may hold values from 0 to 7; in each aligned block of 32 rows (0 to 31, 32 to 63, ...) at most 4 rows name the same one
- order: int32 [8, 32], P('seq'), may hold values from 0 to 31, each once within a row
- tiles: int32 [16], P('seq'), may hold values from 1 to 4
- w_qkv: bfloat16 [1280, 3840], P(None, 'tp'), may hold values from -0.15625 to 0.15625
- w_proj: bfloat16 [1280, 1280], P('tp'), may hold values from -0.15625 to 0.15625
- vit_gain: float32 [1280], replicated, may hold values from 0.1 to 1.9
- merge_gain: float32 [1280], replicated, may hold values from 0.1 to 1.9
- w_merge: bfloat16 [5120, 8192], P('seq', 'tp'), may hold values from -0.078125 to 0.078125
- llm_gain: float32 [8192], P('tp'), may hold values from 0.1 to 1.9
- w_cache: bfloat16 [8192, 2048], P('tp'), may hold values from -0.0625 to 0.0625
Outputs:
- kv_cache: bfloat16 [4096, 2048], P(('seq', 'tp'))
Inputs may be any that keep to these rules, and one draw needn't show every extreme that they name: `route`: each seq index's 32 windows send exactly 4 windows to every seq index. `order`: each row is a permutation of 0 to 31.
All inputs are finite; a program needn't handle non-finite values.
Results may differ from a plain program's by a relative error of at most 0.019.
Values may be sent and summed in bfloat16 or wider, within the bound.
No kernel may reach another device: no remote copies, remote signals or barrier semaphores. Data moves between devices by JAX's collectives and lax.ppermute only.
A program may use at most 192 MiB of HBM per device.

v0:
```python
import jax
import jax.numpy as jnp
from jax import lax
from jax.sharding import PartitionSpec as P

DV = 1280
HV = 16
D = 8192
WIN = 64
MERGE = 4
TILE_WIN = 4
TILE_SLOTS = 4


def attend_windows(full, w_qkv, w_proj, vit_gain):
    count, slots, width, feats = full.shape
    head_size = DV // HV
    heads = w_qkv.shape[1] // (3 * head_size)
    rows = full.reshape(-1, feats).astype(jnp.float32)
    scale_rows = lax.rsqrt(jnp.mean(rows * rows, axis=1, keepdims=True) + 1e-06)
    normed = (rows * scale_rows * vit_gain).astype(jnp.bfloat16)
    packed = jnp.dot(normed, w_qkv, preferred_element_type=jnp.float32).astype(jnp.bfloat16)
    packed = packed.reshape(count * slots, width, heads, 3, head_size)
    query = packed[:, :, :, 0, :]
    keys = packed[:, :, :, 1, :]
    values = packed[:, :, :, 2, :]
    scores = jnp.einsum("wqhd,wkhd->whqk", query, keys, preferred_element_type=jnp.float32)
    scores = scores / jnp.sqrt(jnp.float32(head_size))
    probs = jax.nn.softmax(scores, axis=-1).astype(jnp.bfloat16)
    mixed = jnp.einsum("whqk,wkhd->wqhd", probs, values, preferred_element_type=jnp.float32)
    mixed = mixed.astype(jnp.bfloat16).reshape(-1, heads * head_size)
    partial_value = jnp.dot(mixed, w_proj, preferred_element_type=jnp.float32)
    summed = lax.psum(partial_value.astype(jnp.bfloat16), "tp").astype(jnp.float32)
    return (rows + summed).astype(jnp.bfloat16).reshape(full.shape)


def shards(
    patches, route, order, tiles, w_qkv, w_proj, vit_gain, merge_gain, w_merge, llm_gain, w_cache
):
    seq_count = lax.axis_size("seq")
    win_dev = order.shape[1]
    feats = patches.shape[1]
    windows = patches.reshape(win_dev, -1, feats)
    picks = order[0]
    ordered = jnp.take(windows, picks, axis=0)
    tile_index = picks // TILE_WIN
    frame = tile_index // TILE_SLOTS
    slot = tile_index % TILE_SLOTS
    counts = jnp.take(tiles, frame)
    live = (slot < counts).astype(jnp.int32)
    arrange = jnp.argsort(route[:, 0], stable=True)
    per_peer = win_dev // seq_count
    send = jnp.take(ordered, arrange, axis=0).reshape(seq_count, per_peer, -1, feats)
    live_send = jnp.take(live, arrange).reshape(seq_count, per_peer)
    full = lax.all_gather(send, "tp", axis=3, tiled=True)
    encoded = attend_windows(
        lax.all_to_all(full, "seq", split_axis=0, concat_axis=0, tiled=True),
        w_qkv,
        w_proj,
        vit_gain,
    )
    live_here = lax.all_to_all(live_send, "seq", split_axis=0, concat_axis=0, tiled=True)
    patch_rows = encoded.reshape(-1, MERGE, DV).astype(jnp.float32)
    patch_scale = lax.rsqrt(jnp.mean(patch_rows * patch_rows, axis=2, keepdims=True) + 1e-06)
    merged = (patch_rows * patch_scale * merge_gain).astype(jnp.bfloat16).reshape(-1, MERGE * DV)
    hidden = jnp.dot(
        merged,
        lax.all_gather(w_merge, "seq", axis=0, tiled=True),
        preferred_element_type=jnp.float32,
    ).astype(jnp.bfloat16)
    wide = hidden.astype(jnp.float32)
    scaled = (wide * llm_gain).astype(jnp.bfloat16)
    partial_value = jnp.dot(scaled, w_cache, preferred_element_type=jnp.float32)
    squares = jnp.sum(wide * wide, axis=1, keepdims=True)
    cache, total_squares = (
        lax.psum_scatter(
            partial_value.astype(jnp.bfloat16), "tp", scatter_dimension=0, tiled=True
        ).astype(jnp.float32),
        lax.psum_scatter(
            squares.astype(jnp.bfloat16), "tp", scatter_dimension=0, tiled=True
        ).astype(jnp.float32),
    )
    share = cache.shape[0]
    first_row = lax.axis_index("tp") * share
    live_tokens = jnp.repeat(live_here.reshape(-1), WIN // MERGE)
    mine = lax.dynamic_slice_in_dim(live_tokens, first_row, share).astype(jnp.float32)
    return (cache * lax.rsqrt(total_squares / D + 1e-06) * mine[:, None]).astype(jnp.bfloat16)


def solution(mesh):
    return jax.shard_map(
        shards,
        mesh=mesh,
        in_specs=(
            P("seq", "tp"),
            P("seq", None),
            P("seq", None),
            P("seq"),
            P(None, "tp"),
            P("tp", None),
            P(),
            P(),
            P("seq", "tp"),
            P("tp"),
            P("tp", None),
        ),
        out_specs=P(("seq", "tp"), None),
        check_vma=False,
    )
```

profile of v0, /device:TPU:0, one launch (start us, length us, event | category | flops | bytes accessed | tf_op | source)
XLA Modules:
  0.0 681.2 jit_solution(14711809182567290565)
XLA Ops:
  7.4 0.0 copy-start
  7.4 1.4 fusion.30
  8.8 2.2 sort.17
  11.1 0.7 compare_select_fusion.7
  11.7 2.0 compare_convert_fusion
  13.7 0.7 gather_fusion
  14.4 2.6 copy.42
  17.0 3.3 gather_fusion.1
  20.3 2.8 broadcast_select_fusion.1
  23.1 3.3 gather_fusion.2
  26.4 2.8 broadcast_select_fusion
  29.2 5.9 copy.43
  35.2 0.0 all-gather.3.cloned.1.call-update
  35.2 0.0 all-reduce.2.cloned.1.call-start
  35.2 186.7 %all-gather.3.cloned.1.call-done = bf16[8,4,64,1280]{2,0,1,3:T(8,128)(2,1)} async-done(((bf16[8,4,64,320]{2,0,1,3:T(8,128)(2,1)}), bf16[8,4,64,1280]{2,0,1,3:T(8,128)(2,1)}) %all-gather.3.cloned.1.call-update) | async-done | bytes 5242896 | tf_op jit(solution)/shard_map/all_gather | solution.py:55
  222.0 12.8 %copy.44 = bf16[8,4,64,1280]{3,2,1,0:T(8,128)(2,1)} copy(bf16[8,4,64,1280]{2,0,1,3:T(8,128)(2,1)} %all-gather.3.cloned.1.call-done) | data formatting | bytes 10485760 | tf_op jit(solution)/shard_map/all_gather | solution.py:55
  234.7 64.0 %all_to_all.11 = bf16[8,4,64,1280]{3,2,1,0:T(8,128)(2,1)S(1)} all-to-all(bf16[8,4,64,1280]{3,2,1,0:T(8,128)(2,1)} %copy.44), channel_id=1, replica_groups=mesh['seq'=8,'tp'=4] {'seq'}, dimensions={0} | all-to-all | bytes 10485760 | tf_op jit(solution)/shard_map/all_to_all | solution.py:57
  298.7 2.3 copy-done.2
  301.0 1.1 fusion.1
  302.1 0.1 rsqrt.26
  302.2 3.7 fusion.3
  305.9 6.8 %convolution_convert_fusion.1 = bf16[2048,960]{0,1:T(8,128)(2,1)} fusion(bf16[2048,1280]{1,0:T(8,128)(2,1)S(1)} %fusion.3, bf16[1280,960]{0,1:T(8,128)(2,1)S(1)} %copy-done), kind=kOutput, calls=%fused_computation.25 | convolution fusion | flops 5035130880 | bytes 11632640 | tf_op jit(solution)/shard_map/dot_general | solution.py:22
  312.8 12.3 %reshape.243 = bf16[32,64,4,3,80]{1,0,4,3,2:T(8,128)(2,1)} reshape(bf16[2048,960]{0,1:T(8,128)(2,1)} %convolution_convert_fusion.1) | data formatting | bytes 7864320 | tf_op jit(solution)/shard_map/reshape | solution.py:23
  325.1 5.7 fusion.29
  330.8 3.6 copy.58
  334.4 4.6 copy.59
  339.0 2.8 fusion.16
  341.8 3.1 fusion.31
  345.0 3.8 copy.57
  348.8 3.0 convert_bitcast_fusion
  351.9 0.0 copy-start.5
  351.9 2.0 copy.51
  353.9 2.3 reshape.244
  356.2 6.6 convolution_convert_fusion
  362.8 0.0 all-reduce.2.cloned.1.call-update
  362.8 0.0 all-gather.5.cloned.1.call-start
  362.9 0.5 all-gather.5.cloned.1.call-update
  363.4 0.3 reduce-scatter.7.cloned.1.call-start
  363.8 184.6 %all-reduce.2.cloned.1.call-done = bf16[2048,1280]{1,0:T(8,128)(2,1)} async-done(((bf16[2048,1280]{1,0:T(8,128)(2,1)}), bf16[2048,1280]{1,0:T(8,128)(2,1)}) %all-reduce.2.cloned.1.call-update) | async-done | bytes 5242896 | tf_op jit(solution)/shard_map/psum | solution.py:33
  548.3 9.7 %multiply_reduce_fusion = (f32[2048]{0:T(1024)S(1)}, f32[2048,1280]{1,0:T(8,128)}) fusion(bf16[2048,1280]{1,0:T(8,128)(2,1)} %all-reduce.2.cloned.1.call-done, bf16[8,4,64,1280]{3,2,1,0:T(8,128)(2,1)} %copy-done.2), kind=kLoop, calls=%fused_computation.12 | loop fusion | flops 18348032 | bytes 20979712 | tf_op jit(solution)/shard_map/reduce_sum | solution.py:64
  558.0 0.3 rsqrt.28
  558.3 5.4 mul.86
  563.7 10.1 %copy.60 = f32[64,8,4,1280]{3,1,2,0:T(8,128)} copy(f32[64,8,4,1280]{3,2,1,0:T(4,128)} %bitcast.71) | data formatting | bytes 20971520
  573.8 12.4 %reshape.248 = f32[512,5120]{1,0:T(8,128)} reshape(f32[2048,1280]{1,0:T(8,128)} %get-tuple-element.11) | data formatting | bytes 20971520 | tf_op jit(solution)/shard_map/convert_element_type | solution.py:63
  586.1 22.3 %fusion.9 = (bf16[512]{0:T(512)(128)(2,1)S(1)}, bf16[512,2048]{1,0:T(8,128)(2,1)}) fusion(bf16[5120,2048]{1,0:T(8,128)(2,1)} %all-gather.5.cloned.1.call-done, f32[512,5120]{1,0:T(8,128)} %reshape.248, f32[512,5120]{1,0:T(8,128)} %bitcast.72, f32[5120]{0:T(1024)S(1)} %mul.90), kind=kOutput, calls=%fused_computation.20 | convolution fusion | flops 10749476864 | bytes 44061696 | tf_op jit(solution)/shard_map/dot_general | solution.py:66
  608.5 0.8 reshape.296
  609.3 0.0 reduce-scatter.7.cloned.1.call-update
  609.3 0.3 reduce-scatter.5.cloned.1.call-start
  609.7 0.0 copy-start.1
  609.7 10.0 %convolution_convert_fusion.2 = bf16[512,2048]{1,0:T(8,128)(2,1)} fusion(bf16[2048,2048]{1,0:T(8,128)(2,1)} %param.23, bf16[512,2048]{1,0:T(8,128)(2,1)} %get-tuple-element.22, f32[2048]{0:T(1024)S(1)} %copy-done.6), kind=kOutput, calls=%fused_computation.27 | convolution fusion | flops 4299161600 | bytes 12591104 | tf_op jit(solution)/shard_map/dot_general | solution.py:73
  619.7 0.0 reduce-scatter.5.cloned.1.call-update
  619.7 0.7 select_n.94
  620.4 3.6 all-to-all-start.1
  624.0 4.6 all-to-all-done.1
  628.7 0.5 broadcast.244
  629.2 0.6 reduce.5
  629.8 0.1 reshape.245
  629.9 0.1 broadcast_in_dim.35
  629.9 0.1 reshape.246
  630.0 0.1 dynamic-slice_convert_fusion
  630.1 0.8 add_rsqrt_fusion
  630.9 0.1 copy.61
  630.9 41.0 %reduce-scatter.5.cloned.1.call-done = bf16[128,2048]{1,0:T(8,128)(2,1)} async-done(((bf16[512,2048]{1,0:T(8,128)(2,1)}), bf16[128,2048]{1,0:T(8,128)(2,1)}) %reduce-scatter.5.cloned.1.call-update) | async-done | bytes 524304 | tf_op jit(solution)/shard_map/reduce_scatter | solution.py:76
  672.0 2.1 multiply_convert_fusion.4
  (23 shorter events, 0.1 us)
Async XLA Ops:
  7.4 298.6 %copy-start = (bf16[1280,960]{0,1:T(8,128)(2,1)S(1)}, bf16[1280,960]{0,1:T(8,128)(2,1)}, u32[]{:S(2)}) copy-start(bf16[1280,960]{0,1:T(8,128)(2,1)} %param.17) | copy-start | bytes 7372804
  7.4 214.6 %all-gather.3.cloned.1.call-start = ((), (), s32[]{:S(2)}) async-start(), calls=%async_computation.4 | async-start | bytes 13107200 | tf_op jit(solution)/shard_map/all_gather | solution.py:55
  35.2 513.1 %all-reduce.2.cloned.1.call-start = ((), (), s32[]{:S(2)}) async-start(), calls=%async_computation.5 | async-start | bytes 10485760 | tf_op jit(solution)/shard_map/psum | solution.py:33
  298.7 2.3 copy-start.2
  301.0 1.2 copy-start.3
  351.9 4.3 copy-start.5
  362.8 0.9 copy-start.4
  362.8 223.3 %all-gather.5.cloned.1.call-start = ((), (), s32[]{:S(2)}) async-start(), calls=%async_computation.6 | async-start | bytes 23592960 | tf_op jit(solution)/shard_map/all_gather | solution.py:68
  363.4 266.7 %reduce-scatter.7.cloned.1.call-start = ((), (), s32[]{:S(2)}) async-start(), calls=%async_computation.8 | async-start | bytes 163840
  586.1 23.5 %copy-start.6 = (f32[2048]{0:T(1024)S(1)}, f32[2048]{0:T(1024)}, u32[]{:S(2)}) copy-start(f32[2048]{0:T(1024)} %param.22) | copy-start | bytes 24580
  609.3 62.6 %reduce-scatter.5.cloned.1.call-start = ((), (), s32[]{:S(2)}) async-start(), calls=%async_computation.7 | async-start | bytes 2621440 | tf_op jit(solution)/shard_map/reduce_scatter | solution.py:76
  609.7 64.4 %copy-start.1 = (bf16[1280,960]{0,1:T(8,128)(2,1)S(1)}, bf16[1280,960]{0,1:T(8,128)(2,1)}, u32[]{:S(2)}) copy-start(bf16[1280,960]{0,1:T(8,128)(2,1)} %param.17) | copy-start | bytes 7372804
  620.4 8.3 %all-to-all-start.1 = ((s32[8,1,4]{2,1,0:T(1,128)}), s32[8,1,4]{2,1,0:T(1,128)S(1)}, u32[]{:S(2)}, u32[]{:S(2)}) async-start(s32[8,1,4]{2,1,0:T(1,128)} %bitcast.14), calls=%async_computation.2 | async-start | bytes 8192 | tf_op jit(solution)/shard_map/all_to_all | solution.py:62
Sparse Core Ops, SparseCore 0:
  35.3 186.6 all-gather.2
  363.0 185.3 all-reduce.1
  609.4 18.1 reduce-scatter.6
  629.9 42.0 reduce-scatter.4
Sparse Core Ops, SparseCore 1:
  365.2 103.8 all-gather.4
where the time goes:
time: 683 us; the launch traced here: 681 us
  waiting for transfers between devices  418 us (61%)
  local copies, waits for them, and re-layouts  97.2 us (14%)
  blocking collectives  64 us (9%)
  matrix products  51.7 us (8%)
  other arithmetic  31.8 us (5%)
  between operations  14.7 us (2%)
    all_gather x1, waiting for transfers between devices, shards(): full = lax.all_gather(send, 'tp', axis=3, tiled=True)  187 us
    psum x1, waiting for transfers between devices, attend_windows(): lax.psum(partial_value.astype(jnp.bfloat16), 'tp').astype(jnp.float32)  185 us
    all_to_all x1, blocking collectives, shards(): lax.all_to_all(full, 'seq', split_axis=0, concat_axis=0, tiled=True)  64 us
    reduce_scatter x1, waiting for transfers between devices, shards(): lax.psum_scatter(partial_value.astype(jnp.bfloat16), 'tp', scatter_dimens...  41 us
    unnamed x20, local copies, waits for them, and re-layouts  27.1 us
    dot_general x1, matrix products, shards(): jnp.dot(merged, lax.all_gather(w_merge, 'seq', axis=0, tiled=True), prefe...  22.3 us
  transfers between devices with their start and end apart: 6, of which 4 were waited for; matrix products, arithmetic and copies ran while one was open for 7% of the time, Pallas kernels for 0%

commit v1 on v0

v1 whole, which is shorter than its diff:
```python
import functools

import jax
import jax.numpy as jnp
from jax import lax
from jax.experimental import pallas as pl
from jax.experimental.pallas import tpu as pltpu
from jax.sharding import PartitionSpec as P

DV = 1280
HV = 16
HS = DV // HV
D = 8192
WIN = 64
MERGE = 4
TILE_WIN = 4
TILE_SLOTS = 4
GROUP = 4
F32 = jnp.float32
BF = jnp.bfloat16
MIB = 1024 * 1024


def attend_kernel(tp, moves, nw, aliased, info, *refs):
    own = refs[0]
    right = refs[1:tp]
    left = refs[tp : 2 * tp - 1]
    at = 2 * tp - 1
    w_refs = refs[at : at + nw]
    vit_gain, merge_gain = refs[at + nw : at + nw + 2]
    at += nw + 2 + int(aliased)
    out = refs[at]
    w, xs, nrm, packed, mixed, vit, bias, sem = refs[at + 1 :]
    t = info[0]
    feats = own.shape[1]
    heads = HV // tp
    rows = packed.shape[0]
    first_proj = 3 * DV
    cols = xs.shape[1]
    step = pl.program_id(0)

    @pl.when(step == 0)
    def _():
        for copy in moves(info, w_refs, w, sem):
            copy.start()
        key = lax.broadcasted_iota(jnp.int32, (cols, cols), 0) // (WIN // MERGE) % GROUP
        query = lax.broadcasted_iota(jnp.int32, (cols, cols), 1) // (WIN // MERGE) % GROUP
        bias[...] = jnp.where(key == query, 0.0, -1e30).astype(F32)

    for j in range(tp):
        spot = pl.ds(pl.multiple_of(lax.rem(t + j, tp) * feats, feats), feats)
        if j == 0:
            xs[spot, :] = own[0]
        else:

            @pl.when(t + j < tp)
            def _():
                xs[spot, :] = right[j - 1][0]

            @pl.when(t + j >= tp)
            def _():
                xs[spot, :] = left[tp - j - 1][0]

    xf = xs[...].astype(F32)
    scale = lax.rsqrt(jnp.mean(xf * xf, axis=0, keepdims=True) + 1e-6)
    nrm[...] = (xf * scale * vit_gain[...]).astype(BF)

    @pl.when(step == 0)
    def _():
        for copy in moves(info, w_refs, w, sem):
            copy.wait()

    fold = (HS**-0.5) * 1.4426950408889634

    def group(g, carry):
        mine = w[pl.ds(pl.multiple_of(g * rows, rows), rows), :]
        packed[...] = jnp.dot(mine, nrm[...], preferred_element_type=F32).astype(BF)
        for h in range(heads):
            q, k, v = (packed[(3 * h + i) * HS : (3 * h + i + 1) * HS, :] for i in range(3))
            s = lax.dot_general(k, q, (((0,), (0,)), ((), ())), preferred_element_type=F32)
            s = s * fold + bias[...]
            p = jnp.exp2(s - jnp.max(s, axis=0, keepdims=True))
            total = jnp.sum(p, axis=0, keepdims=True)
            p = (p * (1.0 / total)).astype(BF)
            m = jnp.dot(v, p, preferred_element_type=F32).astype(BF)
            mixed[pl.ds(pl.multiple_of(g * heads * HS, heads * HS) + h * HS, HS), :] = m
        return carry

    lax.fori_loop(0, tp, group, 0)

    width = 256
    sums = jnp.zeros((cols, 1), F32)
    for n in range(DV // width):
        part = slice(n * width, (n + 1) * width)
        proj = lax.dot_general(
            mixed[...],
            w[first_proj : first_proj + DV, part],
            (((0,), (0,)), ((), ())),
            preferred_element_type=F32,
        )
        y = (xs[part, :].T.astype(F32) + proj).astype(BF)
        vit[:, part] = y
        yf = y.astype(F32)
        sums = sums + jnp.sum(yf * yf, axis=1, keepdims=True)
    scale = lax.rsqrt(sums * (1.0 / DV) + 1e-6)
    merged = (vit[...].astype(F32) * scale * merge_gain[...]).astype(BF)
    per = cols // MERGE
    for c in range(MERGE):
        out[c, 0] = merged[c * per : (c + 1) * per, :]


def attend(tp, info, own, right, left, weights, moves, count, vit_gain, merge_gain, blocks, buf):
    nb, feats, cols = own.shape
    per = cols // MERGE
    x_spec = pl.BlockSpec((1, feats, cols), lambda i, s: (i, 0, 0))
    anywhere = pl.BlockSpec(memory_space=pl.ANY)
    ins = [own, *right, *left, *weights, vit_gain, merge_gain]
    specs = [x_spec] * (2 * tp - 1) + [anywhere] * len(weights)
    specs += [pl.BlockSpec((DV, 1), lambda i, s: (0, 0)), pl.BlockSpec((1, DV), lambda i, s: (0, 0))]
    alias = {}
    if buf is not None:
        ins.append(buf)
        specs.append(anywhere)
        alias = {len(ins): 0}
    return pl.pallas_call(
        functools.partial(attend_kernel, tp, moves, len(weights), buf is not None),
        out_shape=jax.ShapeDtypeStruct((MERGE, blocks, per, DV), BF),
        grid_spec=pltpu.PrefetchScalarGridSpec(
            num_scalar_prefetch=1,
            grid=(nb,),
            in_specs=specs,
            out_specs=pl.BlockSpec((MERGE, 1, per, DV), lambda i, s: (0, s[2 + i], 0, 0)),
            scratch_shapes=[
                pltpu.VMEM((4 * DV, DV), BF),
                pltpu.VMEM((DV, cols), BF),
                pltpu.VMEM((DV, cols), BF),
                pltpu.VMEM((3 * DV // tp, cols), BF),
                pltpu.VMEM((DV, cols), BF),
                pltpu.VMEM((cols, DV), BF),
                pltpu.VMEM((cols, cols), F32),
                pltpu.SemaphoreType.DMA((count,)),
            ],
        ),
        input_output_aliases=alias,
        compiler_params=pltpu.CompilerParams(
            vmem_limit_bytes=48 * MIB, dimension_semantics=("arbitrary",)
        ),
        cost_estimate=pl.CostEstimate(
            flops=nb * cols * DV * DV * 10,
            bytes_accessed=14 * MIB,
            transcendentals=nb * cols * cols * HV,
        ),
        name="attend",
    )(info, *ins)


def project_kernel(moves, position, nw, info, *refs):
    merged = refs[0]
    w_refs = refs[1 : 1 + nw]
    w_cache, llm_gain, out = refs[1 + nw : 4 + nw]
    held, slots, cache, acc, scaled, held_sem, slot_sem, cache_sem = refs[4 + nw :]
    units = scaled.shape[1]
    half = units // 2
    rows = held.shape[1]
    depth = slots.shape[0]
    width = min(256, half)
    chunks = [(h, i) for h in range(2) for i in range(MERGE)]

    def bring(n):
        return moves(info, w_refs, *chunks[n], slots.at[n % depth], slot_sem.at[n % depth])

    def bring_merged(i):
        c = position(info, i)
        return pltpu.make_async_copy(merged.at[c], held.at[c], held_sem.at[i])

    load_cache = pltpu.make_async_copy(w_cache, cache, cache_sem)
    for n in range(depth):
        bring_merged(n).start()
        for copy in bring(n):
            copy.start()
    for n in range(depth, MERGE):
        bring_merged(n).start()
    load_cache.start()
    total = jnp.zeros((rows, 1), F32)
    for n, (h, i) in enumerate(chunks):
        c = position(info, i)
        if h == 0:
            bring_merged(i).wait()
        for copy in bring(n):
            copy.wait()
        slot = n % depth

        def tile(j, carry):
            spot = pl.ds(pl.multiple_of(j * width, width), width)
            d = jnp.dot(held[c], slots[slot, :, spot], preferred_element_type=F32)
            if i == 0:
                acc[:, spot] = d
            else:
                acc[:, spot] += d
            return carry

        lax.fori_loop(0, half // width, tile, 0)
        if n + depth < len(chunks):
            for copy in bring(n + depth):
                copy.start()
        if i == MERGE - 1:
            hidden = acc[...].astype(BF).astype(F32)
            total = total + jnp.sum(hidden * hidden, axis=1, keepdims=True)
            part = slice(h * half, (h + 1) * half)
            scaled[:, part] = (hidden * llm_gain[:, part]).astype(BF)
    load_cache.wait()
    kvw = cache.shape[1]

    def kv_tile(j, carry):
        spot = pl.ds(pl.multiple_of(j * 256, 256), 256)
        out[:, spot] = jnp.dot(scaled[...], cache[:, spot], preferred_element_type=F32).astype(BF)
        return carry

    lax.fori_loop(0, kvw // 256, kv_tile, 0)
    out[:, kvw:] = jnp.broadcast_to(total, (rows, 128)).astype(BF)


def project(info, merged, weights, moves, position, w_cache, llm_gain):
    units, kvw = w_cache.shape
    rows = merged.shape[1] * merged.shape[2]
    anywhere = pl.BlockSpec(memory_space=pl.ANY)
    return pl.pallas_call(
        functools.partial(project_kernel, moves, position, len(weights)),
        out_shape=jax.ShapeDtypeStruct((rows, kvw + 128), BF),
        grid_spec=pltpu.PrefetchScalarGridSpec(
            num_scalar_prefetch=1,
            grid=(1,),
            in_specs=[anywhere] * (len(weights) + 2)
            + [pl.BlockSpec((1, units), lambda i, s: (0, 0))],
            out_specs=pl.BlockSpec((rows, kvw + 128), lambda i, s: (0, 0)),
            scratch_shapes=[
                pltpu.VMEM((MERGE, rows, DV), BF),
                pltpu.VMEM((3, DV, units // 2), BF),
                pltpu.VMEM((units, kvw), BF),
                pltpu.VMEM((rows, units // 2), F32),
                pltpu.VMEM((rows, units), BF),
                pltpu.SemaphoreType.DMA((MERGE,)),
                pltpu.SemaphoreType.DMA((3, 2)),
                pltpu.SemaphoreType.DMA,
            ],
        ),
        compiler_params=pltpu.CompilerParams(
            vmem_limit_bytes=48 * MIB, dimension_semantics=("arbitrary",)
        ),
        cost_estimate=pl.CostEstimate(
            flops=2 * rows * units * (MERGE * DV + kvw),
            bytes_accessed=36 * MIB,
            transcendentals=0,
        ),
        name="project",
    )(info, merged.reshape(MERGE, rows, DV), *weights, w_cache, llm_gain)


def shards(
    patches, route, order, tiles, w_qkv, w_proj, vit_gain, merge_gain, w_merge, llm_gain, w_cache
):
    seq_count = lax.axis_size("seq")
    tp = lax.axis_size("tp")
    s = lax.axis_index("seq").astype(jnp.int32)
    t = lax.axis_index("tp").astype(jnp.int32)
    win_dev = order.shape[1]
    feats = patches.shape[1]
    per_peer = win_dev // seq_count
    tokens = WIN // MERGE
    blocks = win_dev // GROUP
    picks = order[0]
    tile_index = picks // TILE_WIN
    counts = jnp.take(tiles, tile_index // TILE_SLOTS)
    live = (tile_index % TILE_SLOTS < counts).astype(jnp.int32)
    arrange = jnp.argsort(route[:, 0], stable=True)
    live_send = jnp.take(live, arrange).reshape(seq_count, per_peer)
    live_here = lax.all_to_all(live_send, "seq", split_axis=0, concat_axis=0, tiled=True)
    window = jnp.take(picks, arrange).reshape(seq_count, per_peer)

    def xor(x, d):
        return lax.ppermute(x, "seq", [(i, i ^ d) for i in range(seq_count)])

    def along(x, k):
        return lax.ppermute(x, "tp", [(i, i + k) for i in range(tp) if 0 <= i + k < tp])

    def spread(x):
        right, left = [], []
        for _ in range(tp - 1):
            right.append(along(right[-1] if right else x, -1))
            left.append(along(left[-1] if left else x, 1))
        return right, left

    paired = per_peer == GROUP and seq_count == 8
    peers = jnp.arange(seq_count, dtype=jnp.int32)
    if paired:
        window = jnp.take(window, s ^ peers, axis=0)
    source = (
        window[:, None, :, None] * WIN
        + jnp.arange(tokens)[None, None, None, :] * MERGE
        + jnp.arange(MERGE)[None, :, None, None]
    ).reshape(-1)
    pick = (jnp.arange(patches.shape[0])[:, None] == source[None, :]).astype(BF)
    sent = lax.dot_general(
        patches, pick, (((0,), (0,)), ((), ())), preferred_element_type=F32
    ).astype(BF)
    step = per_peer * WIN
    wq_t = w_qkv.T

    if paired:
        parts = [sent[:, d * step : (d + 1) * step] for d in range(seq_count)]
        parts = [p if d == 0 else xor(p, d) for d, p in enumerate(parts)]
        groups = [jnp.stack(parts[:4]), jnp.stack(parts[4:])]
        places = [s ^ peers[:4], s ^ peers[4:]]

        share = (wq_t.shape[0] + w_proj.shape[0]) // seq_count
        q_parts = wq_t.shape[0] // share
        mine = jnp.where(
            s < q_parts,
            lax.dynamic_slice_in_dim(wq_t, jnp.minimum(s, q_parts - 1) * share, share),
            lax.dynamic_slice_in_dim(w_proj, jnp.maximum(s - q_parts, 0) * share, share),
        )
        right, left = spread(mine)
        others = jnp.concatenate(
            [jnp.where(t + j < tp, right[j - 1], left[tp - j - 1]) for j in range(1, tp)]
        )

        def plane(x):
            mid = x.shape[1] // 2
            halves = []
            for piece, bits in ((x[:, :mid], (2, 4)), (x[:, mid:], (4, 2))):
                held = {0: piece}
                for b in bits:
                    held.update({k ^ b: xor(v, b) for k, v in list(held.items())})
                held.update({k ^ 1: xor(v, 1) for k, v in list(held.items())})
                halves.append([held[d] for d in range(seq_count)])
            return halves

        vit_halves = plane(others)
        merge_halves = plane(w_merge)
        vit_weights = [wq_t, w_proj] + vit_halves[0] + vit_halves[1]
        merge_weights = merge_halves[0] + merge_halves[1]
        q_rows, p_rows = wq_t.shape[0], w_proj.shape[0]
        vit_count = 2 + 2 * seq_count * (tp - 1)

        def vit_moves(info, refs, w, sem):
            t, s = info[0], info[1]
            copies = [
                pltpu.make_async_copy(
                    refs[0], w.at[pl.ds(pl.multiple_of(t * q_rows, 16), q_rows)], sem.at[0]
                ),
                pltpu.make_async_copy(
                    refs[1], w.at[pl.ds(pl.multiple_of(3 * DV + t * p_rows, 16), p_rows)], sem.at[1]
                ),
            ]
            for h in range(2):
                for d in range(seq_count):
                    part = s ^ d
                    for j in range(1, tp):
                        q = lax.rem(t + j, tp)
                        row = jnp.where(
                            part < q_parts,
                            q * q_rows + part * share,
                            3 * DV + q * p_rows + (part - q_parts) * share,
                        )
                        copies.append(
                            pltpu.make_async_copy(
                                refs[2 + h * seq_count + d].at[(j - 1) * share : j * share],
                                w.at[
                                    pl.ds(pl.multiple_of(row, 16), share),
                                    h * (DV // 2) : (h + 1) * (DV // 2),
                                ],
                                sem.at[len(copies)],
                            )
                        )
            return copies

        def merge_moves(info, refs, h, i, slot, sem):
            s = info[1]
            rows = refs[0].shape[0]
            copies = []
            for e in range(2):
                at = pl.multiple_of(((s & 1) ^ e) * rows, 16)
                copies.append(
                    pltpu.make_async_copy(
                        refs[h * seq_count + 2 * i + e], slot.at[pl.ds(at, rows)], sem.at[e]
                    )
                )
            return copies

        def position(info, i):
            return (info[1] // 2) ^ i

    else:
        full = lax.all_to_all(
            sent.reshape(feats, seq_count, step).transpose(1, 0, 2),
            "seq",
            split_axis=0,
            concat_axis=0,
            tiled=True,
        )
        full = full.reshape(blocks, GROUP // per_peer, feats, MERGE, per_peer, tokens)
        groups = [full.transpose(0, 2, 3, 1, 4, 5).reshape(blocks, feats, GROUP * WIN)]
        places = [jnp.arange(blocks, dtype=jnp.int32)]
        vit_weights = [
            lax.all_gather(wq_t, "tp", axis=0, tiled=True),
            lax.all_gather(w_proj, "tp", axis=0, tiled=True),
        ]
        merge_weights = [lax.all_gather(w_merge, "seq", axis=0, tiled=True)]
        vit_count = 2

        def vit_moves(info, refs, w, sem):
            return [
                pltpu.make_async_copy(refs[0], w.at[0 : 3 * DV], sem.at[0]),
                pltpu.make_async_copy(refs[1], w.at[3 * DV : 4 * DV], sem.at[1]),
            ]

        def merge_moves(info, refs, h, i, slot, sem):
            wide = slot.shape[1]
            part = refs[0].at[i * DV : (i + 1) * DV, h * wide : (h + 1) * wide]
            return [pltpu.make_async_copy(part, slot, sem.at[0])]

        def position(info, i):
            return i

    merged = None
    for own, place in zip(groups, places):
        info = jnp.concatenate([jnp.stack([t, s]), place])
        right, left = spread(own)
        merged = attend(
            tp, info, own, right, left, vit_weights, vit_moves, vit_count,
            vit_gain[:, None], merge_gain[None, :], blocks, merged,
        )
    partial_value = project(
        jnp.stack([t, s]), merged, merge_weights, merge_moves, position, w_cache, llm_gain[None, :]
    )
    summed = lax.psum_scatter(partial_value, "tp", scatter_dimension=0, tiled=True).astype(F32)
    kvw = w_cache.shape[1]
    cache, total_squares = summed[:, :kvw], summed[:, kvw : kvw + 1]
    share = cache.shape[0]
    live_tokens = jnp.repeat(live_here.reshape(-1), tokens)
    mine = lax.dynamic_slice_in_dim(live_tokens, t * share, share).astype(F32)
    return (cache * lax.rsqrt(total_squares / D + 1e-6) * mine[:, None]).astype(BF)


def solution(mesh):
    return jax.shard_map(
        shards,
        mesh=mesh,
        in_specs=(
            P("seq", "tp"),
            P("seq", None),
            P("seq", None),
            P("seq"),
            P(None, "tp"),
            P("tp", None),
            P(),
            P(),
            P("seq", "tp"),
            P("tp"),
            P("tp", None),
        ),
        out_specs=P(("seq", "tp"), None),
        check_vma=False,
    )
```

time: 683 us -> 384 us (0.56)
  waiting for transfers between devices: 418 us -> 142 us
  Pallas kernels: 0 us -> 124 us
  local copies, waits for them, and re-layouts: 97.2 us -> 9.97 us
  starting transfers between devices: 4.38 us -> 77.9 us
  blocking collectives: 64 us -> 0 us
  matrix products: 51.7 us -> 3.45 us
  other arithmetic: 31.8 us -> 12.2 us
    all_gather x2 -> x0, waiting for transfers between devices: 187 us -> none  [the longest x1 187 us: shards(): full = lax.all_gather(send, 'tp', axis=3, tiled=True)]
    psum x1 -> x0, waiting for transfers between devices: 185 us -> none  [attend_windows(): lax.psum(partial_value.astype(jnp.bfloat16), 'tp').astype(jnp.float32)]
    pallas_call x0 -> x3, Pallas kernels: none -> 124 us  [the longest x2 97.4 us: attend(): pl.pallas_call(functools.partial(attend_kernel, tp, moves, len(weights),...]
    ppermute x0 -> x53, waiting for transfers between devices: none -> 99.7 us  [the longest x18 54 us: along(): lax.ppermute(x, 'tp', [(i, i + k) for i in range(tp) if 0 <= i + k < tp])]
    ppermute x0 -> x53, starting transfers between devices: none -> 74.6 us  [the longest x18 56.3 us: along(): lax.ppermute(x, 'tp', [(i, i + k) for i in range(tp) if 0 <= i + k < tp])]
    all_to_all x1 -> x0, blocking collectives: 64 us -> none  [shards(): lax.all_to_all(full, 'seq', split_axis=0, concat_axis=0, tiled=True)]
    dot_general x6 -> x1, matrix products: 51.7 us -> 3.45 us  [shards(): lax.dot_general(patches, pick, (((0,), (0,)), ((), ())), preferred_elemen...]
    unnamed x20 -> x60, local copies, waits for them, and re-layouts: 27.1 us -> 1.16 us
  transfers between devices with their start and end apart: 6 -> 55, of which waited for: 4 -> 19; matrix products, arithmetic and copies ran while one was open for 7% -> 2% of each run, Pallas kernels for 0% -> 25%
where the time goes in v1:
time: 384 us; the launch traced here: 383 us
  waiting for transfers between devices  142 us (37%)
  Pallas kernels  124 us (32%)
  starting transfers between devices  77.9 us (20%)
  between operations  14.1 us (4%)
  other arithmetic  12.2 us (3%)
  local copies, waits for them, and re-layouts  9.97 us (3%)
    pallas_call x2, Pallas kernels, attend(): pl.pallas_call(functools.partial(attend_kernel, tp, moves, len(weights),...  97.4 us
    ppermute x18, starting transfers between devices, along(): lax.ppermute(x, 'tp', [(i, i + k) for i in range(tp) if 0 <= i + k < tp])  56.3 us
    ppermute x18, waiting for transfers between devices, along(): lax.ppermute(x, 'tp', [(i, i + k) for i in range(tp) if 0 <= i + k < tp])  54 us
    ppermute x35, waiting for transfers between devices, xor(): return lax.ppermute(x, 'seq', [(i, i ^ d) for i in range(seq_count)])  45.7 us
    reduce_scatter x1, waiting for transfers between devices, shards(): lax.psum_scatter(partial_value, 'tp', scatter_dimension=0, tiled=True)  37.5 us
    pallas_call x1, Pallas kernels, project(): pl.pallas_call(functools.partial(project_kernel, moves, position, len(wei...  26.6 us
    ppermute x35, starting transfers between devices, xor(): return lax.ppermute(x, 'seq', [(i, i ^ d) for i in range(seq_count)])  18.3 us
  transfers between devices with their start and end apart: 55, of which 19 were waited for; matrix products, arithmetic and copies ran while one was open for 2% of the time, Pallas kernels for 25%

profile of v1, /device:TPU:0, one launch (start us, length us, event | category | flops | bytes accessed | tf_op | source)
XLA Modules:
  0.0 383.4 jit_solution(8206888206827144598)
XLA Ops:
  6.6 2.4 sort.17
  8.9 1.3 fusion.13
  10.3 2.0 compare_convert_fusion
  12.3 0.7 gather_fusion.2
  13.0 1.4 gather_fusion.1
  15.3 3.5 fusion.3
  18.8 3.4 collective-permute-start.3
  22.2 1.1 bitcast_select_fusion
  23.3 3.5 collective-permute-start.11
  26.9 1.3 collective-permute-start.10
  28.2 1.6 collective-permute-start.2
  29.9 0.7 collective-permute-start
  30.7 5.1 %collective-permute-done.2 = bf16[320,256]{1,0:T(8,128)(2,1)S(1)} collective-permute-done((bf16[320,256]{1,0:T(8,128)(2,1)S(1)}, bf16[320,256]{1,0:T(8,128)(2,1)S(1)}, u32[]{:S(2)}, u32[]{:S(2)}) %collective-permute-start.2) | collective-permute-done | bytes 163872 | tf_op jit(solution)/shard_map/ppermute | solution.py:281
  35.8 3.4 collective-permute-done.1
  39.6 3.0 collective-permute-done
  42.8 4.3 %collective-permute-start.7 = (bf16[4,320,256]{2,1,0:T(8,128)(2,1)S(1)}, bf16[4,320,256]{2,1,0:T(8,128)(2,1)S(1)}, u32[]{:S(2)}, u32[]{:S(2)}) collective-permute-start(bf16[4,320,256]{2,1,0:T(8,128)(2,1)S(1)} %pad_maximum_fusion.1.refs_0_), channel_id=1, source_target_pairs={{0,1},{1,2},{2,3},{4,5},{5,6},{6,7},{8,9},{9,10},{10,11},{12,13},{... | collective-permute-start | bytes 1966088 | tf_op jit(solution)/shard_map/ppermute | solution.py:284
  47.2 1.3 collective-permute-start.4
  48.5 5.3 %collective-permute-start.12 = (bf16[160,1280]{1,0:T(8,128)(2,1)S(1)}, bf16[160,1280]{1,0:T(8,128)(2,1)}, u32[]{:S(2)}, u32[]{:S(2)}) collective-permute-start(bf16[160,1280]{1,0:T(8,128)(2,1)S(1)} %collective-permute-done.11), channel_id=1, source_target_pairs={{0,1},{1,2},{2,3},{4,5},{5,6},{6,7},{8,9},{9,10},{10,11},{12,13},{... | collective-permute-start | bytes 1228808 | tf_op jit(solution)/shard_map/ppermute | solution.py:284
  53.8 1.3 collective-permute-start.14
  55.1 2.0 fusion.11
  57.7 1.0 pad_maximum_fusion.2.refs_0_
  58.6 11.8 %collective-permute-done.12 = bf16[160,1280]{1,0:T(8,128)(2,1)} collective-permute-done((bf16[160,1280]{1,0:T(8,128)(2,1)S(1)}, bf16[160,1280]{1,0:T(8,128)(2,1)}, u32[]{:S(2)}, u32[]{:S(2)}) %collective-permute-start.12) | collective-permute-done | bytes 409632 | tf_op jit(solution)/shard_map/ppermute | solution.py:284
  70.4 5.3 %collective-permute-start.36 = (bf16[4,320,256]{2,1,0:T(8,128)(2,1)}, bf16[4,320,256]{2,1,0:T(8,128)(2,1)}, u32[]{:S(2)}, u32[]{:S(2)}) collective-permute-start(bf16[4,320,256]{2,1,0:T(8,128)(2,1)} %pad_maximum_fusion.2.refs_0_), channel_id=1, source_target_pairs={{0,1},{1,2},{2,3},{4,5},{5,6},{6,7},{8,9},{9,10},{10,11},{12,13},{... | collective-permute-start | bytes 1966088 | tf_op jit(solution)/shard_map/ppermute | solution.py:284
  75.7 1.3 collective-permute-start.33
  77.1 5.3 %collective-permute-start.13 = (bf16[160,1280]{1,0:T(8,128)(2,1)}, bf16[160,1280]{1,0:T(8,128)(2,1)}, u32[]{:S(2)}, u32[]{:S(2)}) collective-permute-start(bf16[160,1280]{1,0:T(8,128)(2,1)} %collective-permute-done.12), channel_id=1, source_target_pairs={{0,1},{1,2},{2,3},{4,5},{5,6},{6,7},{8,9},{9,10},{10,11},{12,13},{... | collective-permute-start | bytes 1228808 | tf_op jit(solution)/shard_map/ppermute | solution.py:284
  82.4 0.9 copy-done.17
  83.3 1.3 collective-permute-start.15
  84.6 5.8 %collective-permute-done.36.refs_4_ = bf16[4,320,256]{2,1,0:T(8,128)(2,1)} collective-permute-done((bf16[4,320,256]{2,1,0:T(8,128)(2,1)}, bf16[4,320,256]{2,1,0:T(8,128)(2,1)}, u32[]{:S(2)}, u32[]{:S(2)}) %collective-permute-start.36) | collective-permute-done | bytes 655392 | tf_op jit(solution)/shard_map/ppermute | solution.py:284
  90.9 4.7 %collective-permute-done.33.refs_1_ = bf16[4,320,256]{2,1,0:T(8,128)(2,1)} collective-permute-done((bf16[4,320,256]{2,1,0:T(8,128)(2,1)}, bf16[4,320,256]{2,1,0:T(8,128)(2,1)}, u32[]{:S(2)}, u32[]{:S(2)}) %collective-permute-start.33) | collective-permute-done | bytes 655392 | tf_op jit(solution)/shard_map/ppermute | solution.py:284
  95.6 2.1 collective-permute-done.13
  97.7 0.7 collective-permute-start.42
  98.3 4.3 %collective-permute-done.15 = bf16[160,1280]{1,0:T(8,128)(2,1)} collective-permute-done((bf16[160,1280]{1,0:T(8,128)(2,1)}, bf16[160,1280]{1,0:T(8,128)(2,1)}, u32[]{:S(2)}, u32[]{:S(2)}) %collective-permute-start.15) | collective-permute-done | bytes 409632 | tf_op jit(solution)/shard_map/ppermute | solution.py:284
  103.2 1.0 broadcast_select_fusion.1
  104.5 1.1 broadcast_select_fusion
  105.6 16.4 %collective-permute-done.47.refs_11_ = bf16[640,1024]{1,0:T(8,128)(2,1)S(1)} collective-permute-done((bf16[640,1024]{1,0:T(8,128)(2,1)S(1)}, bf16[640,1024]{1,0:T(8,128)(2,1)S(1)}, u32[]{:S(2)}, u32[]{:S(2)}) %collective-permute-start.47) | collective-permute-done | bytes 1310752 | tf_op jit(solution)/shard_map/ppermute | solution.py:281
  122.1 5.2 %collective-permute-start.8 = (bf16[4,320,256]{2,1,0:T(8,128)(2,1)S(1)}, bf16[4,320,256]{2,1,0:T(8,128)(2,1)}, u32[]{:S(2)}, u32[]{:S(2)}) collective-permute-start(bf16[4,320,256]{2,1,0:T(8,128)(2,1)S(1)} %copy-done.16), channel_id=1, source_target_pairs={{0,1},{1,2},{2,3},{4,5},{5,6},{6,7},{8,9},{9,10},{10,11},{12,13},{... | collective-permute-start | bytes 1966088 | tf_op jit(solution)/shard_map/ppermute | solution.py:284
  127.3 1.3 collective-permute-start.5
  128.6 4.6 %collective-permute-start.37 = (bf16[4,320,256]{2,1,0:T(8,128)(2,1)}, bf16[4,320,256]{2,1,0:T(8,128)(2,1)S(1)}, u32[]{:S(2)}, u32[]{:S(2)}) collective-permute-start(bf16[4,320,256]{2,1,0:T(8,128)(2,1)} %collective-permute-done.36.refs_4_), channel_id=1, source_target_pairs={{0,1},{1,2},{2,3},{4,5},{5,6},{6,7},{8,9},{9,10},{10,11},{12,13},{... | collective-permute-start | bytes 1966088 | tf_op jit(solution)/shard_map/ppermute | solution.py:284
  133.2 13.1 %collective-permute-done.40.refs_3_ = bf16[640,1024]{1,0:T(8,128)(2,1)S(1)} collective-permute-done((bf16[640,1024]{1,0:T(8,128)(2,1)S(1)}, bf16[640,1024]{1,0:T(8,128)(2,1)S(1)}, u32[]{:S(2)}, u32[]{:S(2)}) %collective-permute-start.40) | collective-permute-done | bytes 1310752 | tf_op jit(solution)/shard_map/ppermute | solution.py:281
  146.3 1.3 collective-permute-start.34
  147.7 0.8 collective-permute-start.26
  149.1 1.4 collective-permute-start.19
  150.5 11.6 %collective-permute-done.34.refs_2_ = bf16[4,320,256]{2,1,0:T(8,128)(2,1)S(1)} collective-permute-done((bf16[4,320,256]{2,1,0:T(8,128)(2,1)}, bf16[4,320,256]{2,1,0:T(8,128)(2,1)S(1)}, u32[]{:S(2)}, u32[]{:S(2)}) %collective-permute-start.34) | collective-permute-done | bytes 655392 | tf_op jit(solution)/shard_map/ppermute | solution.py:284
  162.7 1.9 collective-permute-done.26.refs_21_
  164.6 5.1 %collective-permute-start.38 = (bf16[4,320,256]{2,1,0:T(8,128)(2,1)S(1)}, bf16[4,320,256]{2,1,0:T(8,128)(2,1)S(1)}, u32[]{:S(2)}, u32[]{:S(2)}) collective-permute-start(bf16[4,320,256]{2,1,0:T(8,128)(2,1)S(1)} %collective-permute-done.37.refs_5_), channel_id=1, source_target_pairs={{0,1},{1,2},{2,3},{4,5},{5,6},{6,7},{8,9},{9,10},{10,11},{12,13},{... | collective-permute-start | bytes 1966088 | tf_op jit(solution)/shard_map/ppermute | solution.py:284
  169.7 1.3 collective-permute-start.35
  171.0 2.0 collective-permute-done.19.refs_13_
  173.7 1.2 collective-permute-start.21
  174.8 9.4 %collective-permute-done.38.refs_6_ = bf16[4,320,256]{2,1,0:T(8,128)(2,1)S(1)} collective-permute-done((bf16[4,320,256]{2,1,0:T(8,128)(2,1)S(1)}, bf16[4,320,256]{2,1,0:T(8,128)(2,1)S(1)}, u32[]{:S(2)}, u32[]{:S(2)}) %collective-permute-start.38) | collective-permute-done | bytes 655392 | tf_op jit(solution)/shard_map/ppermute | solution.py:284
  184.3 4.4 %collective-permute-done.35.refs_3_ = bf16[4,320,256]{2,1,0:T(8,128)(2,1)S(1)} collective-permute-done((bf16[4,320,256]{2,1,0:T(8,128)(2,1)S(1)}, bf16[4,320,256]{2,1,0:T(8,128)(2,1)S(1)}, u32[]{:S(2)}, u32[]{:S(2)}) %collective-permute-start.35) | collective-permute-done | bytes 655392 | tf_op jit(solution)/shard_map/ppermute | solution.py:284
  190.3 1.1 broadcast_in_dim.52.refs_25_
  191.8 1.1 collective-permute-start.51
  193.1 0.9 collective-permute-start.44
  194.0 5.9 %collective-permute-start.9 = (bf16[4,320,256]{2,1,0:T(8,128)(2,1)}, bf16[4,320,256]{2,1,0:T(8,128)(2,1)}, u32[]{:S(2)}, u32[]{:S(2)}) collective-permute-start(bf16[4,320,256]{2,1,0:T(8,128)(2,1)} %collective-permute-done.8.refs_5_), channel_id=1, source_target_pairs={{0,1},{1,2},{2,3},{4,5},{5,6},{6,7},{8,9},{9,10},{10,11},{12,13},{... | collective-permute-start | bytes 1966088 | tf_op jit(solution)/shard_map/ppermute | solution.py:284
  199.9 1.5 collective-permute-start.6
  201.4 48.7 %attend.2.refs_27_ = bf16[4,8,64,1280]{3,2,1,0:T(8,128)(2,1)} custom-call(s32[6]{0:T(128)S(1)} %pad_add_fusion.3.info, bf16[4,320,256]{2,1,0:T(8,128)(2,1)} %pad_maximum_fusion.2.refs_0_, bf16[4,320,256]{2,1,0:T(8,128)(2,1)} %collective-permute-done.33.refs_1_, bf16[4,320,256]{2,1,0:T(8,128)(2,1)} %copy-done.21, bf16[4,320,256]{2,1,0:T(8,128)(2,1)} %copy-done.23, ...), custom_call_target="tpu_custom_call" | custom-call | flops 16777216000 | bytes 14680064 | tf_op jit(solution)/shard_map/attend/pallas_call | solution.py:125
  251.4 48.7 %attend.3 = bf16[4,8,64,1280]{3,2,1,0:T(8,128)(2,1)} custom-call(s32[6]{0:T(128)S(1)} %pad_add_fusion.1.info, bf16[4,320,256]{2,1,0:T(8,128)(2,1)} %copy-done.4, bf16[4,320,256]{2,1,0:T(8,128)(2,1)} %copy-done.17, bf16[4,320,256]{2,1,0:T(8,128)(2,1)} %copy-done.19, ...), custom_call_target="tpu_custom_call", output_to_operand_aliasing={{}: (28, {})} | custom-call | flops 16777216000 | bytes 14680064 | tf_op jit(solution)/shard_map/attend/pallas_call | solution.py:125
  300.2 26.6 %project.1 = bf16[512,2176]{1,0:T(8,128)(2,1)} custom-call(s32[2]{0:T(128)S(1)} %pad_add_fusion.info, bf16[4,512,1280]{2,1,0:T(8,128)(2,1)} %bitcast.53, bf16[640,1024]{1,0:T(8,128)(2,1)S(1)} %get-tuple-element.9.refs_1_, bf16[640,1024]{1,0:T(8,128)(2,1)S(1)} %collective-permute-done.39.refs_2_, bf16[640,1024]{1,0:T(8,128)(2,1)S(1)} %collective-permute-done.40.refs_3_, ...), custom_call_target="tpu_custom_call" | custom-call | flops 15032385536 | bytes 37748736 | tf_op jit(solution)/shard_map/project/pallas_call | solution.py:227
  326.8 0.7 all_to_all.6
  327.5 3.3 all-to-all-start
  330.8 4.5 %all-to-all-done = s32[8,1,4]{2,1,0:T(1,128)S(1)} async-done(((s32[8,1,4]{2,1,0:T(1,128)}), s32[8,1,4]{2,1,0:T(1,128)S(1)}, u32[]{:S(2)}, u32[]{:S(2)}) %all-to-all-start) | async-done | bytes 160 | tf_op jit(solution)/shard_map/all_to_all | solution.py:277
  336.8 37.5 %reduce-scatter.2.cloned.1.call-done = bf16[128,2176]{1,0:T(8,128)(2,1)} async-done(((bf16[512,2176]{1,0:T(8,128)(2,1)}), bf16[128,2176]{1,0:T(8,128)(2,1)}) %reduce-scatter.2.cloned.1.call-update) | async-done | bytes 557072 | tf_op jit(solution)/shard_map/reduce_scatter | solution.py:436
  374.3 1.1 convert_element_type.21
  375.5 1.0 fusion.5
  (159 shorter events, 10.9 us)
Async XLA Ops:
  6.5 367.8 %reduce-scatter.2.cloned.1.call-start = ((), (), s32[]{:S(2)}) async-start(), calls=%async_computation.2 | async-start | bytes 2785280 | tf_op jit(solution)/shard_map/reduce_scatter | solution.py:436
  18.8 11.1 %collective-permute-start.3 = (bf16[320,256]{1,0:T(8,128)(2,1)S(1)}, bf16[320,256]{1,0:T(8,128)(2,1)S(1)}, u32[]{:S(2)}, u32[]{:S(2)}) collective-permute-start(bf16[320,256]{1,0:T(8,128)(2,1)S(1)} %get-tuple-element.14), channel_id=1, source_target_pairs={{0,28},{4,24},{8,20},{12,16},{16,12},{20,8},{24,4},{28,0},{1,29},{... | collective-permute-start | bytes 491528 | tf_op jit(solution)/shard_map/ppermute | solution.py:281
  23.3 25.1 %collective-permute-start.11 = (bf16[160,1280]{1,0:T(8,128)(2,1)S(1)}, bf16[160,1280]{1,0:T(8,128)(2,1)S(1)}, u32[]{:S(2)}, u32[]{:S(2)}) collective-permute-start(bf16[160,1280]{1,0:T(8,128)(2,1)S(1)} %bitcast_select_fusion), channel_id=1, source_target_pairs={{0,1},{1,2},{2,3},{4,5},{5,6},{6,7},{8,9},{9,10},{10,11},{12,13},{... | collective-permute-start | bytes 1228808 | tf_op jit(solution)/shard_map/ppermute | solution.py:284
  26.9 27.0 %collective-permute-start.10 = (bf16[160,1280]{1,0:T(8,128)(2,1)S(1)}, bf16[160,1280]{1,0:T(8,128)(2,1)S(1)}, u32[]{:S(2)}, u32[]{:S(2)}) collective-permute-start(bf16[160,1280]{1,0:T(8,128)(2,1)S(1)} %bitcast_select_fusion), channel_id=1, source_target_pairs={{1,0},{2,1},{3,2},{5,4},{6,5},{7,6},{9,8},{10,9},{11,10},{13,12},{... | collective-permute-start | bytes 1228808 | tf_op jit(solution)/shard_map/ppermute | solution.py:284
  28.2 7.6 %collective-permute-start.2 = (bf16[320,256]{1,0:T(8,128)(2,1)S(1)}, bf16[320,256]{1,0:T(8,128)(2,1)S(1)}, u32[]{:S(2)}, u32[]{:S(2)}) collective-permute-start(bf16[320,256]{1,0:T(8,128)(2,1)S(1)} %get-tuple-element.15), channel_id=1, source_target_pairs={{0,24},{4,28},{8,16},{12,20},{16,8},{20,12},{24,0},{28,4},{1,25},{... | collective-permute-start | bytes 491528 | tf_op jit(solution)/shard_map/ppermute | solution.py:281
  29.8 9.5 %collective-permute-start.1 = (bf16[320,256]{1,0:T(8,128)(2,1)S(1)}, bf16[320,256]{1,0:T(8,128)(2,1)S(1)}, u32[]{:S(2)}, u32[]{:S(2)}) collective-permute-start(bf16[320,256]{1,0:T(8,128)(2,1)S(1)} %get-tuple-element.16), channel_id=1, source_target_pairs={{0,20},{4,16},{8,28},{12,24},{16,4},{20,0},{24,12},{28,8},{1,21},{... | collective-permute-start | bytes 491528 | tf_op jit(solution)/shard_map/ppermute | solution.py:281
  29.9 12.7 %collective-permute-start = (bf16[320,256]{1,0:T(8,128)(2,1)S(1)}, bf16[320,256]{1,0:T(8,128)(2,1)S(1)}, u32[]{:S(2)}, u32[]{:S(2)}) collective-permute-start(bf16[320,256]{1,0:T(8,128)(2,1)S(1)} %get-tuple-element.17), channel_id=1, source_target_pairs={{0,16},{4,20},{8,24},{12,28},{16,0},{20,4},{24,8},{28,12},{1,17},{... | collective-permute-start | bytes 491528 | tf_op jit(solution)/shard_map/ppermute | solution.py:281
  35.8 7.1 %collective-permute-start.32 = (bf16[320,256]{1,0:T(8,128)(2,1)S(1)}, bf16[320,256]{1,0:T(8,128)(2,1)S(1)}, u32[]{:S(2)}, u32[]{:S(2)}) collective-permute-start(bf16[320,256]{1,0:T(8,128)(2,1)S(1)} %get-tuple-element.11), channel_id=1, source_target_pairs={{0,12},{4,8},{8,4},{12,0},{16,28},{20,24},{24,20},{28,16},{1,13},{... | collective-permute-start | bytes 491528 | tf_op jit(solution)/shard_map/ppermute | solution.py:281
  39.2 8.0 %collective-permute-start.31 = (bf16[320,256]{1,0:T(8,128)(2,1)S(1)}, bf16[320,256]{1,0:T(8,128)(2,1)S(1)}, u32[]{:S(2)}, u32[]{:S(2)}) collective-permute-start(bf16[320,256]{1,0:T(8,128)(2,1)S(1)} %get-tuple-element.12), channel_id=1, source_target_pairs={{0,8},{4,12},{8,0},{12,4},{16,24},{20,28},{24,16},{28,20},{1,9},{5... | collective-permute-start | bytes 491528 | tf_op jit(solution)/shard_map/ppermute | solution.py:281
  42.6 14.5 %collective-permute-start.30 = (bf16[320,256]{1,0:T(8,128)(2,1)S(1)}, bf16[320,256]{1,0:T(8,128)(2,1)S(1)}, u32[]{:S(2)}, u32[]{:S(2)}) collective-permute-start(bf16[320,256]{1,0:T(8,128)(2,1)S(1)} %get-tuple-element.13), channel_id=1, source_target_pairs={{0,4},{4,0},{8,12},{12,8},{16,20},{20,16},{24,28},{28,24},{1,5},{5... | collective-permute-start | bytes 491528 | tf_op jit(solution)/shard_map/ppermute | solution.py:281
  42.8 34.2 %collective-permute-start.7 = (bf16[4,320,256]{2,1,0:T(8,128)(2,1)S(1)}, bf16[4,320,256]{2,1,0:T(8,128)(2,1)S(1)}, u32[]{:S(2)}, u32[]{:S(2)}) collective-permute-start(bf16[4,320,256]{2,1,0:T(8,128)(2,1)S(1)} %pad_maximum_fusion.1.refs_0_), channel_id=1, source_target_pairs={{0,1},{1,2},{2,3},{4,5},{5,6},{6,7},{8,9},{9,10},{10,11},{12,13},{... | collective-permute-start | bytes 1966088 | tf_op jit(solution)/shard_map/ppermute | solution.py:284
  47.2 35.2 %collective-permute-start.4 = (bf16[4,320,256]{2,1,0:T(8,128)(2,1)S(1)}, bf16[4,320,256]{2,1,0:T(8,128)(2,1)S(1)}, u32[]{:S(2)}, u32[]{:S(2)}) collective-permute-start(bf16[4,320,256]{2,1,0:T(8,128)(2,1)S(1)} %pad_maximum_fusion.1.refs_0_), channel_id=1, source_target_pairs={{1,0},{2,1},{3,2},{5,4},{6,5},{7,6},{9,8},{10,9},{11,10},{13,12},{... | collective-permute-start | bytes 1966088 | tf_op jit(solution)/shard_map/ppermute | solution.py:284
  48.5 21.9 %collective-permute-start.12 = (bf16[160,1280]{1,0:T(8,128)(2,1)S(1)}, bf16[160,1280]{1,0:T(8,128)(2,1)}, u32[]{:S(2)}, u32[]{:S(2)}) collective-permute-start(bf16[160,1280]{1,0:T(8,128)(2,1)S(1)} %collective-permute-done.11), channel_id=1, source_target_pairs={{0,1},{1,2},{2,3},{4,5},{5,6},{6,7},{8,9},{9,10},{10,11},{12,13},{... | collective-permute-start | bytes 1228808 | tf_op jit(solution)/shard_map/ppermute | solution.py:284
  53.8 21.9 %collective-permute-start.14 = (bf16[160,1280]{1,0:T(8,128)(2,1)S(1)}, bf16[160,1280]{1,0:T(8,128)(2,1)}, u32[]{:S(2)}, u32[]{:S(2)}) collective-permute-start(bf16[160,1280]{1,0:T(8,128)(2,1)S(1)} %collective-permute-done.10), channel_id=1, source_target_pairs={{1,0},{2,1},{3,2},{5,4},{6,5},{7,6},{9,8},{10,9},{11,10},{13,12},{... | collective-permute-start | bytes 1228808 | tf_op jit(solution)/shard_map/ppermute | solution.py:284
  57.1 47.4 %copy-start.3 = (bf16[640,1024]{1,0:T(8,128)(2,1)}, bf16[640,1024]{1,0:T(8,128)(2,1)S(1)}, u32[]{:S(2)}) copy-start(bf16[640,1024]{1,0:T(8,128)(2,1)S(1)} %get-tuple-element.8.refs_9_) | copy-start | bytes 3932164
  57.1 47.2 %collective-permute-start.49 = (bf16[640,1024]{1,0:T(8,128)(2,1)S(1)}, bf16[640,1024]{1,0:T(8,128)(2,1)}, u32[]{:S(2)}, u32[]{:S(2)}) collective-permute-start(bf16[640,1024]{1,0:T(8,128)(2,1)S(1)} %get-tuple-element.8.refs_9_), channel_id=1, source_target_pairs={{0,16},{4,20},{8,24},{12,28},{16,0},{20,4},{24,8},{28,12},{1,17},{... | collective-permute-start | bytes 3932168 | tf_op jit(solution)/shard_map/ppermute | solution.py:281
  70.4 20.0 %collective-permute-start.36 = (bf16[4,320,256]{2,1,0:T(8,128)(2,1)}, bf16[4,320,256]{2,1,0:T(8,128)(2,1)}, u32[]{:S(2)}, u32[]{:S(2)}) collective-permute-start(bf16[4,320,256]{2,1,0:T(8,128)(2,1)} %pad_maximum_fusion.2.refs_0_), channel_id=1, source_target_pairs={{0,1},{1,2},{2,3},{4,5},{5,6},{6,7},{8,9},{9,10},{10,11},{12,13},{... | collective-permute-start | bytes 1966088 | tf_op jit(solution)/shard_map/ppermute | solution.py:284
  75.7 19.9 %collective-permute-start.33 = (bf16[4,320,256]{2,1,0:T(8,128)(2,1)}, bf16[4,320,256]{2,1,0:T(8,128)(2,1)}, u32[]{:S(2)}, u32[]{:S(2)}) collective-permute-start(bf16[4,320,256]{2,1,0:T(8,128)(2,1)} %pad_maximum_fusion.2.refs_0_), channel_id=1, source_target_pairs={{1,0},{2,1},{3,2},{5,4},{6,5},{7,6},{9,8},{10,9},{11,10},{13,12},{... | collective-permute-start | bytes 1966088 | tf_op jit(solution)/shard_map/ppermute | solution.py:284
  77.1 20.6 %collective-permute-start.13 = (bf16[160,1280]{1,0:T(8,128)(2,1)}, bf16[160,1280]{1,0:T(8,128)(2,1)}, u32[]{:S(2)}, u32[]{:S(2)}) collective-permute-start(bf16[160,1280]{1,0:T(8,128)(2,1)} %collective-permute-done.12), channel_id=1, source_target_pairs={{0,1},{1,2},{2,3},{4,5},{5,6},{6,7},{8,9},{9,10},{10,11},{12,13},{... | collective-permute-start | bytes 1228808 | tf_op jit(solution)/shard_map/ppermute | solution.py:284
  83.3 19.4 %collective-permute-start.15 = (bf16[160,1280]{1,0:T(8,128)(2,1)}, bf16[160,1280]{1,0:T(8,128)(2,1)}, u32[]{:S(2)}, u32[]{:S(2)}) collective-permute-start(bf16[160,1280]{1,0:T(8,128)(2,1)} %collective-permute-done.14), channel_id=1, source_target_pairs={{1,0},{2,1},{3,2},{5,4},{6,5},{7,6},{9,8},{10,9},{11,10},{13,12},{... | collective-permute-start | bytes 1228808 | tf_op jit(solution)/shard_map/ppermute | solution.py:284
  90.4 31.7 %collective-permute-start.47 = (bf16[640,1024]{1,0:T(8,128)(2,1)S(1)}, bf16[640,1024]{1,0:T(8,128)(2,1)S(1)}, u32[]{:S(2)}, u32[]{:S(2)}) collective-permute-start(bf16[640,1024]{1,0:T(8,128)(2,1)S(1)} %get-tuple-element.8.refs_9_), channel_id=1, source_target_pairs={{0,8},{4,12},{8,0},{12,4},{16,24},{20,28},{24,16},{28,20},{1,9},{5... | collective-permute-start | bytes 3932168 | tf_op jit(solution)/shard_map/ppermute | solution.py:281
  95.6 31.7 %collective-permute-start.46 = (bf16[640,1024]{1,0:T(8,128)(2,1)S(1)}, bf16[640,1024]{1,0:T(8,128)(2,1)S(1)}, u32[]{:S(2)}, u32[]{:S(2)}) collective-permute-start(bf16[640,1024]{1,0:T(8,128)(2,1)S(1)} %get-tuple-element.8.refs_9_), channel_id=1, source_target_pairs={{0,4},{4,0},{8,12},{12,8},{16,20},{20,16},{24,28},{28,24},{1,5},{5... | collective-permute-start | bytes 3932168 | tf_op jit(solution)/shard_map/ppermute | solution.py:281
  97.7 30.9 %collective-permute-start.42 = (bf16[640,1024]{1,0:T(8,128)(2,1)S(1)}, bf16[640,1024]{1,0:T(8,128)(2,1)S(1)}, u32[]{:S(2)}, u32[]{:S(2)}) collective-permute-start(bf16[640,1024]{1,0:T(8,128)(2,1)S(1)} %get-tuple-element.9.refs_1_), channel_id=1, source_target_pairs={{0,16},{4,20},{8,24},{12,28},{16,0},{20,4},{24,8},{28,12},{1,17},{... | collective-permute-start | bytes 3932168 | tf_op jit(solution)/shard_map/ppermute | solution.py:281
  102.6 43.7 %collective-permute-start.40 = (bf16[640,1024]{1,0:T(8,128)(2,1)S(1)}, bf16[640,1024]{1,0:T(8,128)(2,1)S(1)}, u32[]{:S(2)}, u32[]{:S(2)}) collective-permute-start(bf16[640,1024]{1,0:T(8,128)(2,1)S(1)} %get-tuple-element.9.refs_1_), channel_id=1, source_target_pairs={{0,8},{4,12},{8,0},{12,4},{16,24},{20,28},{24,16},{28,20},{1,9},{5... | collective-permute-start | bytes 3932168 | tf_op jit(solution)/shard_map/ppermute | solution.py:281
  104.3 43.4 %collective-permute-start.39 = (bf16[640,1024]{1,0:T(8,128)(2,1)S(1)}, bf16[640,1024]{1,0:T(8,128)(2,1)S(1)}, u32[]{:S(2)}, u32[]{:S(2)}) collective-permute-start(bf16[640,1024]{1,0:T(8,128)(2,1)S(1)} %get-tuple-element.9.refs_1_), channel_id=1, source_target_pairs={{0,4},{4,0},{8,12},{12,8},{16,20},{20,16},{24,28},{28,24},{1,5},{5... | collective-permute-start | bytes 3932168 | tf_op jit(solution)/shard_map/ppermute | solution.py:281
  105.6 84.7 %copy-start.8 = (f32[1280]{0:T(1024)S(1)}, f32[1280]{0:T(1024)}, u32[]{:S(2)}) copy-start(f32[1280]{0:T(1024)} %param.20) | copy-start | bytes 15364
  105.6 84.7 %copy-start.9 = (f32[1280]{0:T(1024)S(1)}, f32[1280]{0:T(1024)}, u32[]{:S(2)}) copy-start(f32[1280]{0:T(1024)} %param.19) | copy-start | bytes 15364
  122.1 128.2 %copy-start.10 = (bf16[640,1024]{1,0:T(8,128)(2,1)}, bf16[640,1024]{1,0:T(8,128)(2,1)S(1)}, u32[]{:S(2)}) copy-start(bf16[640,1024]{1,0:T(8,128)(2,1)S(1)} %collective-permute-done.47.refs_11_) | copy-start | bytes 3932164
  122.1 26.5 %collective-permute-start.8 = (bf16[4,320,256]{2,1,0:T(8,128)(2,1)S(1)}, bf16[4,320,256]{2,1,0:T(8,128)(2,1)}, u32[]{:S(2)}, u32[]{:S(2)}) collective-permute-start(bf16[4,320,256]{2,1,0:T(8,128)(2,1)S(1)} %copy-done.16), channel_id=1, source_target_pairs={{0,1},{1,2},{2,3},{4,5},{5,6},{6,7},{8,9},{9,10},{10,11},{12,13},{... | collective-permute-start | bytes 1966088 | tf_op jit(solution)/shard_map/ppermute | solution.py:284
  127.3 64.1 %copy-start.11 = (bf16[640,1024]{1,0:T(8,128)(2,1)}, bf16[640,1024]{1,0:T(8,128)(2,1)S(1)}, u32[]{:S(2)}) copy-start(bf16[640,1024]{1,0:T(8,128)(2,1)S(1)} %collective-permute-done.46.refs_10_) | copy-start | bytes 3932164
  127.3 21.8 %collective-permute-start.5 = (bf16[4,320,256]{2,1,0:T(8,128)(2,1)S(1)}, bf16[4,320,256]{2,1,0:T(8,128)(2,1)S(1)}, u32[]{:S(2)}, u32[]{:S(2)}) collective-permute-start(bf16[4,320,256]{2,1,0:T(8,128)(2,1)S(1)} %copy-done.18), channel_id=1, source_target_pairs={{1,0},{2,1},{3,2},{5,4},{6,5},{7,6},{9,8},{10,9},{11,10},{13,12},{... | collective-permute-start | bytes 1966088 | tf_op jit(solution)/shard_map/ppermute | solution.py:284
  128.6 20.5 %collective-permute-start.37 = (bf16[4,320,256]{2,1,0:T(8,128)(2,1)}, bf16[4,320,256]{2,1,0:T(8,128)(2,1)S(1)}, u32[]{:S(2)}, u32[]{:S(2)}) collective-permute-start(bf16[4,320,256]{2,1,0:T(8,128)(2,1)} %collective-permute-done.36.refs_4_), channel_id=1, source_target_pairs={{0,1},{1,2},{2,3},{4,5},{5,6},{6,7},{8,9},{9,10},{10,11},{12,13},{... | collective-permute-start | bytes 1966088 | tf_op jit(solution)/shard_map/ppermute | solution.py:284
  146.3 15.7 %collective-permute-start.34 = (bf16[4,320,256]{2,1,0:T(8,128)(2,1)}, bf16[4,320,256]{2,1,0:T(8,128)(2,1)S(1)}, u32[]{:S(2)}, u32[]{:S(2)}) collective-permute-start(bf16[4,320,256]{2,1,0:T(8,128)(2,1)} %collective-permute-done.33.refs_1_), channel_id=1, source_target_pairs={{1,0},{2,1},{3,2},{5,4},{6,5},{7,6},{9,8},{10,9},{11,10},{13,12},{... | collective-permute-start | bytes 1966088 | tf_op jit(solution)/shard_map/ppermute | solution.py:284
  147.7 16.9 %collective-permute-start.26 = (bf16[480,640]{1,0:T(8,128)(2,1)S(1)}, bf16[480,640]{1,0:T(8,128)(2,1)S(1)}, u32[]{:S(2)}, u32[]{:S(2)}) collective-permute-start(bf16[480,640]{1,0:T(8,128)(2,1)S(1)} %get-tuple-element.18.refs_17_), channel_id=1, source_target_pairs={{0,16},{4,20},{8,24},{12,28},{16,0},{20,4},{24,8},{28,12},{1,17},{... | collective-permute-start | bytes 1843208 | tf_op jit(solution)/shard_map/ppermute | solution.py:281
  148.6 16.0 %collective-permute-start.24 = (bf16[480,640]{1,0:T(8,128)(2,1)S(1)}, bf16[480,640]{1,0:T(8,128)(2,1)S(1)}, u32[]{:S(2)}, u32[]{:S(2)}) collective-permute-start(bf16[480,640]{1,0:T(8,128)(2,1)S(1)} %get-tuple-element.18.refs_17_), channel_id=1, source_target_pairs={{0,8},{4,12},{8,0},{12,4},{16,24},{20,28},{24,16},{28,20},{1,9},{5... | collective-permute-start | bytes 1843208 | tf_op jit(solution)/shard_map/ppermute | solution.py:281
  149.1 101.0 %copy-start.19 = (bf16[4,320,256]{2,1,0:T(8,128)(2,1)}, bf16[4,320,256]{2,1,0:T(8,128)(2,1)S(1)}, u32[]{:S(2)}) copy-start(bf16[4,320,256]{2,1,0:T(8,128)(2,1)S(1)} %collective-permute-done.5.refs_2_) | copy-start | bytes 1966084
  149.1 20.6 %collective-permute-start.23 = (bf16[480,640]{1,0:T(8,128)(2,1)S(1)}, bf16[480,640]{1,0:T(8,128)(2,1)S(1)}, u32[]{:S(2)}, u32[]{:S(2)}) collective-permute-start(bf16[480,640]{1,0:T(8,128)(2,1)S(1)} %get-tuple-element.18.refs_17_), channel_id=1, source_target_pairs={{0,4},{4,0},{8,12},{12,8},{16,20},{20,16},{24,28},{28,24},{1,5},{5... | collective-permute-start | bytes 1843208 | tf_op jit(solution)/shard_map/ppermute | solution.py:281
  149.1 23.9 %collective-permute-start.19 = (bf16[480,640]{1,0:T(8,128)(2,1)S(1)}, bf16[480,640]{1,0:T(8,128)(2,1)S(1)}, u32[]{:S(2)}, u32[]{:S(2)}) collective-permute-start(bf16[480,640]{1,0:T(8,128)(2,1)S(1)} %get-tuple-element.19.refs_9_), channel_id=1, source_target_pairs={{0,16},{4,20},{8,24},{12,28},{16,0},{20,4},{24,8},{28,12},{1,17},{... | collective-permute-start | bytes 1843208 | tf_op jit(solution)/shard_map/ppermute | solution.py:281
  162.1 11.6 %collective-permute-start.17 = (bf16[480,640]{1,0:T(8,128)(2,1)S(1)}, bf16[480,640]{1,0:T(8,128)(2,1)S(1)}, u32[]{:S(2)}, u32[]{:S(2)}) collective-permute-start(bf16[480,640]{1,0:T(8,128)(2,1)S(1)} %get-tuple-element.19.refs_9_), channel_id=1, source_target_pairs={{0,8},{4,12},{8,0},{12,4},{16,24},{20,28},{24,16},{28,20},{1,9},{5... | collective-permute-start | bytes 1843208 | tf_op jit(solution)/shard_map/ppermute | solution.py:281
  164.6 9.1 %collective-permute-start.16 = (bf16[480,640]{1,0:T(8,128)(2,1)S(1)}, bf16[480,640]{1,0:T(8,128)(2,1)S(1)}, u32[]{:S(2)}, u32[]{:S(2)}) collective-permute-start(bf16[480,640]{1,0:T(8,128)(2,1)S(1)} %get-tuple-element.19.refs_9_), channel_id=1, source_target_pairs={{0,4},{4,0},{8,12},{12,8},{16,20},{20,16},{24,28},{28,24},{1,5},{5... | collective-permute-start | bytes 1843208 | tf_op jit(solution)/shard_map/ppermute | solution.py:281
  164.6 19.6 %collective-permute-start.38 = (bf16[4,320,256]{2,1,0:T(8,128)(2,1)S(1)}, bf16[4,320,256]{2,1,0:T(8,128)(2,1)S(1)}, u32[]{:S(2)}, u32[]{:S(2)}) collective-permute-start(bf16[4,320,256]{2,1,0:T(8,128)(2,1)S(1)} %collective-permute-done.37.refs_5_), channel_id=1, source_target_pairs={{0,1},{1,2},{2,3},{4,5},{5,6},{6,7},{8,9},{9,10},{10,11},{12,13},{... | collective-permute-start | bytes 1966088 | tf_op jit(solution)/shard_map/ppermute | solution.py:284
  169.7 19.0 %collective-permute-start.35 = (bf16[4,320,256]{2,1,0:T(8,128)(2,1)S(1)}, bf16[4,320,256]{2,1,0:T(8,128)(2,1)S(1)}, u32[]{:S(2)}, u32[]{:S(2)}) collective-permute-start(bf16[4,320,256]{2,1,0:T(8,128)(2,1)S(1)} %collective-permute-done.34.refs_2_), channel_id=1, source_target_pairs={{1,0},{2,1},{3,2},{5,4},{6,5},{7,6},{9,8},{10,9},{11,10},{13,12},{... | collective-permute-start | bytes 1966088 | tf_op jit(solution)/shard_map/ppermute | solution.py:284
  173.0 15.7 %collective-permute-start.28 = (bf16[480,640]{1,0:T(8,128)(2,1)S(1)}, bf16[480,640]{1,0:T(8,128)(2,1)S(1)}, u32[]{:S(2)}, u32[]{:S(2)}) collective-permute-start(bf16[480,640]{1,0:T(8,128)(2,1)S(1)} %collective-permute-done.26.refs_21_), channel_id=1, source_target_pairs={{0,8},{4,12},{8,0},{12,4},{16,24},{20,28},{24,16},{28,20},{1,9},{5... | collective-permute-start | bytes 1843208 | tf_op jit(solution)/shard_map/ppermute | solution.py:281
  173.7 15.6 %collective-permute-start.27 = (bf16[480,640]{1,0:T(8,128)(2,1)S(1)}, bf16[480,640]{1,0:T(8,128)(2,1)S(1)}, u32[]{:S(2)}, u32[]{:S(2)}) collective-permute-start(bf16[480,640]{1,0:T(8,128)(2,1)S(1)} %collective-permute-done.26.refs_21_), channel_id=1, source_target_pairs={{0,4},{4,0},{8,12},{12,8},{16,20},{20,16},{24,28},{28,24},{1,5},{5... | collective-permute-start | bytes 1843208 | tf_op jit(solution)/shard_map/ppermute | solution.py:281
  173.7 16.3 %collective-permute-start.21 = (bf16[480,640]{1,0:T(8,128)(2,1)S(1)}, bf16[480,640]{1,0:T(8,128)(2,1)S(1)}, u32[]{:S(2)}, u32[]{:S(2)}) collective-permute-start(bf16[480,640]{1,0:T(8,128)(2,1)S(1)} %collective-permute-done.17.refs_11_), channel_id=1, source_target_pairs={{0,16},{4,20},{8,24},{12,28},{16,0},{20,4},{24,8},{28,12},{1,17},{... | collective-permute-start | bytes 1843208 | tf_op jit(solution)/shard_map/ppermute | solution.py:281
  184.3 8.8 %collective-permute-start.18 = (bf16[480,640]{1,0:T(8,128)(2,1)S(1)}, bf16[480,640]{1,0:T(8,128)(2,1)S(1)}, u32[]{:S(2)}, u32[]{:S(2)}) collective-permute-start(bf16[480,640]{1,0:T(8,128)(2,1)S(1)} %collective-permute-done.17.refs_11_), channel_id=1, source_target_pairs={{0,4},{4,0},{8,12},{12,8},{16,20},{20,16},{24,28},{28,24},{1,5},{5... | collective-permute-start | bytes 1843208 | tf_op jit(solution)/shard_map/ppermute | solution.py:281
  188.7 3.1 collective-permute-start.25
  188.7 4.2 %collective-permute-start.20 = (bf16[480,640]{1,0:T(8,128)(2,1)S(1)}, bf16[480,640]{1,0:T(8,128)(2,1)S(1)}, u32[]{:S(2)}, u32[]{:S(2)}) collective-permute-start(bf16[480,640]{1,0:T(8,128)(2,1)S(1)} %collective-permute-done.19.refs_13_), channel_id=1, source_target_pairs={{0,4},{4,0},{8,12},{12,8},{16,20},{20,16},{24,28},{28,24},{1,5},{5... | collective-permute-start | bytes 1843208 | tf_op jit(solution)/shard_map/ppermute | solution.py:281
  189.3 4.8 %collective-permute-start.29 = (bf16[480,640]{1,0:T(8,128)(2,1)S(1)}, bf16[480,640]{1,0:T(8,128)(2,1)S(1)}, u32[]{:S(2)}, u32[]{:S(2)}) collective-permute-start(bf16[480,640]{1,0:T(8,128)(2,1)S(1)} %collective-permute-done.28.refs_23_), channel_id=1, source_target_pairs={{0,4},{4,0},{8,12},{12,8},{16,20},{20,16},{24,28},{28,24},{1,5},{5... | collective-permute-start | bytes 1843208 | tf_op jit(solution)/shard_map/ppermute | solution.py:281
  190.1 9.8 %collective-permute-start.22 = (bf16[480,640]{1,0:T(8,128)(2,1)S(1)}, bf16[480,640]{1,0:T(8,128)(2,1)S(1)}, u32[]{:S(2)}, u32[]{:S(2)}) collective-permute-start(bf16[480,640]{1,0:T(8,128)(2,1)S(1)} %collective-permute-done.21.refs_15_), channel_id=1, source_target_pairs={{0,4},{4,0},{8,12},{12,8},{16,20},{20,16},{24,28},{28,24},{1,5},{5... | collective-permute-start | bytes 1843208 | tf_op jit(solution)/shard_map/ppermute | solution.py:281
  191.8 59.0 %collective-permute-start.51 = (bf16[640,1024]{1,0:T(8,128)(2,1)}, bf16[640,1024]{1,0:T(8,128)(2,1)S(1)}, u32[]{:S(2)}, u32[]{:S(2)}) collective-permute-start(bf16[640,1024]{1,0:T(8,128)(2,1)} %collective-permute-done.49.refs_13_), channel_id=1, source_target_pairs={{0,8},{4,12},{8,0},{12,4},{16,24},{20,28},{24,16},{28,20},{1,9},{5... | collective-permute-start | bytes 3932168 | tf_op jit(solution)/shard_map/ppermute | solution.py:281
  192.9 58.0 %collective-permute-start.50 = (bf16[640,1024]{1,0:T(8,128)(2,1)}, bf16[640,1024]{1,0:T(8,128)(2,1)}, u32[]{:S(2)}, u32[]{:S(2)}) collective-permute-start(bf16[640,1024]{1,0:T(8,128)(2,1)} %collective-permute-done.49.refs_13_), channel_id=1, source_target_pairs={{0,4},{4,0},{8,12},{12,8},{16,20},{20,16},{24,28},{28,24},{1,5},{5... | collective-permute-start | bytes 3932168 | tf_op jit(solution)/shard_map/ppermute | solution.py:281
  193.1 58.2 %collective-permute-start.44 = (bf16[640,1024]{1,0:T(8,128)(2,1)S(1)}, bf16[640,1024]{1,0:T(8,128)(2,1)}, u32[]{:S(2)}, u32[]{:S(2)}) collective-permute-start(bf16[640,1024]{1,0:T(8,128)(2,1)S(1)} %collective-permute-done.40.refs_3_), channel_id=1, source_target_pairs={{0,16},{4,20},{8,24},{12,28},{16,0},{20,4},{24,8},{28,12},{1,17},{... | collective-permute-start | bytes 3932168 | tf_op jit(solution)/shard_map/ppermute | solution.py:281
  194.0 56.1 %collective-permute-start.9 = (bf16[4,320,256]{2,1,0:T(8,128)(2,1)}, bf16[4,320,256]{2,1,0:T(8,128)(2,1)}, u32[]{:S(2)}, u32[]{:S(2)}) collective-permute-start(bf16[4,320,256]{2,1,0:T(8,128)(2,1)} %collective-permute-done.8.refs_5_), channel_id=1, source_target_pairs={{0,1},{1,2},{2,3},{4,5},{5,6},{6,7},{8,9},{9,10},{10,11},{12,13},{... | collective-permute-start | bytes 1966088 | tf_op jit(solution)/shard_map/ppermute | solution.py:284
  199.9 50.4 %collective-permute-start.6 = (bf16[4,320,256]{2,1,0:T(8,128)(2,1)S(1)}, bf16[4,320,256]{2,1,0:T(8,128)(2,1)}, u32[]{:S(2)}, u32[]{:S(2)}) collective-permute-start(bf16[4,320,256]{2,1,0:T(8,128)(2,1)S(1)} %collective-permute-done.5.refs_2_), channel_id=1, source_target_pairs={{1,0},{2,1},{3,2},{5,4},{6,5},{7,6},{9,8},{10,9},{11,10},{13,12},{... | collective-permute-start | bytes 1966088 | tf_op jit(solution)/shard_map/ppermute | solution.py:284
  201.4 49.3 %copy-start.13 = (bf16[640,1024]{1,0:T(8,128)(2,1)S(1)}, bf16[640,1024]{1,0:T(8,128)(2,1)}, u32[]{:S(2)}) copy-start(bf16[640,1024]{1,0:T(8,128)(2,1)} %copy-done.12) | copy-start | bytes 3932164
  250.2 50.1 %copy-start.2 = (f32[2048]{0:T(1024)S(1)}, f32[2048]{0:T(1024)}, u32[]{:S(2)}) copy-start(f32[2048]{0:T(1024)} %param.22) | copy-start | bytes 24580
  250.2 50.0 %collective-permute-start.41 = (bf16[640,1024]{1,0:T(8,128)(2,1)S(1)}, bf16[640,1024]{1,0:T(8,128)(2,1)S(1)}, u32[]{:S(2)}, u32[]{:S(2)}) collective-permute-start(bf16[640,1024]{1,0:T(8,128)(2,1)S(1)} %collective-permute-done.40.refs_3_), channel_id=1, source_target_pairs={{0,4},{4,0},{8,12},{12,8},{16,20},{20,16},{24,28},{28,24},{1,5},{5... | collective-permute-start | bytes 3932168 | tf_op jit(solution)/shard_map/ppermute | solution.py:281
  250.3 49.9 %collective-permute-start.48 = (bf16[640,1024]{1,0:T(8,128)(2,1)S(1)}, bf16[640,1024]{1,0:T(8,128)(2,1)}, u32[]{:S(2)}, u32[]{:S(2)}) collective-permute-start(bf16[640,1024]{1,0:T(8,128)(2,1)S(1)} %collective-permute-done.47.refs_11_), channel_id=1, source_target_pairs={{0,4},{4,0},{8,12},{12,8},{16,20},{20,16},{24,28},{28,24},{1,5},{5... | collective-permute-start | bytes 3932168 | tf_op jit(solution)/shard_map/ppermute | solution.py:281
  250.8 49.4 %copy-start.14 = (bf16[640,1024]{1,0:T(8,128)(2,1)}, bf16[640,1024]{1,0:T(8,128)(2,1)S(1)}, u32[]{:S(2)}) copy-start(bf16[640,1024]{1,0:T(8,128)(2,1)S(1)} %collective-permute-done.51.refs_15_) | copy-start | bytes 3932164
  250.8 49.4 %collective-permute-start.43 = (bf16[640,1024]{1,0:T(8,128)(2,1)S(1)}, bf16[640,1024]{1,0:T(8,128)(2,1)}, u32[]{:S(2)}, u32[]{:S(2)}) collective-permute-start(bf16[640,1024]{1,0:T(8,128)(2,1)S(1)} %copy-done.13), channel_id=1, source_target_pairs={{0,4},{4,0},{8,12},{12,8},{16,20},{20,16},{24,28},{28,24},{1,5},{5... | collective-permute-start | bytes 3932168 | tf_op jit(solution)/shard_map/ppermute | solution.py:281
  250.9 49.3 %collective-permute-start.52 = (bf16[640,1024]{1,0:T(8,128)(2,1)S(1)}, bf16[640,1024]{1,0:T(8,128)(2,1)}, u32[]{:S(2)}, u32[]{:S(2)}) collective-permute-start(bf16[640,1024]{1,0:T(8,128)(2,1)S(1)} %collective-permute-done.51.refs_15_), channel_id=1, source_target_pairs={{0,4},{4,0},{8,12},{12,8},{16,20},{20,16},{24,28},{28,24},{1,5},{5... | collective-permute-start | bytes 3932168 | tf_op jit(solution)/shard_map/ppermute | solution.py:281
  251.3 48.9 %collective-permute-start.45 = (bf16[640,1024]{1,0:T(8,128)(2,1)}, bf16[640,1024]{1,0:T(8,128)(2,1)}, u32[]{:S(2)}, u32[]{:S(2)}) collective-permute-start(bf16[640,1024]{1,0:T(8,128)(2,1)} %collective-permute-done.44.refs_7_), channel_id=1, source_target_pairs={{0,4},{4,0},{8,12},{12,8},{16,20},{20,16},{24,28},{28,24},{1,5},{5... | collective-permute-start | bytes 3932168 | tf_op jit(solution)/shard_map/ppermute | solution.py:281
  327.5 7.8 %all-to-all-start = ((s32[8,1,4]{2,1,0:T(1,128)}), s32[8,1,4]{2,1,0:T(1,128)S(1)}, u32[]{:S(2)}, u32[]{:S(2)}) async-start(s32[8,1,4]{2,1,0:T(1,128)} %bitcast.22), calls=%async_computation.1 | async-start | bytes 8192 | tf_op jit(solution)/shard_map/all_to_all | solution.py:277
  (21 other events, 349.3 us)
Sparse Core Ops, SparseCore 0:
  326.9 47.3 reduce-scatter.1

commit v2 on v1

--- a/solution.py
+++ b/solution.py
@@ -22,17 +22,15 @@
 
 
 def attend_kernel(tp, moves, nw, aliased, info, *refs):
-    own = refs[0]
-    right = refs[1:tp]
-    left = refs[tp : 2 * tp - 1]
-    at = 2 * tp - 1
+    pieces = refs[:tp]
+    at = tp
     w_refs = refs[at : at + nw]
     vit_gain, merge_gain = refs[at + nw : at + nw + 2]
     at += nw + 2 + int(aliased)
     out = refs[at]
     w, xs, nrm, packed, mixed, vit, bias, sem = refs[at + 1 :]
     t = info[0]
-    feats = own.shape[1]
+    feats = pieces[0].shape[1]
     heads = HV // tp
     rows = packed.shape[0]
     first_proj = 3 * DV
@@ -47,19 +45,8 @@
         query = lax.broadcasted_iota(jnp.int32, (cols, cols), 1) // (WIN // MERGE) % GROUP
         bias[...] = jnp.where(key == query, 0.0, -1e30).astype(F32)
 
-    for j in range(tp):
-        spot = pl.ds(pl.multiple_of(lax.rem(t + j, tp) * feats, feats), feats)
-        if j == 0:
-            xs[spot, :] = own[0]
-        else:
-
-            @pl.when(t + j < tp)
-            def _():
-                xs[spot, :] = right[j - 1][0]
-
-            @pl.when(t + j >= tp)
-            def _():
-                xs[spot, :] = left[tp - j - 1][0]
+    for d, piece in enumerate(pieces):
+        xs[pl.ds(pl.multiple_of((t ^ d) * feats, feats), feats), :] = piece[0]
 
     xf = xs[...].astype(F32)
     scale = lax.rsqrt(jnp.mean(xf * xf, axis=0, keepdims=True) + 1e-6)
@@ -109,13 +96,13 @@
         out[c, 0] = merged[c * per : (c + 1) * per, :]
 
 
-def attend(tp, info, own, right, left, weights, moves, count, vit_gain, merge_gain, blocks, buf):
-    nb, feats, cols = own.shape
+def attend(tp, info, pieces, weights, moves, count, vit_gain, merge_gain, blocks, buf):
+    nb, feats, cols = pieces[0].shape
     per = cols // MERGE
     x_spec = pl.BlockSpec((1, feats, cols), lambda i, s: (i, 0, 0))
     anywhere = pl.BlockSpec(memory_space=pl.ANY)
-    ins = [own, *right, *left, *weights, vit_gain, merge_gain]
-    specs = [x_spec] * (2 * tp - 1) + [anywhere] * len(weights)
+    ins = [*pieces, *weights, vit_gain, merge_gain]
+    specs = [x_spec] * tp + [anywhere] * len(weights)
     specs += [pl.BlockSpec((DV, 1), lambda i, s: (0, 0)), pl.BlockSpec((1, DV), lambda i, s: (0, 0))]
     alias = {}
     if buf is not None:
@@ -240,7 +227,7 @@
                 pltpu.VMEM((rows, units // 2), F32),
                 pltpu.VMEM((rows, units), BF),
                 pltpu.SemaphoreType.DMA((MERGE,)),
-                pltpu.SemaphoreType.DMA((3, 2)),
+                pltpu.SemaphoreType.DMA((3, 4)),
                 pltpu.SemaphoreType.DMA,
             ],
         ),
@@ -280,20 +267,22 @@
     def xor(x, d):
         return lax.ppermute(x, "seq", [(i, i ^ d) for i in range(seq_count)])
 
-    def along(x, k):
-        return lax.ppermute(x, "tp", [(i, i + k) for i in range(tp) if 0 <= i + k < tp])
+    def tie(x, after):
+        return lax.optimization_barrier((x, after))[0]
+
+    def tp_xor(x, d):
+        return lax.ppermute(x, "tp", [(i, i ^ d) for i in range(tp)])
 
     def spread(x):
-        right, left = [], []
-        for _ in range(tp - 1):
-            right.append(along(right[-1] if right else x, -1))
-            left.append(along(left[-1] if left else x, 1))
-        return right, left
-
-    paired = per_peer == GROUP and seq_count == 8
-    peers = jnp.arange(seq_count, dtype=jnp.int32)
-    if paired:
-        window = jnp.take(window, s ^ peers, axis=0)
+        held = {0: x}
+        d = tp // 2
+        while d:
+            held.update({k ^ d: tp_xor(v, d) for k, v in list(held.items())})
+            d //= 2
+        return [held[d] for d in range(tp)]
+
+    paired = seq_count == 8 and per_peer == GROUP
+
     source = (
         window[:, None, :, None] * WIN
         + jnp.arange(tokens)[None, None, None, :] * MERGE
@@ -306,12 +295,18 @@
     step = per_peer * WIN
     wq_t = w_qkv.T
 
+    full = lax.all_to_all(
+        sent.reshape(feats, seq_count, step).transpose(1, 0, 2),
+        "seq",
+        split_axis=0,
+        concat_axis=0,
+        tiled=True,
+    )
+    full = full.reshape(blocks, GROUP // per_peer, feats, MERGE, per_peer, tokens)
+    full = full.transpose(0, 2, 3, 1, 4, 5).reshape(blocks, feats, GROUP * WIN)
+    mid = blocks // 2
+
     if paired:
-        parts = [sent[:, d * step : (d + 1) * step] for d in range(seq_count)]
-        parts = [p if d == 0 else xor(p, d) for d, p in enumerate(parts)]
-        groups = [jnp.stack(parts[:4]), jnp.stack(parts[4:])]
-        places = [s ^ peers[:4], s ^ peers[4:]]
-
         share = (wq_t.shape[0] + w_proj.shape[0]) // seq_count
         q_parts = wq_t.shape[0] // share
         mine = jnp.where(
@@ -319,28 +314,35 @@
             lax.dynamic_slice_in_dim(wq_t, jnp.minimum(s, q_parts - 1) * share, share),
             lax.dynamic_slice_in_dim(w_proj, jnp.maximum(s - q_parts, 0) * share, share),
         )
-        right, left = spread(mine)
-        others = jnp.concatenate(
-            [jnp.where(t + j < tp, right[j - 1], left[tp - j - 1]) for j in range(1, tp)]
-        )
-
-        def plane(x):
-            mid = x.shape[1] // 2
-            halves = []
-            for piece, bits in ((x[:, :mid], (2, 4)), (x[:, mid:], (4, 2))):
-                held = {0: piece}
-                for b in bits:
-                    held.update({k ^ b: xor(v, b) for k, v in list(held.items())})
-                held.update({k ^ 1: xor(v, 1) for k, v in list(held.items())})
-                halves.append([held[d] for d in range(seq_count)])
-            return halves
-
-        vit_halves = plane(others)
-        merge_halves = plane(w_merge)
-        vit_weights = [wq_t, w_proj] + vit_halves[0] + vit_halves[1]
-        merge_weights = merge_halves[0] + merge_halves[1]
+        others = jnp.concatenate(spread(mine)[1:])
+
+        def sides(x):
+            return list(lax.optimization_barrier((xor(x, 2), xor(x, 4))))
+
+        def corners(by_x, by_y):
+            half = by_x.shape[0] // 2
+            return [xor(by_x[:half], 4), xor(by_y[half:], 2)]
+
+        def cores(pieces):
+            return [xor(v, 1) for v in pieces]
+
+        vit_pieces = [others] + sides(others)
+        vit_pieces += list(lax.optimization_barrier(tuple(corners(*vit_pieces[1:]))))
+        merge_pieces = [w_merge] + sides(tie(w_merge, vit_pieces[3]))
+        vit_weights = [wq_t, w_proj] + vit_pieces + cores(vit_pieces)
         q_rows, p_rows = wq_t.shape[0], w_proj.shape[0]
-        vit_count = 2 + 2 * seq_count * (tp - 1)
+
+        def spans(rows):
+            whole = [(0, 0, rows), (2, 0, rows), (4, 0, rows), (6, 0, rows // 2), (6, rows // 2, rows)]
+            return [(d ^ e, lo, hi) for e in range(2) for d, lo, hi in whole]
+
+        vit_parts = []
+        for n, (d, lo, hi) in enumerate(spans(others.shape[0])):
+            for j in range(1, tp):
+                first, last = max(lo, (j - 1) * share), min(hi, j * share)
+                if first < last:
+                    vit_parts.append((n, d, j, first - lo, first - (j - 1) * share, last - first))
+        vit_count = 2 + len(vit_parts)
 
         def vit_moves(info, refs, w, sem):
             t, s = info[0], info[1]
@@ -352,55 +354,44 @@
                     refs[1], w.at[pl.ds(pl.multiple_of(3 * DV + t * p_rows, 16), p_rows)], sem.at[1]
                 ),
             ]
-            for h in range(2):
-                for d in range(seq_count):
-                    part = s ^ d
-                    for j in range(1, tp):
-                        q = lax.rem(t + j, tp)
-                        row = jnp.where(
-                            part < q_parts,
-                            q * q_rows + part * share,
-                            3 * DV + q * p_rows + (part - q_parts) * share,
-                        )
-                        copies.append(
-                            pltpu.make_async_copy(
-                                refs[2 + h * seq_count + d].at[(j - 1) * share : j * share],
-                                w.at[
-                                    pl.ds(pl.multiple_of(row, 16), share),
-                                    h * (DV // 2) : (h + 1) * (DV // 2),
-                                ],
-                                sem.at[len(copies)],
-                            )
-                        )
-            return copies
-
-        def merge_moves(info, refs, h, i, slot, sem):
-            s = info[1]
-            rows = refs[0].shape[0]
-            copies = []
-            for e in range(2):
-                at = pl.multiple_of(((s & 1) ^ e) * rows, 16)
+            for n, d, j, source, offset, count in vit_parts:
+                part = s ^ d
+                q = t ^ j
+                row = offset + jnp.where(
+                    part < q_parts,
+                    q * q_rows + part * share,
+                    3 * DV + q * p_rows + (part - q_parts) * share,
+                )
                 copies.append(
                     pltpu.make_async_copy(
-                        refs[h * seq_count + 2 * i + e], slot.at[pl.ds(at, rows)], sem.at[e]
+                        refs[2 + n].at[source : source + count],
+                        w.at[pl.ds(pl.multiple_of(row, 16), count)],
+                        sem.at[len(copies)],
                     )
                 )
             return copies
 
+        def merge_moves(info, refs, h, i, slot, sem):
+            s = info[1]
+            wide = slot.shape[1]
+            rows = slot.shape[0] // 2
+            copies = []
+            for n, (d, lo, hi) in enumerate(spans(rows)):
+                if d // 2 == i:
+                    at = pl.multiple_of(((s ^ d) & 1) * rows + lo, 16)
+                    copies.append(
+                        pltpu.make_async_copy(
+                            refs[n].at[:, h * wide : (h + 1) * wide],
+                            slot.at[pl.ds(at, hi - lo)],
+                            sem.at[len(copies)],
+                        )
+                    )
+            return copies
+
         def position(info, i):
             return (info[1] // 2) ^ i
 
     else:
-        full = lax.all_to_all(
-            sent.reshape(feats, seq_count, step).transpose(1, 0, 2),
-            "seq",
-            split_axis=0,
-            concat_axis=0,
-            tiled=True,
-        )
-        full = full.reshape(blocks, GROUP // per_peer, feats, MERGE, per_peer, tokens)
-        groups = [full.transpose(0, 2, 3, 1, 4, 5).reshape(blocks, feats, GROUP * WIN)]
-        places = [jnp.arange(blocks, dtype=jnp.int32)]
         vit_weights = [
             lax.all_gather(wq_t, "tp", axis=0, tiled=True),
             lax.all_gather(w_proj, "tp", axis=0, tiled=True),
@@ -422,14 +413,26 @@
         def position(info, i):
             return i
 
-    merged = None
-    for own, place in zip(groups, places):
-        info = jnp.concatenate([jnp.stack([t, s]), place])
-        right, left = spread(own)
-        merged = attend(
-            tp, info, own, right, left, vit_weights, vit_moves, vit_count,
-            vit_gain[:, None], merge_gain[None, :], blocks, merged,
+    def encode(first, pieces, buf):
+        info = jnp.concatenate([jnp.stack([t, s]), first + jnp.arange(mid, dtype=jnp.int32)])
+        return attend(
+            tp, info, pieces, vit_weights, vit_moves, vit_count,
+            vit_gain[:, None], merge_gain[None, :], blocks, buf,
         )
+
+    if paired:
+        near = list(lax.optimization_barrier((tp_xor(full[:mid], 2), tp_xor(full[:mid], 1))))
+        later = tie(full[mid:], near[0])
+        far = [tp_xor(later, 2), tp_xor(later, 1)]
+        merged = encode(0, [full[:mid], near[1], near[0], tp_xor(near[0], 1)], None)
+        merged, far, by = lax.optimization_barrier((merged, far, merge_pieces[1:]))
+        merge_pieces = [w_merge] + by + corners(*by)
+        merge_weights = merge_pieces + cores(merge_pieces)
+        merged = encode(mid, [full[mid:], far[1], far[0], tp_xor(far[0], 1)], merged)
+    else:
+        merged = None
+        for first in (0, mid):
+            merged = encode(first, spread(full[first : first + mid]), merged)
     partial_value = project(
         jnp.stack([t, s]), merged, merge_weights, merge_moves, position, w_cache, llm_gain[None, :]
     )

time: 384 us -> 323 us (0.84)
  starting transfers between devices: 77.9 us -> 28.8 us
  waiting for transfers between devices: 142 us -> 122 us
  local copies, waits for them, and re-layouts: 9.97 us -> 19.5 us
    ppermute x18 -> x9, starting transfers between devices: 56.3 us -> 10.1 us  [tp_xor(): return lax.ppermute(x, 'tp', [(i, i ^ d) for i in range(tp)])]
    ppermute x18 -> x9, waiting for transfers between devices: 54 us -> 18.7 us  [tp_xor(): return lax.ppermute(x, 'tp', [(i, i ^ d) for i in range(tp)])]
    ppermute x35 -> x18, waiting for transfers between devices: 45.7 us -> 60.9 us  [xor(): return lax.ppermute(x, 'seq', [(i, i ^ d) for i in range(seq_count)])]
    ppermute x35 -> x18, starting transfers between devices: 18.3 us -> 11.6 us  [xor(): return lax.ppermute(x, 'seq', [(i, i ^ d) for i in range(seq_count)])]
    unnamed x60 -> x28, local copies, waits for them, and re-layouts: 1.16 us -> 7.7 us
  transfers between devices with their start and end apart: 55 -> 30, of which waited for: 19 -> 14; matrix products, arithmetic and copies ran while one was open for 2% -> 7% of each run, Pallas kernels for 25% -> 30%
where the time goes in v2:
time: 323 us
  Pallas kernels  126 us (39%)
  waiting for transfers between devices  122 us (38%)
  starting transfers between devices  28.8 us (9%)
  local copies, waits for them, and re-layouts  19.5 us (6%)
  between operations  13.7 us (4%)
  other arithmetic  9.63 us (3%)
  matrix products  3.47 us (1%)
    pallas_call x2, Pallas kernels, attend(): pl.pallas_call(functools.partial(attend_kernel, tp, moves, len(weights),...  96.1 us
    ppermute x18, waiting for transfers between devices, xor(): return lax.ppermute(x, 'seq', [(i, i ^ d) for i in range(seq_count)])  60.9 us
    reduce_scatter x1, waiting for transfers between devices, shards(): lax.psum_scatter(partial_value, 'tp', scatter_dimension=0, tiled=True)  34.4 us
    pallas_call x1, Pallas kernels, project(): pl.pallas_call(functools.partial(project_kernel, moves, position, len(wei...  30.1 us
    ppermute x9, waiting for transfers between devices, tp_xor(): return lax.ppermute(x, 'tp', [(i, i ^ d) for i in range(tp)])  18.7 us
    ppermute x18, starting transfers between devices, xor(): return lax.ppermute(x, 'seq', [(i, i ^ d) for i in range(seq_count)])  11.6 us
    ppermute x9, starting transfers between devices, tp_xor(): return lax.ppermute(x, 'tp', [(i, i ^ d) for i in range(tp)])  10.1 us
    unnamed x28, local copies, waits for them, and re-layouts  7.7 us
  transfers between devices with their start and end apart: 30, of which 14 were waited for; matrix products, arithmetic and copies ran while one was open for 7% of the time, Pallas kernels for 30%

profile of v2, /device:TPU:0, one launch (start us, length us, event | category | flops | bytes accessed | tf_op | source)
XLA Modules:
  0.0 322.8 jit_solution(14116540462159904824)
XLA Ops:
  6.5 2.1 bitcast_select_fusion
  8.6 4.0 %collective-permute-start.4 = (bf16[160,1280]{1,0:T(8,128)(2,1)}, bf16[160,1280]{1,0:T(8,128)(2,1)S(1)}, u32[]{:S(2)}, u32[]{:S(2)}) collective-permute-start(bf16[160,1280]{1,0:T(8,128)(2,1)} %bitcast_select_fusion), channel_id=1, source_target_pairs={{0,2},{1,3},{2,0},{3,1},{4,6},{5,7},{6,4},{7,5},{8,10},{9,11},{10,... | collective-permute-start | bytes 1228808 | tf_op jit(solution)/shard_map/ppermute | solution.py:274
  12.7 1.6 collective-permute-start.3
  14.2 2.3 sort.17
  16.6 1.4 fusion.10
  18.0 1.9 compare_convert_fusion
  19.9 0.7 gather_fusion.1
  20.6 0.7 gather_fusion
  21.6 3.5 %fusion.2 = bf16[2048,320]{0,1:T(8,128)(2,1)S(1)} fusion(bf16[2048,320]{0,1:T(8,128)(2,1)S(1)} %copy-done, s32[2048]{0:T(1024)S(1)} %add.115), kind=kOutput, calls=%fused_computation.5 | convolution fusion | flops 2689204224 | bytes 2629632 | tf_op jit(solution)/shard_map/dot_general | solution.py:292
  25.1 1.2 copy.22
  26.2 3.7 %all-to-all-start = ((bf16[8,320,256]{2,1,0:T(8,128)(2,1)}), bf16[8,320,256]{2,1,0:T(8,128)(2,1)S(1)}, u32[]{:S(2)}, u32[]{:S(2)}) async-start(bf16[8,320,256]{2,1,0:T(8,128)(2,1)} %bitcast.35), calls=%async_computation | async-start | bytes 2621440 | tf_op jit(solution)/shard_map/all_to_all | solution.py:298
  30.0 1.2 collective-permute-done.4
  31.2 0.7 collective-permute-start.5
  31.9 0.8 constant_dynamic-update-slice_fusion.2
  32.7 0.8 constant_dynamic-update-slice_fusion.1
  33.5 8.4 %collective-permute-done.5 = bf16[160,1280]{1,0:T(8,128)(2,1)S(1)} collective-permute-done((bf16[160,1280]{1,0:T(8,128)(2,1)S(1)}, bf16[160,1280]{1,0:T(8,128)(2,1)S(1)}, u32[]{:S(2)}, u32[]{:S(2)}) %collective-permute-start.5) | collective-permute-done | bytes 409632 | tf_op jit(solution)/shard_map/ppermute | solution.py:274
  41.9 0.8 constant_dynamic-update-slice_fusion.refs_6_
  42.7 1.7 collective-permute-start.7
  44.4 1.5 collective-permute-start.6
  45.8 2.9 all-to-all-done
  48.8 0.5 collective-permute-start.1
  49.3 1.3 collective-permute-start
  50.6 23.3 %collective-permute-done.7.refs_8_ = bf16[480,1280]{1,0:T(8,128)(2,1)} collective-permute-done((bf16[480,1280]{1,0:T(8,128)(2,1)}, bf16[480,1280]{1,0:T(8,128)(2,1)}, u32[]{:S(2)}, u32[]{:S(2)}) %collective-permute-start.7) | collective-permute-done | bytes 1228832 | tf_op jit(solution)/shard_map/ppermute | solution.py:268
  73.9 1.1 slice.29
  75.0 1.1 slice.30
  76.1 1.3 collective-permute-start.9
  77.4 0.6 collective-permute-start.8
  78.1 0.5 collective-permute-start.2
  78.5 13.0 %collective-permute-done.9.refs_10_ = bf16[240,1280]{1,0:T(8,128)(2,1)S(1)} collective-permute-done((bf16[240,1280]{1,0:T(8,128)(2,1)S(1)}, bf16[240,1280]{1,0:T(8,128)(2,1)S(1)}, u32[]{:S(2)}, u32[]{:S(2)}) %collective-permute-start.9) | collective-permute-done | bytes 614432 | tf_op jit(solution)/shard_map/ppermute | solution.py:268
  91.5 1.6 collective-permute-done.8.refs_9_
  93.1 0.9 copy-done.2
  93.9 0.5 collective-permute-start.11
  94.5 0.4 collective-permute-start.18
  94.8 1.7 collective-permute-start.17
  96.5 0.8 copy-done.4
  97.4 0.2 broadcast_in_dim.39.refs_16_
  97.7 2.3 collective-permute-done.13.refs_14_
  100.0 0.3 collective-permute-start.16
  100.2 1.1 collective-permute-start.15
  101.3 1.1 copy-done.3
  102.4 1.1 copy-done.5
  103.4 48.2 %attend.2.refs_18_ = bf16[4,8,64,1280]{3,2,1,0:T(8,128)(2,1)} custom-call(s32[6]{0:T(128)S(1)} %pad_add_fusion.3.info, bf16[4,320,256]{2,1,0:T(8,128)(2,1)S(1)} %get-tuple-element.38.refs_0_, bf16[4,320,256]{2,1,0:T(8,128)(2,1)S(1)} %collective-permute-done.1.refs_1_, bf16[4,320,256]{2,1,0:T(8,128)(2,1)S(1)} %collective-permute-done.refs_2_, ...), custom_call_target="tpu_custom_call" | custom-call | flops 16777216000 | bytes 14680064 | tf_op jit(solution)/shard_map/attend/pallas_call | solution.py:112
  151.6 2.4 collective-permute-done.18.refs_3_
  154.1 0.3 collective-permute-start.19
  154.4 1.4 slice.32
  155.9 1.7 collective-permute-start.21
  157.6 1.4 slice.31
  159.1 1.7 collective-permute-start.20
  160.8 0.5 collective-permute-start.23
  161.3 9.1 %collective-permute-done.19.refs_3_ = bf16[4,320,256]{2,1,0:T(8,128)(2,1)S(1)} collective-permute-done((bf16[4,320,256]{2,1,0:T(8,128)(2,1)S(1)}, bf16[4,320,256]{2,1,0:T(8,128)(2,1)S(1)}, u32[]{:S(2)}, u32[]{:S(2)}) %collective-permute-start.19) | collective-permute-done | bytes 655392 | tf_op jit(solution)/shard_map/ppermute | solution.py:274
  170.6 15.4 %collective-permute-done.21.refs_5_ = bf16[320,2048]{1,0:T(8,128)(2,1)S(1)} collective-permute-done((bf16[320,2048]{1,0:T(8,128)(2,1)S(1)}, bf16[320,2048]{1,0:T(8,128)(2,1)S(1)}, u32[]{:S(2)}, u32[]{:S(2)}) %collective-permute-start.21) | collective-permute-done | bytes 1310752 | tf_op jit(solution)/shard_map/ppermute | solution.py:268
  186.0 2.9 collective-permute-done.20.refs_4_
  188.9 48.0 %attend.3 = bf16[4,8,64,1280]{3,2,1,0:T(8,128)(2,1)} custom-call(s32[6]{0:T(128)S(1)} %pad_add_fusion.1.info, bf16[4,320,256]{2,1,0:T(8,128)(2,1)S(1)} %get-tuple-element.29.refs_0_, bf16[4,320,256]{2,1,0:T(8,128)(2,1)S(1)} %collective-permute-done.16.refs_1_, ...), custom_call_target="tpu_custom_call", output_to_operand_aliasing={{}: (19, {})} | custom-call | flops 16777216000 | bytes 14680064 | tf_op jit(solution)/shard_map/attend/pallas_call | solution.py:112
  236.9 1.4 copy-done.10
  238.3 0.8 copy-done.11
  239.1 30.1 %project.1 = bf16[512,2176]{1,0:T(8,128)(2,1)} custom-call(s32[2]{0:T(128)S(1)} %pad_add_fusion.info, bf16[4,512,1280]{2,1,0:T(8,128)(2,1)} %bitcast.42, bf16[640,2048]{1,0:T(8,128)(2,1)} %refs_1_.1, bf16[640,2048]{1,0:T(8,128)(2,1)} %collective-permute-done.17.refs_2_, bf16[640,2048]{1,0:T(8,128)(2,1)} %collective-permute-done.18.refs_3_, ...), custom_call_target="tpu_custom_call" | custom-call | flops 15032385536 | bytes 37748736 | tf_op jit(solution)/shard_map/project/pallas_call | solution.py:214
  269.3 0.7 all_to_all.10
  270.0 3.3 %all-to-all-start.1 = ((s32[8,1,4]{2,1,0:T(1,128)}), s32[8,1,4]{2,1,0:T(1,128)S(1)}, u32[]{:S(2)}, u32[]{:S(2)}) async-start(s32[8,1,4]{2,1,0:T(1,128)} %bitcast.14), calls=%async_computation.2 | async-start | bytes 8192 | tf_op jit(solution)/shard_map/all_to_all | solution.py:264
  273.3 4.5 %all-to-all-done.1 = s32[8,1,4]{2,1,0:T(1,128)S(1)} async-done(((s32[8,1,4]{2,1,0:T(1,128)}), s32[8,1,4]{2,1,0:T(1,128)S(1)}, u32[]{:S(2)}, u32[]{:S(2)}) %all-to-all-start.1) | async-done | bytes 160 | tf_op jit(solution)/shard_map/all_to_all | solution.py:264
  277.8 0.5 broadcast.226
  278.3 0.7 reduce.5
  279.3 34.4 %reduce-scatter.2.cloned.1.call-done = bf16[128,2176]{1,0:T(8,128)(2,1)} async-done(((bf16[512,2176]{1,0:T(8,128)(2,1)}), bf16[128,2176]{1,0:T(8,128)(2,1)}) %reduce-scatter.2.cloned.1.call-update) | async-done | bytes 557072 | tf_op jit(solution)/shard_map/reduce_scatter | solution.py:439
  313.7 1.1 convert_element_type.21
  315.0 1.0 fusion.4
  (68 shorter events, 1.3 us)
Async XLA Ops:
  6.5 15.1 %copy-start = (bf16[2048,320]{0,1:T(8,128)(2,1)S(1)}, bf16[2048,320]{0,1:T(8,128)(2,1)}, u32[]{:S(2)}) copy-start(bf16[2048,320]{0,1:T(8,128)(2,1)} %param.13) | copy-start | bytes 3932164
  6.5 14.0 %copy-start.7 = (s32[1,32]{1,0:T(1,128)S(1)}, s32[1,32]{1,0:T(1,128)}, u32[]{:S(2)}) copy-start(s32[1,32]{1,0:T(1,128)} %param.15) | copy-start | bytes 388
  8.6 22.6 %collective-permute-start.4 = (bf16[160,1280]{1,0:T(8,128)(2,1)}, bf16[160,1280]{1,0:T(8,128)(2,1)S(1)}, u32[]{:S(2)}, u32[]{:S(2)}) collective-permute-start(bf16[160,1280]{1,0:T(8,128)(2,1)} %bitcast_select_fusion), channel_id=1, source_target_pairs={{0,2},{1,3},{2,0},{3,1},{4,6},{5,7},{6,4},{7,5},{8,10},{9,11},{10,... | collective-permute-start | bytes 1228808 | tf_op jit(solution)/shard_map/ppermute | solution.py:274
  12.7 19.3 %collective-permute-start.3 = (bf16[160,1280]{1,0:T(8,128)(2,1)}, bf16[160,1280]{1,0:T(8,128)(2,1)S(1)}, u32[]{:S(2)}, u32[]{:S(2)}) collective-permute-start(bf16[160,1280]{1,0:T(8,128)(2,1)} %bitcast_select_fusion), channel_id=1, source_target_pairs={{0,1},{1,0},{2,3},{3,2},{4,5},{5,4},{6,7},{7,6},{8,9},{9,8},{10,11... | collective-permute-start | bytes 1228808 | tf_op jit(solution)/shard_map/ppermute | solution.py:274
  26.2 22.5 %all-to-all-start = ((bf16[8,320,256]{2,1,0:T(8,128)(2,1)}), bf16[8,320,256]{2,1,0:T(8,128)(2,1)S(1)}, u32[]{:S(2)}, u32[]{:S(2)}) async-start(bf16[8,320,256]{2,1,0:T(8,128)(2,1)} %bitcast.35), calls=%async_computation | async-start | bytes 2621440 | tf_op jit(solution)/shard_map/all_to_all | solution.py:298
  30.0 283.8 %reduce-scatter.2.cloned.1.call-start = ((), (), s32[]{:S(2)}) async-start(), calls=%async_computation.3 | async-start | bytes 2785280 | tf_op jit(solution)/shard_map/reduce_scatter | solution.py:439
  31.2 10.7 %collective-permute-start.5 = (bf16[160,1280]{1,0:T(8,128)(2,1)S(1)}, bf16[160,1280]{1,0:T(8,128)(2,1)S(1)}, u32[]{:S(2)}, u32[]{:S(2)}) collective-permute-start(bf16[160,1280]{1,0:T(8,128)(2,1)S(1)} %collective-permute-done.4), channel_id=1, source_target_pairs={{0,1},{1,0},{2,3},{3,2},{4,5},{5,4},{6,7},{7,6},{8,9},{9,8},{10,11... | collective-permute-start | bytes 1228808 | tf_op jit(solution)/shard_map/ppermute | solution.py:274
  42.7 31.2 %collective-permute-start.7 = (bf16[480,1280]{1,0:T(8,128)(2,1)}, bf16[480,1280]{1,0:T(8,128)(2,1)}, u32[]{:S(2)}, u32[]{:S(2)}) collective-permute-start(bf16[480,1280]{1,0:T(8,128)(2,1)} %constant_dynamic-update-slice_fusion.refs_6_), channel_id=1, source_target_pairs={{0,16},{4,20},{8,24},{12,28},{16,0},{20,4},{24,8},{28,12},{1,17},{... | collective-permute-start | bytes 3686408 | tf_op jit(solution)/shard_map/ppermute | solution.py:268
  44.4 29.5 %collective-permute-start.6 = (bf16[480,1280]{1,0:T(8,128)(2,1)}, bf16[480,1280]{1,0:T(8,128)(2,1)}, u32[]{:S(2)}, u32[]{:S(2)}) collective-permute-start(bf16[480,1280]{1,0:T(8,128)(2,1)} %constant_dynamic-update-slice_fusion.refs_6_), channel_id=1, source_target_pairs={{0,8},{4,12},{8,0},{12,4},{16,24},{20,28},{24,16},{28,20},{1,9},{5... | collective-permute-start | bytes 3686408 | tf_op jit(solution)/shard_map/ppermute | solution.py:268
  48.8 48.6 %copy-start.8 = (f32[1280]{0:T(1024)S(1)}, f32[1280]{0:T(1024)}, u32[]{:S(2)}) copy-start(f32[1280]{0:T(1024)} %param.20) | copy-start | bytes 15364
  48.8 48.6 %copy-start.9 = (f32[1280]{0:T(1024)S(1)}, f32[1280]{0:T(1024)}, u32[]{:S(2)}) copy-start(f32[1280]{0:T(1024)} %param.19) | copy-start | bytes 15364
  48.8 29.3 %collective-permute-start.1 = (bf16[4,320,256]{2,1,0:T(8,128)(2,1)S(1)}, bf16[4,320,256]{2,1,0:T(8,128)(2,1)S(1)}, u32[]{:S(2)}, u32[]{:S(2)}) collective-permute-start(bf16[4,320,256]{2,1,0:T(8,128)(2,1)S(1)} %get-tuple-element.38.refs_0_), channel_id=1, source_target_pairs={{0,1},{1,0},{2,3},{3,2},{4,5},{5,4},{6,7},{7,6},{8,9},{9,8},{10,11... | collective-permute-start | bytes 1966088 | tf_op jit(solution)/shard_map/ppermute | solution.py:274
  49.3 28.8 %collective-permute-start = (bf16[4,320,256]{2,1,0:T(8,128)(2,1)S(1)}, bf16[4,320,256]{2,1,0:T(8,128)(2,1)S(1)}, u32[]{:S(2)}, u32[]{:S(2)}) collective-permute-start(bf16[4,320,256]{2,1,0:T(8,128)(2,1)S(1)} %get-tuple-element.38.refs_0_), channel_id=1, source_target_pairs={{0,2},{1,3},{2,0},{3,1},{4,6},{5,7},{6,4},{7,5},{8,10},{9,11},{10,... | collective-permute-start | bytes 1966088 | tf_op jit(solution)/shard_map/ppermute | solution.py:274
  50.6 43.9 %collective-permute-start.10 = (bf16[480,1280]{1,0:T(8,128)(2,1)}, bf16[480,1280]{1,0:T(8,128)(2,1)S(1)}, u32[]{:S(2)}, u32[]{:S(2)}) collective-permute-start(bf16[480,1280]{1,0:T(8,128)(2,1)} %constant_dynamic-update-slice_fusion.refs_6_), channel_id=1, source_target_pairs={{0,4},{4,0},{8,12},{12,8},{16,20},{20,16},{24,28},{28,24},{1,5},{5... | collective-permute-start | bytes 3686408 | tf_op jit(solution)/shard_map/ppermute | solution.py:268
  76.1 15.4 %collective-permute-start.9 = (bf16[240,1280]{1,0:T(8,128)(2,1)S(1)}, bf16[240,1280]{1,0:T(8,128)(2,1)S(1)}, u32[]{:S(2)}, u32[]{:S(2)}) collective-permute-start(bf16[240,1280]{1,0:T(8,128)(2,1)S(1)} %slice.30), channel_id=1, source_target_pairs={{0,8},{4,12},{8,0},{12,4},{16,24},{20,28},{24,16},{28,20},{1,9},{5... | collective-permute-start | bytes 1843208 | tf_op jit(solution)/shard_map/ppermute | solution.py:268
  77.4 15.7 %collective-permute-start.8 = (bf16[240,1280]{1,0:T(8,128)(2,1)S(1)}, bf16[240,1280]{1,0:T(8,128)(2,1)}, u32[]{:S(2)}, u32[]{:S(2)}) collective-permute-start(bf16[240,1280]{1,0:T(8,128)(2,1)S(1)} %slice.29), channel_id=1, source_target_pairs={{0,16},{4,20},{8,24},{12,28},{16,0},{20,4},{24,8},{28,12},{1,17},{... | collective-permute-start | bytes 1843208 | tf_op jit(solution)/shard_map/ppermute | solution.py:268
  78.1 16.7 %collective-permute-start.2 = (bf16[4,320,256]{2,1,0:T(8,128)(2,1)S(1)}, bf16[4,320,256]{2,1,0:T(8,128)(2,1)S(1)}, u32[]{:S(2)}, u32[]{:S(2)}) collective-permute-start(bf16[4,320,256]{2,1,0:T(8,128)(2,1)S(1)} %collective-permute-done.refs_2_), channel_id=1, source_target_pairs={{0,1},{1,0},{2,3},{3,2},{4,5},{5,4},{6,7},{7,6},{8,9},{9,8},{10,11... | collective-permute-start | bytes 1966088 | tf_op jit(solution)/shard_map/ppermute | solution.py:274
  93.1 3.4 %collective-permute-start.14 = (bf16[240,1280]{1,0:T(8,128)(2,1)S(1)}, bf16[240,1280]{1,0:T(8,128)(2,1)S(1)}, u32[]{:S(2)}, u32[]{:S(2)}) collective-permute-start(bf16[240,1280]{1,0:T(8,128)(2,1)S(1)} %collective-permute-done.9.refs_10_), channel_id=1, source_target_pairs={{0,4},{4,0},{8,12},{12,8},{16,20},{20,16},{24,28},{28,24},{1,5},{5... | collective-permute-start | bytes 1843208 | tf_op jit(solution)/shard_map/ppermute | solution.py:268
  93.1 0.9 copy-start.2
  93.9 6.3 %collective-permute-start.11 = (bf16[480,1280]{1,0:T(8,128)(2,1)}, bf16[480,1280]{1,0:T(8,128)(2,1)}, u32[]{:S(2)}, u32[]{:S(2)}) collective-permute-start(bf16[480,1280]{1,0:T(8,128)(2,1)} %collective-permute-done.6.refs_7_), channel_id=1, source_target_pairs={{0,4},{4,0},{8,12},{12,8},{16,20},{20,16},{24,28},{28,24},{1,5},{5... | collective-permute-start | bytes 3686408 | tf_op jit(solution)/shard_map/ppermute | solution.py:268
  94.5 6.8 %collective-permute-start.12 = (bf16[480,1280]{1,0:T(8,128)(2,1)}, bf16[480,1280]{1,0:T(8,128)(2,1)}, u32[]{:S(2)}, u32[]{:S(2)}) collective-permute-start(bf16[480,1280]{1,0:T(8,128)(2,1)} %collective-permute-done.7.refs_8_), channel_id=1, source_target_pairs={{0,4},{4,0},{8,12},{12,8},{16,20},{20,16},{24,28},{28,24},{1,5},{5... | collective-permute-start | bytes 3686408 | tf_op jit(solution)/shard_map/ppermute | solution.py:268
  94.5 2.0 copy-start.12
  94.5 59.6 %collective-permute-start.18 = (bf16[640,2048]{1,0:T(8,128)(2,1)}, bf16[640,2048]{1,0:T(8,128)(2,1)}, u32[]{:S(2)}, u32[]{:S(2)}) collective-permute-start(bf16[640,2048]{1,0:T(8,128)(2,1)} %refs_1_.1), channel_id=1, source_target_pairs={{0,16},{4,20},{8,24},{12,28},{16,0},{20,4},{24,8},{28,12},{1,17},{... | collective-permute-start | bytes 7864328 | tf_op jit(solution)/shard_map/ppermute | solution.py:268
  94.8 59.3 %collective-permute-start.17 = (bf16[640,2048]{1,0:T(8,128)(2,1)}, bf16[640,2048]{1,0:T(8,128)(2,1)}, u32[]{:S(2)}, u32[]{:S(2)}) collective-permute-start(bf16[640,2048]{1,0:T(8,128)(2,1)} %refs_1_.1), channel_id=1, source_target_pairs={{0,8},{4,12},{8,0},{12,4},{16,24},{20,28},{24,16},{28,20},{1,9},{5... | collective-permute-start | bytes 7864328 | tf_op jit(solution)/shard_map/ppermute | solution.py:268
  96.5 0.8 copy-start.4
  97.3 2.6 collective-permute-start.13
  100.0 54.2 %collective-permute-start.16 = (bf16[4,320,256]{2,1,0:T(8,128)(2,1)S(1)}, bf16[4,320,256]{2,1,0:T(8,128)(2,1)S(1)}, u32[]{:S(2)}, u32[]{:S(2)}) collective-permute-start(bf16[4,320,256]{2,1,0:T(8,128)(2,1)S(1)} %get-tuple-element.29.refs_0_), channel_id=1, source_target_pairs={{0,1},{1,0},{2,3},{3,2},{4,5},{5,4},{6,7},{7,6},{8,9},{9,8},{10,11... | collective-permute-start | bytes 1966088 | tf_op jit(solution)/shard_map/ppermute | solution.py:274
  100.2 53.9 %collective-permute-start.15 = (bf16[4,320,256]{2,1,0:T(8,128)(2,1)S(1)}, bf16[4,320,256]{2,1,0:T(8,128)(2,1)S(1)}, u32[]{:S(2)}, u32[]{:S(2)}) collective-permute-start(bf16[4,320,256]{2,1,0:T(8,128)(2,1)S(1)} %get-tuple-element.29.refs_0_), channel_id=1, source_target_pairs={{0,2},{1,3},{2,0},{3,1},{4,6},{5,7},{6,4},{7,5},{8,10},{9,11},{10,... | collective-permute-start | bytes 1966088 | tf_op jit(solution)/shard_map/ppermute | solution.py:274
  101.3 1.1 copy-start.3
  102.4 1.1 copy-start.5
  154.1 16.3 %collective-permute-start.19 = (bf16[4,320,256]{2,1,0:T(8,128)(2,1)S(1)}, bf16[4,320,256]{2,1,0:T(8,128)(2,1)S(1)}, u32[]{:S(2)}, u32[]{:S(2)}) collective-permute-start(bf16[4,320,256]{2,1,0:T(8,128)(2,1)S(1)} %collective-permute-done.15.refs_2_), channel_id=1, source_target_pairs={{0,1},{1,0},{2,3},{3,2},{4,5},{5,4},{6,7},{7,6},{8,9},{9,8},{10,11... | collective-permute-start | bytes 1966088 | tf_op jit(solution)/shard_map/ppermute | solution.py:274
  155.9 30.1 %collective-permute-start.21 = (bf16[320,2048]{1,0:T(8,128)(2,1)S(1)}, bf16[320,2048]{1,0:T(8,128)(2,1)S(1)}, u32[]{:S(2)}, u32[]{:S(2)}) collective-permute-start(bf16[320,2048]{1,0:T(8,128)(2,1)S(1)} %slice.32), channel_id=1, source_target_pairs={{0,8},{4,12},{8,0},{12,4},{16,24},{20,28},{24,16},{28,20},{1,9},{5... | collective-permute-start | bytes 3932168 | tf_op jit(solution)/shard_map/ppermute | solution.py:268
  159.1 29.8 %collective-permute-start.20 = (bf16[320,2048]{1,0:T(8,128)(2,1)S(1)}, bf16[320,2048]{1,0:T(8,128)(2,1)S(1)}, u32[]{:S(2)}, u32[]{:S(2)}) collective-permute-start(bf16[320,2048]{1,0:T(8,128)(2,1)S(1)} %slice.31), channel_id=1, source_target_pairs={{0,16},{4,20},{8,24},{12,28},{16,0},{20,4},{24,8},{28,12},{1,17},{... | collective-permute-start | bytes 3932168 | tf_op jit(solution)/shard_map/ppermute | solution.py:268
  160.8 76.1 %collective-permute-start.22 = (bf16[640,2048]{1,0:T(8,128)(2,1)}, bf16[640,2048]{1,0:T(8,128)(2,1)S(1)}, u32[]{:S(2)}, u32[]{:S(2)}) collective-permute-start(bf16[640,2048]{1,0:T(8,128)(2,1)} %refs_1_.1), channel_id=1, source_target_pairs={{0,4},{4,0},{8,12},{12,8},{16,20},{20,16},{24,28},{28,24},{1,5},{5... | collective-permute-start | bytes 7864328 | tf_op jit(solution)/shard_map/ppermute | solution.py:268
  160.8 76.1 %collective-permute-start.23 = (bf16[640,2048]{1,0:T(8,128)(2,1)}, bf16[640,2048]{1,0:T(8,128)(2,1)S(1)}, u32[]{:S(2)}, u32[]{:S(2)}) collective-permute-start(bf16[640,2048]{1,0:T(8,128)(2,1)} %collective-permute-done.17.refs_2_), channel_id=1, source_target_pairs={{0,4},{4,0},{8,12},{12,8},{16,20},{20,16},{24,28},{28,24},{1,5},{5... | collective-permute-start | bytes 7864328 | tf_op jit(solution)/shard_map/ppermute | solution.py:268
  170.4 66.5 %collective-permute-start.24 = (bf16[640,2048]{1,0:T(8,128)(2,1)}, bf16[640,2048]{1,0:T(8,128)(2,1)}, u32[]{:S(2)}, u32[]{:S(2)}) collective-permute-start(bf16[640,2048]{1,0:T(8,128)(2,1)} %collective-permute-done.18.refs_3_), channel_id=1, source_target_pairs={{0,4},{4,0},{8,12},{12,8},{16,20},{20,16},{24,28},{28,24},{1,5},{5... | collective-permute-start | bytes 7864328 | tf_op jit(solution)/shard_map/ppermute | solution.py:268
  170.6 68.6 %copy-start.6 = (f32[2048]{0:T(1024)S(1)}, f32[2048]{0:T(1024)}, u32[]{:S(2)}) copy-start(f32[2048]{0:T(1024)} %param.22) | copy-start | bytes 24580
  186.0 50.9 %collective-permute-start.26 = (bf16[320,2048]{1,0:T(8,128)(2,1)S(1)}, bf16[320,2048]{1,0:T(8,128)(2,1)S(1)}, u32[]{:S(2)}, u32[]{:S(2)}) collective-permute-start(bf16[320,2048]{1,0:T(8,128)(2,1)S(1)} %collective-permute-done.21.refs_5_), channel_id=1, source_target_pairs={{0,4},{4,0},{8,12},{12,8},{16,20},{20,16},{24,28},{28,24},{1,5},{5... | collective-permute-start | bytes 3932168 | tf_op jit(solution)/shard_map/ppermute | solution.py:268
  188.9 48.0 %collective-permute-start.25 = (bf16[320,2048]{1,0:T(8,128)(2,1)S(1)}, bf16[320,2048]{1,0:T(8,128)(2,1)S(1)}, u32[]{:S(2)}, u32[]{:S(2)}) collective-permute-start(bf16[320,2048]{1,0:T(8,128)(2,1)S(1)} %collective-permute-done.20.refs_4_), channel_id=1, source_target_pairs={{0,4},{4,0},{8,12},{12,8},{16,20},{20,16},{24,28},{28,24},{1,5},{5... | collective-permute-start | bytes 3932168 | tf_op jit(solution)/shard_map/ppermute | solution.py:268
  236.9 1.5 copy-start.10
  236.9 2.2 copy-start.11
  270.0 7.8 %all-to-all-start.1 = ((s32[8,1,4]{2,1,0:T(1,128)}), s32[8,1,4]{2,1,0:T(1,128)S(1)}, u32[]{:S(2)}, u32[]{:S(2)}) async-start(s32[8,1,4]{2,1,0:T(1,128)} %bitcast.14), calls=%async_computation.2 | async-start | bytes 8192 | tf_op jit(solution)/shard_map/all_to_all | solution.py:264
  279.2 36.8 %copy-start.1 = (bf16[2048,320]{0,1:T(8,128)(2,1)S(1)}, bf16[2048,320]{0,1:T(8,128)(2,1)}, u32[]{:S(2)}) copy-start(bf16[2048,320]{0,1:T(8,128)(2,1)} %param.13) | copy-start | bytes 3932164
Sparse Core Ops, SparseCore 0:
  269.4 44.2 reduce-scatter.1

commit v3 on v2

--- a/solution.py
+++ b/solution.py
@@ -28,22 +28,20 @@
     vit_gain, merge_gain = refs[at + nw : at + nw + 2]
     at += nw + 2 + int(aliased)
     out = refs[at]
-    w, xs, nrm, packed, mixed, vit, bias, sem = refs[at + 1 :]
+    w, xs, nrm, packed, mixed, vit, sem = refs[at + 1 :]
     t = info[0]
+    heads = HV // tp
+    rows = packed.shape[1]
     feats = pieces[0].shape[1]
-    heads = HV // tp
-    rows = packed.shape[0]
     first_proj = 3 * DV
     cols = xs.shape[1]
     step = pl.program_id(0)
 
     @pl.when(step == 0)
     def _():
-        for copy in moves(info, w_refs, w, sem):
-            copy.start()
-        key = lax.broadcasted_iota(jnp.int32, (cols, cols), 0) // (WIN // MERGE) % GROUP
-        query = lax.broadcasted_iota(jnp.int32, (cols, cols), 1) // (WIN // MERGE) % GROUP
-        bias[...] = jnp.where(key == query, 0.0, -1e30).astype(F32)
+        for part in moves(info, w_refs, w, sem):
+            for copy in part:
+                copy.start()
 
     for d, piece in enumerate(pieces):
         xs[pl.ds(pl.multiple_of((t ^ d) * feats, feats), feats), :] = piece[0]
@@ -52,28 +50,64 @@
     scale = lax.rsqrt(jnp.mean(xf * xf, axis=0, keepdims=True) + 1e-6)
     nrm[...] = (xf * scale * vit_gain[...]).astype(BF)
 
-    @pl.when(step == 0)
-    def _():
-        for copy in moves(info, w_refs, w, sem):
-            copy.wait()
-
+    pair = 2 * WIN
+    first = lax.broadcasted_iota(jnp.int32, (WIN, pair), 1) < WIN
     fold = (HS**-0.5) * 1.4426950408889634
 
-    def group(g, carry):
-        mine = w[pl.ds(pl.multiple_of(g * rows, rows), rows), :]
-        packed[...] = jnp.dot(mine, nrm[...], preferred_element_type=F32).astype(BF)
+    none = jnp.zeros((pair, pair), BF)
+
+    def arrived(d):
+        @pl.when(step == 0)
+        def _():
+            for copy in moves(info, w_refs, w, sem)[d]:
+                copy.wait()
+
+    def pack(d, slot):
+        mine = w[pl.ds(pl.multiple_of((t ^ d) * rows, rows), rows), :]
+        packed[slot] = jnp.dot(mine, nrm[...], preferred_element_type=F32).astype(BF)
+
+    def heads_of(d, more):
+        slot = lax.rem(d, 2)
+        now = packed.at[slot]
+        scores = []
         for h in range(heads):
-            q, k, v = (packed[(3 * h + i) * HS : (3 * h + i + 1) * HS, :] for i in range(3))
+            q, k = (now[(3 * h + n) * HS : (3 * h + n + 1) * HS, :] for n in range(2))
             s = lax.dot_general(k, q, (((0,), (0,)), ((), ())), preferred_element_type=F32)
-            s = s * fold + bias[...]
+            for n in range(cols // pair):
+                at = n * pair
+                s0, s1 = s[at : at + WIN, at : at + pair], s[at + WIN : at + pair, at : at + pair]
+                scores.append(jnp.where(first, s0, s1) * fold)
+        if more:
+            pack(d + 1, 1 - slot)
+        probs = []
+        for s in scores:
             p = jnp.exp2(s - jnp.max(s, axis=0, keepdims=True))
-            total = jnp.sum(p, axis=0, keepdims=True)
-            p = (p * (1.0 / total)).astype(BF)
-            m = jnp.dot(v, p, preferred_element_type=F32).astype(BF)
-            mixed[pl.ds(pl.multiple_of(g * heads * HS, heads * HS) + h * HS, HS), :] = m
+            p = p * (1.0 / jnp.sum(p, axis=0, keepdims=True))
+            probs.append(
+                jnp.concatenate([jnp.where(first, p, 0.0), jnp.where(first, 0.0, p)]).astype(BF)
+            )
+        for h in range(heads):
+            v = now[(3 * h + 2) * HS : (3 * h + 3) * HS, :]
+            p = jnp.concatenate(
+                [
+                    jnp.concatenate([probs[2 * h], none], axis=1),
+                    jnp.concatenate([none, probs[2 * h + 1]], axis=1),
+                ]
+            )
+            m = jnp.dot(v, p, preferred_element_type=F32)
+            at = pl.multiple_of((t ^ d) * heads * HS, heads * HS) + h * HS
+            mixed[pl.ds(at, HS), :] = m.astype(BF)
+
+    def one(d, carry):
+        for later in range(1, tp):
+            pl.when(d + 1 == later)(functools.partial(arrived, later))
+        heads_of(d, True)
         return carry
 
-    lax.fori_loop(0, tp, group, 0)
+    arrived(0)
+    pack(0, 0)
+    lax.fori_loop(0, tp - 1, one, 0)
+    heads_of(jnp.int32(tp - 1), False)
 
     width = 256
     sums = jnp.zeros((cols, 1), F32)
@@ -91,9 +125,11 @@
         sums = sums + jnp.sum(yf * yf, axis=1, keepdims=True)
     scale = lax.rsqrt(sums * (1.0 / DV) + 1e-6)
     merged = (vit[...].astype(F32) * scale * merge_gain[...]).astype(BF)
-    per = cols // MERGE
-    for c in range(MERGE):
-        out[c, 0] = merged[c * per : (c + 1) * per, :]
+    per = WIN // MERGE
+    for w_at in range(cols // WIN):
+        for c in range(MERGE):
+            at = w_at * WIN + c * per
+            out[c, 0, w_at * per : (w_at + 1) * per] = merged[at : at + per, :]
 
 
 def attend(tp, info, pieces, weights, moves, count, vit_gain, merge_gain, blocks, buf):
@@ -121,10 +157,9 @@
                 pltpu.VMEM((4 * DV, DV), BF),
                 pltpu.VMEM((DV, cols), BF),
                 pltpu.VMEM((DV, cols), BF),
-                pltpu.VMEM((3 * DV // tp, cols), BF),
+                pltpu.VMEM((2, 3 * DV // tp, cols), BF),
                 pltpu.VMEM((DV, cols), BF),
                 pltpu.VMEM((cols, DV), BF),
-                pltpu.VMEM((cols, cols), F32),
                 pltpu.SemaphoreType.DMA((count,)),
             ],
         ),
@@ -284,9 +319,9 @@
     paired = seq_count == 8 and per_peer == GROUP
 
     source = (
-        window[:, None, :, None] * WIN
+        window[:, :, None, None] * WIN
         + jnp.arange(tokens)[None, None, None, :] * MERGE
-        + jnp.arange(MERGE)[None, :, None, None]
+        + jnp.arange(MERGE)[None, None, :, None]
     ).reshape(-1)
     pick = (jnp.arange(patches.shape[0])[:, None] == source[None, :]).astype(BF)
     sent = lax.dot_general(
@@ -302,8 +337,8 @@
         concat_axis=0,
         tiled=True,
     )
-    full = full.reshape(blocks, GROUP // per_peer, feats, MERGE, per_peer, tokens)
-    full = full.transpose(0, 2, 3, 1, 4, 5).reshape(blocks, feats, GROUP * WIN)
+    full = full.reshape(blocks, GROUP // per_peer, feats, step)
+    full = full.transpose(0, 2, 1, 3).reshape(blocks, feats, GROUP * WIN)
     mid = blocks // 2
 
     if paired:
@@ -314,7 +349,9 @@
             lax.dynamic_slice_in_dim(wq_t, jnp.minimum(s, q_parts - 1) * share, share),
             lax.dynamic_slice_in_dim(w_proj, jnp.maximum(s - q_parts, 0) * share, share),
         )
-        others = jnp.concatenate(spread(mine)[1:])
+        early = lax.optimization_barrier((tp_xor(mine, 1), tp_xor(mine, 2)))
+        others = [jnp.concatenate(early), tp_xor(early[1], 1)]
+        held_planes = [(1, 2), (3,)]
 
         def sides(x):
             return list(lax.optimization_barrier((xor(x, 2), xor(x, 4))))
@@ -326,10 +363,12 @@
         def cores(pieces):
             return [xor(v, 1) for v in pieces]
 
-        vit_pieces = [others] + sides(others)
-        vit_pieces += list(lax.optimization_barrier(tuple(corners(*vit_pieces[1:]))))
-        merge_pieces = [w_merge] + sides(tie(w_merge, vit_pieces[3]))
-        vit_weights = [wq_t, w_proj] + vit_pieces + cores(vit_pieces)
+        first_by = sides(others[0])
+        last_by = sides(tie(others[1], first_by))
+        first_set = [others[0]] + first_by + corners(*first_by)
+        last_set = [others[1]] + last_by + corners(*last_by)
+        vit_weights = [wq_t, w_proj] + first_set + cores(first_set) + last_set + cores(last_set)
+        merge_by = sides(tie(w_merge, last_by))
         q_rows, p_rows = wq_t.shape[0], w_proj.shape[0]
 
         def spans(rows):
@@ -337,16 +376,19 @@
             return [(d ^ e, lo, hi) for e in range(2) for d, lo, hi in whole]
 
         vit_parts = []
-        for n, (d, lo, hi) in enumerate(spans(others.shape[0])):
-            for j in range(1, tp):
-                first, last = max(lo, (j - 1) * share), min(hi, j * share)
-                if first < last:
-                    vit_parts.append((n, d, j, first - lo, first - (j - 1) * share, last - first))
+        for planes in held_planes:
+            base = 2 + 10 * held_planes.index(planes)
+            for n, (d, lo, hi) in enumerate(spans(share * len(planes))):
+                for k, j in enumerate(planes):
+                    top, end = max(lo, k * share), min(hi, (k + 1) * share)
+                    if top < end:
+                        vit_parts.append((base + n, d, j, top - lo, top - k * share, end - top))
         vit_count = 2 + len(vit_parts)
 
         def vit_moves(info, refs, w, sem):
             t, s = info[0], info[1]
-            copies = [
+            copies = [[] for _ in range(tp)]
+            copies[0] = [
                 pltpu.make_async_copy(
                     refs[0], w.at[pl.ds(pl.multiple_of(t * q_rows, 16), q_rows)], sem.at[0]
                 ),
@@ -354,7 +396,7 @@
                     refs[1], w.at[pl.ds(pl.multiple_of(3 * DV + t * p_rows, 16), p_rows)], sem.at[1]
                 ),
             ]
-            for n, d, j, source, offset, count in vit_parts:
+            for at, (n, d, j, source, offset, count) in enumerate(vit_parts):
                 part = s ^ d
                 q = t ^ j
                 row = offset + jnp.where(
@@ -362,11 +404,11 @@
                     q * q_rows + part * share,
                     3 * DV + q * p_rows + (part - q_parts) * share,
                 )
-                copies.append(
+                copies[j].append(
                     pltpu.make_async_copy(
-                        refs[2 + n].at[source : source + count],
+                        refs[n].at[source : source + count],
                         w.at[pl.ds(pl.multiple_of(row, 16), count)],
-                        sem.at[len(copies)],
+                        sem.at[2 + at],
                     )
                 )
             return copies
@@ -397,13 +439,23 @@
             lax.all_gather(w_proj, "tp", axis=0, tiled=True),
         ]
         merge_weights = [lax.all_gather(w_merge, "seq", axis=0, tiled=True)]
-        vit_count = 2
+        vit_count = 2 * tp
+        q_rows, p_rows = wq_t.shape[0], w_proj.shape[0]
 
         def vit_moves(info, refs, w, sem):
-            return [
-                pltpu.make_async_copy(refs[0], w.at[0 : 3 * DV], sem.at[0]),
-                pltpu.make_async_copy(refs[1], w.at[3 * DV : 4 * DV], sem.at[1]),
-            ]
+            copies = []
+            for d in range(tp):
+                g = info[0] ^ d
+                q_part = pl.ds(pl.multiple_of(g * q_rows, 16), q_rows)
+                p_part = pl.ds(pl.multiple_of(g * p_rows, 16), p_rows)
+                p_spot = pl.ds(pl.multiple_of(3 * DV + g * p_rows, 16), p_rows)
+                copies.append(
+                    [
+                        pltpu.make_async_copy(refs[0].at[q_part], w.at[q_part], sem.at[2 * d]),
+                        pltpu.make_async_copy(refs[1].at[p_part], w.at[p_spot], sem.at[2 * d + 1]),
+                    ]
+                )
+            return copies
 
         def merge_moves(info, refs, h, i, slot, sem):
             wide = slot.shape[1]
@@ -414,23 +466,35 @@
             return i
 
     def encode(first, pieces, buf):
-        info = jnp.concatenate([jnp.stack([t, s]), first + jnp.arange(mid, dtype=jnp.int32)])
+        count = pieces[0].shape[0]
+        info = jnp.concatenate([jnp.stack([t, s]), first + jnp.arange(count, dtype=jnp.int32)])
         return attend(
             tp, info, pieces, vit_weights, vit_moves, vit_count,
             vit_gain[:, None], merge_gain[None, :], blocks, buf,
         )
 
+    merged = None
     if paired:
-        near = list(lax.optimization_barrier((tp_xor(full[:mid], 2), tp_xor(full[:mid], 1))))
-        later = tie(full[mid:], near[0])
-        far = [tp_xor(later, 2), tp_xor(later, 1)]
-        merged = encode(0, [full[:mid], near[1], near[0], tp_xor(near[0], 1)], None)
-        merged, far, by = lax.optimization_barrier((merged, far, merge_pieces[1:]))
-        merge_pieces = [w_merge] + by + corners(*by)
+        cuts = [0, 2, 5, 8]
+        near, done = [], []
+        for lo, hi in zip(cuts[:-1], cuts[1:]):
+            own = full[lo:hi] if not near else tie(full[lo:hi], near[-1])
+            near.append(lax.optimization_barrier((tp_xor(own, 1), tp_xor(own, 2))))
+        for n, lo in enumerate(cuts[:-1]):
+            by1, by2 = near[n]
+            if n >= 2:
+                merged, by2 = lax.optimization_barrier((merged, by2))
+            far = tp_xor(by2, 1)
+            if n == len(cuts) - 2:
+                merged, far, merge_by = lax.optimization_barrier((merged, far, merge_by))
+            if n == 1:
+                merged, live_here = lax.optimization_barrier((merged, live_here))
+            merged = encode(lo, [full[lo : cuts[n + 1]], by1, by2, far], merged)
+        merge_corners = corners(*merge_by)
+        merged, merge_corners = lax.optimization_barrier((merged, merge_corners))
+        merge_pieces = [w_merge] + list(merge_by) + list(merge_corners)
         merge_weights = merge_pieces + cores(merge_pieces)
-        merged = encode(mid, [full[mid:], far[1], far[0], tp_xor(far[0], 1)], merged)
     else:
-        merged = None
         for first in (0, mid):
             merged = encode(first, spread(full[first : first + mid]), merged)
     partial_value = project(

time: 323 us -> 325 us (level)
  Pallas kernels: 126 us -> 96.8 us
  waiting for transfers between devices: 122 us -> 142 us
  starting transfers between devices: 28.8 us -> 35.8 us
    pallas_call x2 -> x3, Pallas kernels: 96.1 us -> 66.6 us  [attend(): pl.pallas_call(functools.partial(attend_kernel, tp, moves, len(weights),...]
    ppermute x9 -> x12, waiting for transfers between devices: 18.7 us -> 47.9 us  [tp_xor(): return lax.ppermute(x, 'tp', [(i, i ^ d) for i in range(tp)])]
    ppermute x18 -> x27, waiting for transfers between devices: 60.9 us -> 40.9 us  [xor(): return lax.ppermute(x, 'seq', [(i, i ^ d) for i in range(seq_count)])]
    reduce_scatter x1, waiting for transfers between devices: 34.4 us -> 43.1 us  [shards(): lax.psum_scatter(partial_value, 'tp', scatter_dimension=0, tiled=True)]
    all_to_all x1, waiting for transfers between devices: 2.88 us -> 10.6 us  [shards(): lax.all_to_all(sent.reshape(feats, seq_count, step).transpose(1, 0, 2), '...]
    ppermute x18 -> x27, starting transfers between devices: 11.6 us -> 17 us  [xor(): return lax.ppermute(x, 'seq', [(i, i ^ d) for i in range(seq_count)])]
    all_to_all x1, waiting for transfers between devices: 4.51 us -> 0.01 us  [shards(): lax.all_to_all(live_send, 'seq', split_axis=0, concat_axis=0, tiled=True)]
    ppermute x9 -> x12, starting transfers between devices: 10.1 us -> 11.5 us  [tp_xor(): return lax.ppermute(x, 'tp', [(i, i ^ d) for i in range(tp)])]
  transfers between devices with their start and end apart: 30 -> 42, of which waited for: 14 -> 17; matrix products, arithmetic and copies ran while one was open for 7% -> 7% of each run, Pallas kernels for 30% -> 21%
where the time goes in v3:
time: 325 us; the launch traced here: 324 us
  waiting for transfers between devices  142 us (44%)
  Pallas kernels  96.8 us (30%)
  starting transfers between devices  35.8 us (11%)
  local copies, waits for them, and re-layouts  22.6 us (7%)
  between operations  13.8 us (4%)
  other arithmetic  9 us (3%)
  matrix products  3.47 us (1%)
    pallas_call x3, Pallas kernels, attend(): pl.pallas_call(functools.partial(attend_kernel, tp, moves, len(weights),...  66.6 us
    ppermute x12, waiting for transfers between devices, tp_xor(): return lax.ppermute(x, 'tp', [(i, i ^ d) for i in range(tp)])  47.9 us
    reduce_scatter x1, waiting for transfers between devices, shards(): lax.psum_scatter(partial_value, 'tp', scatter_dimension=0, tiled=True)  43.1 us
    ppermute x27, waiting for transfers between devices, xor(): return lax.ppermute(x, 'seq', [(i, i ^ d) for i in range(seq_count)])  40.9 us
    pallas_call x1, Pallas kernels, project(): pl.pallas_call(functools.partial(project_kernel, moves, position, len(wei...  30.2 us
    ppermute x27, starting transfers between devices, xor(): return lax.ppermute(x, 'seq', [(i, i ^ d) for i in range(seq_count)])  17 us
    ppermute x12, starting transfers between devices, tp_xor(): return lax.ppermute(x, 'tp', [(i, i ^ d) for i in range(tp)])  11.5 us
    all_to_all x1, waiting for transfers between devices, shards(): lax.all_to_all(sent.reshape(feats, seq_count, step).transpose(1, 0, 2), '...  10.6 us
  transfers between devices with their start and end apart: 42, of which 17 were waited for; matrix products, arithmetic and copies ran while one was open for 7% of the time, Pallas kernels for 21%

profile of v3, /device:TPU:0, one launch (start us, length us, event | category | flops | bytes accessed | tf_op | source)
XLA Modules:
  0.0 323.9 jit_solution(7736861884394277332)
XLA Ops:
  6.5 2.1 bitcast_select_fusion
  8.6 3.0 collective-permute-start.7
  11.6 2.6 collective-permute-start.8
  14.2 1.3 fusion.10
  15.5 2.3 sort.17
  17.9 1.9 compare_convert_fusion
  19.8 0.7 gather_fusion.1
  20.5 1.4 gather_fusion
  22.1 3.5 %fusion.2 = bf16[2048,320]{0,1:T(8,128)(2,1)S(1)} fusion(bf16[2048,320]{0,1:T(8,128)(2,1)S(1)} %copy-done, s32[2048]{0:T(1024)S(1)} %add.118), kind=kOutput, calls=%fused_computation.5 | convolution fusion | flops 2689204224 | bytes 2629632 | tf_op jit(solution)/shard_map/dot_general | solution.py:327
  25.6 1.2 copy.31
  26.8 3.7 %all-to-all-start = ((bf16[8,320,256]{2,1,0:T(8,128)(2,1)}), bf16[8,320,256]{2,1,0:T(8,128)(2,1)S(1)}, u32[]{:S(2)}, u32[]{:S(2)}) async-start(bf16[8,320,256]{2,1,0:T(8,128)(2,1)} %bitcast.36), calls=%async_computation | async-start | bytes 2621440 | tf_op jit(solution)/shard_map/all_to_all | solution.py:333
  30.5 2.1 collective-permute-done.8
  32.6 0.8 constant_dynamic-update-slice_fusion.1
  33.4 1.8 constant_dynamic-update-slice_fusion.refs_6_
  35.2 1.5 collective-permute-start.9
  36.7 1.5 collective-permute-start.10
  38.6 10.6 %all-to-all-done = bf16[8,320,256]{2,1,0:T(8,128)(2,1)S(1)} async-done(((bf16[8,320,256]{2,1,0:T(8,128)(2,1)}), bf16[8,320,256]{2,1,0:T(8,128)(2,1)S(1)}, u32[]{:S(2)}, u32[]{:S(2)}) %all-to-all-start) | async-done | bytes 1310752 | tf_op jit(solution)/shard_map/all_to_all | solution.py:333
  49.8 0.9 collective-permute-done.18.refs_16_
  50.7 14.8 %collective-permute-done.9.refs_7_ = bf16[320,1280]{1,0:T(8,128)(2,1)} collective-permute-done((bf16[320,1280]{1,0:T(8,128)(2,1)}, bf16[320,1280]{1,0:T(8,128)(2,1)}, u32[]{:S(2)}, u32[]{:S(2)}) %collective-permute-start.9) | collective-permute-done | bytes 819232 | tf_op jit(solution)/shard_map/ppermute | solution.py:303
  65.5 1.0 slice.39
  66.6 1.5 collective-permute-start.11
  68.5 0.6 collective-permute-start.19
  69.0 0.7 copy-done.2
  69.7 1.4 collective-permute-start.20
  71.1 1.0 slice.40
  72.1 12.8 %collective-permute-done.1.refs_2_ = bf16[2,320,256]{2,1,0:T(8,128)(2,1)S(1)} collective-permute-done((bf16[2,320,256]{2,1,0:T(8,128)(2,1)S(1)}, bf16[2,320,256]{2,1,0:T(8,128)(2,1)S(1)}, u32[]{:S(2)}, u32[]{:S(2)}) %collective-permute-start.1) | collective-permute-done | bytes 327712 | tf_op jit(solution)/shard_map/ppermute | solution.py:309
  84.9 0.7 collective-permute-start.12
  85.7 1.2 fusion.9
  86.9 2.1 collective-permute-start.2
  89.0 7.3 %collective-permute-done.12.refs_10_ = bf16[160,1280]{1,0:T(8,128)(2,1)} collective-permute-done((bf16[160,1280]{1,0:T(8,128)(2,1)S(1)}, bf16[160,1280]{1,0:T(8,128)(2,1)}, u32[]{:S(2)}, u32[]{:S(2)}) %collective-permute-start.12) | collective-permute-done | bytes 409632 | tf_op jit(solution)/shard_map/ppermute | solution.py:303
  96.4 10.3 %collective-permute-done.28.refs_3_ = bf16[2,320,256]{2,1,0:T(8,128)(2,1)S(1)} collective-permute-done((bf16[2,320,256]{2,1,0:T(8,128)(2,1)S(1)}, bf16[2,320,256]{2,1,0:T(8,128)(2,1)S(1)}, u32[]{:S(2)}, u32[]{:S(2)}) %collective-permute-start.28) | collective-permute-done | bytes 327712 | tf_op jit(solution)/shard_map/ppermute | solution.py:309
  106.7 1.7 collective-permute-start.21
  108.4 4.5 %collective-permute-done.21.refs_19_ = bf16[80,1280]{1,0:T(8,128)(2,1)S(1)} collective-permute-done((bf16[80,1280]{1,0:T(8,128)(2,1)S(1)}, bf16[80,1280]{1,0:T(8,128)(2,1)S(1)}, u32[]{:S(2)}, u32[]{:S(2)}) %collective-permute-start.21) | collective-permute-done | bytes 204832 | tf_op jit(solution)/shard_map/ppermute | solution.py:303
  112.9 1.3 collective-permute-start.22
  114.3 4.4 %collective-permute-done.22.refs_20_ = bf16[80,1280]{1,0:T(8,128)(2,1)S(1)} collective-permute-done((bf16[80,1280]{1,0:T(8,128)(2,1)S(1)}, bf16[80,1280]{1,0:T(8,128)(2,1)S(1)}, u32[]{:S(2)}, u32[]{:S(2)}) %collective-permute-start.22) | collective-permute-done | bytes 204832 | tf_op jit(solution)/shard_map/ppermute | solution.py:303
  120.3 0.7 all_to_all.12
  120.9 3.3 %all-to-all-start.1 = ((s32[8,1,4]{2,1,0:T(1,128)}), s32[8,1,4]{2,1,0:T(1,128)S(1)}, u32[]{:S(2)}, u32[]{:S(2)}) async-start(s32[8,1,4]{2,1,0:T(1,128)} %bitcast.12), calls=%async_computation.1 | async-start | bytes 8192 | tf_op jit(solution)/shard_map/all_to_all | solution.py:299
  124.5 1.8 collective-permute-start.30
  126.3 1.5 collective-permute-start.31
  128.4 1.1 broadcast_in_dim.41.refs_26_
  129.6 0.9 collective-permute-start.5
  130.5 1.2 collective-permute-start.6
  131.7 1.0 copy-done.3
  132.7 1.0 copy-done.5
  133.7 1.0 copy-done.7
  134.7 0.9 copy-done.9
  135.6 0.9 copy-done.12
  136.5 17.6 %attend.3.refs_28_ = bf16[4,8,64,1280]{3,2,1,0:T(8,128)(2,1)} custom-call(s32[4]{0:T(128)S(1)} %pad_add_fusion.4.info, bf16[2,320,256]{2,1,0:T(8,128)(2,1)S(1)} %slice.56.refs_0_, bf16[2,320,256]{2,1,0:T(8,128)(2,1)S(1)} %copy-done.3, bf16[2,320,256]{2,1,0:T(8,128)(2,1)S(1)} %copy-done.5, bf16[2,320,256]{2,1,0:T(8,128)(2,1)S(1)} %copy-done.7, ...), custom_call_target="tpu_custom_call" | custom-call | flops 8388608000 | bytes 14680064 | tf_op jit(solution)/shard_map/attend/pallas_call | solution.py:148
  154.5 9.4 %collective-permute-done.6.refs_3_ = bf16[3,320,256]{2,1,0:T(8,128)(2,1)S(1)} collective-permute-done((bf16[3,320,256]{2,1,0:T(8,128)(2,1)}, bf16[3,320,256]{2,1,0:T(8,128)(2,1)S(1)}, u32[]{:S(2)}, u32[]{:S(2)}) %collective-permute-start.6) | collective-permute-done | bytes 491552 | tf_op jit(solution)/shard_map/ppermute | solution.py:309
  163.9 0.8 copy-done.23
  164.7 24.4 %attend.4.refs_28_ = bf16[4,8,64,1280]{3,2,1,0:T(8,128)(2,1)} custom-call(s32[5]{0:T(128)S(1)} %pad_add_fusion.3.info, bf16[3,320,256]{2,1,0:T(8,128)(2,1)S(1)} %get-tuple-element.39.refs_0_, bf16[3,320,256]{2,1,0:T(8,128)(2,1)S(1)} %collective-permute-done.2.refs_1_, bf16[3,320,256]{2,1,0:T(8,128)(2,1)} %copy-done.20, ...), custom_call_target="tpu_custom_call", output_to_operand_aliasing={{}: (29, {})} | custom-call | flops 12582912000 | bytes 14680064 | tf_op jit(solution)/shard_map/attend/pallas_call | solution.py:148
  189.5 12.1 %collective-permute-done.29.refs_3_ = bf16[3,320,256]{2,1,0:T(8,128)(2,1)S(1)} collective-permute-done((bf16[3,320,256]{2,1,0:T(8,128)(2,1)S(1)}, bf16[3,320,256]{2,1,0:T(8,128)(2,1)S(1)}, u32[]{:S(2)}, u32[]{:S(2)}) %collective-permute-start.29) | collective-permute-done | bytes 491552 | tf_op jit(solution)/shard_map/ppermute | solution.py:309
  201.6 1.6 slice.43
  203.3 1.4 slice.44
  204.7 0.6 collective-permute-start.36
  205.2 0.5 collective-permute-start.32
  206.2 24.7 %attend.5 = bf16[4,8,64,1280]{3,2,1,0:T(8,128)(2,1)} custom-call(s32[5]{0:T(128)S(1)} %pad_add_fusion.1.info, bf16[3,320,256]{2,1,0:T(8,128)(2,1)S(1)} %get-tuple-element.42.refs_0_, bf16[3,320,256]{2,1,0:T(8,128)(2,1)S(1)} %collective-permute-done.4.refs_1_, bf16[3,320,256]{2,1,0:T(8,128)(2,1)} %copy-done.21, ...), custom_call_target="tpu_custom_call", output_to_operand_aliasing={{}: (29, {})} | custom-call | flops 12582912000 | bytes 14680064 | tf_op jit(solution)/shard_map/attend/pallas_call | solution.py:148
  230.9 5.1 %collective-permute-done.32.refs_4_ = bf16[320,2048]{1,0:T(8,128)(2,1)S(1)} collective-permute-done((bf16[320,2048]{1,0:T(8,128)(2,1)S(1)}, bf16[320,2048]{1,0:T(8,128)(2,1)S(1)}, u32[]{:S(2)}, u32[]{:S(2)}) %collective-permute-start.32) | collective-permute-done | bytes 1310752 | tf_op jit(solution)/shard_map/ppermute | solution.py:303
  236.9 2.4 collective-permute-done.37.refs_9_
  239.3 1.9 collective-permute-done.38.refs_10_
  241.2 30.2 %project.1 = bf16[512,2176]{1,0:T(8,128)(2,1)} custom-call(s32[2]{0:T(128)S(1)} %pad_add_fusion.info, bf16[4,512,1280]{2,1,0:T(8,128)(2,1)} %bitcast.45, bf16[640,2048]{1,0:T(8,128)(2,1)} %refs_1_.1, bf16[640,2048]{1,0:T(8,128)(2,1)} %collective-permute-done.30.refs_2_, bf16[640,2048]{1,0:T(8,128)(2,1)} %collective-permute-done.31.refs_3_, ...), custom_call_target="tpu_custom_call" | custom-call | flops 15032385536 | bytes 37748736 | tf_op jit(solution)/shard_map/project/pallas_call | solution.py:249
  271.8 43.1 %reduce-scatter.2.cloned.1.call-done = bf16[128,2176]{1,0:T(8,128)(2,1)} async-done(((bf16[512,2176]{1,0:T(8,128)(2,1)}), bf16[128,2176]{1,0:T(8,128)(2,1)}) %reduce-scatter.2.cloned.1.call-update) | async-done | bytes 557072 | tf_op jit(solution)/shard_map/reduce_scatter | solution.py:503
  314.9 1.1 convert_element_type.22
  316.1 1.0 fusion.4
  (119 shorter events, 7.0 us)
Async XLA Ops:
  6.5 15.6 %copy-start = (bf16[2048,320]{0,1:T(8,128)(2,1)S(1)}, bf16[2048,320]{0,1:T(8,128)(2,1)}, u32[]{:S(2)}) copy-start(bf16[2048,320]{0,1:T(8,128)(2,1)} %param.13) | copy-start | bytes 3932164
  8.6 21.9 %collective-permute-start.7 = (bf16[160,1280]{1,0:T(8,128)(2,1)}, bf16[160,1280]{1,0:T(8,128)(2,1)S(1)}, u32[]{:S(2)}, u32[]{:S(2)}) collective-permute-start(bf16[160,1280]{1,0:T(8,128)(2,1)} %bitcast_select_fusion), channel_id=1, source_target_pairs={{0,1},{1,0},{2,3},{3,2},{4,5},{5,4},{6,7},{7,6},{8,9},{9,8},{10,11... | collective-permute-start | bytes 1228808 | tf_op jit(solution)/shard_map/ppermute | solution.py:309
  11.6 21.0 %collective-permute-start.8 = (bf16[160,1280]{1,0:T(8,128)(2,1)}, bf16[160,1280]{1,0:T(8,128)(2,1)}, u32[]{:S(2)}, u32[]{:S(2)}) collective-permute-start(bf16[160,1280]{1,0:T(8,128)(2,1)} %bitcast_select_fusion), channel_id=1, source_target_pairs={{0,2},{1,3},{2,0},{3,1},{4,6},{5,7},{6,4},{7,5},{8,10},{9,11},{10,... | collective-permute-start | bytes 1228808 | tf_op jit(solution)/shard_map/ppermute | solution.py:309
  26.8 22.5 %all-to-all-start = ((bf16[8,320,256]{2,1,0:T(8,128)(2,1)}), bf16[8,320,256]{2,1,0:T(8,128)(2,1)S(1)}, u32[]{:S(2)}, u32[]{:S(2)}) async-start(bf16[8,320,256]{2,1,0:T(8,128)(2,1)} %bitcast.36), calls=%async_computation | async-start | bytes 2621440 | tf_op jit(solution)/shard_map/all_to_all | solution.py:333
  35.2 30.3 %collective-permute-start.9 = (bf16[320,1280]{1,0:T(8,128)(2,1)}, bf16[320,1280]{1,0:T(8,128)(2,1)}, u32[]{:S(2)}, u32[]{:S(2)}) collective-permute-start(bf16[320,1280]{1,0:T(8,128)(2,1)} %constant_dynamic-update-slice_fusion.refs_6_), channel_id=1, source_target_pairs={{0,8},{4,12},{8,0},{12,4},{16,24},{20,28},{24,16},{28,20},{1,9},{5... | collective-permute-start | bytes 2457608 | tf_op jit(solution)/shard_map/ppermute | solution.py:303
  36.7 28.8 %collective-permute-start.10 = (bf16[320,1280]{1,0:T(8,128)(2,1)}, bf16[320,1280]{1,0:T(8,128)(2,1)}, u32[]{:S(2)}, u32[]{:S(2)}) collective-permute-start(bf16[320,1280]{1,0:T(8,128)(2,1)} %constant_dynamic-update-slice_fusion.refs_6_), channel_id=1, source_target_pairs={{0,16},{4,20},{8,24},{12,28},{16,0},{20,4},{24,8},{28,12},{1,17},{... | collective-permute-start | bytes 2457608 | tf_op jit(solution)/shard_map/ppermute | solution.py:303
  38.2 30.2 %collective-permute-start.13 = (bf16[320,1280]{1,0:T(8,128)(2,1)}, bf16[320,1280]{1,0:T(8,128)(2,1)}, u32[]{:S(2)}, u32[]{:S(2)}) collective-permute-start(bf16[320,1280]{1,0:T(8,128)(2,1)} %constant_dynamic-update-slice_fusion.refs_6_), channel_id=1, source_target_pairs={{0,4},{4,0},{8,12},{12,8},{16,20},{20,16},{24,28},{28,24},{1,5},{5... | collective-permute-start | bytes 2457608 | tf_op jit(solution)/shard_map/ppermute | solution.py:303
  38.2 12.5 %collective-permute-start.18 = (bf16[160,1280]{1,0:T(8,128)(2,1)}, bf16[160,1280]{1,0:T(8,128)(2,1)S(1)}, u32[]{:S(2)}, u32[]{:S(2)}) collective-permute-start(bf16[160,1280]{1,0:T(8,128)(2,1)} %collective-permute-done.8), channel_id=1, source_target_pairs={{0,1},{1,0},{2,3},{3,2},{4,5},{5,4},{6,7},{7,6},{8,9},{9,8},{10,11... | collective-permute-start | bytes 1228808 | tf_op jit(solution)/shard_map/ppermute | solution.py:309
  49.2 36.4 %copy-start.15 = (bf16[8,320,256]{2,1,0:T(8,128)(2,1)}, bf16[8,320,256]{2,1,0:T(8,128)(2,1)S(1)}, u32[]{:S(2)}) copy-start(bf16[8,320,256]{2,1,0:T(8,128)(2,1)S(1)} %all-to-all-done) | copy-start | bytes 3932164
  49.3 79.1 %copy-start.17 = (f32[1280]{0:T(1024)S(1)}, f32[1280]{0:T(1024)}, u32[]{:S(2)}) copy-start(f32[1280]{0:T(1024)} %param.19) | copy-start | bytes 15364
  49.3 19.7 %collective-permute-start = (bf16[2,320,256]{2,1,0:T(8,128)(2,1)S(1)}, bf16[2,320,256]{2,1,0:T(8,128)(2,1)S(1)}, u32[]{:S(2)}, u32[]{:S(2)}) collective-permute-start(bf16[2,320,256]{2,1,0:T(8,128)(2,1)S(1)} %slice.56.refs_0_), channel_id=1, source_target_pairs={{0,1},{1,0},{2,3},{3,2},{4,5},{5,4},{6,7},{7,6},{8,9},{9,8},{10,11... | collective-permute-start | bytes 983048 | tf_op jit(solution)/shard_map/ppermute | solution.py:309
  50.7 34.9 %collective-permute-start.23 = (bf16[160,1280]{1,0:T(8,128)(2,1)S(1)}, bf16[160,1280]{1,0:T(8,128)(2,1)S(1)}, u32[]{:S(2)}, u32[]{:S(2)}) collective-permute-start(bf16[160,1280]{1,0:T(8,128)(2,1)S(1)} %collective-permute-done.18.refs_16_), channel_id=1, source_target_pairs={{0,4},{4,0},{8,12},{12,8},{16,20},{20,16},{24,28},{28,24},{1,5},{5... | collective-permute-start | bytes 1228808 | tf_op jit(solution)/shard_map/ppermute | solution.py:303
  66.6 63.0 %copy-start.16 = (f32[1280]{0:T(1024)S(1)}, f32[1280]{0:T(1024)}, u32[]{:S(2)}) copy-start(f32[1280]{0:T(1024)} %param.20) | copy-start | bytes 15364
  66.6 19.0 %collective-permute-start.11 = (bf16[160,1280]{1,0:T(8,128)(2,1)S(1)}, bf16[160,1280]{1,0:T(8,128)(2,1)}, u32[]{:S(2)}, u32[]{:S(2)}) collective-permute-start(bf16[160,1280]{1,0:T(8,128)(2,1)S(1)} %slice.39), channel_id=1, source_target_pairs={{0,16},{4,20},{8,24},{12,28},{16,0},{20,4},{24,8},{28,12},{1,17},{... | collective-permute-start | bytes 1228808 | tf_op jit(solution)/shard_map/ppermute | solution.py:303
  68.1 16.8 %collective-permute-start.1 = (bf16[2,320,256]{2,1,0:T(8,128)(2,1)S(1)}, bf16[2,320,256]{2,1,0:T(8,128)(2,1)S(1)}, u32[]{:S(2)}, u32[]{:S(2)}) collective-permute-start(bf16[2,320,256]{2,1,0:T(8,128)(2,1)S(1)} %slice.56.refs_0_), channel_id=1, source_target_pairs={{0,2},{1,3},{2,0},{3,1},{4,6},{5,7},{6,4},{7,5},{8,10},{9,11},{10,... | collective-permute-start | bytes 983048 | tf_op jit(solution)/shard_map/ppermute | solution.py:309
  68.5 18.5 %collective-permute-start.19 = (bf16[160,1280]{1,0:T(8,128)(2,1)S(1)}, bf16[160,1280]{1,0:T(8,128)(2,1)S(1)}, u32[]{:S(2)}, u32[]{:S(2)}) collective-permute-start(bf16[160,1280]{1,0:T(8,128)(2,1)S(1)} %collective-permute-done.18.refs_16_), channel_id=1, source_target_pairs={{0,8},{4,12},{8,0},{12,4},{16,24},{20,28},{24,16},{28,20},{1,9},{5... | collective-permute-start | bytes 1228808 | tf_op jit(solution)/shard_map/ppermute | solution.py:303
  69.7 19.3 %collective-permute-start.20 = (bf16[160,1280]{1,0:T(8,128)(2,1)S(1)}, bf16[160,1280]{1,0:T(8,128)(2,1)S(1)}, u32[]{:S(2)}, u32[]{:S(2)}) collective-permute-start(bf16[160,1280]{1,0:T(8,128)(2,1)S(1)} %collective-permute-done.18.refs_16_), channel_id=1, source_target_pairs={{0,16},{4,20},{8,24},{12,28},{16,0},{20,4},{24,8},{28,12},{1,17},{... | collective-permute-start | bytes 1228808 | tf_op jit(solution)/shard_map/ppermute | solution.py:303
  84.9 34.4 %copy-start.4 = (bf16[2,320,256]{2,1,0:T(8,128)(2,1)}, bf16[2,320,256]{2,1,0:T(8,128)(2,1)S(1)}, u32[]{:S(2)}) copy-start(bf16[2,320,256]{2,1,0:T(8,128)(2,1)S(1)} %collective-permute-done.1.refs_2_) | copy-start | bytes 983044
  84.9 11.5 %collective-permute-start.12 = (bf16[160,1280]{1,0:T(8,128)(2,1)S(1)}, bf16[160,1280]{1,0:T(8,128)(2,1)}, u32[]{:S(2)}, u32[]{:S(2)}) collective-permute-start(bf16[160,1280]{1,0:T(8,128)(2,1)S(1)} %slice.40), channel_id=1, source_target_pairs={{0,8},{4,12},{8,0},{12,4},{16,24},{20,28},{24,16},{28,20},{1,9},{5... | collective-permute-start | bytes 1228808 | tf_op jit(solution)/shard_map/ppermute | solution.py:303
  85.6 33.7 %collective-permute-start.14 = (bf16[320,1280]{1,0:T(8,128)(2,1)}, bf16[320,1280]{1,0:T(8,128)(2,1)S(1)}, u32[]{:S(2)}, u32[]{:S(2)}) collective-permute-start(bf16[320,1280]{1,0:T(8,128)(2,1)} %collective-permute-done.9.refs_7_), channel_id=1, source_target_pairs={{0,4},{4,0},{8,12},{12,8},{16,20},{20,16},{24,28},{28,24},{1,5},{5... | collective-permute-start | bytes 2457608 | tf_op jit(solution)/shard_map/ppermute | solution.py:303
  85.6 21.1 %collective-permute-start.28 = (bf16[2,320,256]{2,1,0:T(8,128)(2,1)S(1)}, bf16[2,320,256]{2,1,0:T(8,128)(2,1)S(1)}, u32[]{:S(2)}, u32[]{:S(2)}) collective-permute-start(bf16[2,320,256]{2,1,0:T(8,128)(2,1)S(1)} %collective-permute-done.1.refs_2_), channel_id=1, source_target_pairs={{0,1},{1,0},{2,3},{3,2},{4,5},{5,4},{6,7},{7,6},{8,9},{9,8},{10,11... | collective-permute-start | bytes 983048 | tf_op jit(solution)/shard_map/ppermute | solution.py:309
  86.9 31.7 %collective-permute-start.2 = (bf16[3,320,256]{2,1,0:T(8,128)(2,1)S(1)}, bf16[3,320,256]{2,1,0:T(8,128)(2,1)S(1)}, u32[]{:S(2)}, u32[]{:S(2)}) collective-permute-start(bf16[3,320,256]{2,1,0:T(8,128)(2,1)S(1)} %get-tuple-element.39.refs_0_), channel_id=1, source_target_pairs={{0,1},{1,0},{2,3},{3,2},{4,5},{5,4},{6,7},{7,6},{8,9},{9,8},{10,11... | collective-permute-start | bytes 1474568 | tf_op jit(solution)/shard_map/ppermute | solution.py:309
  89.0 30.2 %collective-permute-start.3 = (bf16[3,320,256]{2,1,0:T(8,128)(2,1)S(1)}, bf16[3,320,256]{2,1,0:T(8,128)(2,1)S(1)}, u32[]{:S(2)}, u32[]{:S(2)}) collective-permute-start(bf16[3,320,256]{2,1,0:T(8,128)(2,1)S(1)} %get-tuple-element.39.refs_0_), channel_id=1, source_target_pairs={{0,2},{1,3},{2,0},{3,1},{4,6},{5,7},{6,4},{7,5},{8,10},{9,11},{10,... | collective-permute-start | bytes 1474568 | tf_op jit(solution)/shard_map/ppermute | solution.py:309
  96.4 28.1 %collective-permute-start.15 = (bf16[320,1280]{1,0:T(8,128)(2,1)}, bf16[320,1280]{1,0:T(8,128)(2,1)}, u32[]{:S(2)}, u32[]{:S(2)}) collective-permute-start(bf16[320,1280]{1,0:T(8,128)(2,1)} %collective-permute-done.10.refs_8_), channel_id=1, source_target_pairs={{0,4},{4,0},{8,12},{12,8},{16,20},{20,16},{24,28},{28,24},{1,5},{5... | collective-permute-start | bytes 2457608 | tf_op jit(solution)/shard_map/ppermute | solution.py:303
  106.7 12.6 %copy-start.6 = (bf16[2,320,256]{2,1,0:T(8,128)(2,1)}, bf16[2,320,256]{2,1,0:T(8,128)(2,1)S(1)}, u32[]{:S(2)}) copy-start(bf16[2,320,256]{2,1,0:T(8,128)(2,1)S(1)} %collective-permute-done.28.refs_3_) | copy-start | bytes 983044
  106.7 6.2 %collective-permute-start.21 = (bf16[80,1280]{1,0:T(8,128)(2,1)S(1)}, bf16[80,1280]{1,0:T(8,128)(2,1)S(1)}, u32[]{:S(2)}, u32[]{:S(2)}) collective-permute-start(bf16[80,1280]{1,0:T(8,128)(2,1)S(1)} %slice.41), channel_id=1, source_target_pairs={{0,16},{4,20},{8,24},{12,28},{16,0},{20,4},{24,8},{28,12},{1,17},{... | collective-permute-start | bytes 614408 | tf_op jit(solution)/shard_map/ppermute | solution.py:303
  112.9 6.9 %copy-start.8 = (bf16[80,1280]{1,0:T(8,128)(2,1)}, bf16[80,1280]{1,0:T(8,128)(2,1)S(1)}, u32[]{:S(2)}) copy-start(bf16[80,1280]{1,0:T(8,128)(2,1)S(1)} %collective-permute-done.21.refs_19_) | copy-start | bytes 614404
  112.9 5.8 %collective-permute-start.22 = (bf16[80,1280]{1,0:T(8,128)(2,1)S(1)}, bf16[80,1280]{1,0:T(8,128)(2,1)S(1)}, u32[]{:S(2)}, u32[]{:S(2)}) collective-permute-start(bf16[80,1280]{1,0:T(8,128)(2,1)S(1)} %slice.42), channel_id=1, source_target_pairs={{0,8},{4,12},{8,0},{12,4},{16,24},{20,28},{24,16},{28,20},{1,9},{5... | collective-permute-start | bytes 614408 | tf_op jit(solution)/shard_map/ppermute | solution.py:303
  118.7 1.1 copy-start.11
  118.7 7.6 %collective-permute-start.16 = (bf16[160,1280]{1,0:T(8,128)(2,1)}, bf16[160,1280]{1,0:T(8,128)(2,1)}, u32[]{:S(2)}, u32[]{:S(2)}) collective-permute-start(bf16[160,1280]{1,0:T(8,128)(2,1)} %collective-permute-done.11.refs_9_), channel_id=1, source_target_pairs={{0,4},{4,0},{8,12},{12,8},{16,20},{20,16},{24,28},{28,24},{1,5},{5... | collective-permute-start | bytes 1228808 | tf_op jit(solution)/shard_map/ppermute | solution.py:303
  118.7 9.1 %collective-permute-start.17 = (bf16[160,1280]{1,0:T(8,128)(2,1)}, bf16[160,1280]{1,0:T(8,128)(2,1)}, u32[]{:S(2)}, u32[]{:S(2)}) collective-permute-start(bf16[160,1280]{1,0:T(8,128)(2,1)} %collective-permute-done.12.refs_10_), channel_id=1, source_target_pairs={{0,4},{4,0},{8,12},{12,8},{16,20},{20,16},{24,28},{28,24},{1,5},{5... | collective-permute-start | bytes 1228808 | tf_op jit(solution)/shard_map/ppermute | solution.py:303
  119.2 0.8 copy-start.20
  119.2 8.6 %collective-permute-start.24 = (bf16[160,1280]{1,0:T(8,128)(2,1)S(1)}, bf16[160,1280]{1,0:T(8,128)(2,1)}, u32[]{:S(2)}, u32[]{:S(2)}) collective-permute-start(bf16[160,1280]{1,0:T(8,128)(2,1)S(1)} %collective-permute-done.19.refs_17_), channel_id=1, source_target_pairs={{0,4},{4,0},{8,12},{12,8},{16,20},{20,16},{24,28},{28,24},{1,5},{5... | collective-permute-start | bytes 1228808 | tf_op jit(solution)/shard_map/ppermute | solution.py:303
  119.3 1.0 copy-start.19
  119.3 10.3 %collective-permute-start.25 = (bf16[160,1280]{1,0:T(8,128)(2,1)S(1)}, bf16[160,1280]{1,0:T(8,128)(2,1)}, u32[]{:S(2)}, u32[]{:S(2)}) collective-permute-start(bf16[160,1280]{1,0:T(8,128)(2,1)S(1)} %collective-permute-done.20.refs_18_), channel_id=1, source_target_pairs={{0,4},{4,0},{8,12},{12,8},{16,20},{20,16},{24,28},{28,24},{1,5},{5... | collective-permute-start | bytes 1228808 | tf_op jit(solution)/shard_map/ppermute | solution.py:303
  120.9 8.6 %all-to-all-start.1 = ((s32[8,1,4]{2,1,0:T(1,128)}), s32[8,1,4]{2,1,0:T(1,128)S(1)}, u32[]{:S(2)}, u32[]{:S(2)}) async-start(s32[8,1,4]{2,1,0:T(1,128)} %bitcast.12), calls=%async_computation.1 | async-start | bytes 8192 | tf_op jit(solution)/shard_map/all_to_all | solution.py:299
  124.3 190.6 %reduce-scatter.2.cloned.1.call-start = ((), (), s32[]{:S(2)}) async-start(), calls=%async_computation.3 | async-start | bytes 2785280 | tf_op jit(solution)/shard_map/reduce_scatter | solution.py:503
  124.5 65.0 %collective-permute-start.30 = (bf16[640,2048]{1,0:T(8,128)(2,1)}, bf16[640,2048]{1,0:T(8,128)(2,1)}, u32[]{:S(2)}, u32[]{:S(2)}) collective-permute-start(bf16[640,2048]{1,0:T(8,128)(2,1)} %refs_1_.1), channel_id=1, source_target_pairs={{0,8},{4,12},{8,0},{12,4},{16,24},{20,28},{24,16},{28,20},{1,9},{5... | collective-permute-start | bytes 7864328 | tf_op jit(solution)/shard_map/ppermute | solution.py:303
  126.3 63.2 %collective-permute-start.31 = (bf16[640,2048]{1,0:T(8,128)(2,1)}, bf16[640,2048]{1,0:T(8,128)(2,1)}, u32[]{:S(2)}, u32[]{:S(2)}) collective-permute-start(bf16[640,2048]{1,0:T(8,128)(2,1)} %refs_1_.1), channel_id=1, source_target_pairs={{0,16},{4,20},{8,24},{12,28},{16,0},{20,4},{24,8},{28,12},{1,17},{... | collective-permute-start | bytes 7864328 | tf_op jit(solution)/shard_map/ppermute | solution.py:303
  127.8 1.9 collective-permute-start.26
  127.8 2.8 collective-permute-start.27
  129.6 24.5 %collective-permute-start.4 = (bf16[3,320,256]{2,1,0:T(8,128)(2,1)S(1)}, bf16[3,320,256]{2,1,0:T(8,128)(2,1)S(1)}, u32[]{:S(2)}, u32[]{:S(2)}) collective-permute-start(bf16[3,320,256]{2,1,0:T(8,128)(2,1)S(1)} %get-tuple-element.42.refs_0_), channel_id=1, source_target_pairs={{0,1},{1,0},{2,3},{3,2},{4,5},{5,4},{6,7},{7,6},{8,9},{9,8},{10,11... | collective-permute-start | bytes 1474568 | tf_op jit(solution)/shard_map/ppermute | solution.py:309
  129.6 24.8 %collective-permute-start.5 = (bf16[3,320,256]{2,1,0:T(8,128)(2,1)S(1)}, bf16[3,320,256]{2,1,0:T(8,128)(2,1)S(1)}, u32[]{:S(2)}, u32[]{:S(2)}) collective-permute-start(bf16[3,320,256]{2,1,0:T(8,128)(2,1)S(1)} %get-tuple-element.42.refs_0_), channel_id=1, source_target_pairs={{0,2},{1,3},{2,0},{3,1},{4,6},{5,7},{6,4},{7,5},{8,10},{9,11},{10,... | collective-permute-start | bytes 1474568 | tf_op jit(solution)/shard_map/ppermute | solution.py:309
  130.5 33.4 %collective-permute-start.6 = (bf16[3,320,256]{2,1,0:T(8,128)(2,1)}, bf16[3,320,256]{2,1,0:T(8,128)(2,1)S(1)}, u32[]{:S(2)}, u32[]{:S(2)}) collective-permute-start(bf16[3,320,256]{2,1,0:T(8,128)(2,1)} %copy-done.20), channel_id=1, source_target_pairs={{0,1},{1,0},{2,3},{3,2},{4,5},{5,4},{6,7},{7,6},{8,9},{9,8},{10,11... | collective-permute-start | bytes 1474568 | tf_op jit(solution)/shard_map/ppermute | solution.py:309
  131.7 1.0 copy-start.3
  132.7 1.0 copy-start.5
  133.7 1.0 copy-start.7
  134.6 0.9 copy-start.9
  135.6 0.9 copy-start.12
  154.1 35.3 %copy-start.18 = (bf16[640,2048]{1,0:T(8,128)(2,1)S(1)}, bf16[640,2048]{1,0:T(8,128)(2,1)}, u32[]{:S(2)}) copy-start(bf16[640,2048]{1,0:T(8,128)(2,1)} %refs_1_.1) | copy-start | bytes 7864324
  154.5 34.5 %copy-start.21 = (bf16[3,320,256]{2,1,0:T(8,128)(2,1)}, bf16[3,320,256]{2,1,0:T(8,128)(2,1)S(1)}, u32[]{:S(2)}) copy-start(bf16[3,320,256]{2,1,0:T(8,128)(2,1)S(1)} %collective-permute-done.5.refs_2_) | copy-start | bytes 1474564
  189.0 17.1 %copy-start.10 = (bf16[80,1280]{1,0:T(8,128)(2,1)S(1)}, bf16[80,1280]{1,0:T(8,128)(2,1)}, u32[]{:S(2)}) copy-start(bf16[80,1280]{1,0:T(8,128)(2,1)} %copy-done.8) | copy-start | bytes 614404
  189.1 17.1 %copy-start.13 = (bf16[80,1280]{1,0:T(8,128)(2,1)S(1)}, bf16[80,1280]{1,0:T(8,128)(2,1)}, u32[]{:S(2)}) copy-start(bf16[80,1280]{1,0:T(8,128)(2,1)} %copy-done.11) | copy-start | bytes 614404
  189.1 12.5 %collective-permute-start.29 = (bf16[3,320,256]{2,1,0:T(8,128)(2,1)S(1)}, bf16[3,320,256]{2,1,0:T(8,128)(2,1)S(1)}, u32[]{:S(2)}, u32[]{:S(2)}) collective-permute-start(bf16[3,320,256]{2,1,0:T(8,128)(2,1)S(1)} %collective-permute-done.5.refs_2_), channel_id=1, source_target_pairs={{0,1},{1,0},{2,3},{3,2},{4,5},{5,4},{6,7},{7,6},{8,9},{9,8},{10,11... | collective-permute-start | bytes 1474568 | tf_op jit(solution)/shard_map/ppermute | solution.py:309
  189.5 47.4 %collective-permute-start.34 = (bf16[640,2048]{1,0:T(8,128)(2,1)S(1)}, bf16[640,2048]{1,0:T(8,128)(2,1)}, u32[]{:S(2)}, u32[]{:S(2)}) collective-permute-start(bf16[640,2048]{1,0:T(8,128)(2,1)S(1)} %copy-done.18), channel_id=1, source_target_pairs={{0,4},{4,0},{8,12},{12,8},{16,20},{20,16},{24,28},{28,24},{1,5},{5... | collective-permute-start | bytes 7864328 | tf_op jit(solution)/shard_map/ppermute | solution.py:303
  201.6 3.1 copy-start.22
  203.2 33.7 %collective-permute-start.35 = (bf16[640,2048]{1,0:T(8,128)(2,1)}, bf16[640,2048]{1,0:T(8,128)(2,1)}, u32[]{:S(2)}, u32[]{:S(2)}) collective-permute-start(bf16[640,2048]{1,0:T(8,128)(2,1)} %collective-permute-done.30.refs_2_), channel_id=1, source_target_pairs={{0,4},{4,0},{8,12},{12,8},{16,20},{20,16},{24,28},{28,24},{1,5},{5... | collective-permute-start | bytes 7864328 | tf_op jit(solution)/shard_map/ppermute | solution.py:303
  204.7 32.2 %collective-permute-start.36 = (bf16[640,2048]{1,0:T(8,128)(2,1)}, bf16[640,2048]{1,0:T(8,128)(2,1)}, u32[]{:S(2)}, u32[]{:S(2)}) collective-permute-start(bf16[640,2048]{1,0:T(8,128)(2,1)} %collective-permute-done.31.refs_3_), channel_id=1, source_target_pairs={{0,4},{4,0},{8,12},{12,8},{16,20},{20,16},{24,28},{28,24},{1,5},{5... | collective-permute-start | bytes 7864328 | tf_op jit(solution)/shard_map/ppermute | solution.py:303
  205.2 30.8 %collective-permute-start.32 = (bf16[320,2048]{1,0:T(8,128)(2,1)S(1)}, bf16[320,2048]{1,0:T(8,128)(2,1)S(1)}, u32[]{:S(2)}, u32[]{:S(2)}) collective-permute-start(bf16[320,2048]{1,0:T(8,128)(2,1)S(1)} %slice.43), channel_id=1, source_target_pairs={{0,16},{4,20},{8,24},{12,28},{16,0},{20,4},{24,8},{28,12},{1,17},{... | collective-permute-start | bytes 3932168 | tf_op jit(solution)/shard_map/ppermute | solution.py:303
  205.8 30.5 %collective-permute-start.33 = (bf16[320,2048]{1,0:T(8,128)(2,1)S(1)}, bf16[320,2048]{1,0:T(8,128)(2,1)S(1)}, u32[]{:S(2)}, u32[]{:S(2)}) collective-permute-start(bf16[320,2048]{1,0:T(8,128)(2,1)S(1)} %slice.44), channel_id=1, source_target_pairs={{0,8},{4,12},{8,0},{12,4},{16,24},{20,28},{24,16},{28,20},{1,9},{5... | collective-permute-start | bytes 3932168 | tf_op jit(solution)/shard_map/ppermute | solution.py:303
  206.2 35.0 %copy-start.14 = (f32[2048]{0:T(1024)S(1)}, f32[2048]{0:T(1024)}, u32[]{:S(2)}) copy-start(f32[2048]{0:T(1024)} %param.22) | copy-start | bytes 24580
  236.3 3.0 collective-permute-start.37
  236.3 4.9 %collective-permute-start.38 = (bf16[320,2048]{1,0:T(8,128)(2,1)S(1)}, bf16[320,2048]{1,0:T(8,128)(2,1)S(1)}, u32[]{:S(2)}, u32[]{:S(2)}) collective-permute-start(bf16[320,2048]{1,0:T(8,128)(2,1)S(1)} %collective-permute-done.33.refs_5_), channel_id=1, source_target_pairs={{0,4},{4,0},{8,12},{12,8},{16,20},{20,16},{24,28},{28,24},{1,5},{5... | collective-permute-start | bytes 3932168 | tf_op jit(solution)/shard_map/ppermute | solution.py:303
  271.4 45.7 %copy-start.1 = (bf16[2048,320]{0,1:T(8,128)(2,1)S(1)}, bf16[2048,320]{0,1:T(8,128)(2,1)}, u32[]{:S(2)}) copy-start(bf16[2048,320]{0,1:T(8,128)(2,1)} %param.13) | copy-start | bytes 3932164
  (2 other events, 1.5 us)
Sparse Core Ops, SparseCore 0:
  271.5 43.3 reduce-scatter.1

commit v4 on v3

--- a/solution.py
+++ b/solution.py
@@ -262,7 +262,7 @@
                 pltpu.VMEM((rows, units // 2), F32),
                 pltpu.VMEM((rows, units), BF),
                 pltpu.SemaphoreType.DMA((MERGE,)),
-                pltpu.SemaphoreType.DMA((3, 4)),
+                pltpu.SemaphoreType.DMA((3, 2)),
                 pltpu.SemaphoreType.DMA,
             ],
         ),
@@ -349,41 +349,42 @@
             lax.dynamic_slice_in_dim(wq_t, jnp.minimum(s, q_parts - 1) * share, share),
             lax.dynamic_slice_in_dim(w_proj, jnp.maximum(s - q_parts, 0) * share, share),
         )
-        early = lax.optimization_barrier((tp_xor(mine, 1), tp_xor(mine, 2)))
-        others = [jnp.concatenate(early), tp_xor(early[1], 1)]
-        held_planes = [(1, 2), (3,)]
-
-        def sides(x):
-            return list(lax.optimization_barrier((xor(x, 2), xor(x, 4))))
-
-        def corners(by_x, by_y):
-            half = by_x.shape[0] // 2
-            return [xor(by_x[:half], 4), xor(by_y[half:], 2)]
-
-        def cores(pieces):
-            return [xor(v, 1) for v in pieces]
-
-        first_by = sides(others[0])
-        last_by = sides(tie(others[1], first_by))
-        first_set = [others[0]] + first_by + corners(*first_by)
-        last_set = [others[1]] + last_by + corners(*last_by)
-        vit_weights = [wq_t, w_proj] + first_set + cores(first_set) + last_set + cores(last_set)
-        merge_by = sides(tie(w_merge, last_by))
+        def halves(x):
+            mid = x.shape[1] // 2
+            return x[:, :mid], x[:, mid:]
+
+        def across(left, right):
+            return xor(left, 2), xor(right, 4)
+
+        def joined(left, right, others):
+            return jnp.concatenate([left, others[0]]), jnp.concatenate([right, others[1]])
+
+        def along(left, right):
+            return xor(left, 4), xor(right, 2)
+
+        def with_cores(pieces):
+            return list(pieces) + [xor(v, 1) for v in pieces]
+
+        above = {(0, 0): (0, 2), (1, 0): (0, 4), (0, 1): (4, 6), (1, 1): (2, 6)}
+        places = [
+            (4 * e + 2 * k + h, h, row, d ^ e)
+            for e in range(2)
+            for (h, k), peers in above.items()
+            for row, d in enumerate(peers)
+        ]
+
+        by1, by2 = lax.optimization_barrier((tp_xor(mine, 1), tp_xor(mine, 2)))
+        merge_halves = halves(w_merge)
+        merge_across = across(*merge_halves)
+        vit_halves = halves(jnp.concatenate([by1, by2, tp_xor(by2, 1)]))
+        vit_joined = joined(*vit_halves, across(*vit_halves))
+        merge_joined = joined(*merge_halves, merge_across)
+        vit_joined, merge_joined = lax.optimization_barrier((vit_joined, merge_joined))
+        vit_along = along(*vit_joined)
+        vit_weights = [wq_t, w_proj] + with_cores(vit_joined + vit_along)
         q_rows, p_rows = wq_t.shape[0], w_proj.shape[0]
 
-        def spans(rows):
-            whole = [(0, 0, rows), (2, 0, rows), (4, 0, rows), (6, 0, rows // 2), (6, rows // 2, rows)]
-            return [(d ^ e, lo, hi) for e in range(2) for d, lo, hi in whole]
-
-        vit_parts = []
-        for planes in held_planes:
-            base = 2 + 10 * held_planes.index(planes)
-            for n, (d, lo, hi) in enumerate(spans(share * len(planes))):
-                for k, j in enumerate(planes):
-                    top, end = max(lo, k * share), min(hi, (k + 1) * share)
-                    if top < end:
-                        vit_parts.append((base + n, d, j, top - lo, top - k * share, end - top))
-        vit_count = 2 + len(vit_parts)
+        vit_count = 2 + len(places) * (tp - 1)
 
         def vit_moves(info, refs, w, sem):
             t, s = info[0], info[1]
@@ -396,38 +397,37 @@
                     refs[1], w.at[pl.ds(pl.multiple_of(3 * DV + t * p_rows, 16), p_rows)], sem.at[1]
                 ),
             ]
-            for at, (n, d, j, source, offset, count) in enumerate(vit_parts):
-                part = s ^ d
-                q = t ^ j
-                row = offset + jnp.where(
-                    part < q_parts,
-                    q * q_rows + part * share,
-                    3 * DV + q * p_rows + (part - q_parts) * share,
-                )
-                copies[j].append(
-                    pltpu.make_async_copy(
-                        refs[n].at[source : source + count],
-                        w.at[pl.ds(pl.multiple_of(row, 16), count)],
-                        sem.at[2 + at],
+            for at, (n, h, above, d) in enumerate(places):
+                for j in range(1, tp):
+                    part = s ^ d
+                    q = t ^ j
+                    row = jnp.where(
+                        part < q_parts,
+                        q * q_rows + part * share,
+                        3 * DV + q * p_rows + (part - q_parts) * share,
                     )
-                )
+                    first = (above * (tp - 1) + j - 1) * share
+                    copies[j].append(
+                        pltpu.make_async_copy(
+                            refs[2 + n].at[first : first + share],
+                            w.at[
+                                pl.ds(pl.multiple_of(row, 16), share),
+                                h * (DV // 2) : (h + 1) * (DV // 2),
+                            ],
+                            sem.at[2 + at * (tp - 1) + j - 1],
+                        )
+                    )
             return copies
 
         def merge_moves(info, refs, h, i, slot, sem):
             s = info[1]
-            wide = slot.shape[1]
             rows = slot.shape[0] // 2
             copies = []
-            for n, (d, lo, hi) in enumerate(spans(rows)):
-                if d // 2 == i:
-                    at = pl.multiple_of(((s ^ d) & 1) * rows + lo, 16)
-                    copies.append(
-                        pltpu.make_async_copy(
-                            refs[n].at[:, h * wide : (h + 1) * wide],
-                            slot.at[pl.ds(at, hi - lo)],
-                            sem.at[len(copies)],
-                        )
-                    )
+            for n, half, above, d in places:
+                if half == h and d // 2 == i:
+                    spot = pl.ds(pl.multiple_of(((s ^ d) & 1) * rows, 16), rows)
+                    part = refs[n].at[above * rows : (above + 1) * rows]
+                    copies.append(pltpu.make_async_copy(part, slot.at[spot], sem.at[len(copies)]))
             return copies
 
         def position(info, i):
@@ -475,25 +475,20 @@
 
     merged = None
     if paired:
-        cuts = [0, 2, 5, 8]
-        near, done = [], []
-        for lo, hi in zip(cuts[:-1], cuts[1:]):
-            own = full[lo:hi] if not near else tie(full[lo:hi], near[-1])
-            near.append(lax.optimization_barrier((tp_xor(own, 1), tp_xor(own, 2))))
+        cuts = [0, 5 * blocks // 8, blocks]
+        merge_joined = tie(merge_joined, vit_along)
+        merge_along = along(*merge_joined)
+        far = None
         for n, lo in enumerate(cuts[:-1]):
-            by1, by2 = near[n]
-            if n >= 2:
-                merged, by2 = lax.optimization_barrier((merged, by2))
+            own = full[lo : cuts[n + 1]]
+            near = own if far is None else tie(own, (far, vit_weights[2:]))
+            by1, by2 = lax.optimization_barrier((tp_xor(near, 1), tp_xor(near, 2)))
+            if n:
+                merged, by2, live_here = lax.optimization_barrier((merged, by2, live_here))
             far = tp_xor(by2, 1)
-            if n == len(cuts) - 2:
-                merged, far, merge_by = lax.optimization_barrier((merged, far, merge_by))
-            if n == 1:
-                merged, live_here = lax.optimization_barrier((merged, live_here))
-            merged = encode(lo, [full[lo : cuts[n + 1]], by1, by2, far], merged)
-        merge_corners = corners(*merge_by)
-        merged, merge_corners = lax.optimization_barrier((merged, merge_corners))
-        merge_pieces = [w_merge] + list(merge_by) + list(merge_corners)
-        merge_weights = merge_pieces + cores(merge_pieces)
+            merged = encode(lo, [own, by1, by2, far], merged)
+        merged, merge_along = lax.optimization_barrier((merged, merge_along))
+        merge_weights = with_cores(merge_joined + merge_along)
     else:
         for first in (0, mid):
             merged = encode(first, spread(full[first : first + mid]), merged)

time: 325 us -> 324 us (level)
  waiting for transfers between devices: 142 us -> 160 us
  Pallas kernels: 96.8 us -> 87.2 us
  starting transfers between devices: 35.8 us -> 27.1 us
  other arithmetic: 9 us -> 14.5 us
  local copies, waits for them, and re-layouts: 22.6 us -> 18.2 us
    ppermute x12 -> x9, waiting for transfers between devices: 47.9 us -> 65.8 us  [tp_xor(): return lax.ppermute(x, 'tp', [(i, i ^ d) for i in range(tp)])]
    all_to_all x1, waiting for transfers between devices: 10.6 us -> 0.01 us  [shards(): lax.all_to_all(sent.reshape(feats, seq_count, step).transpose(1, 0, 2), '...]
    concatenate x0 -> x4, other arithmetic: none -> 6.9 us  [the longest x2 4.2 us: joined(): jnp.concatenate([right, others[1]])]
    ppermute x27 -> x16, starting transfers between devices: 17 us -> 10.3 us  [xor(): return lax.ppermute(x, 'seq', [(i, i ^ d) for i in range(seq_count)])]
    pallas_call x3 -> x2, Pallas kernels: 66.6 us -> 61.5 us  [attend(): pl.pallas_call(functools.partial(attend_kernel, tp, moves, len(weights),...]
    ppermute x27 -> x16, waiting for transfers between devices: 40.9 us -> 45.6 us  [xor(): return lax.ppermute(x, 'seq', [(i, i ^ d) for i in range(seq_count)])]
    pallas_call x1, Pallas kernels: 30.2 us -> 25.7 us  [project(): pl.pallas_call(functools.partial(project_kernel, moves, position, len(wei...]
    all_to_all x1, waiting for transfers between devices: 0.01 us -> 3.27 us  [shards(): lax.all_to_all(live_send, 'seq', split_axis=0, concat_axis=0, tiled=True)]
  transfers between devices with their start and end apart: 42 -> 28, of which waited for: 17 -> 12; matrix products, arithmetic and copies ran while one was open for 7% -> 7% of each run, Pallas kernels for 21% -> 19%
where the time goes in v4:
time: 324 us
  waiting for transfers between devices  160 us (49%)
  Pallas kernels  87.2 us (27%)
  starting transfers between devices  27.1 us (8%)
  local copies, waits for them, and re-layouts  18.2 us (6%)
  other arithmetic  14.5 us (4%)
  between operations  13.7 us (4%)
  matrix products  3.45 us (1%)
    ppermute x9, waiting for transfers between devices, tp_xor(): return lax.ppermute(x, 'tp', [(i, i ^ d) for i in range(tp)])  65.8 us
    pallas_call x2, Pallas kernels, attend(): pl.pallas_call(functools.partial(attend_kernel, tp, moves, len(weights),...  61.5 us
    ppermute x16, waiting for transfers between devices, xor(): return lax.ppermute(x, 'seq', [(i, i ^ d) for i in range(seq_count)])  45.6 us
    reduce_scatter x1, waiting for transfers between devices, shards(): lax.psum_scatter(partial_value, 'tp', scatter_dimension=0, tiled=True)  44.9 us
    pallas_call x1, Pallas kernels, project(): pl.pallas_call(functools.partial(project_kernel, moves, position, len(wei...  25.7 us
    ppermute x16, starting transfers between devices, xor(): return lax.ppermute(x, 'seq', [(i, i ^ d) for i in range(seq_count)])  10.3 us
    ppermute x9, starting transfers between devices, tp_xor(): return lax.ppermute(x, 'tp', [(i, i ^ d) for i in range(tp)])  9.2 us
    unnamed x42, local copies, waits for them, and re-layouts  7.28 us
  transfers between devices with their start and end apart: 28, of which 12 were waited for; matrix products, arithmetic and copies ran while one was open for 7% of the time, Pallas kernels for 19%

profile of v4, /device:TPU:0, one launch (start us, length us, event | category | flops | bytes accessed | tf_op | source)
XLA Modules:
  0.0 323.6 jit_solution(2510837537470591099)
XLA Ops:
  6.5 2.1 bitcast_select_fusion
  8.6 3.0 collective-permute-start.3
  11.6 2.6 collective-permute-start.4
  14.2 3.0 fusion.9
  17.3 1.5 collective-permute-start.8
  18.8 0.6 fusion.11
  19.4 1.6 sort.17
  21.0 1.2 compare_convert_fusion
  22.2 0.7 gather_fusion.1
  22.9 0.7 gather_fusion
  23.8 0.1 add.115
  23.9 3.5 %fusion.2 = bf16[2048,320]{0,1:T(8,128)(2,1)S(1)} fusion(bf16[2048,320]{0,1:T(8,128)(2,1)S(1)} %copy-done, s32[2048]{0:T(1024)S(1)} %add.115), kind=kOutput, calls=%fused_computation.5 | convolution fusion | flops 2689204224 | bytes 2629632 | tf_op jit(solution)/shard_map/dot_general | solution.py:327
  27.4 1.1 copy.28
  28.5 4.3 %all-to-all-start = ((bf16[8,320,256]{2,1,0:T(8,128)(2,1)}), bf16[8,320,256]{2,1,0:T(8,128)(2,1)}, u32[]{:S(2)}, u32[]{:S(2)}) async-start(bf16[8,320,256]{2,1,0:T(8,128)(2,1)} %bitcast.36), calls=%async_computation | async-start | bytes 2621440 | tf_op jit(solution)/shard_map/all_to_all | solution.py:333
  32.8 1.9 collective-permute-start.9
  34.7 0.5 collective-permute-start.5
  35.3 10.7 %collective-permute-done.5 = bf16[160,1280]{1,0:T(8,128)(2,1)S(1)} collective-permute-done((bf16[160,1280]{1,0:T(8,128)(2,1)S(1)}, bf16[160,1280]{1,0:T(8,128)(2,1)S(1)}, u32[]{:S(2)}, u32[]{:S(2)}) %collective-permute-start.5) | collective-permute-done | bytes 409632 | tf_op jit(solution)/shard_map/ppermute | solution.py:309
  46.0 0.1 fusion.10
  46.1 1.5 collective-permute-start.6
  47.7 0.5 collective-permute-start.7
  48.2 0.9 collective-permute-done.8
  49.1 1.6 pad_maximum_fusion.refs_1_
  50.6 27.9 %collective-permute-done.9 = bf16[640,1024]{1,0:T(8,128)(2,1)S(1)} collective-permute-done((bf16[640,1024]{1,0:T(8,128)(2,1)}, bf16[640,1024]{1,0:T(8,128)(2,1)S(1)}, u32[]{:S(2)}, u32[]{:S(2)}) %collective-permute-start.9) | collective-permute-done | bytes 1310752 | tf_op jit(solution)/shard_map/ppermute | solution.py:303
  78.5 3.1 pad_maximum_fusion.1.refs_2_
  81.6 1.1 pad_maximum_fusion.2.refs_6_
  82.7 8.5 %collective-permute-done.7 = bf16[480,640]{1,0:T(8,128)(2,1)S(1)} collective-permute-done((bf16[480,640]{1,0:T(8,128)(2,1)S(1)}, bf16[480,640]{1,0:T(8,128)(2,1)S(1)}, u32[]{:S(2)}, u32[]{:S(2)}) %collective-permute-start.7) | collective-permute-done | bytes 614432 | tf_op jit(solution)/shard_map/ppermute | solution.py:303
  91.2 1.1 pad_maximum_fusion.3.refs_7_
  92.4 0.3 collective-permute-start.10
  92.7 1.7 collective-permute-start.11
  94.4 1.2 slice.40.refs_0_
  95.6 0.5 collective-permute-start
  96.1 0.3 collective-permute-start.1
  96.5 34.7 %collective-permute-done.refs_1_ = bf16[5,320,256]{2,1,0:T(8,128)(2,1)S(1)} collective-permute-done((bf16[5,320,256]{2,1,0:T(8,128)(2,1)S(1)}, bf16[5,320,256]{2,1,0:T(8,128)(2,1)S(1)}, u32[]{:S(2)}, u32[]{:S(2)}) %collective-permute-start) | collective-permute-done | bytes 819232 | tf_op jit(solution)/shard_map/ppermute | solution.py:309
  131.2 0.9 copy-done.7
  132.1 0.5 collective-permute-start.14
  132.7 1.0 collective-permute-done.1.refs_2_
  133.7 0.7 all_to_all.12
  134.4 3.3 %all-to-all-start.1 = ((s32[8,1,4]{2,1,0:T(1,128)}), s32[8,1,4]{2,1,0:T(1,128)S(1)}, u32[]{:S(2)}, u32[]{:S(2)}) async-start(s32[8,1,4]{2,1,0:T(1,128)} %bitcast.12), calls=%async_computation.1 | async-start | bytes 8192 | tf_op jit(solution)/shard_map/all_to_all | solution.py:299
  137.7 1.1 broadcast_in_dim.39.refs_14_
  138.9 3.3 %all-to-all-done.1 = s32[8,1,4]{2,1,0:T(1,128)S(1)} async-done(((s32[8,1,4]{2,1,0:T(1,128)}), s32[8,1,4]{2,1,0:T(1,128)S(1)}, u32[]{:S(2)}, u32[]{:S(2)}) %all-to-all-start.1) | async-done | bytes 160 | tf_op jit(solution)/shard_map/all_to_all | solution.py:299
  142.3 1.1 slice.39.refs_0_
  143.3 0.6 collective-permute-start.19
  144.0 0.6 collective-permute-start.20
  144.5 9.1 %collective-permute-done.2.refs_3_ = bf16[5,320,256]{2,1,0:T(8,128)(2,1)} collective-permute-done((bf16[5,320,256]{2,1,0:T(8,128)(2,1)}, bf16[5,320,256]{2,1,0:T(8,128)(2,1)}, u32[]{:S(2)}, u32[]{:S(2)}) %collective-permute-start.2) | collective-permute-done | bytes 819232 | tf_op jit(solution)/shard_map/ppermute | solution.py:309
  153.6 0.3 collective-permute-start.16
  153.9 1.6 collective-permute-start.17
  155.6 1.1 copy-done.3
  156.6 1.1 copy-done.5
  157.8 1.1 copy-done.8
  158.9 38.2 %attend.2.refs_16_ = bf16[4,8,64,1280]{3,2,1,0:T(8,128)(2,1)} custom-call(s32[7]{0:T(128)S(1)} %pad_add_fusion.2.info, bf16[5,320,256]{2,1,0:T(8,128)(2,1)S(1)} %slice.40.refs_0_, bf16[5,320,256]{2,1,0:T(8,128)(2,1)S(1)} %copy-done.8, bf16[5,320,256]{2,1,0:T(8,128)(2,1)} %collective-permute-done.1.refs_2_, ...), custom_call_target="tpu_custom_call" | custom-call | flops 20971520000 | bytes 14680064 | tf_op jit(solution)/shard_map/attend/pallas_call | solution.py:148
  197.1 0.4 collective-permute-start.18
  197.6 0.5 collective-permute-start.22
  198.1 10.2 %collective-permute-done.18.refs_3_ = bf16[3,320,256]{2,1,0:T(8,128)(2,1)S(1)} collective-permute-done((bf16[3,320,256]{2,1,0:T(8,128)(2,1)S(1)}, bf16[3,320,256]{2,1,0:T(8,128)(2,1)S(1)}, u32[]{:S(2)}, u32[]{:S(2)}) %collective-permute-start.18) | collective-permute-done | bytes 491552 | tf_op jit(solution)/shard_map/ppermute | solution.py:309
  208.3 23.3 %attend.3 = bf16[4,8,64,1280]{3,2,1,0:T(8,128)(2,1)} custom-call(s32[5]{0:T(128)S(1)} %pad_add_fusion.1.info, bf16[3,320,256]{2,1,0:T(8,128)(2,1)S(1)} %slice.39.refs_0_, bf16[3,320,256]{2,1,0:T(8,128)(2,1)S(1)} %collective-permute-done.16.refs_1_, bf16[3,320,256]{2,1,0:T(8,128)(2,1)S(1)} %collective-permute-done.17.refs_2_, ...), custom_call_target="tpu_custom_call", output_to_operand_aliasing={{}: (17, {})} | custom-call | flops 12582912000 | bytes 14680064 | tf_op jit(solution)/shard_map/attend/pallas_call | solution.py:148
  231.8 0.5 collective-permute-start.24
  232.3 4.5 %collective-permute-done.23.refs_7_ = bf16[1280,1024]{1,0:T(8,128)(2,1)S(1)} collective-permute-done((bf16[1280,1024]{1,0:T(8,128)(2,1)}, bf16[1280,1024]{1,0:T(8,128)(2,1)S(1)}, u32[]{:S(2)}, u32[]{:S(2)}) %collective-permute-start.23) | collective-permute-done | bytes 2621472 | tf_op jit(solution)/shard_map/ppermute | solution.py:303
  236.9 3.7 %collective-permute-done.24.refs_8_ = bf16[1280,1024]{1,0:T(8,128)(2,1)S(1)} collective-permute-done((bf16[1280,1024]{1,0:T(8,128)(2,1)}, bf16[1280,1024]{1,0:T(8,128)(2,1)S(1)}, u32[]{:S(2)}, u32[]{:S(2)}) %collective-permute-start.24) | collective-permute-done | bytes 2621472 | tf_op jit(solution)/shard_map/ppermute | solution.py:303
  240.6 1.5 copy-done.18
  242.1 25.7 %project.1 = bf16[512,2176]{1,0:T(8,128)(2,1)S(1)} custom-call(s32[2]{0:T(128)S(1)} %pad_add_fusion.info, bf16[4,512,1280]{2,1,0:T(8,128)(2,1)} %bitcast.44, bf16[1280,1024]{1,0:T(8,128)(2,1)S(1)} %pad_maximum_fusion.refs_1_, bf16[1280,1024]{1,0:T(8,128)(2,1)} %pad_maximum_fusion.1.refs_2_, bf16[1280,1024]{1,0:T(8,128)(2,1)} %collective-permute-done.19.refs_3_, ...), custom_call_target="tpu_custom_call" | custom-call | flops 15032385536 | bytes 37748736 | tf_op jit(solution)/shard_map/project/pallas_call | solution.py:249
  267.9 1.4 copy-done.2
  269.7 44.9 %reduce-scatter.2.cloned.1.call-done = bf16[128,2176]{1,0:T(8,128)(2,1)} async-done(((bf16[512,2176]{1,0:T(8,128)(2,1)}), bf16[128,2176]{1,0:T(8,128)(2,1)}) %reduce-scatter.2.cloned.1.call-update) | async-done | bytes 557072 | tf_op jit(solution)/shard_map/reduce_scatter | solution.py:498
  314.6 1.1 convert_element_type.22
  315.7 0.1 fusion.7
  315.8 1.0 fusion.4
  (81 shorter events, 1.3 us)
Async XLA Ops:
  6.5 17.4 %copy-start = (bf16[2048,320]{0,1:T(8,128)(2,1)S(1)}, bf16[2048,320]{0,1:T(8,128)(2,1)}, u32[]{:S(2)}) copy-start(bf16[2048,320]{0,1:T(8,128)(2,1)} %param.13) | copy-start | bytes 3932164
  8.6 10.1 %copy-start.16 = (s32[2]{0:T(128)S(1)}, s32[2]{0:T(128)}, u32[]{:S(2)}) copy-start(s32[2]{0:T(128)} %param.16) | copy-start | bytes 28
  8.6 10.7 %copy-start.19 = (s32[32,1]{0,1:T(1,128)S(1)}, s32[32,1]{0,1:T(1,128)}, u32[]{:S(2)}) copy-start(s32[32,1]{0,1:T(1,128)} %param.14) | copy-start | bytes 388
  8.6 12.4 %copy-start.10 = (s32[1,32]{1,0:T(1,128)S(1)}, s32[1,32]{1,0:T(1,128)}, u32[]{:S(2)}) copy-start(s32[1,32]{1,0:T(1,128)} %param.15) | copy-start | bytes 388
  8.6 26.1 %collective-permute-start.3 = (bf16[160,1280]{1,0:T(8,128)(2,1)}, bf16[160,1280]{1,0:T(8,128)(2,1)S(1)}, u32[]{:S(2)}, u32[]{:S(2)}) collective-permute-start(bf16[160,1280]{1,0:T(8,128)(2,1)} %bitcast_select_fusion), channel_id=1, source_target_pairs={{0,1},{1,0},{2,3},{3,2},{4,5},{5,4},{6,7},{7,6},{8,9},{9,8},{10,11... | collective-permute-start | bytes 1228808 | tf_op jit(solution)/shard_map/ppermute | solution.py:309
  11.6 23.1 %collective-permute-start.4 = (bf16[160,1280]{1,0:T(8,128)(2,1)}, bf16[160,1280]{1,0:T(8,128)(2,1)S(1)}, u32[]{:S(2)}, u32[]{:S(2)}) collective-permute-start(bf16[160,1280]{1,0:T(8,128)(2,1)} %bitcast_select_fusion), channel_id=1, source_target_pairs={{0,2},{1,3},{2,0},{3,1},{4,6},{5,7},{6,4},{7,5},{8,10},{9,11},{10,... | collective-permute-start | bytes 1228808 | tf_op jit(solution)/shard_map/ppermute | solution.py:309
  17.3 10.1 %copy-start.11 = (bf16[640,1024]{1,0:T(8,128)(2,1)}, bf16[640,1024]{1,0:T(8,128)(2,1)S(1)}, u32[]{:S(2)}) copy-start(bf16[640,1024]{1,0:T(8,128)(2,1)S(1)} %get-tuple-element.47) | copy-start | bytes 3932164
  17.3 31.8 %collective-permute-start.8 = (bf16[640,1024]{1,0:T(8,128)(2,1)S(1)}, bf16[640,1024]{1,0:T(8,128)(2,1)}, u32[]{:S(2)}, u32[]{:S(2)}) collective-permute-start(bf16[640,1024]{1,0:T(8,128)(2,1)S(1)} %get-tuple-element.47), channel_id=1, source_target_pairs={{0,8},{4,12},{8,0},{12,4},{16,24},{20,28},{24,16},{28,20},{1,9},{5... | collective-permute-start | bytes 3932168 | tf_op jit(solution)/shard_map/ppermute | solution.py:303
  28.5 65.9 %all-to-all-start = ((bf16[8,320,256]{2,1,0:T(8,128)(2,1)}), bf16[8,320,256]{2,1,0:T(8,128)(2,1)}, u32[]{:S(2)}, u32[]{:S(2)}) async-start(bf16[8,320,256]{2,1,0:T(8,128)(2,1)} %bitcast.36), calls=%async_computation | async-start | bytes 2621440 | tf_op jit(solution)/shard_map/all_to_all | solution.py:333
  32.8 45.7 %collective-permute-start.9 = (bf16[640,1024]{1,0:T(8,128)(2,1)}, bf16[640,1024]{1,0:T(8,128)(2,1)S(1)}, u32[]{:S(2)}, u32[]{:S(2)}) collective-permute-start(bf16[640,1024]{1,0:T(8,128)(2,1)} %get-tuple-element.46), channel_id=1, source_target_pairs={{0,16},{4,20},{8,24},{12,28},{16,0},{20,4},{24,8},{28,12},{1,17},{... | collective-permute-start | bytes 3932168 | tf_op jit(solution)/shard_map/ppermute | solution.py:303
  34.7 11.2 %collective-permute-start.5 = (bf16[160,1280]{1,0:T(8,128)(2,1)S(1)}, bf16[160,1280]{1,0:T(8,128)(2,1)S(1)}, u32[]{:S(2)}, u32[]{:S(2)}) collective-permute-start(bf16[160,1280]{1,0:T(8,128)(2,1)S(1)} %collective-permute-done.4), channel_id=1, source_target_pairs={{0,1},{1,0},{2,3},{3,2},{4,5},{5,4},{6,7},{7,6},{8,9},{9,8},{10,11... | collective-permute-start | bytes 1228808 | tf_op jit(solution)/shard_map/ppermute | solution.py:309
  46.0 3.1 copy-start.12
  46.1 35.5 %collective-permute-start.6 = (bf16[480,640]{1,0:T(8,128)(2,1)S(1)}, bf16[480,640]{1,0:T(8,128)(2,1)S(1)}, u32[]{:S(2)}, u32[]{:S(2)}) collective-permute-start(bf16[480,640]{1,0:T(8,128)(2,1)S(1)} %get-tuple-element.49), channel_id=1, source_target_pairs={{0,8},{4,12},{8,0},{12,4},{16,24},{20,28},{24,16},{28,20},{1,9},{5... | collective-permute-start | bytes 1843208 | tf_op jit(solution)/shard_map/ppermute | solution.py:303
  47.7 43.6 %collective-permute-start.7 = (bf16[480,640]{1,0:T(8,128)(2,1)S(1)}, bf16[480,640]{1,0:T(8,128)(2,1)S(1)}, u32[]{:S(2)}, u32[]{:S(2)}) collective-permute-start(bf16[480,640]{1,0:T(8,128)(2,1)S(1)} %get-tuple-element.48), channel_id=1, source_target_pairs={{0,16},{4,20},{8,24},{12,28},{16,0},{20,4},{24,8},{28,12},{1,17},{... | collective-permute-start | bytes 1843208 | tf_op jit(solution)/shard_map/ppermute | solution.py:303
  92.4 45.3 %copy-start.15 = (f32[1280]{0:T(1024)S(1)}, f32[1280]{0:T(1024)}, u32[]{:S(2)}) copy-start(f32[1280]{0:T(1024)} %param.19) | copy-start | bytes 15364
  92.4 46.5 %copy-start.14 = (f32[1280]{0:T(1024)S(1)}, f32[1280]{0:T(1024)}, u32[]{:S(2)}) copy-start(f32[1280]{0:T(1024)} %param.20) | copy-start | bytes 15364
  92.4 39.7 %collective-permute-start.10 = (bf16[960,640]{1,0:T(8,128)(2,1)}, bf16[960,640]{1,0:T(8,128)(2,1)}, u32[]{:S(2)}, u32[]{:S(2)}) collective-permute-start(bf16[960,640]{1,0:T(8,128)(2,1)} %pad_maximum_fusion.2.refs_6_), channel_id=1, source_target_pairs={{0,16},{4,20},{8,24},{12,28},{16,0},{20,4},{24,8},{28,12},{1,17},{... | collective-permute-start | bytes 3686408 | tf_op jit(solution)/shard_map/ppermute | solution.py:303
  92.7 39.9 %collective-permute-start.11 = (bf16[960,640]{1,0:T(8,128)(2,1)}, bf16[960,640]{1,0:T(8,128)(2,1)}, u32[]{:S(2)}, u32[]{:S(2)}) collective-permute-start(bf16[960,640]{1,0:T(8,128)(2,1)} %pad_maximum_fusion.3.refs_7_), channel_id=1, source_target_pairs={{0,8},{4,12},{8,0},{12,4},{16,24},{20,28},{24,16},{28,20},{1,9},{5... | collective-permute-start | bytes 3686408 | tf_op jit(solution)/shard_map/ppermute | solution.py:303
  95.6 35.6 %collective-permute-start = (bf16[5,320,256]{2,1,0:T(8,128)(2,1)S(1)}, bf16[5,320,256]{2,1,0:T(8,128)(2,1)S(1)}, u32[]{:S(2)}, u32[]{:S(2)}) collective-permute-start(bf16[5,320,256]{2,1,0:T(8,128)(2,1)S(1)} %slice.40.refs_0_), channel_id=1, source_target_pairs={{0,1},{1,0},{2,3},{3,2},{4,5},{5,4},{6,7},{7,6},{8,9},{9,8},{10,11... | collective-permute-start | bytes 2457608 | tf_op jit(solution)/shard_map/ppermute | solution.py:309
  96.1 37.6 %collective-permute-start.1 = (bf16[5,320,256]{2,1,0:T(8,128)(2,1)S(1)}, bf16[5,320,256]{2,1,0:T(8,128)(2,1)}, u32[]{:S(2)}, u32[]{:S(2)}) collective-permute-start(bf16[5,320,256]{2,1,0:T(8,128)(2,1)S(1)} %slice.40.refs_0_), channel_id=1, source_target_pairs={{0,2},{1,3},{2,0},{3,1},{4,6},{5,7},{6,4},{7,5},{8,10},{9,11},{10,... | collective-permute-start | bytes 2457608 | tf_op jit(solution)/shard_map/ppermute | solution.py:309
  96.5 46.9 %collective-permute-start.12 = (bf16[960,640]{1,0:T(8,128)(2,1)}, bf16[960,640]{1,0:T(8,128)(2,1)}, u32[]{:S(2)}, u32[]{:S(2)}) collective-permute-start(bf16[960,640]{1,0:T(8,128)(2,1)} %pad_maximum_fusion.2.refs_6_), channel_id=1, source_target_pairs={{0,4},{4,0},{8,12},{12,8},{16,20},{20,16},{24,28},{28,24},{1,5},{5... | collective-permute-start | bytes 3686408 | tf_op jit(solution)/shard_map/ppermute | solution.py:303
  131.2 0.9 copy-start.7
  132.1 11.9 %collective-permute-start.13 = (bf16[960,640]{1,0:T(8,128)(2,1)}, bf16[960,640]{1,0:T(8,128)(2,1)}, u32[]{:S(2)}, u32[]{:S(2)}) collective-permute-start(bf16[960,640]{1,0:T(8,128)(2,1)} %pad_maximum_fusion.3.refs_7_), channel_id=1, source_target_pairs={{0,4},{4,0},{8,12},{12,8},{16,20},{20,16},{24,28},{28,24},{1,5},{5... | collective-permute-start | bytes 3686408 | tf_op jit(solution)/shard_map/ppermute | solution.py:303
  132.1 21.5 %collective-permute-start.14 = (bf16[960,640]{1,0:T(8,128)(2,1)}, bf16[960,640]{1,0:T(8,128)(2,1)}, u32[]{:S(2)}, u32[]{:S(2)}) collective-permute-start(bf16[960,640]{1,0:T(8,128)(2,1)} %collective-permute-done.10.refs_8_), channel_id=1, source_target_pairs={{0,4},{4,0},{8,12},{12,8},{16,20},{20,16},{24,28},{28,24},{1,5},{5... | collective-permute-start | bytes 3686408 | tf_op jit(solution)/shard_map/ppermute | solution.py:303
  132.6 21.0 %collective-permute-start.15 = (bf16[960,640]{1,0:T(8,128)(2,1)}, bf16[960,640]{1,0:T(8,128)(2,1)}, u32[]{:S(2)}, u32[]{:S(2)}) collective-permute-start(bf16[960,640]{1,0:T(8,128)(2,1)} %collective-permute-done.11.refs_9_), channel_id=1, source_target_pairs={{0,4},{4,0},{8,12},{12,8},{16,20},{20,16},{24,28},{28,24},{1,5},{5... | collective-permute-start | bytes 3686408 | tf_op jit(solution)/shard_map/ppermute | solution.py:303
  133.7 19.9 %collective-permute-start.2 = (bf16[5,320,256]{2,1,0:T(8,128)(2,1)}, bf16[5,320,256]{2,1,0:T(8,128)(2,1)}, u32[]{:S(2)}, u32[]{:S(2)}) collective-permute-start(bf16[5,320,256]{2,1,0:T(8,128)(2,1)} %collective-permute-done.1.refs_2_), channel_id=1, source_target_pairs={{0,1},{1,0},{2,3},{3,2},{4,5},{5,4},{6,7},{7,6},{8,9},{9,8},{10,11... | collective-permute-start | bytes 2457608 | tf_op jit(solution)/shard_map/ppermute | solution.py:309
  134.4 7.8 %all-to-all-start.1 = ((s32[8,1,4]{2,1,0:T(1,128)}), s32[8,1,4]{2,1,0:T(1,128)S(1)}, u32[]{:S(2)}, u32[]{:S(2)}) async-start(s32[8,1,4]{2,1,0:T(1,128)} %bitcast.12), calls=%async_computation.1 | async-start | bytes 8192 | tf_op jit(solution)/shard_map/all_to_all | solution.py:299
  137.7 176.9 %reduce-scatter.2.cloned.1.call-start = ((), (), s32[]{:S(2)}) async-start(), calls=%async_computation.3 | async-start | bytes 2785280 | tf_op jit(solution)/shard_map/reduce_scatter | solution.py:498
  143.3 88.3 %collective-permute-start.19 = (bf16[1280,1024]{1,0:T(8,128)(2,1)S(1)}, bf16[1280,1024]{1,0:T(8,128)(2,1)}, u32[]{:S(2)}, u32[]{:S(2)}) collective-permute-start(bf16[1280,1024]{1,0:T(8,128)(2,1)S(1)} %pad_maximum_fusion.refs_1_), channel_id=1, source_target_pairs={{0,16},{4,20},{8,24},{12,28},{16,0},{20,4},{24,8},{28,12},{1,17},{... | collective-permute-start | bytes 7864328 | tf_op jit(solution)/shard_map/ppermute | solution.py:303
  144.0 87.7 %collective-permute-start.20 = (bf16[1280,1024]{1,0:T(8,128)(2,1)}, bf16[1280,1024]{1,0:T(8,128)(2,1)}, u32[]{:S(2)}, u32[]{:S(2)}) collective-permute-start(bf16[1280,1024]{1,0:T(8,128)(2,1)} %pad_maximum_fusion.1.refs_2_), channel_id=1, source_target_pairs={{0,8},{4,12},{8,0},{12,4},{16,24},{20,28},{24,16},{28,20},{1,9},{5... | collective-permute-start | bytes 7864328 | tf_op jit(solution)/shard_map/ppermute | solution.py:303
  153.6 43.5 %collective-permute-start.16 = (bf16[3,320,256]{2,1,0:T(8,128)(2,1)S(1)}, bf16[3,320,256]{2,1,0:T(8,128)(2,1)S(1)}, u32[]{:S(2)}, u32[]{:S(2)}) collective-permute-start(bf16[3,320,256]{2,1,0:T(8,128)(2,1)S(1)} %slice.39.refs_0_), channel_id=1, source_target_pairs={{0,1},{1,0},{2,3},{3,2},{4,5},{5,4},{6,7},{7,6},{8,9},{9,8},{10,11... | collective-permute-start | bytes 1474568 | tf_op jit(solution)/shard_map/ppermute | solution.py:309
  153.9 43.2 %collective-permute-start.17 = (bf16[3,320,256]{2,1,0:T(8,128)(2,1)S(1)}, bf16[3,320,256]{2,1,0:T(8,128)(2,1)S(1)}, u32[]{:S(2)}, u32[]{:S(2)}) collective-permute-start(bf16[3,320,256]{2,1,0:T(8,128)(2,1)S(1)} %slice.39.refs_0_), channel_id=1, source_target_pairs={{0,2},{1,3},{2,0},{3,1},{4,6},{5,7},{6,4},{7,5},{8,10},{9,11},{10,... | collective-permute-start | bytes 1474568 | tf_op jit(solution)/shard_map/ppermute | solution.py:309
  155.6 1.1 copy-start.3
  156.6 1.1 copy-start.5
  157.8 1.1 copy-start.8
  158.9 38.7 %copy-start.13 = (bf16[1280,1024]{1,0:T(8,128)(2,1)S(1)}, bf16[1280,1024]{1,0:T(8,128)(2,1)}, u32[]{:S(2)}) copy-start(bf16[1280,1024]{1,0:T(8,128)(2,1)} %pad_maximum_fusion.1.refs_2_) | copy-start | bytes 7864324
  158.9 49.4 %copy-start.4 = (f32[1280,1]{1,0:T(8,128)S(1)}, f32[1280,1]{1,0:T(8,128)}, u32[]{:S(2)}) copy-start(f32[1280,1]{1,0:T(8,128)} %broadcast_in_dim.39.refs_14_) | copy-start | bytes 15364
  158.9 49.4 %copy-start.6 = (bf16[320,1280]{1,0:T(8,128)(2,1)S(1)}, bf16[320,1280]{1,0:T(8,128)(2,1)}, u32[]{:S(2)}) copy-start(bf16[320,1280]{1,0:T(8,128)(2,1)} %refs_5_.3) | copy-start | bytes 2457604
  197.1 11.2 %collective-permute-start.18 = (bf16[3,320,256]{2,1,0:T(8,128)(2,1)S(1)}, bf16[3,320,256]{2,1,0:T(8,128)(2,1)S(1)}, u32[]{:S(2)}, u32[]{:S(2)}) collective-permute-start(bf16[3,320,256]{2,1,0:T(8,128)(2,1)S(1)} %collective-permute-done.17.refs_2_), channel_id=1, source_target_pairs={{0,1},{1,0},{2,3},{3,2},{4,5},{5,4},{6,7},{7,6},{8,9},{9,8},{10,11... | collective-permute-start | bytes 1474568 | tf_op jit(solution)/shard_map/ppermute | solution.py:309
  197.6 44.6 %copy-start.9 = (f32[2048]{0:T(1024)S(1)}, f32[2048]{0:T(1024)}, u32[]{:S(2)}) copy-start(f32[2048]{0:T(1024)} %param.22) | copy-start | bytes 24580
  197.6 34.8 %collective-permute-start.21 = (bf16[1280,1024]{1,0:T(8,128)(2,1)S(1)}, bf16[1280,1024]{1,0:T(8,128)(2,1)}, u32[]{:S(2)}, u32[]{:S(2)}) collective-permute-start(bf16[1280,1024]{1,0:T(8,128)(2,1)S(1)} %pad_maximum_fusion.refs_1_), channel_id=1, source_target_pairs={{0,4},{4,0},{8,12},{12,8},{16,20},{20,16},{24,28},{28,24},{1,5},{5... | collective-permute-start | bytes 7864328 | tf_op jit(solution)/shard_map/ppermute | solution.py:303
  197.6 34.7 %collective-permute-start.22 = (bf16[1280,1024]{1,0:T(8,128)(2,1)S(1)}, bf16[1280,1024]{1,0:T(8,128)(2,1)}, u32[]{:S(2)}, u32[]{:S(2)}) collective-permute-start(bf16[1280,1024]{1,0:T(8,128)(2,1)S(1)} %copy-done.13), channel_id=1, source_target_pairs={{0,4},{4,0},{8,12},{12,8},{16,20},{20,16},{24,28},{28,24},{1,5},{5... | collective-permute-start | bytes 7864328 | tf_op jit(solution)/shard_map/ppermute | solution.py:303
  231.7 5.2 %collective-permute-start.23 = (bf16[1280,1024]{1,0:T(8,128)(2,1)}, bf16[1280,1024]{1,0:T(8,128)(2,1)S(1)}, u32[]{:S(2)}, u32[]{:S(2)}) collective-permute-start(bf16[1280,1024]{1,0:T(8,128)(2,1)} %collective-permute-done.19.refs_3_), channel_id=1, source_target_pairs={{0,4},{4,0},{8,12},{12,8},{16,20},{20,16},{24,28},{28,24},{1,5},{5... | collective-permute-start | bytes 7864328 | tf_op jit(solution)/shard_map/ppermute | solution.py:303
  231.8 8.9 %collective-permute-start.24 = (bf16[1280,1024]{1,0:T(8,128)(2,1)}, bf16[1280,1024]{1,0:T(8,128)(2,1)S(1)}, u32[]{:S(2)}, u32[]{:S(2)}) collective-permute-start(bf16[1280,1024]{1,0:T(8,128)(2,1)} %collective-permute-done.20.refs_4_), channel_id=1, source_target_pairs={{0,4},{4,0},{8,12},{12,8},{16,20},{20,16},{24,28},{28,24},{1,5},{5... | collective-permute-start | bytes 7864328 | tf_op jit(solution)/shard_map/ppermute | solution.py:303
  236.9 5.3 %copy-start.17 = (bf16[1280,1024]{1,0:T(8,128)(2,1)}, bf16[1280,1024]{1,0:T(8,128)(2,1)S(1)}, u32[]{:S(2)}) copy-start(bf16[1280,1024]{1,0:T(8,128)(2,1)S(1)} %collective-permute-done.23.refs_7_) | copy-start | bytes 7864324
  240.6 1.5 copy-start.18
  267.9 1.4 copy-start.2
  269.6 47.2 %copy-start.1 = (bf16[2048,320]{0,1:T(8,128)(2,1)S(1)}, bf16[2048,320]{0,1:T(8,128)(2,1)}, u32[]{:S(2)}) copy-start(bf16[2048,320]{0,1:T(8,128)(2,1)} %param.13) | copy-start | bytes 3932164
Sparse Core Ops, SparseCore 0:
  269.4 45.1 reduce-scatter.1

commit v5 on v3

--- a/solution.py
+++ b/solution.py
@@ -349,40 +349,34 @@
             lax.dynamic_slice_in_dim(wq_t, jnp.minimum(s, q_parts - 1) * share, share),
             lax.dynamic_slice_in_dim(w_proj, jnp.maximum(s - q_parts, 0) * share, share),
         )
-        early = lax.optimization_barrier((tp_xor(mine, 1), tp_xor(mine, 2)))
-        others = [jnp.concatenate(early), tp_xor(early[1], 1)]
-        held_planes = [(1, 2), (3,)]
-
         def sides(x):
-            return list(lax.optimization_barrier((xor(x, 2), xor(x, 4))))
+            return lax.optimization_barrier((xor(x, 2), xor(x, 4)))
 
         def corners(by_x, by_y):
             half = by_x.shape[0] // 2
-            return [xor(by_x[:half], 4), xor(by_y[half:], 2)]
-
-        def cores(pieces):
-            return [xor(v, 1) for v in pieces]
-
-        first_by = sides(others[0])
-        last_by = sides(tie(others[1], first_by))
-        first_set = [others[0]] + first_by + corners(*first_by)
-        last_set = [others[1]] + last_by + corners(*last_by)
-        vit_weights = [wq_t, w_proj] + first_set + cores(first_set) + last_set + cores(last_set)
-        merge_by = sides(tie(w_merge, last_by))
+            return xor(by_x[:half], 4), xor(by_y[half:], 2)
+
+        def with_cores(pieces):
+            return list(pieces) + [xor(v, 1) for v in pieces]
+
+        def parts(rows):
+            half = rows // 2
+            own = [(0, 0, rows), (2, 0, rows), (4, 0, rows), (6, 0, half), (6, half, rows)]
+            return own + [(d ^ 1, lo, hi) for d, lo, hi in own]
+
+        by1, by2 = lax.optimization_barrier((tp_xor(mine, 1), tp_xor(mine, 2)))
+        others = jnp.concatenate([by1, by2, tp_xor(by2, 1)])
+        vit_sides = sides(others)
+        vit_corners = lax.optimization_barrier(corners(*vit_sides))
+        vit_weights = [wq_t, w_proj] + with_cores([others, *vit_sides, *vit_corners])
+        merge_sides = sides(tie(w_merge, vit_corners))
         q_rows, p_rows = wq_t.shape[0], w_proj.shape[0]
-
-        def spans(rows):
-            whole = [(0, 0, rows), (2, 0, rows), (4, 0, rows), (6, 0, rows // 2), (6, rows // 2, rows)]
-            return [(d ^ e, lo, hi) for e in range(2) for d, lo, hi in whole]
-
         vit_parts = []
-        for planes in held_planes:
-            base = 2 + 10 * held_planes.index(planes)
-            for n, (d, lo, hi) in enumerate(spans(share * len(planes))):
-                for k, j in enumerate(planes):
-                    top, end = max(lo, k * share), min(hi, (k + 1) * share)
-                    if top < end:
-                        vit_parts.append((base + n, d, j, top - lo, top - k * share, end - top))
+        for n, (d, lo, hi) in enumerate(parts(others.shape[0])):
+            for j in range(1, tp):
+                top, end = max(lo, (j - 1) * share), min(hi, j * share)
+                if top < end:
+                    vit_parts.append((2 + n, d, j, top - lo, top - (j - 1) * share, end - top))
         vit_count = 2 + len(vit_parts)
 
         def vit_moves(info, refs, w, sem):
@@ -418,16 +412,11 @@
             wide = slot.shape[1]
             rows = slot.shape[0] // 2
             copies = []
-            for n, (d, lo, hi) in enumerate(spans(rows)):
+            for n, (d, lo, hi) in enumerate(parts(rows)):
                 if d // 2 == i:
-                    at = pl.multiple_of(((s ^ d) & 1) * rows + lo, 16)
-                    copies.append(
-                        pltpu.make_async_copy(
-                            refs[n].at[:, h * wide : (h + 1) * wide],
-                            slot.at[pl.ds(at, hi - lo)],
-                            sem.at[len(copies)],
-                        )
-                    )
+                    spot = pl.ds(pl.multiple_of(((s ^ d) & 1) * rows + lo, 16), hi - lo)
+                    part = refs[n].at[:, h * wide : (h + 1) * wide]
+                    copies.append(pltpu.make_async_copy(part, slot.at[spot], sem.at[len(copies)]))
             return copies
 
         def position(info, i):
@@ -475,25 +464,21 @@
 
     merged = None
     if paired:
-        cuts = [0, 2, 5, 8]
-        near, done = [], []
-        for lo, hi in zip(cuts[:-1], cuts[1:]):
-            own = full[lo:hi] if not near else tie(full[lo:hi], near[-1])
-            near.append(lax.optimization_barrier((tp_xor(own, 1), tp_xor(own, 2))))
+        cuts = [0, mid, blocks]
+        far = None
         for n, lo in enumerate(cuts[:-1]):
-            by1, by2 = near[n]
-            if n >= 2:
-                merged, by2 = lax.optimization_barrier((merged, by2))
+            own = full[lo : cuts[n + 1]]
+            near = own if far is None else tie(own, (far, vit_weights[2:]))
+            by1, by2 = lax.optimization_barrier((tp_xor(near, 1), tp_xor(near, 2)))
+            if n:
+                merged, by2, live_here = lax.optimization_barrier((merged, by2, live_here))
             far = tp_xor(by2, 1)
-            if n == len(cuts) - 2:
-                merged, far, merge_by = lax.optimization_barrier((merged, far, merge_by))
-            if n == 1:
-                merged, live_here = lax.optimization_barrier((merged, live_here))
-            merged = encode(lo, [full[lo : cuts[n + 1]], by1, by2, far], merged)
-        merge_corners = corners(*merge_by)
+            if n:
+                far, merge_sides = lax.optimization_barrier((far, merge_sides))
+            merged = encode(lo, [own, by1, by2, far], merged)
+        merge_corners = corners(*merge_sides)
         merged, merge_corners = lax.optimization_barrier((merged, merge_corners))
-        merge_pieces = [w_merge] + list(merge_by) + list(merge_corners)
-        merge_weights = merge_pieces + cores(merge_pieces)
+        merge_weights = with_cores([w_merge, *merge_sides, *merge_corners])
     else:
         for first in (0, mid):
             merged = encode(first, spread(full[first : first + mid]), merged)

time: 325 us -> 345 us (1.062)
  waiting for transfers between devices: 142 us -> 181 us
  starting transfers between devices: 35.8 us -> 27.5 us
  Pallas kernels: 96.8 us -> 89.4 us
    all_to_all x1, waiting for transfers between devices: 0.01 us -> 52.9 us  [shards(): lax.all_to_all(live_send, 'seq', split_axis=0, concat_axis=0, tiled=True)]
    ppermute x12 -> x9, waiting for transfers between devices: 47.9 us -> 36.3 us  [tp_xor(): return lax.ppermute(x, 'tp', [(i, i ^ d) for i in range(tp)])]
    all_to_all x1, waiting for transfers between devices: 10.6 us -> 2.87 us  [shards(): lax.all_to_all(sent.reshape(feats, seq_count, step).transpose(1, 0, 2), '...]
    pallas_call x3 -> x2, Pallas kernels: 66.6 us -> 59.3 us  [attend(): pl.pallas_call(functools.partial(attend_kernel, tp, moves, len(weights),...]
    ppermute x27 -> x18, starting transfers between devices: 17 us -> 10.5 us  [xor(): return lax.ppermute(x, 'seq', [(i, i ^ d) for i in range(seq_count)])]
    reduce_scatter x1, waiting for transfers between devices: 43.1 us -> 46.7 us  [shards(): lax.psum_scatter(partial_value, 'tp', scatter_dimension=0, tiled=True)]
    ppermute x27 -> x18, waiting for transfers between devices: 40.9 us -> 42.4 us  [xor(): return lax.ppermute(x, 'seq', [(i, i ^ d) for i in range(seq_count)])]
    ppermute x12 -> x9, starting transfers between devices: 11.5 us -> 9.99 us  [tp_xor(): return lax.ppermute(x, 'tp', [(i, i ^ d) for i in range(tp)])]
  transfers between devices with their start and end apart: 42 -> 30, of which waited for: 17 -> 16; matrix products, arithmetic and copies ran while one was open for 7% -> 6% of each run, Pallas kernels for 21% -> 17%
where the time goes in v5:
time: 345 us; the launch traced here: 344 us
  waiting for transfers between devices  181 us (52%)
  Pallas kernels  89.4 us (26%)
  starting transfers between devices  27.5 us (8%)
  local copies, waits for them, and re-layouts  20.1 us (6%)
  between operations  13.6 us (4%)
  other arithmetic  8.91 us (3%)
  matrix products  3.47 us (1%)
    pallas_call x2, Pallas kernels, attend(): pl.pallas_call(functools.partial(attend_kernel, tp, moves, len(weights),...  59.3 us
    all_to_all x1, waiting for transfers between devices, shards(): lax.all_to_all(live_send, 'seq', split_axis=0, concat_axis=0, tiled=True)  52.9 us
    reduce_scatter x1, waiting for transfers between devices, shards(): lax.psum_scatter(partial_value, 'tp', scatter_dimension=0, tiled=True)  46.7 us
    ppermute x18, waiting for transfers between devices, xor(): return lax.ppermute(x, 'seq', [(i, i ^ d) for i in range(seq_count)])  42.4 us
    ppermute x9, waiting for transfers between devices, tp_xor(): return lax.ppermute(x, 'tp', [(i, i ^ d) for i in range(tp)])  36.3 us
    pallas_call x1, Pallas kernels, project(): pl.pallas_call(functools.partial(project_kernel, moves, position, len(wei...  30.1 us
    ppermute x18, starting transfers between devices, xor(): return lax.ppermute(x, 'seq', [(i, i ^ d) for i in range(seq_count)])  10.5 us
    ppermute x9, starting transfers between devices, tp_xor(): return lax.ppermute(x, 'tp', [(i, i ^ d) for i in range(tp)])  9.99 us
  transfers between devices with their start and end apart: 30, of which 16 were waited for; matrix products, arithmetic and copies ran while one was open for 6% of the time, Pallas kernels for 17%

profile of v5, /device:TPU:0, one launch (start us, length us, event | category | flops | bytes accessed | tf_op | source)
XLA Modules:
  0.0 344.2 jit_solution(4646255717214341267)
XLA Ops:
  6.5 2.1 bitcast_select_fusion
  8.6 3.0 collective-permute-start.3
  11.7 2.6 collective-permute-start.4
  14.2 2.3 sort.17
  16.5 1.3 fusion.10
  17.9 1.9 compare_convert_fusion
  19.8 0.7 gather_fusion.1
  20.5 0.7 gather_fusion
  21.5 3.5 %fusion.2 = bf16[2048,320]{0,1:T(8,128)(2,1)S(1)} fusion(bf16[2048,320]{0,1:T(8,128)(2,1)S(1)} %copy-done, s32[2048]{0:T(1024)S(1)} %add.115), kind=kOutput, calls=%fused_computation.5 | convolution fusion | flops 2689204224 | bytes 2629632 | tf_op jit(solution)/shard_map/dot_general | solution.py:327
  25.0 1.2 copy.28
  26.1 3.7 %all-to-all-start = ((bf16[8,320,256]{2,1,0:T(8,128)(2,1)}), bf16[8,320,256]{2,1,0:T(8,128)(2,1)S(1)}, u32[]{:S(2)}, u32[]{:S(2)}) async-start(bf16[8,320,256]{2,1,0:T(8,128)(2,1)} %bitcast.36), calls=%async_computation | async-start | bytes 2621440 | tf_op jit(solution)/shard_map/all_to_all | solution.py:333
  30.0 2.6 collective-permute-done.4
  32.5 0.4 collective-permute-start.5
  33.0 0.8 constant_dynamic-update-slice_fusion.2
  33.7 0.8 constant_dynamic-update-slice_fusion.1
  34.5 7.3 %collective-permute-done.5 = bf16[160,1280]{1,0:T(8,128)(2,1)S(1)} collective-permute-done((bf16[160,1280]{1,0:T(8,128)(2,1)S(1)}, bf16[160,1280]{1,0:T(8,128)(2,1)S(1)}, u32[]{:S(2)}, u32[]{:S(2)}) %collective-permute-start.5) | collective-permute-done | bytes 409632 | tf_op jit(solution)/shard_map/ppermute | solution.py:309
  41.8 0.8 constant_dynamic-update-slice_fusion.refs_6_
  42.6 1.7 collective-permute-start.6
  44.3 1.5 collective-permute-start.7
  45.7 2.9 all-to-all-done
  48.7 0.5 collective-permute-start
  49.2 0.3 collective-permute-start.1
  49.6 24.1 %collective-permute-done.6.refs_7_ = bf16[480,1280]{1,0:T(8,128)(2,1)} collective-permute-done((bf16[480,1280]{1,0:T(8,128)(2,1)}, bf16[480,1280]{1,0:T(8,128)(2,1)}, u32[]{:S(2)}, u32[]{:S(2)}) %collective-permute-start.6) | collective-permute-done | bytes 1228832 | tf_op jit(solution)/shard_map/ppermute | solution.py:303
  73.7 0.2 collective-permute-done.7.refs_8_
  73.9 1.1 slice.26
  75.0 1.3 collective-permute-start.8
  76.3 1.1 slice.27
  77.4 0.6 collective-permute-start.9
  78.1 0.5 collective-permute-start.12
  78.6 11.7 %collective-permute-done.8.refs_9_ = bf16[240,1280]{1,0:T(8,128)(2,1)S(1)} collective-permute-done((bf16[240,1280]{1,0:T(8,128)(2,1)S(1)}, bf16[240,1280]{1,0:T(8,128)(2,1)S(1)}, u32[]{:S(2)}, u32[]{:S(2)}) %collective-permute-start.8) | collective-permute-done | bytes 614432 | tf_op jit(solution)/shard_map/ppermute | solution.py:303
  90.2 0.9 collective-permute-start.2
  91.2 1.5 collective-permute-done.9.refs_10_
  92.7 0.8 copy-done.4
  93.6 0.5 collective-permute-start.14
  94.1 11.4 %collective-permute-done.2.refs_3_ = bf16[4,320,256]{2,1,0:T(8,128)(2,1)S(1)} collective-permute-done((bf16[4,320,256]{2,1,0:T(8,128)(2,1)S(1)}, bf16[4,320,256]{2,1,0:T(8,128)(2,1)S(1)}, u32[]{:S(2)}, u32[]{:S(2)}) %collective-permute-start.2) | collective-permute-done | bytes 655392 | tf_op jit(solution)/shard_map/ppermute | solution.py:309
  105.5 0.8 copy-done.2
  106.3 2.5 collective-permute-start.18
  108.8 0.8 copy-done.7
  109.7 0.7 all_to_all.12
  110.3 3.3 all-to-all-start.1
  113.7 0.2 broadcast_in_dim.39.refs_16_
  114.1 52.9 %all-to-all-done.1 = s32[8,1,4]{2,1,0:T(1,128)S(1)} async-done(((s32[8,1,4]{2,1,0:T(1,128)}), s32[8,1,4]{2,1,0:T(1,128)S(1)}, u32[]{:S(2)}, u32[]{:S(2)}) %all-to-all-start.1) | async-done | bytes 160 | tf_op jit(solution)/shard_map/all_to_all | solution.py:299
  167.0 0.6 collective-permute-start.15
  167.7 1.1 copy-done.3
  168.7 1.1 copy-done.5
  169.8 1.1 copy-done.8
  170.9 29.7 %attend.2.refs_18_ = bf16[4,8,64,1280]{3,2,1,0:T(8,128)(2,1)} custom-call(s32[6]{0:T(128)S(1)} %pad_add_fusion.3.info, bf16[4,320,256]{2,1,0:T(8,128)(2,1)S(1)} %get-tuple-element.54.refs_0_, bf16[4,320,256]{2,1,0:T(8,128)(2,1)S(1)} %collective-permute-done.refs_1_, bf16[4,320,256]{2,1,0:T(8,128)(2,1)S(1)} %collective-permute-done.1.refs_2_, ...), custom_call_target="tpu_custom_call" | custom-call | flops 16777216000 | bytes 14680064 | tf_op jit(solution)/shard_map/attend/pallas_call | solution.py:148
  200.7 1.5 collective-permute-start.17
  202.3 14.9 %collective-permute-done.17.refs_3_ = bf16[4,320,256]{2,1,0:T(8,128)(2,1)S(1)} collective-permute-done((bf16[4,320,256]{2,1,0:T(8,128)(2,1)S(1)}, bf16[4,320,256]{2,1,0:T(8,128)(2,1)S(1)}, u32[]{:S(2)}, u32[]{:S(2)}) %collective-permute-start.17) | collective-permute-done | bytes 655392 | tf_op jit(solution)/shard_map/ppermute | solution.py:309
  217.2 1.4 slice.28
  218.7 1.4 slice.29
  220.1 0.5 collective-permute-start.24
  220.7 0.3 collective-permute-start.20
  220.9 0.5 collective-permute-start.21
  221.4 29.5 %attend.3 = bf16[4,8,64,1280]{3,2,1,0:T(8,128)(2,1)} custom-call(s32[6]{0:T(128)S(1)} %pad_add_fusion.1.info, bf16[4,320,256]{2,1,0:T(8,128)(2,1)S(1)} %get-tuple-element.38.refs_0_, bf16[4,320,256]{2,1,0:T(8,128)(2,1)S(1)} %collective-permute-done.15.refs_1_, ...), custom_call_target="tpu_custom_call", output_to_operand_aliasing={{}: (19, {})} | custom-call | flops 16777216000 | bytes 14680064 | tf_op jit(solution)/shard_map/attend/pallas_call | solution.py:148
  250.9 0.5 collective-permute-done.20.refs_4_
  251.5 0.5 collective-permute-start.26
  252.1 2.4 collective-permute-done.25.refs_9_
  254.5 1.9 collective-permute-done.26.refs_10_
  256.4 1.5 copy-done.14
  257.9 30.1 %project.1 = bf16[512,2176]{1,0:T(8,128)(2,1)} custom-call(s32[2]{0:T(128)S(1)} %pad_add_fusion.info, bf16[4,512,1280]{2,1,0:T(8,128)(2,1)} %bitcast.44, bf16[640,2048]{1,0:T(8,128)(2,1)} %refs_1_.1, bf16[640,2048]{1,0:T(8,128)(2,1)} %collective-permute-done.18.refs_2_, bf16[640,2048]{1,0:T(8,128)(2,1)} %collective-permute-done.19.refs_3_, ...), custom_call_target="tpu_custom_call" | custom-call | flops 15032385536 | bytes 37748736 | tf_op jit(solution)/shard_map/project/pallas_call | solution.py:249
  288.4 46.7 %reduce-scatter.2.cloned.1.call-done = bf16[128,2176]{1,0:T(8,128)(2,1)} async-done(((bf16[512,2176]{1,0:T(8,128)(2,1)}), bf16[128,2176]{1,0:T(8,128)(2,1)}) %reduce-scatter.2.cloned.1.call-update) | async-done | bytes 557072 | tf_op jit(solution)/shard_map/reduce_scatter | solution.py:488
  335.2 1.1 convert_element_type.22
  336.4 1.0 fusion.4
  (74 shorter events, 1.7 us)
Async XLA Ops:
  6.5 14.9 %copy-start = (bf16[2048,320]{0,1:T(8,128)(2,1)S(1)}, bf16[2048,320]{0,1:T(8,128)(2,1)}, u32[]{:S(2)}) copy-start(bf16[2048,320]{0,1:T(8,128)(2,1)} %param.13) | copy-start | bytes 3932164
  6.5 13.9 %copy-start.10 = (s32[1,32]{1,0:T(1,128)S(1)}, s32[1,32]{1,0:T(1,128)}, u32[]{:S(2)}) copy-start(s32[1,32]{1,0:T(1,128)} %param.15) | copy-start | bytes 388
  8.6 21.3 %collective-permute-start.3 = (bf16[160,1280]{1,0:T(8,128)(2,1)}, bf16[160,1280]{1,0:T(8,128)(2,1)S(1)}, u32[]{:S(2)}, u32[]{:S(2)}) collective-permute-start(bf16[160,1280]{1,0:T(8,128)(2,1)} %bitcast_select_fusion), channel_id=1, source_target_pairs={{0,1},{1,0},{2,3},{3,2},{4,5},{5,4},{6,7},{7,6},{8,9},{9,8},{10,11... | collective-permute-start | bytes 1228808 | tf_op jit(solution)/shard_map/ppermute | solution.py:309
  11.7 20.9 %collective-permute-start.4 = (bf16[160,1280]{1,0:T(8,128)(2,1)}, bf16[160,1280]{1,0:T(8,128)(2,1)S(1)}, u32[]{:S(2)}, u32[]{:S(2)}) collective-permute-start(bf16[160,1280]{1,0:T(8,128)(2,1)} %bitcast_select_fusion), channel_id=1, source_target_pairs={{0,2},{1,3},{2,0},{3,1},{4,6},{5,7},{6,4},{7,5},{8,10},{9,11},{10,... | collective-permute-start | bytes 1228808 | tf_op jit(solution)/shard_map/ppermute | solution.py:309
  26.1 22.5 %all-to-all-start = ((bf16[8,320,256]{2,1,0:T(8,128)(2,1)}), bf16[8,320,256]{2,1,0:T(8,128)(2,1)S(1)}, u32[]{:S(2)}, u32[]{:S(2)}) async-start(bf16[8,320,256]{2,1,0:T(8,128)(2,1)} %bitcast.36), calls=%async_computation | async-start | bytes 2621440 | tf_op jit(solution)/shard_map/all_to_all | solution.py:333
  32.5 9.3 %collective-permute-start.5 = (bf16[160,1280]{1,0:T(8,128)(2,1)S(1)}, bf16[160,1280]{1,0:T(8,128)(2,1)S(1)}, u32[]{:S(2)}, u32[]{:S(2)}) collective-permute-start(bf16[160,1280]{1,0:T(8,128)(2,1)S(1)} %collective-permute-done.4), channel_id=1, source_target_pairs={{0,1},{1,0},{2,3},{3,2},{4,5},{5,4},{6,7},{7,6},{8,9},{9,8},{10,11... | collective-permute-start | bytes 1228808 | tf_op jit(solution)/shard_map/ppermute | solution.py:309
  42.6 31.1 %collective-permute-start.6 = (bf16[480,1280]{1,0:T(8,128)(2,1)}, bf16[480,1280]{1,0:T(8,128)(2,1)}, u32[]{:S(2)}, u32[]{:S(2)}) collective-permute-start(bf16[480,1280]{1,0:T(8,128)(2,1)} %constant_dynamic-update-slice_fusion.refs_6_), channel_id=1, source_target_pairs={{0,8},{4,12},{8,0},{12,4},{16,24},{20,28},{24,16},{28,20},{1,9},{5... | collective-permute-start | bytes 3686408 | tf_op jit(solution)/shard_map/ppermute | solution.py:303
  44.3 29.6 %collective-permute-start.7 = (bf16[480,1280]{1,0:T(8,128)(2,1)}, bf16[480,1280]{1,0:T(8,128)(2,1)}, u32[]{:S(2)}, u32[]{:S(2)}) collective-permute-start(bf16[480,1280]{1,0:T(8,128)(2,1)} %constant_dynamic-update-slice_fusion.refs_6_), channel_id=1, source_target_pairs={{0,16},{4,20},{8,24},{12,28},{16,0},{20,4},{24,8},{28,12},{1,17},{... | collective-permute-start | bytes 3686408 | tf_op jit(solution)/shard_map/ppermute | solution.py:303
  48.7 65.0 %copy-start.12 = (f32[1280]{0:T(1024)S(1)}, f32[1280]{0:T(1024)}, u32[]{:S(2)}) copy-start(f32[1280]{0:T(1024)} %param.19) | copy-start | bytes 15364
  48.7 65.3 %copy-start.11 = (f32[1280]{0:T(1024)S(1)}, f32[1280]{0:T(1024)}, u32[]{:S(2)}) copy-start(f32[1280]{0:T(1024)} %param.20) | copy-start | bytes 15364
  48.7 29.3 %collective-permute-start = (bf16[4,320,256]{2,1,0:T(8,128)(2,1)S(1)}, bf16[4,320,256]{2,1,0:T(8,128)(2,1)S(1)}, u32[]{:S(2)}, u32[]{:S(2)}) collective-permute-start(bf16[4,320,256]{2,1,0:T(8,128)(2,1)S(1)} %get-tuple-element.54.refs_0_), channel_id=1, source_target_pairs={{0,1},{1,0},{2,3},{3,2},{4,5},{5,4},{6,7},{7,6},{8,9},{9,8},{10,11... | collective-permute-start | bytes 1966088 | tf_op jit(solution)/shard_map/ppermute | solution.py:309
  49.2 28.8 %collective-permute-start.1 = (bf16[4,320,256]{2,1,0:T(8,128)(2,1)S(1)}, bf16[4,320,256]{2,1,0:T(8,128)(2,1)S(1)}, u32[]{:S(2)}, u32[]{:S(2)}) collective-permute-start(bf16[4,320,256]{2,1,0:T(8,128)(2,1)S(1)} %get-tuple-element.54.refs_0_), channel_id=1, source_target_pairs={{0,2},{1,3},{2,0},{3,1},{4,6},{5,7},{6,4},{7,5},{8,10},{9,11},{10,... | collective-permute-start | bytes 1966088 | tf_op jit(solution)/shard_map/ppermute | solution.py:309
  49.6 44.0 %collective-permute-start.10 = (bf16[480,1280]{1,0:T(8,128)(2,1)}, bf16[480,1280]{1,0:T(8,128)(2,1)S(1)}, u32[]{:S(2)}, u32[]{:S(2)}) collective-permute-start(bf16[480,1280]{1,0:T(8,128)(2,1)} %constant_dynamic-update-slice_fusion.refs_6_), channel_id=1, source_target_pairs={{0,4},{4,0},{8,12},{12,8},{16,20},{20,16},{24,28},{28,24},{1,5},{5... | collective-permute-start | bytes 3686408 | tf_op jit(solution)/shard_map/ppermute | solution.py:303
  75.0 15.2 %collective-permute-start.8 = (bf16[240,1280]{1,0:T(8,128)(2,1)S(1)}, bf16[240,1280]{1,0:T(8,128)(2,1)S(1)}, u32[]{:S(2)}, u32[]{:S(2)}) collective-permute-start(bf16[240,1280]{1,0:T(8,128)(2,1)S(1)} %slice.26), channel_id=1, source_target_pairs={{0,16},{4,20},{8,24},{12,28},{16,0},{20,4},{24,8},{28,12},{1,17},{... | collective-permute-start | bytes 1843208 | tf_op jit(solution)/shard_map/ppermute | solution.py:303
  77.4 15.3 %collective-permute-start.9 = (bf16[240,1280]{1,0:T(8,128)(2,1)S(1)}, bf16[240,1280]{1,0:T(8,128)(2,1)}, u32[]{:S(2)}, u32[]{:S(2)}) collective-permute-start(bf16[240,1280]{1,0:T(8,128)(2,1)S(1)} %slice.27), channel_id=1, source_target_pairs={{0,8},{4,12},{8,0},{12,4},{16,24},{20,28},{24,16},{28,20},{1,9},{5... | collective-permute-start | bytes 1843208 | tf_op jit(solution)/shard_map/ppermute | solution.py:303
  78.0 89.0 %collective-permute-start.11 = (bf16[480,1280]{1,0:T(8,128)(2,1)}, bf16[480,1280]{1,0:T(8,128)(2,1)}, u32[]{:S(2)}, u32[]{:S(2)}) collective-permute-start(bf16[480,1280]{1,0:T(8,128)(2,1)} %collective-permute-done.6.refs_7_), channel_id=1, source_target_pairs={{0,4},{4,0},{8,12},{12,8},{16,20},{20,16},{24,28},{28,24},{1,5},{5... | collective-permute-start | bytes 3686408 | tf_op jit(solution)/shard_map/ppermute | solution.py:303
  78.1 88.9 %collective-permute-start.12 = (bf16[480,1280]{1,0:T(8,128)(2,1)}, bf16[480,1280]{1,0:T(8,128)(2,1)}, u32[]{:S(2)}, u32[]{:S(2)}) collective-permute-start(bf16[480,1280]{1,0:T(8,128)(2,1)} %collective-permute-done.7.refs_8_), channel_id=1, source_target_pairs={{0,4},{4,0},{8,12},{12,8},{16,20},{20,16},{24,28},{28,24},{1,5},{5... | collective-permute-start | bytes 3686408 | tf_op jit(solution)/shard_map/ppermute | solution.py:303
  90.2 15.2 %collective-permute-start.2 = (bf16[4,320,256]{2,1,0:T(8,128)(2,1)S(1)}, bf16[4,320,256]{2,1,0:T(8,128)(2,1)S(1)}, u32[]{:S(2)}, u32[]{:S(2)}) collective-permute-start(bf16[4,320,256]{2,1,0:T(8,128)(2,1)S(1)} %collective-permute-done.1.refs_2_), channel_id=1, source_target_pairs={{0,1},{1,0},{2,3},{3,2},{4,5},{5,4},{6,7},{7,6},{8,9},{9,8},{10,11... | collective-permute-start | bytes 1966088 | tf_op jit(solution)/shard_map/ppermute | solution.py:309
  92.7 16.1 %collective-permute-start.13 = (bf16[240,1280]{1,0:T(8,128)(2,1)S(1)}, bf16[240,1280]{1,0:T(8,128)(2,1)S(1)}, u32[]{:S(2)}, u32[]{:S(2)}) collective-permute-start(bf16[240,1280]{1,0:T(8,128)(2,1)S(1)} %collective-permute-done.8.refs_9_), channel_id=1, source_target_pairs={{0,4},{4,0},{8,12},{12,8},{16,20},{20,16},{24,28},{28,24},{1,5},{5... | collective-permute-start | bytes 1843208 | tf_op jit(solution)/shard_map/ppermute | solution.py:303
  92.7 0.8 copy-start.4
  93.6 15.3 %copy-start.15 = (bf16[480,1280]{1,0:T(8,128)(2,1)}, bf16[480,1280]{1,0:T(8,128)(2,1)S(1)}, u32[]{:S(2)}) copy-start(bf16[480,1280]{1,0:T(8,128)(2,1)S(1)} %collective-permute-done.10.refs_11_) | copy-start | bytes 3686404
  93.6 73.4 %collective-permute-start.14 = (bf16[240,1280]{1,0:T(8,128)(2,1)}, bf16[240,1280]{1,0:T(8,128)(2,1)}, u32[]{:S(2)}, u32[]{:S(2)}) collective-permute-start(bf16[240,1280]{1,0:T(8,128)(2,1)} %collective-permute-done.9.refs_10_), channel_id=1, source_target_pairs={{0,4},{4,0},{8,12},{12,8},{16,20},{20,16},{24,28},{28,24},{1,5},{5... | collective-permute-start | bytes 1843208 | tf_op jit(solution)/shard_map/ppermute | solution.py:303
  105.5 0.8 copy-start.2
  106.3 96.0 %collective-permute-start.18 = (bf16[640,2048]{1,0:T(8,128)(2,1)}, bf16[640,2048]{1,0:T(8,128)(2,1)}, u32[]{:S(2)}, u32[]{:S(2)}) collective-permute-start(bf16[640,2048]{1,0:T(8,128)(2,1)} %refs_1_.1), channel_id=1, source_target_pairs={{0,8},{4,12},{8,0},{12,4},{16,24},{20,28},{24,16},{28,20},{1,9},{5... | collective-permute-start | bytes 7864328 | tf_op jit(solution)/shard_map/ppermute | solution.py:303
  108.8 0.8 copy-start.7
  109.7 92.6 %collective-permute-start.19 = (bf16[640,2048]{1,0:T(8,128)(2,1)}, bf16[640,2048]{1,0:T(8,128)(2,1)}, u32[]{:S(2)}, u32[]{:S(2)}) collective-permute-start(bf16[640,2048]{1,0:T(8,128)(2,1)} %refs_1_.1), channel_id=1, source_target_pairs={{0,16},{4,20},{8,24},{12,28},{16,0},{20,4},{24,8},{28,12},{1,17},{... | collective-permute-start | bytes 7864328 | tf_op jit(solution)/shard_map/ppermute | solution.py:303
  110.3 56.6 %all-to-all-start.1 = ((s32[8,1,4]{2,1,0:T(1,128)}), s32[8,1,4]{2,1,0:T(1,128)S(1)}, u32[]{:S(2)}, u32[]{:S(2)}) async-start(s32[8,1,4]{2,1,0:T(1,128)} %bitcast.12), calls=%async_computation.1 | async-start | bytes 8192 | tf_op jit(solution)/shard_map/all_to_all | solution.py:299
  113.7 221.5 %reduce-scatter.2.cloned.1.call-start = ((), (), s32[]{:S(2)}) async-start(), calls=%async_computation.3 | async-start | bytes 2785280 | tf_op jit(solution)/shard_map/reduce_scatter | solution.py:488
  167.0 33.6 %collective-permute-start.15 = (bf16[4,320,256]{2,1,0:T(8,128)(2,1)S(1)}, bf16[4,320,256]{2,1,0:T(8,128)(2,1)S(1)}, u32[]{:S(2)}, u32[]{:S(2)}) collective-permute-start(bf16[4,320,256]{2,1,0:T(8,128)(2,1)S(1)} %get-tuple-element.38.refs_0_), channel_id=1, source_target_pairs={{0,1},{1,0},{2,3},{3,2},{4,5},{5,4},{6,7},{7,6},{8,9},{9,8},{10,11... | collective-permute-start | bytes 1966088 | tf_op jit(solution)/shard_map/ppermute | solution.py:309
  167.7 33.0 %collective-permute-start.16 = (bf16[4,320,256]{2,1,0:T(8,128)(2,1)S(1)}, bf16[4,320,256]{2,1,0:T(8,128)(2,1)S(1)}, u32[]{:S(2)}, u32[]{:S(2)}) collective-permute-start(bf16[4,320,256]{2,1,0:T(8,128)(2,1)S(1)} %get-tuple-element.38.refs_0_), channel_id=1, source_target_pairs={{0,2},{1,3},{2,0},{3,1},{4,6},{5,7},{6,4},{7,5},{8,10},{9,11},{10,... | collective-permute-start | bytes 1966088 | tf_op jit(solution)/shard_map/ppermute | solution.py:309
  167.7 1.1 copy-start.3
  168.7 1.1 copy-start.5
  169.8 1.1 copy-start.8
  200.7 16.5 %collective-permute-start.17 = (bf16[4,320,256]{2,1,0:T(8,128)(2,1)S(1)}, bf16[4,320,256]{2,1,0:T(8,128)(2,1)S(1)}, u32[]{:S(2)}, u32[]{:S(2)}) collective-permute-start(bf16[4,320,256]{2,1,0:T(8,128)(2,1)S(1)} %collective-permute-done.16.refs_2_), channel_id=1, source_target_pairs={{0,1},{1,0},{2,3},{3,2},{4,5},{5,4},{6,7},{7,6},{8,9},{9,8},{10,11... | collective-permute-start | bytes 1966088 | tf_op jit(solution)/shard_map/ppermute | solution.py:309
  202.2 49.9 %collective-permute-start.22 = (bf16[640,2048]{1,0:T(8,128)(2,1)}, bf16[640,2048]{1,0:T(8,128)(2,1)S(1)}, u32[]{:S(2)}, u32[]{:S(2)}) collective-permute-start(bf16[640,2048]{1,0:T(8,128)(2,1)} %refs_1_.1), channel_id=1, source_target_pairs={{0,4},{4,0},{8,12},{12,8},{16,20},{20,16},{24,28},{28,24},{1,5},{5... | collective-permute-start | bytes 7864328 | tf_op jit(solution)/shard_map/ppermute | solution.py:303
  218.6 2.8 copy-start.6
  218.6 37.8 %collective-permute-start.23 = (bf16[640,2048]{1,0:T(8,128)(2,1)}, bf16[640,2048]{1,0:T(8,128)(2,1)S(1)}, u32[]{:S(2)}, u32[]{:S(2)}) collective-permute-start(bf16[640,2048]{1,0:T(8,128)(2,1)} %collective-permute-done.18.refs_2_), channel_id=1, source_target_pairs={{0,4},{4,0},{8,12},{12,8},{16,20},{20,16},{24,28},{28,24},{1,5},{5... | collective-permute-start | bytes 7864328 | tf_op jit(solution)/shard_map/ppermute | solution.py:303
  220.1 37.8 %copy-start.9 = (f32[2048]{0:T(1024)S(1)}, f32[2048]{0:T(1024)}, u32[]{:S(2)}) copy-start(f32[2048]{0:T(1024)} %param.22) | copy-start | bytes 24580
  220.1 36.3 %collective-permute-start.24 = (bf16[640,2048]{1,0:T(8,128)(2,1)}, bf16[640,2048]{1,0:T(8,128)(2,1)}, u32[]{:S(2)}, u32[]{:S(2)}) collective-permute-start(bf16[640,2048]{1,0:T(8,128)(2,1)} %collective-permute-done.19.refs_3_), channel_id=1, source_target_pairs={{0,4},{4,0},{8,12},{12,8},{16,20},{20,16},{24,28},{28,24},{1,5},{5... | collective-permute-start | bytes 7864328 | tf_op jit(solution)/shard_map/ppermute | solution.py:303
  220.7 30.8 %collective-permute-start.20 = (bf16[320,2048]{1,0:T(8,128)(2,1)S(1)}, bf16[320,2048]{1,0:T(8,128)(2,1)S(1)}, u32[]{:S(2)}, u32[]{:S(2)}) collective-permute-start(bf16[320,2048]{1,0:T(8,128)(2,1)S(1)} %slice.28), channel_id=1, source_target_pairs={{0,16},{4,20},{8,24},{12,28},{16,0},{20,4},{24,8},{28,12},{1,17},{... | collective-permute-start | bytes 3932168 | tf_op jit(solution)/shard_map/ppermute | solution.py:303
  220.9 30.6 %collective-permute-start.21 = (bf16[320,2048]{1,0:T(8,128)(2,1)S(1)}, bf16[320,2048]{1,0:T(8,128)(2,1)S(1)}, u32[]{:S(2)}, u32[]{:S(2)}) collective-permute-start(bf16[320,2048]{1,0:T(8,128)(2,1)S(1)} %slice.29), channel_id=1, source_target_pairs={{0,8},{4,12},{8,0},{12,4},{16,24},{20,28},{24,16},{28,20},{1,9},{5... | collective-permute-start | bytes 3932168 | tf_op jit(solution)/shard_map/ppermute | solution.py:303
  251.5 3.0 collective-permute-start.25
  251.5 4.9 %collective-permute-start.26 = (bf16[320,2048]{1,0:T(8,128)(2,1)S(1)}, bf16[320,2048]{1,0:T(8,128)(2,1)S(1)}, u32[]{:S(2)}, u32[]{:S(2)}) collective-permute-start(bf16[320,2048]{1,0:T(8,128)(2,1)S(1)} %collective-permute-done.21.refs_5_), channel_id=1, source_target_pairs={{0,4},{4,0},{8,12},{12,8},{16,20},{20,16},{24,28},{28,24},{1,5},{5... | collective-permute-start | bytes 3932168 | tf_op jit(solution)/shard_map/ppermute | solution.py:303
  252.1 4.3 %copy-start.13 = (bf16[640,2048]{1,0:T(8,128)(2,1)}, bf16[640,2048]{1,0:T(8,128)(2,1)S(1)}, u32[]{:S(2)}) copy-start(bf16[640,2048]{1,0:T(8,128)(2,1)S(1)} %collective-permute-done.22.refs_6_) | copy-start | bytes 7864324
  256.4 1.5 copy-start.14
  288.4 49.0 %copy-start.1 = (bf16[2048,320]{0,1:T(8,128)(2,1)S(1)}, bf16[2048,320]{0,1:T(8,128)(2,1)}, u32[]{:S(2)}) copy-start(bf16[2048,320]{0,1:T(8,128)(2,1)} %param.13) | copy-start | bytes 3932164
Sparse Core Ops, SparseCore 0:
  288.2 46.9 reduce-scatter.1

commit v6 on v5

--- a/solution.py
+++ b/solution.py
@@ -185,7 +185,7 @@
     half = units // 2
     rows = held.shape[1]
     depth = slots.shape[0]
-    width = min(256, half)
+    width = min(1024, half)
     chunks = [(h, i) for h in range(2) for i in range(MERGE)]
 
     def bring(n):
@@ -296,7 +296,6 @@
     live = (tile_index % TILE_SLOTS < counts).astype(jnp.int32)
     arrange = jnp.argsort(route[:, 0], stable=True)
     live_send = jnp.take(live, arrange).reshape(seq_count, per_peer)
-    live_here = lax.all_to_all(live_send, "seq", split_axis=0, concat_axis=0, tiled=True)
     window = jnp.take(picks, arrange).reshape(seq_count, per_peer)
 
     def xor(x, d):
@@ -327,17 +326,20 @@
     sent = lax.dot_general(
         patches, pick, (((0,), (0,)), ((), ())), preferred_element_type=F32
     ).astype(BF)
+    alive = jnp.repeat(live_send.reshape(-1), WIN).astype(BF)
+    sent = jnp.concatenate([sent, jnp.broadcast_to(alive, (16, alive.shape[0]))])
     step = per_peer * WIN
     wq_t = w_qkv.T
 
     full = lax.all_to_all(
-        sent.reshape(feats, seq_count, step).transpose(1, 0, 2),
+        sent.reshape(feats + 16, seq_count, step).transpose(1, 0, 2),
         "seq",
         split_axis=0,
         concat_axis=0,
         tiled=True,
     )
-    full = full.reshape(blocks, GROUP // per_peer, feats, step)
+    live_here = full[:, feats, ::WIN]
+    full = full[:, :feats].reshape(blocks, GROUP // per_peer, feats, step)
     full = full.transpose(0, 2, 1, 3).reshape(blocks, feats, GROUP * WIN)
     mid = blocks // 2
 
@@ -364,19 +366,28 @@
             own = [(0, 0, rows), (2, 0, rows), (4, 0, rows), (6, 0, half), (6, half, rows)]
             return own + [(d ^ 1, lo, hi) for d, lo, hi in own]
 
-        by1, by2 = lax.optimization_barrier((tp_xor(mine, 1), tp_xor(mine, 2)))
+        def sides_of_tp(x):
+            return lax.optimization_barrier((tp_xor(x, 1), tp_xor(x, 2)))
+
+        by1, by2 = sides_of_tp(mine)
         others = jnp.concatenate([by1, by2, tp_xor(by2, 1)])
-        vit_sides = sides(others)
-        vit_corners = lax.optimization_barrier(corners(*vit_sides))
-        vit_weights = [wq_t, w_proj] + with_cores([others, *vit_sides, *vit_corners])
-        merge_sides = sides(tie(w_merge, vit_corners))
+        vit_sides = sides(tie(others, full))
+        near = sides_of_tp(full[:mid])
+        vit_sides, near = lax.optimization_barrier((vit_sides, near))
+        far = tp_xor(near[1], 1)
+        far, vit_corners = lax.optimization_barrier((far, corners(*vit_sides)))
+        vit_weights = [wq_t, w_proj] + with_cores([jnp.concatenate([others, *vit_sides, *vit_corners])])
+        merge_sides = sides(tie(w_merge, vit_sides))
         q_rows, p_rows = wq_t.shape[0], w_proj.shape[0]
         vit_parts = []
         for n, (d, lo, hi) in enumerate(parts(others.shape[0])):
+            base = sum(last - first for _, first, last in parts(others.shape[0])[n // 5 * 5 : n])
             for j in range(1, tp):
                 top, end = max(lo, (j - 1) * share), min(hi, j * share)
                 if top < end:
-                    vit_parts.append((2 + n, d, j, top - lo, top - (j - 1) * share, end - top))
+                    vit_parts.append(
+                        (2 + n // 5, d, j, base + top - lo, top - (j - 1) * share, end - top)
+                    )
         vit_count = 2 + len(vit_parts)
 
         def vit_moves(info, refs, w, sem):
@@ -464,18 +475,13 @@
 
     merged = None
     if paired:
-        cuts = [0, mid, blocks]
-        far = None
-        for n, lo in enumerate(cuts[:-1]):
-            own = full[lo : cuts[n + 1]]
-            near = own if far is None else tie(own, (far, vit_weights[2:]))
-            by1, by2 = lax.optimization_barrier((tp_xor(near, 1), tp_xor(near, 2)))
-            if n:
-                merged, by2, live_here = lax.optimization_barrier((merged, by2, live_here))
-            far = tp_xor(by2, 1)
-            if n:
-                far, merge_sides = lax.optimization_barrier((far, merge_sides))
-            merged = encode(lo, [own, by1, by2, far], merged)
+        by1, by2 = near
+        own = tie(full[mid:], (far, vit_weights[2:]))
+        merged = encode(0, [full[:mid], by1, by2, far], None)
+        by1, by2 = sides_of_tp(own)
+        merged, by2 = lax.optimization_barrier((merged, by2))
+        far, merge_sides = lax.optimization_barrier((tp_xor(by2, 1), merge_sides))
+        merged = encode(mid, [full[mid:], by1, by2, far], merged)
         merge_corners = corners(*merge_sides)
         merged, merge_corners = lax.optimization_barrier((merged, merge_corners))
         merge_weights = with_cores([w_merge, *merge_sides, *merge_corners])

time: 345 us -> 284 us (0.82)
  waiting for transfers between devices: 181 us -> 118 us
  local copies, waits for them, and re-layouts: 20.1 us -> 27 us
  Pallas kernels: 89.4 us -> 84 us
    all_to_all x2 -> x1, waiting for transfers between devices: 55.7 us -> 3.14 us  [shards(): lax.all_to_all(sent.reshape(feats + 16, seq_count, step).transpose(1, 0,...]
    ppermute x18 -> x14, waiting for transfers between devices: 42.4 us -> 35.3 us  [xor(): return lax.ppermute(x, 'seq', [(i, i ^ d) for i in range(seq_count)])]
    unnamed x34 -> x36, local copies, waits for them, and re-layouts: 8.79 us -> 14.7 us
    reduce_scatter x1, waiting for transfers between devices: 46.7 us -> 41.5 us  [shards(): lax.psum_scatter(partial_value, 'tp', scatter_dimension=0, tiled=True)]
    pallas_call x1, Pallas kernels: 30.1 us -> 25.1 us  [project(): pl.pallas_call(functools.partial(project_kernel, moves, position, len(wei...]
    ppermute x18 -> x14, starting transfers between devices: 10.5 us -> 13.8 us  [xor(): return lax.ppermute(x, 'seq', [(i, i ^ d) for i in range(seq_count)])]
    all_to_all x2 -> x1, starting transfers between devices: 7.03 us -> 3.73 us  [shards(): lax.all_to_all(sent.reshape(feats + 16, seq_count, step).transpose(1, 0,...]
  transfers between devices with their start and end apart: 30 -> 25, of which waited for: 16 -> 15; matrix products, arithmetic and copies ran while one was open for 6% -> 10% of each run, Pallas kernels for 17% -> 21%
where the time goes in v6:
time: 284 us; the launch traced here: 283 us
  waiting for transfers between devices  118 us (42%)
  Pallas kernels  84 us (30%)
  local copies, waits for them, and re-layouts  27 us (10%)
  starting transfers between devices  26.9 us (9%)
  between operations  13.7 us (5%)
  other arithmetic  10.3 us (4%)
  matrix products  3.45 us (1%)
    pallas_call x2, Pallas kernels, attend(): pl.pallas_call(functools.partial(attend_kernel, tp, moves, len(weights),...  59 us
    reduce_scatter x1, waiting for transfers between devices, shards(): lax.psum_scatter(partial_value, 'tp', scatter_dimension=0, tiled=True)  41.5 us
    ppermute x9, waiting for transfers between devices, tp_xor(): return lax.ppermute(x, 'tp', [(i, i ^ d) for i in range(tp)])  37.9 us
    ppermute x14, waiting for transfers between devices, xor(): return lax.ppermute(x, 'seq', [(i, i ^ d) for i in range(seq_count)])  35.3 us
    pallas_call x1, Pallas kernels, project(): pl.pallas_call(functools.partial(project_kernel, moves, position, len(wei...  25.1 us
    unnamed x36, local copies, waits for them, and re-layouts  14.7 us
    ppermute x14, starting transfers between devices, xor(): return lax.ppermute(x, 'seq', [(i, i ^ d) for i in range(seq_count)])  13.8 us
    ppermute x9, starting transfers between devices, tp_xor(): return lax.ppermute(x, 'tp', [(i, i ^ d) for i in range(tp)])  9.16 us
  transfers between devices with their start and end apart: 25, of which 15 were waited for; matrix products, arithmetic and copies ran while one was open for 10% of the time, Pallas kernels for 21%

profile of v6, /device:TPU:0, one launch (start us, length us, event | category | flops | bytes accessed | tf_op | source)
XLA Modules:
  0.0 283.3 jit_solution(10596253974355167267)
XLA Ops:
  6.5 2.1 bitcast_select_fusion
  8.6 3.0 %collective-permute-start = (bf16[160,1280]{1,0:T(8,128)(2,1)}, bf16[160,1280]{1,0:T(8,128)(2,1)S(1)}, u32[]{:S(2)}, u32[]{:S(2)}) collective-permute-start(bf16[160,1280]{1,0:T(8,128)(2,1)} %bitcast_select_fusion), channel_id=1, source_target_pairs={{0,1},{1,0},{2,3},{3,2},{4,5},{5,4},{6,7},{7,6},{8,9},{9,8},{10,11... | collective-permute-start | bytes 1228808 | tf_op jit(solution)/shard_map/ppermute | solution.py:308
  11.6 2.6 collective-permute-start.1
  14.2 2.3 sort.17
  16.5 1.3 fusion.11
  17.9 1.9 compare_convert_fusion
  19.8 0.7 gather_fusion.1
  20.5 1.4 gather_fusion
  22.3 3.5 %fusion.3 = bf16[320,2048]{1,0:T(8,128)(2,1)S(1)} fusion(bf16[2048,320]{0,1:T(8,128)(2,1)S(1)} %copy-done, s32[2048]{0:T(1024)S(1)} %add.115), kind=kOutput, calls=%fused_computation.6 | convolution fusion | flops 2689204224 | bytes 2629632 | tf_op jit(solution)/shard_map/dot_general | solution.py:326
  25.9 1.2 copy.18
  27.1 3.7 %all-to-all-start = ((bf16[8,336,256]{2,1,0:T(8,128)(2,1)}), bf16[8,336,256]{2,1,0:T(8,128)(2,1)S(1)}, u32[]{:S(2)}, u32[]{:S(2)}) async-start(bf16[8,336,256]{2,1,0:T(8,128)(2,1)} %bitcast.35), calls=%async_computation | async-start | bytes 2752512 | tf_op jit(solution)/shard_map/all_to_all | solution.py:334
  31.1 1.4 collective-permute-done.1
  32.5 0.4 collective-permute-start.2
  32.9 9.9 %collective-permute-done.2 = bf16[160,1280]{1,0:T(8,128)(2,1)S(1)} collective-permute-done((bf16[160,1280]{1,0:T(8,128)(2,1)S(1)}, bf16[160,1280]{1,0:T(8,128)(2,1)S(1)}, u32[]{:S(2)}, u32[]{:S(2)}) %collective-permute-start.2) | collective-permute-done | bytes 409632 | tf_op jit(solution)/shard_map/ppermute | solution.py:308
  42.8 1.2 pad_maximum_fusion.1
  44.0 1.7 collective-permute-start.3
  45.7 1.5 collective-permute-start.4
  47.1 3.1 %all-to-all-done = bf16[8,336,256]{2,1,0:T(8,128)(2,1)S(1)} async-done(((bf16[8,336,256]{2,1,0:T(8,128)(2,1)}), bf16[8,336,256]{2,1,0:T(8,128)(2,1)S(1)}, u32[]{:S(2)}, u32[]{:S(2)}) %all-to-all-start) | async-done | bytes 1376288 | tf_op jit(solution)/shard_map/all_to_all | solution.py:334
  50.4 1.0 copy-done.6
  51.4 0.4 collective-permute-start.5
  51.8 0.3 collective-permute-start.6
  52.2 1.8 constant_dynamic-update-slice_fusion.6
  54.0 1.8 constant_dynamic-update-slice_fusion.5
  55.8 21.6 %collective-permute-done.5.refs_1_ = bf16[4,320,256]{2,1,0:T(8,128)(2,1)S(1)} collective-permute-done((bf16[4,320,256]{2,1,0:T(8,128)(2,1)S(1)}, bf16[4,320,256]{2,1,0:T(8,128)(2,1)S(1)}, u32[]{:S(2)}, u32[]{:S(2)}) %collective-permute-start.5) | collective-permute-done | bytes 655392 | tf_op jit(solution)/shard_map/ppermute | solution.py:308
  77.3 2.4 collective-permute-done.6.refs_2_
  79.7 1.1 slice.34
  80.8 1.4 collective-permute-start.8
  82.3 1.1 slice.35
  83.4 2.6 collective-permute-start.9
  86.0 0.8 constant_dynamic-update-slice_fusion.4
  86.7 2.4 constant_dynamic-update-slice_fusion.3
  89.2 2.5 constant_dynamic-update-slice_fusion.2
  91.7 1.5 collective-permute-done.8
  93.2 5.6 %collective-permute-done.9 = bf16[240,1280]{1,0:T(8,128)(2,1)S(1)} collective-permute-done((bf16[240,1280]{1,0:T(8,128)(2,1)S(1)}, bf16[240,1280]{1,0:T(8,128)(2,1)S(1)}, u32[]{:S(2)}, u32[]{:S(2)}) %collective-permute-start.9) | collective-permute-done | bytes 614432 | tf_op jit(solution)/shard_map/ppermute | solution.py:302
  98.8 2.3 collective-permute-done.7.refs_3_
  101.1 0.8 copy-done.3
  101.9 0.9 constant_dynamic-update-slice_fusion.1
  102.8 0.9 constant_dynamic-update-slice_fusion.refs_6_
  103.7 0.4 collective-permute-start.14
  104.0 1.7 collective-permute-start.15
  105.8 0.2 broadcast_in_dim.47.refs_8_
  106.1 6.1 %collective-permute-done.10.refs_7_ = bf16[1920,1280]{1,0:T(8,128)(2,1)} collective-permute-done((bf16[1920,1280]{1,0:T(8,128)(2,1)}, bf16[1920,1280]{1,0:T(8,128)(2,1)}, u32[]{:S(2)}, u32[]{:S(2)}) %collective-permute-start.10) | collective-permute-done | bytes 4915232 | tf_op jit(solution)/shard_map/ppermute | solution.py:302
  112.2 0.3 collective-permute-start.11
  112.5 0.6 collective-permute-start.12
  113.0 1.1 copy-done.4
  114.1 29.5 %attend.2.refs_10_ = bf16[4,8,64,1280]{3,2,1,0:T(8,128)(2,1)} custom-call(s32[6]{0:T(128)S(1)} %pad_add_fusion.3.info, bf16[4,320,256]{2,1,0:T(8,128)(2,1)S(1)} %get-tuple-element.62.refs_0_, bf16[4,320,256]{2,1,0:T(8,128)(2,1)S(1)} %collective-permute-done.5.refs_1_, bf16[4,320,256]{2,1,0:T(8,128)(2,1)S(1)} %collective-permute-done.6.refs_2_, ...), custom_call_target="tpu_custom_call" | custom-call | flops 16777216000 | bytes 14680064 | tf_op jit(solution)/shard_map/attend/pallas_call | solution.py:148
  143.6 0.3 collective-permute-done.12.refs_2_
  144.0 1.5 collective-permute-start.13
  145.5 17.7 %collective-permute-done.14.refs_2_ = bf16[640,2048]{1,0:T(8,128)(2,1)} collective-permute-done((bf16[640,2048]{1,0:T(8,128)(2,1)}, bf16[640,2048]{1,0:T(8,128)(2,1)}, u32[]{:S(2)}, u32[]{:S(2)}) %collective-permute-start.14) | collective-permute-done | bytes 2621472 | tf_op jit(solution)/shard_map/ppermute | solution.py:302
  163.4 1.4 slice.36
  164.8 1.4 slice.37
  166.3 0.6 collective-permute-start.20
  166.8 1.7 collective-permute-start.16
  168.5 1.7 collective-permute-start.17
  170.2 29.5 %attend.3 = bf16[4,8,64,1280]{3,2,1,0:T(8,128)(2,1)} custom-call(s32[6]{0:T(128)S(1)} %pad_add_fusion.1.info, bf16[4,320,256]{2,1,0:T(8,128)(2,1)S(1)} %get-tuple-element.47.refs_0_, bf16[4,320,256]{2,1,0:T(8,128)(2,1)S(1)} %collective-permute-done.11.refs_1_, ...), custom_call_target="tpu_custom_call", output_to_operand_aliasing={{}: (11, {})} | custom-call | flops 16777216000 | bytes 14680064 | tf_op jit(solution)/shard_map/attend/pallas_call | solution.py:148
  199.8 0.5 collective-permute-start.22
  200.4 2.4 collective-permute-done.21.refs_9_
  202.8 1.9 collective-permute-done.22.refs_10_
  204.7 1.6 copy-done.14
  206.3 25.1 %project.1 = bf16[512,2176]{1,0:T(8,128)(2,1)} custom-call(s32[2]{0:T(128)S(1)} %pad_add_fusion.info, bf16[4,512,1280]{2,1,0:T(8,128)(2,1)} %bitcast.42, bf16[640,2048]{1,0:T(8,128)(2,1)} %refs_1_.1, bf16[640,2048]{1,0:T(8,128)(2,1)} %collective-permute-done.14.refs_2_, bf16[640,2048]{1,0:T(8,128)(2,1)} %collective-permute-done.15.refs_3_, ...), custom_call_target="tpu_custom_call" | custom-call | flops 15032385536 | bytes 37748736 | tf_op jit(solution)/shard_map/project/pallas_call | solution.py:249
  231.4 1.0 slice.40
  232.7 41.5 %reduce-scatter.2.cloned.1.call-done = bf16[128,2176]{1,0:T(8,128)(2,1)} async-done(((bf16[512,2176]{1,0:T(8,128)(2,1)}), bf16[128,2176]{1,0:T(8,128)(2,1)}) %reduce-scatter.2.cloned.1.call-update) | async-done | bytes 557072 | tf_op jit(solution)/shard_map/reduce_scatter | solution.py:494
  274.2 1.1 convert_element_type.31
  275.5 1.0 fusion.5
  (70 shorter events, 2.0 us)
Async XLA Ops:
  6.5 15.8 %copy-start = (bf16[2048,320]{0,1:T(8,128)(2,1)S(1)}, bf16[2048,320]{0,1:T(8,128)(2,1)}, u32[]{:S(2)}) copy-start(bf16[2048,320]{0,1:T(8,128)(2,1)} %param.13) | copy-start | bytes 3932164
  8.6 22.5 %collective-permute-start = (bf16[160,1280]{1,0:T(8,128)(2,1)}, bf16[160,1280]{1,0:T(8,128)(2,1)S(1)}, u32[]{:S(2)}, u32[]{:S(2)}) collective-permute-start(bf16[160,1280]{1,0:T(8,128)(2,1)} %bitcast_select_fusion), channel_id=1, source_target_pairs={{0,1},{1,0},{2,3},{3,2},{4,5},{5,4},{6,7},{7,6},{8,9},{9,8},{10,11... | collective-permute-start | bytes 1228808 | tf_op jit(solution)/shard_map/ppermute | solution.py:308
  11.6 20.9 %collective-permute-start.1 = (bf16[160,1280]{1,0:T(8,128)(2,1)}, bf16[160,1280]{1,0:T(8,128)(2,1)S(1)}, u32[]{:S(2)}, u32[]{:S(2)}) collective-permute-start(bf16[160,1280]{1,0:T(8,128)(2,1)} %bitcast_select_fusion), channel_id=1, source_target_pairs={{0,2},{1,3},{2,0},{3,1},{4,6},{5,7},{6,4},{7,5},{8,10},{9,11},{10,... | collective-permute-start | bytes 1228808 | tf_op jit(solution)/shard_map/ppermute | solution.py:308
  27.1 23.2 %all-to-all-start = ((bf16[8,336,256]{2,1,0:T(8,128)(2,1)}), bf16[8,336,256]{2,1,0:T(8,128)(2,1)S(1)}, u32[]{:S(2)}, u32[]{:S(2)}) async-start(bf16[8,336,256]{2,1,0:T(8,128)(2,1)} %bitcast.35), calls=%async_computation | async-start | bytes 2752512 | tf_op jit(solution)/shard_map/all_to_all | solution.py:334
  30.9 243.4 %reduce-scatter.2.cloned.1.call-start = ((), (), s32[]{:S(2)}) async-start(), calls=%async_computation.2 | async-start | bytes 2785280 | tf_op jit(solution)/shard_map/reduce_scatter | solution.py:494
  31.1 19.3 %copy-start.7 = (bf16[160,1280]{1,0:T(8,128)(2,1)}, bf16[160,1280]{1,0:T(8,128)(2,1)S(1)}, u32[]{:S(2)}) copy-start(bf16[160,1280]{1,0:T(8,128)(2,1)S(1)} %collective-permute-done) | copy-start | bytes 1228804
  32.5 17.9 %copy-start.8 = (bf16[160,1280]{1,0:T(8,128)(2,1)}, bf16[160,1280]{1,0:T(8,128)(2,1)S(1)}, u32[]{:S(2)}) copy-start(bf16[160,1280]{1,0:T(8,128)(2,1)S(1)} %collective-permute-done.1) | copy-start | bytes 1228804
  32.5 10.3 %collective-permute-start.2 = (bf16[160,1280]{1,0:T(8,128)(2,1)S(1)}, bf16[160,1280]{1,0:T(8,128)(2,1)S(1)}, u32[]{:S(2)}, u32[]{:S(2)}) collective-permute-start(bf16[160,1280]{1,0:T(8,128)(2,1)S(1)} %collective-permute-done.1), channel_id=1, source_target_pairs={{0,1},{1,0},{2,3},{3,2},{4,5},{5,4},{6,7},{7,6},{8,9},{9,8},{10,11... | collective-permute-start | bytes 1228808 | tf_op jit(solution)/shard_map/ppermute | solution.py:308
  42.8 4.3 %copy-start.9 = (bf16[160,1280]{1,0:T(8,128)(2,1)}, bf16[160,1280]{1,0:T(8,128)(2,1)S(1)}, u32[]{:S(2)}) copy-start(bf16[160,1280]{1,0:T(8,128)(2,1)S(1)} %collective-permute-done.2) | copy-start | bytes 1228804
  44.0 35.7 %collective-permute-start.3 = (bf16[480,1280]{1,0:T(8,128)(2,1)}, bf16[480,1280]{1,0:T(8,128)(2,1)}, u32[]{:S(2)}, u32[]{:S(2)}) collective-permute-start(bf16[480,1280]{1,0:T(8,128)(2,1)} %pad_maximum_fusion.1), channel_id=1, source_target_pairs={{0,8},{4,12},{8,0},{12,4},{16,24},{20,28},{24,16},{28,20},{1,9},{5... | collective-permute-start | bytes 3686408 | tf_op jit(solution)/shard_map/ppermute | solution.py:302
  45.7 34.0 %collective-permute-start.4 = (bf16[480,1280]{1,0:T(8,128)(2,1)}, bf16[480,1280]{1,0:T(8,128)(2,1)}, u32[]{:S(2)}, u32[]{:S(2)}) collective-permute-start(bf16[480,1280]{1,0:T(8,128)(2,1)} %pad_maximum_fusion.1), channel_id=1, source_target_pairs={{0,16},{4,20},{8,24},{12,28},{16,0},{20,4},{24,8},{28,12},{1,17},{... | collective-permute-start | bytes 3686408 | tf_op jit(solution)/shard_map/ppermute | solution.py:302
  50.3 1.1 copy-start.6
  51.4 34.6 %copy-start.10 = (bf16[160,1280]{1,0:T(8,128)(2,1)S(1)}, bf16[160,1280]{1,0:T(8,128)(2,1)}, u32[]{:S(2)}) copy-start(bf16[160,1280]{1,0:T(8,128)(2,1)} %copy-done.9) | copy-start | bytes 1228804
  51.4 26.0 %collective-permute-start.5 = (bf16[4,320,256]{2,1,0:T(8,128)(2,1)S(1)}, bf16[4,320,256]{2,1,0:T(8,128)(2,1)S(1)}, u32[]{:S(2)}, u32[]{:S(2)}) collective-permute-start(bf16[4,320,256]{2,1,0:T(8,128)(2,1)S(1)} %get-tuple-element.62.refs_0_), channel_id=1, source_target_pairs={{0,1},{1,0},{2,3},{3,2},{4,5},{5,4},{6,7},{7,6},{8,9},{9,8},{10,11... | collective-permute-start | bytes 1966088 | tf_op jit(solution)/shard_map/ppermute | solution.py:308
  51.8 27.9 %collective-permute-start.6 = (bf16[4,320,256]{2,1,0:T(8,128)(2,1)S(1)}, bf16[4,320,256]{2,1,0:T(8,128)(2,1)S(1)}, u32[]{:S(2)}, u32[]{:S(2)}) collective-permute-start(bf16[4,320,256]{2,1,0:T(8,128)(2,1)S(1)} %get-tuple-element.62.refs_0_), channel_id=1, source_target_pairs={{0,2},{1,3},{2,0},{3,1},{4,6},{5,7},{6,4},{7,5},{8,10},{9,11},{10,... | collective-permute-start | bytes 1966088 | tf_op jit(solution)/shard_map/ppermute | solution.py:308
  80.8 12.4 %collective-permute-start.8 = (bf16[240,1280]{1,0:T(8,128)(2,1)S(1)}, bf16[240,1280]{1,0:T(8,128)(2,1)S(1)}, u32[]{:S(2)}, u32[]{:S(2)}) collective-permute-start(bf16[240,1280]{1,0:T(8,128)(2,1)S(1)} %slice.34), channel_id=1, source_target_pairs={{0,16},{4,20},{8,24},{12,28},{16,0},{20,4},{24,8},{28,12},{1,17},{... | collective-permute-start | bytes 1843208 | tf_op jit(solution)/shard_map/ppermute | solution.py:302
  83.4 15.4 %collective-permute-start.9 = (bf16[240,1280]{1,0:T(8,128)(2,1)S(1)}, bf16[240,1280]{1,0:T(8,128)(2,1)S(1)}, u32[]{:S(2)}, u32[]{:S(2)}) collective-permute-start(bf16[240,1280]{1,0:T(8,128)(2,1)S(1)} %slice.35), channel_id=1, source_target_pairs={{0,8},{4,12},{8,0},{12,4},{16,24},{20,28},{24,16},{28,20},{1,9},{5... | collective-permute-start | bytes 1843208 | tf_op jit(solution)/shard_map/ppermute | solution.py:302
  86.0 15.1 %collective-permute-start.7 = (bf16[4,320,256]{2,1,0:T(8,128)(2,1)S(1)}, bf16[4,320,256]{2,1,0:T(8,128)(2,1)S(1)}, u32[]{:S(2)}, u32[]{:S(2)}) collective-permute-start(bf16[4,320,256]{2,1,0:T(8,128)(2,1)S(1)} %collective-permute-done.6.refs_2_), channel_id=1, source_target_pairs={{0,1},{1,0},{2,3},{3,2},{4,5},{5,4},{6,7},{7,6},{8,9},{9,8},{10,11... | collective-permute-start | bytes 1966088 | tf_op jit(solution)/shard_map/ppermute | solution.py:308
  89.2 16.6 %copy-start.12 = (f32[1280]{0:T(1024)S(1)}, f32[1280]{0:T(1024)}, u32[]{:S(2)}) copy-start(f32[1280]{0:T(1024)} %param.19) | copy-start | bytes 15364
  89.2 16.8 %copy-start.11 = (f32[1280]{0:T(1024)S(1)}, f32[1280]{0:T(1024)}, u32[]{:S(2)}) copy-start(f32[1280]{0:T(1024)} %param.20) | copy-start | bytes 15364
  89.2 23.8 %copy-start.2 = (bf16[320,1280]{1,0:T(8,128)(2,1)S(1)}, bf16[320,1280]{1,0:T(8,128)(2,1)}, u32[]{:S(2)}) copy-start(bf16[320,1280]{1,0:T(8,128)(2,1)} %refs_5_.3) | copy-start | bytes 2457604
  101.1 0.8 copy-start.3
  103.7 8.5 %collective-permute-start.10 = (bf16[1920,1280]{1,0:T(8,128)(2,1)}, bf16[1920,1280]{1,0:T(8,128)(2,1)}, u32[]{:S(2)}, u32[]{:S(2)}) collective-permute-start(bf16[1920,1280]{1,0:T(8,128)(2,1)} %constant_dynamic-update-slice_fusion.refs_6_), channel_id=1, source_target_pairs={{0,4},{4,0},{8,12},{12,8},{16,20},{20,16},{24,28},{28,24},{1,5},{5... | collective-permute-start | bytes 14745608 | tf_op jit(solution)/shard_map/ppermute | solution.py:302
  103.7 59.6 %collective-permute-start.14 = (bf16[640,2048]{1,0:T(8,128)(2,1)}, bf16[640,2048]{1,0:T(8,128)(2,1)}, u32[]{:S(2)}, u32[]{:S(2)}) collective-permute-start(bf16[640,2048]{1,0:T(8,128)(2,1)} %refs_1_.1), channel_id=1, source_target_pairs={{0,8},{4,12},{8,0},{12,4},{16,24},{20,28},{24,16},{28,20},{1,9},{5... | collective-permute-start | bytes 7864328 | tf_op jit(solution)/shard_map/ppermute | solution.py:302
  104.0 59.3 %collective-permute-start.15 = (bf16[640,2048]{1,0:T(8,128)(2,1)}, bf16[640,2048]{1,0:T(8,128)(2,1)}, u32[]{:S(2)}, u32[]{:S(2)}) collective-permute-start(bf16[640,2048]{1,0:T(8,128)(2,1)} %refs_1_.1), channel_id=1, source_target_pairs={{0,16},{4,20},{8,24},{12,28},{16,0},{20,4},{24,8},{28,12},{1,17},{... | collective-permute-start | bytes 7864328 | tf_op jit(solution)/shard_map/ppermute | solution.py:302
  112.2 31.4 %collective-permute-start.11 = (bf16[4,320,256]{2,1,0:T(8,128)(2,1)S(1)}, bf16[4,320,256]{2,1,0:T(8,128)(2,1)S(1)}, u32[]{:S(2)}, u32[]{:S(2)}) collective-permute-start(bf16[4,320,256]{2,1,0:T(8,128)(2,1)S(1)} %get-tuple-element.47.refs_0_), channel_id=1, source_target_pairs={{0,1},{1,0},{2,3},{3,2},{4,5},{5,4},{6,7},{7,6},{8,9},{9,8},{10,11... | collective-permute-start | bytes 1966088 | tf_op jit(solution)/shard_map/ppermute | solution.py:308
  112.5 31.5 %collective-permute-start.12 = (bf16[4,320,256]{2,1,0:T(8,128)(2,1)S(1)}, bf16[4,320,256]{2,1,0:T(8,128)(2,1)S(1)}, u32[]{:S(2)}, u32[]{:S(2)}) collective-permute-start(bf16[4,320,256]{2,1,0:T(8,128)(2,1)S(1)} %get-tuple-element.47.refs_0_), channel_id=1, source_target_pairs={{0,2},{1,3},{2,0},{3,1},{4,6},{5,7},{6,4},{7,5},{8,10},{9,11},{10,... | collective-permute-start | bytes 1966088 | tf_op jit(solution)/shard_map/ppermute | solution.py:308
  113.0 1.1 copy-start.4
  144.0 19.4 %collective-permute-start.13 = (bf16[4,320,256]{2,1,0:T(8,128)(2,1)S(1)}, bf16[4,320,256]{2,1,0:T(8,128)(2,1)S(1)}, u32[]{:S(2)}, u32[]{:S(2)}) collective-permute-start(bf16[4,320,256]{2,1,0:T(8,128)(2,1)S(1)} %collective-permute-done.12.refs_2_), channel_id=1, source_target_pairs={{0,1},{1,0},{2,3},{3,2},{4,5},{5,4},{6,7},{7,6},{8,9},{9,8},{10,11... | collective-permute-start | bytes 1966088 | tf_op jit(solution)/shard_map/ppermute | solution.py:308
  145.4 54.9 %collective-permute-start.18 = (bf16[640,2048]{1,0:T(8,128)(2,1)}, bf16[640,2048]{1,0:T(8,128)(2,1)S(1)}, u32[]{:S(2)}, u32[]{:S(2)}) collective-permute-start(bf16[640,2048]{1,0:T(8,128)(2,1)} %refs_1_.1), channel_id=1, source_target_pairs={{0,4},{4,0},{8,12},{12,8},{16,20},{20,16},{24,28},{28,24},{1,5},{5... | collective-permute-start | bytes 7864328 | tf_op jit(solution)/shard_map/ppermute | solution.py:302
  164.8 39.9 %collective-permute-start.19 = (bf16[640,2048]{1,0:T(8,128)(2,1)}, bf16[640,2048]{1,0:T(8,128)(2,1)S(1)}, u32[]{:S(2)}, u32[]{:S(2)}) collective-permute-start(bf16[640,2048]{1,0:T(8,128)(2,1)} %collective-permute-done.14.refs_2_), channel_id=1, source_target_pairs={{0,4},{4,0},{8,12},{12,8},{16,20},{20,16},{24,28},{28,24},{1,5},{5... | collective-permute-start | bytes 7864328 | tf_op jit(solution)/shard_map/ppermute | solution.py:302
  166.3 40.0 %copy-start.5 = (f32[2048]{0:T(1024)S(1)}, f32[2048]{0:T(1024)}, u32[]{:S(2)}) copy-start(f32[2048]{0:T(1024)} %param.22) | copy-start | bytes 24580
  166.3 38.4 %collective-permute-start.20 = (bf16[640,2048]{1,0:T(8,128)(2,1)}, bf16[640,2048]{1,0:T(8,128)(2,1)}, u32[]{:S(2)}, u32[]{:S(2)}) collective-permute-start(bf16[640,2048]{1,0:T(8,128)(2,1)} %collective-permute-done.15.refs_3_), channel_id=1, source_target_pairs={{0,4},{4,0},{8,12},{12,8},{16,20},{20,16},{24,28},{28,24},{1,5},{5... | collective-permute-start | bytes 7864328 | tf_op jit(solution)/shard_map/ppermute | solution.py:302
  166.8 32.9 %collective-permute-start.16 = (bf16[320,2048]{1,0:T(8,128)(2,1)S(1)}, bf16[320,2048]{1,0:T(8,128)(2,1)S(1)}, u32[]{:S(2)}, u32[]{:S(2)}) collective-permute-start(bf16[320,2048]{1,0:T(8,128)(2,1)S(1)} %slice.36), channel_id=1, source_target_pairs={{0,16},{4,20},{8,24},{12,28},{16,0},{20,4},{24,8},{28,12},{1,17},{... | collective-permute-start | bytes 3932168 | tf_op jit(solution)/shard_map/ppermute | solution.py:302
  168.5 31.2 %collective-permute-start.17 = (bf16[320,2048]{1,0:T(8,128)(2,1)S(1)}, bf16[320,2048]{1,0:T(8,128)(2,1)S(1)}, u32[]{:S(2)}, u32[]{:S(2)}) collective-permute-start(bf16[320,2048]{1,0:T(8,128)(2,1)S(1)} %slice.37), channel_id=1, source_target_pairs={{0,8},{4,12},{8,0},{12,4},{16,24},{20,28},{24,16},{28,20},{1,9},{5... | collective-permute-start | bytes 3932168 | tf_op jit(solution)/shard_map/ppermute | solution.py:302
  199.7 3.1 %collective-permute-start.21 = (bf16[320,2048]{1,0:T(8,128)(2,1)S(1)}, bf16[320,2048]{1,0:T(8,128)(2,1)S(1)}, u32[]{:S(2)}, u32[]{:S(2)}) collective-permute-start(bf16[320,2048]{1,0:T(8,128)(2,1)S(1)} %collective-permute-done.16.refs_4_), channel_id=1, source_target_pairs={{0,4},{4,0},{8,12},{12,8},{16,20},{20,16},{24,28},{28,24},{1,5},{5... | collective-permute-start | bytes 3932168 | tf_op jit(solution)/shard_map/ppermute | solution.py:302
  199.8 4.9 %collective-permute-start.22 = (bf16[320,2048]{1,0:T(8,128)(2,1)S(1)}, bf16[320,2048]{1,0:T(8,128)(2,1)S(1)}, u32[]{:S(2)}, u32[]{:S(2)}) collective-permute-start(bf16[320,2048]{1,0:T(8,128)(2,1)S(1)} %collective-permute-done.17.refs_5_), channel_id=1, source_target_pairs={{0,4},{4,0},{8,12},{12,8},{16,20},{20,16},{24,28},{28,24},{1,5},{5... | collective-permute-start | bytes 3932168 | tf_op jit(solution)/shard_map/ppermute | solution.py:302
  200.4 4.3 %copy-start.13 = (bf16[640,2048]{1,0:T(8,128)(2,1)}, bf16[640,2048]{1,0:T(8,128)(2,1)S(1)}, u32[]{:S(2)}) copy-start(bf16[640,2048]{1,0:T(8,128)(2,1)S(1)} %collective-permute-done.18.refs_6_) | copy-start | bytes 7864324
  204.7 1.6 copy-start.14
  231.3 45.1 %copy-start.1 = (bf16[2048,320]{0,1:T(8,128)(2,1)S(1)}, bf16[2048,320]{0,1:T(8,128)(2,1)}, u32[]{:S(2)}) copy-start(bf16[2048,320]{0,1:T(8,128)(2,1)} %param.13) | copy-start | bytes 3932164
Sparse Core Ops, SparseCore 0:
  231.5 42.6 reduce-scatter.1

commit v7 on v6

--- a/solution.py
+++ b/solution.py
@@ -132,10 +132,10 @@
             out[c, 0, w_at * per : (w_at + 1) * per] = merged[at : at + per, :]
 
 
-def attend(tp, info, pieces, weights, moves, count, vit_gain, merge_gain, blocks, buf):
-    nb, feats, cols = pieces[0].shape
+def attend(tp, info, pieces, weights, moves, count, vit_gain, merge_gain, blocks, buf, skip, nb):
+    _, feats, cols = pieces[0].shape
     per = cols // MERGE
-    x_spec = pl.BlockSpec((1, feats, cols), lambda i, s: (i, 0, 0))
+    x_spec = pl.BlockSpec((1, feats, cols), lambda i, s: (skip + i, 0, 0))
     anywhere = pl.BlockSpec(memory_space=pl.ANY)
     ins = [*pieces, *weights, vit_gain, merge_gain]
     specs = [x_spec] * tp + [anywhere] * len(weights)
@@ -344,51 +344,57 @@
     mid = blocks // 2
 
     if paired:
-        share = (wq_t.shape[0] + w_proj.shape[0]) // seq_count
+        share = w_proj.shape[0]
         q_parts = wq_t.shape[0] // share
-        mine = jnp.where(
-            s < q_parts,
-            lax.dynamic_slice_in_dim(wq_t, jnp.minimum(s, q_parts - 1) * share, share),
-            lax.dynamic_slice_in_dim(w_proj, jnp.maximum(s - q_parts, 0) * share, share),
-        )
-        def sides(x):
-            return lax.optimization_barrier((xor(x, 2), xor(x, 4)))
-
-        def corners(by_x, by_y):
-            half = by_x.shape[0] // 2
-            return xor(by_x[:half], 4), xor(by_y[half:], 2)
-
-        def with_cores(pieces):
-            return list(pieces) + [xor(v, 1) for v in pieces]
-
-        def parts(rows):
-            half = rows // 2
-            own = [(0, 0, rows), (2, 0, rows), (4, 0, rows), (6, 0, half), (6, half, rows)]
-            return own + [(d ^ 1, lo, hi) for d, lo, hi in own]
+
+        def left_part(s):
+            return s & 3
+
+        def right_part(s):
+            return (s & 1) + (s // 4) * 2
+
+        def shard_part(n):
+            first = jnp.minimum(n, q_parts - 1) * share
+            return jnp.where(n < q_parts, lax.dynamic_slice_in_dim(wq_t, first, share), w_proj)
 
         def sides_of_tp(x):
             return lax.optimization_barrier((tp_xor(x, 1), tp_xor(x, 2)))
 
+        wide = DV // 2
+        mine = jnp.concatenate(
+            [shard_part(left_part(s))[:, :wide], shard_part(right_part(s))[:, wide:]], axis=1
+        )
         by1, by2 = sides_of_tp(mine)
-        others = jnp.concatenate([by1, by2, tp_xor(by2, 1)])
-        vit_sides = sides(tie(others, full))
-        near = sides_of_tp(full[:mid])
-        vit_sides, near = lax.optimization_barrier((vit_sides, near))
+        by3 = tp_xor(by2, 1)
+        near = sides_of_tp(tie(full[:mid], by3))
+
+        cut = w_merge.shape[0] // 2
+        upper, lower = w_merge[:cut], w_merge[cut:]
+        first_upper, first_lower = tie((upper, lower), full)
+        first_upper, first_lower = xor(first_upper, 2), xor(first_lower, 4)
+
+        left = jnp.concatenate([b[:, :wide] for b in (by1, by2, by3)])
+        right = jnp.concatenate([b[:, wide:] for b in (by1, by2, by3)])
+        (left, right), (first_upper, first_lower) = lax.optimization_barrier(
+            ((left, right), (first_upper, first_lower))
+        )
+        by_x, by_y, near = lax.optimization_barrier((xor(left, 2), xor(right, 4), near))
         far = tp_xor(near[1], 1)
-        far, vit_corners = lax.optimization_barrier((far, corners(*vit_sides)))
-        vit_weights = [wq_t, w_proj] + with_cores([jnp.concatenate([others, *vit_sides, *vit_corners])])
-        merge_sides = sides(tie(w_merge, vit_sides))
+        upper = jnp.concatenate([upper, first_upper])
+        lower = jnp.concatenate([lower, first_lower])
+        upper, lower = tie((upper, lower), (by_x, by_y))
+        merge_along = xor(upper, 4), xor(lower, 2)
+        stack = jnp.concatenate([left, by_x, right, by_y])
+        vit_weights = [wq_t, w_proj, stack, xor(stack, 1)]
         q_rows, p_rows = wq_t.shape[0], w_proj.shape[0]
-        vit_parts = []
-        for n, (d, lo, hi) in enumerate(parts(others.shape[0])):
-            base = sum(last - first for _, first, last in parts(others.shape[0])[n // 5 * 5 : n])
-            for j in range(1, tp):
-                top, end = max(lo, (j - 1) * share), min(hi, j * share)
-                if top < end:
-                    vit_parts.append(
-                        (2 + n // 5, d, j, base + top - lo, top - (j - 1) * share, end - top)
-                    )
-        vit_count = 2 + len(vit_parts)
+        vit_count = 2 + 8 * (tp - 1)
+        halves = [[(0, 0), (2, 0)], [(0, 1), (4, 1)], [(4, 0), (6, 0)], [(2, 1), (6, 1)]]
+        merge_parts = [
+            (4 * e + n, d ^ e, half, at)
+            for e in range(2)
+            for n, pieces in enumerate(halves)
+            for at, (d, half) in enumerate(pieces)
+        ]
 
         def vit_moves(info, refs, w, sem):
             t, s = info[0], info[1]
@@ -401,21 +407,25 @@
                     refs[1], w.at[pl.ds(pl.multiple_of(3 * DV + t * p_rows, 16), p_rows)], sem.at[1]
                 ),
             ]
-            for at, (n, d, j, source, offset, count) in enumerate(vit_parts):
-                part = s ^ d
-                q = t ^ j
-                row = offset + jnp.where(
-                    part < q_parts,
-                    q * q_rows + part * share,
-                    3 * DV + q * p_rows + (part - q_parts) * share,
-                )
-                copies[j].append(
-                    pltpu.make_async_copy(
-                        refs[n].at[source : source + count],
-                        w.at[pl.ds(pl.multiple_of(row, 16), count)],
-                        sem.at[2 + at],
-                    )
-                )
+            for e in range(2):
+                parts = [left_part(s ^ e), left_part(s ^ e ^ 2), right_part(s ^ e), right_part(s ^ e ^ 4)]
+                for b, part in enumerate(parts):
+                    for j in range(1, tp):
+                        q = t ^ j
+                        row = jnp.where(
+                            part < q_parts, q * q_rows + part * share, 3 * DV + q * p_rows
+                        )
+                        first = (b * (tp - 1) + j - 1) * share
+                        copies[j].append(
+                            pltpu.make_async_copy(
+                                refs[2 + e].at[first : first + share],
+                                w.at[
+                                    pl.ds(pl.multiple_of(row, 16), share),
+                                    b // 2 * wide : (b // 2 + 1) * wide,
+                                ],
+                                sem.at[2 + (e * 4 + b) * (tp - 1) + j - 1],
+                            )
+                        )
             return copies
 
         def merge_moves(info, refs, h, i, slot, sem):
@@ -423,10 +433,10 @@
             wide = slot.shape[1]
             rows = slot.shape[0] // 2
             copies = []
-            for n, (d, lo, hi) in enumerate(parts(rows)):
+            for n, d, half, at in merge_parts:
                 if d // 2 == i:
-                    spot = pl.ds(pl.multiple_of(((s ^ d) & 1) * rows + lo, 16), hi - lo)
-                    part = refs[n].at[:, h * wide : (h + 1) * wide]
+                    spot = pl.ds(pl.multiple_of(((s ^ d) & 1) * rows + half * cut, 16), cut)
+                    part = refs[n].at[at * cut : (at + 1) * cut, h * wide : (h + 1) * wide]
                     copies.append(pltpu.make_async_copy(part, slot.at[spot], sem.at[len(copies)]))
             return copies
 
@@ -465,12 +475,12 @@
         def position(info, i):
             return i
 
-    def encode(first, pieces, buf):
-        count = pieces[0].shape[0]
+    def encode(first, pieces, buf, skip=0, count=None):
+        count = pieces[0].shape[0] if count is None else count
         info = jnp.concatenate([jnp.stack([t, s]), first + jnp.arange(count, dtype=jnp.int32)])
         return attend(
             tp, info, pieces, vit_weights, vit_moves, vit_count,
-            vit_gain[:, None], merge_gain[None, :], blocks, buf,
+            vit_gain[:, None], merge_gain[None, :], blocks, buf, skip, count,
         )
 
     merged = None
@@ -480,11 +490,13 @@
         merged = encode(0, [full[:mid], by1, by2, far], None)
         by1, by2 = sides_of_tp(own)
         merged, by2 = lax.optimization_barrier((merged, by2))
-        far, merge_sides = lax.optimization_barrier((tp_xor(by2, 1), merge_sides))
-        merged = encode(mid, [full[mid:], by1, by2, far], merged)
-        merge_corners = corners(*merge_sides)
-        merged, merge_corners = lax.optimization_barrier((merged, merge_corners))
-        merge_weights = with_cores([w_merge, *merge_sides, *merge_corners])
+        pieces = [full[mid:], by1, by2, tp_xor(by2, 1)]
+        part = mid // 2
+        merged = encode(mid, pieces, merged, 0, part)
+        merged, merge_along = lax.optimization_barrier((merged, merge_along))
+        merge_weights = [upper, lower, *merge_along]
+        merge_weights += [xor(v, 1) for v in merge_weights]
+        merged = encode(mid + part, pieces, merged, part, mid - part)
     else:
         for first in (0, mid):
             merged = encode(first, spread(full[first : first + mid]), merged)

time: 284 us -> 298 us (1.049)
  waiting for transfers between devices: 118 us -> 131 us
  local copies, waits for them, and re-layouts: 27 us -> 23.2 us
    ppermute x9, waiting for transfers between devices: 37.9 us -> 82.1 us  [tp_xor(): return lax.ppermute(x, 'tp', [(i, i ^ d) for i in range(tp)])]
    ppermute x14 -> x11, waiting for transfers between devices: 35.3 us -> 0.03 us  [xor(): return lax.ppermute(x, 'seq', [(i, i ^ d) for i in range(seq_count)])]
    concatenate x1 -> x5, other arithmetic: 1.17 us -> 7.17 us  [the longest x1 1.89 us: shards(): lower = jnp.concatenate([lower, first_lower])]
    unnamed x36 -> x35, local copies, waits for them, and re-layouts: 14.7 us -> 9.95 us
    reduce_scatter x1, waiting for transfers between devices: 41.5 us -> 45 us  [shards(): lax.psum_scatter(partial_value, 'tp', scatter_dimension=0, tiled=True)]
    pallas_call x2 -> x3, Pallas kernels: 59 us -> 62.3 us  [attend(): pl.pallas_call(functools.partial(attend_kernel, tp, moves, len(weights),...]
    ppermute x9, starting transfers between devices: 9.16 us -> 12.5 us  [tp_xor(): return lax.ppermute(x, 'tp', [(i, i ^ d) for i in range(tp)])]
    ppermute x14 -> x11, starting transfers between devices: 13.8 us -> 11 us  [xor(): return lax.ppermute(x, 'seq', [(i, i ^ d) for i in range(seq_count)])]
  transfers between devices with their start and end apart: 25 -> 22, of which waited for: 15 -> 9; matrix products, arithmetic and copies ran while one was open for 10% -> 8% of each run, Pallas kernels for 21% -> 21%
where the time goes in v7:
time: 298 us
  waiting for transfers between devices  131 us (44%)
  Pallas kernels  86.1 us (29%)
  starting transfers between devices  27.3 us (9%)
  local copies, waits for them, and re-layouts  23.2 us (8%)
  between operations  13.7 us (5%)
  other arithmetic  13 us (4%)
  matrix products  3.45 us (1%)
    ppermute x9, waiting for transfers between devices, tp_xor(): return lax.ppermute(x, 'tp', [(i, i ^ d) for i in range(tp)])  82.1 us
    pallas_call x3, Pallas kernels, attend(): pl.pallas_call(functools.partial(attend_kernel, tp, moves, len(weights),...  62.3 us
    reduce_scatter x1, waiting for transfers between devices, shards(): lax.psum_scatter(partial_value, 'tp', scatter_dimension=0, tiled=True)  45 us
    pallas_call x1, Pallas kernels, project(): pl.pallas_call(functools.partial(project_kernel, moves, position, len(wei...  23.8 us
    ppermute x9, starting transfers between devices, tp_xor(): return lax.ppermute(x, 'tp', [(i, i ^ d) for i in range(tp)])  12.5 us
    ppermute x11, starting transfers between devices, xor(): return lax.ppermute(x, 'seq', [(i, i ^ d) for i in range(seq_count)])  11 us
    unnamed x35, local copies, waits for them, and re-layouts  9.95 us
  transfers between devices with their start and end apart: 22, of which 9 were waited for; matrix products, arithmetic and copies ran while one was open for 8% of the time, Pallas kernels for 21%

profile of v7, /device:TPU:0, one launch (start us, length us, event | category | flops | bytes accessed | tf_op | source)
XLA Modules:
  0.0 297.7 jit_solution(4716677865199799471)
XLA Ops:
  6.5 1.6 dynamic-slice_bitcast_fusion.1
  8.3 0.1 slice_select_fusion.1
  8.4 1.0 pad_maximum_fusion.5
  9.4 3.0 %collective-permute-start = (bf16[320,1280]{1,0:T(8,128)(2,1)}, bf16[320,1280]{1,0:T(8,128)(2,1)S(1)}, u32[]{:S(2)}, u32[]{:S(2)}) collective-permute-start(bf16[320,1280]{1,0:T(8,128)(2,1)} %pad_maximum_fusion.5), channel_id=1, source_target_pairs={{0,1},{1,0},{2,3},{3,2},{4,5},{5,4},{6,7},{7,6},{8,9},{9,8},{10,11... | collective-permute-start | bytes 2457608 | tf_op jit(solution)/shard_map/ppermute | solution.py:308
  12.4 2.6 collective-permute-start.1
  15.0 1.7 fusion.10
  16.7 1.5 collective-permute-start.3
  18.2 1.5 collective-permute-start.4
  19.7 1.6 sort.17
  21.3 0.6 fusion.15
  21.9 1.2 compare_convert_fusion
  23.1 0.7 gather_fusion.1
  23.8 0.7 gather_fusion
  24.7 0.1 add.121
  24.8 23.4 %collective-permute-done = bf16[320,1280]{1,0:T(8,128)(2,1)S(1)} collective-permute-done((bf16[320,1280]{1,0:T(8,128)(2,1)}, bf16[320,1280]{1,0:T(8,128)(2,1)S(1)}, u32[]{:S(2)}, u32[]{:S(2)}) %collective-permute-start) | collective-permute-done | bytes 819232 | tf_op jit(solution)/shard_map/ppermute | solution.py:308
  48.3 2.7 collective-permute-done.1
  51.0 0.4 collective-permute-start.2
  51.4 3.5 %fusion.3 = bf16[320,2048]{1,0:T(8,128)(2,1)S(1)} fusion(bf16[2048,320]{0,1:T(8,128)(2,1)S(1)} %copy-done, s32[2048]{0:T(1024)S(1)} %add.121), kind=kOutput, calls=%fused_computation.8 | convolution fusion | flops 2689204224 | bytes 2629632 | tf_op jit(solution)/shard_map/dot_general | solution.py:326
  54.9 0.1 convert_element_type.30
  55.0 0.1 pad_maximum_fusion.2
  55.1 1.2 copy.20
  56.3 3.7 %all-to-all-start = ((bf16[8,336,256]{2,1,0:T(8,128)(2,1)}), bf16[8,336,256]{2,1,0:T(8,128)(2,1)S(1)}, u32[]{:S(2)}, u32[]{:S(2)}) async-start(bf16[8,336,256]{2,1,0:T(8,128)(2,1)} %bitcast.37), calls=%async_computation | async-start | bytes 2752512 | tf_op jit(solution)/shard_map/all_to_all | solution.py:334
  60.1 1.3 fusion.12
  61.4 7.7 %collective-permute-done.2 = bf16[320,1280]{1,0:T(8,128)(2,1)} collective-permute-done((bf16[320,1280]{1,0:T(8,128)(2,1)}, bf16[320,1280]{1,0:T(8,128)(2,1)}, u32[]{:S(2)}, u32[]{:S(2)}) %collective-permute-start.2) | collective-permute-done | bytes 819232 | tf_op jit(solution)/shard_map/ppermute | solution.py:308
  69.0 1.2 fusion.14
  70.2 1.2 pad_maximum_fusion.4
  71.4 1.2 pad_maximum_fusion.3
  72.7 1.5 collective-permute-start.5
  74.1 1.5 collective-permute-start.6
  75.6 3.8 %all-to-all-done = bf16[8,336,256]{2,1,0:T(8,128)(2,1)S(1)} async-done(((bf16[8,336,256]{2,1,0:T(8,128)(2,1)}), bf16[8,336,256]{2,1,0:T(8,128)(2,1)S(1)}, u32[]{:S(2)}, u32[]{:S(2)}) %all-to-all-start) | async-done | bytes 1376288 | tf_op jit(solution)/shard_map/all_to_all | solution.py:334
  79.6 1.0 copy-done.5
  80.6 1.6 collective-permute-start.7
  82.2 1.0 collective-permute-start.8
  83.2 2.4 constant_dynamic-update-slice_fusion.3
  85.6 22.0 %collective-permute-done.7.refs_1_ = bf16[4,320,256]{2,1,0:T(8,128)(2,1)S(1)} collective-permute-done((bf16[4,320,256]{2,1,0:T(8,128)(2,1)S(1)}, bf16[4,320,256]{2,1,0:T(8,128)(2,1)S(1)}, u32[]{:S(2)}, u32[]{:S(2)}) %collective-permute-start.7) | collective-permute-done | bytes 655392 | tf_op jit(solution)/shard_map/ppermute | solution.py:308
  107.7 2.4 collective-permute-done.8.refs_2_
  110.1 2.5 constant_dynamic-update-slice_fusion.2
  112.5 2.5 constant_dynamic-update-slice_fusion.1
  115.0 2.4 constant_dynamic-update-slice_fusion.refs_6_
  117.4 0.2 broadcast_in_dim.49.refs_8_
  117.6 0.5 collective-permute-start.9
  118.2 1.9 pad_maximum_fusion.refs_1_
  120.1 1.9 pad_maximum_fusion.1.refs_2_
  122.0 1.4 collective-permute-start.14
  123.5 2.5 collective-permute-start.15
  126.0 8.9 %collective-permute-done.9.refs_3_ = bf16[4,320,256]{2,1,0:T(8,128)(2,1)S(1)} collective-permute-done((bf16[4,320,256]{2,1,0:T(8,128)(2,1)S(1)}, bf16[4,320,256]{2,1,0:T(8,128)(2,1)S(1)}, u32[]{:S(2)}, u32[]{:S(2)}) %collective-permute-start.9) | collective-permute-done | bytes 655392 | tf_op jit(solution)/shard_map/ppermute | solution.py:308
  134.9 0.4 collective-permute-start.11
  135.3 2.6 collective-permute-start.12
  137.9 29.7 %attend.3.refs_10_ = bf16[4,8,64,1280]{3,2,1,0:T(8,128)(2,1)} custom-call(s32[6]{0:T(128)S(1)} %pad_add_fusion.3.info, bf16[4,320,256]{2,1,0:T(8,128)(2,1)S(1)} %get-tuple-element.39.refs_0_, bf16[4,320,256]{2,1,0:T(8,128)(2,1)S(1)} %collective-permute-done.7.refs_1_, bf16[4,320,256]{2,1,0:T(8,128)(2,1)S(1)} %collective-permute-done.8.refs_2_, ...), custom_call_target="tpu_custom_call" | custom-call | flops 16777216000 | bytes 14680064 | tf_op jit(solution)/shard_map/attend/pallas_call | solution.py:148
  167.6 0.3 collective-permute-start.13
  168.1 0.5 collective-permute-start.17
  168.5 15.0 %collective-permute-done.13.refs_3_ = bf16[4,320,256]{2,1,0:T(8,128)(2,1)S(1)} collective-permute-done((bf16[4,320,256]{2,1,0:T(8,128)(2,1)S(1)}, bf16[4,320,256]{2,1,0:T(8,128)(2,1)S(1)}, u32[]{:S(2)}, u32[]{:S(2)}) %collective-permute-start.13) | collective-permute-done | bytes 655392 | tf_op jit(solution)/shard_map/ppermute | solution.py:308
  183.6 16.3 %attend.4.refs_10_ = bf16[4,8,64,1280]{3,2,1,0:T(8,128)(2,1)} custom-call(s32[4]{0:T(128)S(1)} %pad_add_fusion.4.info, bf16[4,320,256]{2,1,0:T(8,128)(2,1)S(1)} %get-tuple-element.45.refs_0_, bf16[4,320,256]{2,1,0:T(8,128)(2,1)S(1)} %collective-permute-done.11.refs_1_, ...), custom_call_target="tpu_custom_call", output_to_operand_aliasing={{}: (11, {})} | custom-call | flops 8388608000 | bytes 14680064 | tf_op jit(solution)/shard_map/attend/pallas_call | solution.py:148
  200.0 0.5 collective-permute-start.19
  200.7 16.3 %attend.5 = bf16[4,8,64,1280]{3,2,1,0:T(8,128)(2,1)} custom-call(s32[4]{0:T(128)S(1)} %pad_add_fusion.1.info, bf16[4,320,256]{2,1,0:T(8,128)(2,1)S(1)} %get-tuple-element.45.refs_0_, bf16[4,320,256]{2,1,0:T(8,128)(2,1)S(1)} %collective-permute-done.11.refs_1_, ...), custom_call_target="tpu_custom_call", output_to_operand_aliasing={{}: (11, {})} | custom-call | flops 8388608000 | bytes 14680064 | tf_op jit(solution)/shard_map/attend/pallas_call | solution.py:148
  217.1 1.5 copy-done.14
  218.5 23.8 %project.1 = bf16[512,2176]{1,0:T(8,128)(2,1)} custom-call(s32[2]{0:T(128)S(1)} %pad_add_fusion.info, bf16[4,512,1280]{2,1,0:T(8,128)(2,1)} %bitcast.45, bf16[640,2048]{1,0:T(8,128)(2,1)S(1)} %pad_maximum_fusion.refs_1_, bf16[640,2048]{1,0:T(8,128)(2,1)} %copy-done.7, bf16[640,2048]{1,0:T(8,128)(2,1)} %copy-done.13, ...), custom_call_target="tpu_custom_call" | custom-call | flops 15032385536 | bytes 37748736 | tf_op jit(solution)/shard_map/project/pallas_call | solution.py:249
  242.3 1.0 slice.64
  243.3 0.1 reshape_squeeze.3
  243.5 0.1 reshape.183
  243.6 45.0 %reduce-scatter.2.cloned.1.call-done = bf16[128,2176]{1,0:T(8,128)(2,1)} async-done(((bf16[512,2176]{1,0:T(8,128)(2,1)}), bf16[128,2176]{1,0:T(8,128)(2,1)}) %reduce-scatter.2.cloned.1.call-update) | async-done | bytes 557072 | tf_op jit(solution)/shard_map/reduce_scatter | solution.py:506
  288.7 1.1 convert_element_type.31
  289.8 0.1 fusion.8
  289.9 1.0 fusion.5
  (70 shorter events, 1.2 us)
Async XLA Ops:
  6.5 44.9 %copy-start = (bf16[2048,320]{0,1:T(8,128)(2,1)S(1)}, bf16[2048,320]{0,1:T(8,128)(2,1)}, u32[]{:S(2)}) copy-start(bf16[2048,320]{0,1:T(8,128)(2,1)} %param.13) | copy-start | bytes 3932164
  6.5 1.7 copy-start.2
  8.2 6.8 %copy-start.6 = (bf16[640,2048]{1,0:T(8,128)(2,1)S(1)}, bf16[640,2048]{1,0:T(8,128)(2,1)}, u32[]{:S(2)}) copy-start(bf16[640,2048]{1,0:T(8,128)(2,1)} %param.21) | copy-start | bytes 7864324
  9.4 10.3 %copy-start.15 = (s32[32,1]{0,1:T(1,128)S(1)}, s32[32,1]{0,1:T(1,128)}, u32[]{:S(2)}) copy-start(s32[32,1]{0,1:T(1,128)} %param.14) | copy-start | bytes 388
  9.4 11.9 %copy-start.12 = (s32[2]{0:T(128)S(1)}, s32[2]{0:T(128)}, u32[]{:S(2)}) copy-start(s32[2]{0:T(128)} %param.16) | copy-start | bytes 28
  9.4 12.5 %copy-start.4 = (s32[1,32]{1,0:T(1,128)S(1)}, s32[1,32]{1,0:T(1,128)}, u32[]{:S(2)}) copy-start(s32[1,32]{1,0:T(1,128)} %param.15) | copy-start | bytes 388
  9.4 38.9 %collective-permute-start = (bf16[320,1280]{1,0:T(8,128)(2,1)}, bf16[320,1280]{1,0:T(8,128)(2,1)S(1)}, u32[]{:S(2)}, u32[]{:S(2)}) collective-permute-start(bf16[320,1280]{1,0:T(8,128)(2,1)} %pad_maximum_fusion.5), channel_id=1, source_target_pairs={{0,1},{1,0},{2,3},{3,2},{4,5},{5,4},{6,7},{7,6},{8,9},{9,8},{10,11... | collective-permute-start | bytes 2457608 | tf_op jit(solution)/shard_map/ppermute | solution.py:308
  12.4 38.5 %collective-permute-start.1 = (bf16[320,1280]{1,0:T(8,128)(2,1)}, bf16[320,1280]{1,0:T(8,128)(2,1)}, u32[]{:S(2)}, u32[]{:S(2)}) collective-permute-start(bf16[320,1280]{1,0:T(8,128)(2,1)} %pad_maximum_fusion.5), channel_id=1, source_target_pairs={{0,2},{1,3},{2,0},{3,1},{4,6},{5,7},{6,4},{7,5},{8,10},{9,11},{10,... | collective-permute-start | bytes 2457608 | tf_op jit(solution)/shard_map/ppermute | solution.py:308
  16.7 56.0 %collective-permute-start.3 = (bf16[320,2048]{1,0:T(8,128)(2,1)}, bf16[320,2048]{1,0:T(8,128)(2,1)}, u32[]{:S(2)}, u32[]{:S(2)}) collective-permute-start(bf16[320,2048]{1,0:T(8,128)(2,1)} %get-tuple-element.35), channel_id=1, source_target_pairs={{0,8},{4,12},{8,0},{12,4},{16,24},{20,28},{24,16},{28,20},{1,9},{5... | collective-permute-start | bytes 3932168 | tf_op jit(solution)/shard_map/ppermute | solution.py:302
  18.2 54.5 %collective-permute-start.4 = (bf16[320,2048]{1,0:T(8,128)(2,1)}, bf16[320,2048]{1,0:T(8,128)(2,1)}, u32[]{:S(2)}, u32[]{:S(2)}) collective-permute-start(bf16[320,2048]{1,0:T(8,128)(2,1)} %get-tuple-element.36), channel_id=1, source_target_pairs={{0,16},{4,20},{8,24},{12,28},{16,0},{20,4},{24,8},{28,12},{1,17},{... | collective-permute-start | bytes 3932168 | tf_op jit(solution)/shard_map/ppermute | solution.py:302
  48.3 2.7 copy-start.8
  51.0 18.1 %collective-permute-start.2 = (bf16[320,1280]{1,0:T(8,128)(2,1)}, bf16[320,1280]{1,0:T(8,128)(2,1)}, u32[]{:S(2)}, u32[]{:S(2)}) collective-permute-start(bf16[320,1280]{1,0:T(8,128)(2,1)} %collective-permute-done.1), channel_id=1, source_target_pairs={{0,1},{1,0},{2,3},{3,2},{4,5},{5,4},{6,7},{7,6},{8,9},{9,8},{10,11... | collective-permute-start | bytes 2457608 | tf_op jit(solution)/shard_map/ppermute | solution.py:308
  55.1 5.0 %copy-start.9 = (bf16[320,1280]{1,0:T(8,128)(2,1)S(1)}, bf16[320,1280]{1,0:T(8,128)(2,1)}, u32[]{:S(2)}) copy-start(bf16[320,1280]{1,0:T(8,128)(2,1)} %copy-done.8) | copy-start | bytes 2457604
  56.3 23.2 %all-to-all-start = ((bf16[8,336,256]{2,1,0:T(8,128)(2,1)}), bf16[8,336,256]{2,1,0:T(8,128)(2,1)S(1)}, u32[]{:S(2)}, u32[]{:S(2)}) async-start(bf16[8,336,256]{2,1,0:T(8,128)(2,1)} %bitcast.37), calls=%async_computation | async-start | bytes 2752512 | tf_op jit(solution)/shard_map/all_to_all | solution.py:334
  60.0 228.6 %reduce-scatter.2.cloned.1.call-start = ((), (), s32[]{:S(2)}) async-start(), calls=%async_computation.2 | async-start | bytes 2785280 | tf_op jit(solution)/shard_map/reduce_scatter | solution.py:506
  72.7 37.4 %collective-permute-start.5 = (bf16[960,640]{1,0:T(8,128)(2,1)}, bf16[960,640]{1,0:T(8,128)(2,1)}, u32[]{:S(2)}, u32[]{:S(2)}) collective-permute-start(bf16[960,640]{1,0:T(8,128)(2,1)} %pad_maximum_fusion.3), channel_id=1, source_target_pairs={{0,8},{4,12},{8,0},{12,4},{16,24},{20,28},{24,16},{28,20},{1,9},{5... | collective-permute-start | bytes 3686408 | tf_op jit(solution)/shard_map/ppermute | solution.py:302
  74.1 35.9 %collective-permute-start.6 = (bf16[960,640]{1,0:T(8,128)(2,1)}, bf16[960,640]{1,0:T(8,128)(2,1)}, u32[]{:S(2)}, u32[]{:S(2)}) collective-permute-start(bf16[960,640]{1,0:T(8,128)(2,1)} %pad_maximum_fusion.4), channel_id=1, source_target_pairs={{0,16},{4,20},{8,24},{12,28},{16,0},{20,4},{24,8},{28,12},{1,17},{... | collective-permute-start | bytes 3686408 | tf_op jit(solution)/shard_map/ppermute | solution.py:302
  79.5 1.1 copy-start.5
  80.6 27.1 %collective-permute-start.7 = (bf16[4,320,256]{2,1,0:T(8,128)(2,1)S(1)}, bf16[4,320,256]{2,1,0:T(8,128)(2,1)S(1)}, u32[]{:S(2)}, u32[]{:S(2)}) collective-permute-start(bf16[4,320,256]{2,1,0:T(8,128)(2,1)S(1)} %get-tuple-element.39.refs_0_), channel_id=1, source_target_pairs={{0,1},{1,0},{2,3},{3,2},{4,5},{5,4},{6,7},{7,6},{8,9},{9,8},{10,11... | collective-permute-start | bytes 1966088 | tf_op jit(solution)/shard_map/ppermute | solution.py:308
  82.2 27.9 %collective-permute-start.8 = (bf16[4,320,256]{2,1,0:T(8,128)(2,1)S(1)}, bf16[4,320,256]{2,1,0:T(8,128)(2,1)S(1)}, u32[]{:S(2)}, u32[]{:S(2)}) collective-permute-start(bf16[4,320,256]{2,1,0:T(8,128)(2,1)S(1)} %get-tuple-element.39.refs_0_), channel_id=1, source_target_pairs={{0,2},{1,3},{2,0},{3,1},{4,6},{5,7},{6,4},{7,5},{8,10},{9,11},{10,... | collective-permute-start | bytes 1966088 | tf_op jit(solution)/shard_map/ppermute | solution.py:308
  112.5 4.9 %copy-start.11 = (f32[1280]{0:T(1024)S(1)}, f32[1280]{0:T(1024)}, u32[]{:S(2)}) copy-start(f32[1280]{0:T(1024)} %param.19) | copy-start | bytes 15364
  112.5 5.1 %copy-start.10 = (f32[1280]{0:T(1024)S(1)}, f32[1280]{0:T(1024)}, u32[]{:S(2)}) copy-start(f32[1280]{0:T(1024)} %param.20) | copy-start | bytes 15364
  117.4 17.5 %collective-permute-start.10 = (bf16[3840,640]{1,0:T(8,128)(2,1)}, bf16[3840,640]{1,0:T(8,128)(2,1)}, u32[]{:S(2)}, u32[]{:S(2)}) collective-permute-start(bf16[3840,640]{1,0:T(8,128)(2,1)} %constant_dynamic-update-slice_fusion.refs_6_), channel_id=1, source_target_pairs={{0,4},{4,0},{8,12},{12,8},{16,20},{20,16},{24,28},{28,24},{1,5},{5... | collective-permute-start | bytes 14745608 | tf_op jit(solution)/shard_map/ppermute | solution.py:302
  117.6 17.2 %collective-permute-start.9 = (bf16[4,320,256]{2,1,0:T(8,128)(2,1)S(1)}, bf16[4,320,256]{2,1,0:T(8,128)(2,1)S(1)}, u32[]{:S(2)}, u32[]{:S(2)}) collective-permute-start(bf16[4,320,256]{2,1,0:T(8,128)(2,1)S(1)} %collective-permute-done.8.refs_2_), channel_id=1, source_target_pairs={{0,1},{1,0},{2,3},{3,2},{4,5},{5,4},{6,7},{7,6},{8,9},{9,8},{10,11... | collective-permute-start | bytes 1966088 | tf_op jit(solution)/shard_map/ppermute | solution.py:308
  122.0 46.0 %copy-start.7 = (bf16[640,2048]{1,0:T(8,128)(2,1)}, bf16[640,2048]{1,0:T(8,128)(2,1)S(1)}, u32[]{:S(2)}) copy-start(bf16[640,2048]{1,0:T(8,128)(2,1)S(1)} %pad_maximum_fusion.1.refs_2_) | copy-start | bytes 7864324
  122.0 77.9 %collective-permute-start.14 = (bf16[640,2048]{1,0:T(8,128)(2,1)S(1)}, bf16[640,2048]{1,0:T(8,128)(2,1)S(1)}, u32[]{:S(2)}, u32[]{:S(2)}) collective-permute-start(bf16[640,2048]{1,0:T(8,128)(2,1)S(1)} %pad_maximum_fusion.refs_1_), channel_id=1, source_target_pairs={{0,16},{4,20},{8,24},{12,28},{16,0},{20,4},{24,8},{28,12},{1,17},{... | collective-permute-start | bytes 7864328 | tf_op jit(solution)/shard_map/ppermute | solution.py:302
  123.5 76.5 %collective-permute-start.15 = (bf16[640,2048]{1,0:T(8,128)(2,1)S(1)}, bf16[640,2048]{1,0:T(8,128)(2,1)}, u32[]{:S(2)}, u32[]{:S(2)}) collective-permute-start(bf16[640,2048]{1,0:T(8,128)(2,1)S(1)} %pad_maximum_fusion.1.refs_2_), channel_id=1, source_target_pairs={{0,8},{4,12},{8,0},{12,4},{16,24},{20,28},{24,16},{28,20},{1,9},{5... | collective-permute-start | bytes 7864328 | tf_op jit(solution)/shard_map/ppermute | solution.py:302
  134.9 32.7 %collective-permute-start.11 = (bf16[4,320,256]{2,1,0:T(8,128)(2,1)S(1)}, bf16[4,320,256]{2,1,0:T(8,128)(2,1)S(1)}, u32[]{:S(2)}, u32[]{:S(2)}) collective-permute-start(bf16[4,320,256]{2,1,0:T(8,128)(2,1)S(1)} %get-tuple-element.45.refs_0_), channel_id=1, source_target_pairs={{0,1},{1,0},{2,3},{3,2},{4,5},{5,4},{6,7},{7,6},{8,9},{9,8},{10,11... | collective-permute-start | bytes 1966088 | tf_op jit(solution)/shard_map/ppermute | solution.py:308
  135.3 32.3 %collective-permute-start.12 = (bf16[4,320,256]{2,1,0:T(8,128)(2,1)S(1)}, bf16[4,320,256]{2,1,0:T(8,128)(2,1)S(1)}, u32[]{:S(2)}, u32[]{:S(2)}) collective-permute-start(bf16[4,320,256]{2,1,0:T(8,128)(2,1)S(1)} %get-tuple-element.45.refs_0_), channel_id=1, source_target_pairs={{0,2},{1,3},{2,0},{3,1},{4,6},{5,7},{6,4},{7,5},{8,10},{9,11},{10,... | collective-permute-start | bytes 1966088 | tf_op jit(solution)/shard_map/ppermute | solution.py:308
  167.6 16.0 %collective-permute-start.13 = (bf16[4,320,256]{2,1,0:T(8,128)(2,1)S(1)}, bf16[4,320,256]{2,1,0:T(8,128)(2,1)S(1)}, u32[]{:S(2)}, u32[]{:S(2)}) collective-permute-start(bf16[4,320,256]{2,1,0:T(8,128)(2,1)S(1)} %collective-permute-done.12.refs_2_), channel_id=1, source_target_pairs={{0,1},{1,0},{2,3},{3,2},{4,5},{5,4},{6,7},{7,6},{8,9},{9,8},{10,11... | collective-permute-start | bytes 1966088 | tf_op jit(solution)/shard_map/ppermute | solution.py:308
  168.0 49.0 %collective-permute-start.16 = (bf16[640,2048]{1,0:T(8,128)(2,1)S(1)}, bf16[640,2048]{1,0:T(8,128)(2,1)S(1)}, u32[]{:S(2)}, u32[]{:S(2)}) collective-permute-start(bf16[640,2048]{1,0:T(8,128)(2,1)S(1)} %pad_maximum_fusion.refs_1_), channel_id=1, source_target_pairs={{0,4},{4,0},{8,12},{12,8},{16,20},{20,16},{24,28},{28,24},{1,5},{5... | collective-permute-start | bytes 7864328 | tf_op jit(solution)/shard_map/ppermute | solution.py:302
  168.1 49.0 %collective-permute-start.17 = (bf16[640,2048]{1,0:T(8,128)(2,1)S(1)}, bf16[640,2048]{1,0:T(8,128)(2,1)}, u32[]{:S(2)}, u32[]{:S(2)}) collective-permute-start(bf16[640,2048]{1,0:T(8,128)(2,1)S(1)} %pad_maximum_fusion.1.refs_2_), channel_id=1, source_target_pairs={{0,4},{4,0},{8,12},{12,8},{16,20},{20,16},{24,28},{28,24},{1,5},{5... | collective-permute-start | bytes 7864328 | tf_op jit(solution)/shard_map/ppermute | solution.py:302
  199.9 17.1 %copy-start.13 = (bf16[640,2048]{1,0:T(8,128)(2,1)}, bf16[640,2048]{1,0:T(8,128)(2,1)S(1)}, u32[]{:S(2)}) copy-start(bf16[640,2048]{1,0:T(8,128)(2,1)S(1)} %collective-permute-done.14.refs_3_) | copy-start | bytes 7864324
  199.9 17.1 %collective-permute-start.18 = (bf16[640,2048]{1,0:T(8,128)(2,1)S(1)}, bf16[640,2048]{1,0:T(8,128)(2,1)}, u32[]{:S(2)}, u32[]{:S(2)}) collective-permute-start(bf16[640,2048]{1,0:T(8,128)(2,1)S(1)} %collective-permute-done.14.refs_3_), channel_id=1, source_target_pairs={{0,4},{4,0},{8,12},{12,8},{16,20},{20,16},{24,28},{28,24},{1,5},{5... | collective-permute-start | bytes 7864328 | tf_op jit(solution)/shard_map/ppermute | solution.py:302
  200.0 18.5 %collective-permute-start.19 = (bf16[640,2048]{1,0:T(8,128)(2,1)}, bf16[640,2048]{1,0:T(8,128)(2,1)}, u32[]{:S(2)}, u32[]{:S(2)}) collective-permute-start(bf16[640,2048]{1,0:T(8,128)(2,1)} %collective-permute-done.15.refs_4_), channel_id=1, source_target_pairs={{0,4},{4,0},{8,12},{12,8},{16,20},{20,16},{24,28},{28,24},{1,5},{5... | collective-permute-start | bytes 7864328 | tf_op jit(solution)/shard_map/ppermute | solution.py:302
  200.7 17.9 %copy-start.3 = (f32[2048]{0:T(1024)S(1)}, f32[2048]{0:T(1024)}, u32[]{:S(2)}) copy-start(f32[2048]{0:T(1024)} %param.22) | copy-start | bytes 24580
  217.0 1.5 copy-start.14
  242.3 48.6 %copy-start.1 = (bf16[2048,320]{0,1:T(8,128)(2,1)S(1)}, bf16[2048,320]{0,1:T(8,128)(2,1)}, u32[]{:S(2)}) copy-start(bf16[2048,320]{0,1:T(8,128)(2,1)} %param.13) | copy-start | bytes 3932164
Sparse Core Ops, SparseCore 0:
  242.4 46.1 reduce-scatter.1

commit v8 on v6

--- a/solution.py
+++ b/solution.py
@@ -375,19 +375,21 @@
         near = sides_of_tp(full[:mid])
         vit_sides, near = lax.optimization_barrier((vit_sides, near))
         far = tp_xor(near[1], 1)
-        far, vit_corners = lax.optimization_barrier((far, corners(*vit_sides)))
-        vit_weights = [wq_t, w_proj] + with_cores([jnp.concatenate([others, *vit_sides, *vit_corners])])
+        straight = jnp.concatenate([others, *vit_sides])
+        swapped = xor(straight, 1)
+        far, vit_corners, swapped = lax.optimization_barrier((far, corners(*vit_sides), swapped))
+        diagonal = jnp.concatenate(vit_corners)
+        vit_weights = [wq_t, w_proj, straight, swapped, diagonal, xor(diagonal, 1)]
         merge_sides = sides(tie(w_merge, vit_sides))
         q_rows, p_rows = wq_t.shape[0], w_proj.shape[0]
         vit_parts = []
         for n, (d, lo, hi) in enumerate(parts(others.shape[0])):
-            base = sum(last - first for _, first, last in parts(others.shape[0])[n // 5 * 5 : n])
+            at, piece = 2 + n // 5 + 2 * (n % 5 // 3), n % 5 - n % 5 // 3 * 3
             for j in range(1, tp):
                 top, end = max(lo, (j - 1) * share), min(hi, j * share)
                 if top < end:
-                    vit_parts.append(
-                        (2 + n // 5, d, j, base + top - lo, top - (j - 1) * share, end - top)
-                    )
+                    first = piece * (hi - lo) + top - lo
+                    vit_parts.append((at, d, j, first, top - (j - 1) * share, end - top))
         vit_count = 2 + len(vit_parts)
 
         def vit_moves(info, refs, w, sem):

time: 284 us -> 286 us (level)
  waiting for transfers between devices: 118 us -> 122 us
  local copies, waits for them, and re-layouts: 27 us -> 23.8 us
    unnamed x36 -> x43, local copies, waits for them, and re-layouts: 14.7 us -> 10.4 us
    ppermute x14 -> x15, waiting for transfers between devices: 35.3 us -> 38.4 us  [xor(): return lax.ppermute(x, 'seq', [(i, i ^ d) for i in range(seq_count)])]
    ppermute x14 -> x15, starting transfers between devices: 13.8 us -> 13.7 us  [xor(): return lax.ppermute(x, 'seq', [(i, i ^ d) for i in range(seq_count)])]
  transfers between devices with their start and end apart: 25 -> 26, of which waited for: 15 -> 13; matrix products, arithmetic and copies ran while one was open for 10% -> 8% of each run, Pallas kernels for 21% -> 21%
where the time goes in v8:
time: 286 us
  waiting for transfers between devices  122 us (43%)
  Pallas kernels  83.9 us (29%)
  starting transfers between devices  28.3 us (10%)
  local copies, waits for them, and re-layouts  23.8 us (8%)
  between operations  13.8 us (5%)
  other arithmetic  10.2 us (4%)
  matrix products  3.46 us (1%)
    pallas_call x2, Pallas kernels, attend(): pl.pallas_call(functools.partial(attend_kernel, tp, moves, len(weights),...  58.9 us
    reduce_scatter x1, waiting for transfers between devices, shards(): lax.psum_scatter(partial_value, 'tp', scatter_dimension=0, tiled=True)  42.9 us
    ppermute x15, waiting for transfers between devices, xor(): return lax.ppermute(x, 'seq', [(i, i ^ d) for i in range(seq_count)])  38.4 us
    ppermute x9, waiting for transfers between devices, tp_xor(): return lax.ppermute(x, 'tp', [(i, i ^ d) for i in range(tp)])  37.9 us
    pallas_call x1, Pallas kernels, project(): pl.pallas_call(functools.partial(project_kernel, moves, position, len(wei...  25.1 us
    ppermute x15, starting transfers between devices, xor(): return lax.ppermute(x, 'seq', [(i, i ^ d) for i in range(seq_count)])  13.7 us
    ppermute x9, starting transfers between devices, tp_xor(): return lax.ppermute(x, 'tp', [(i, i ^ d) for i in range(tp)])  10.7 us
    unnamed x43, local copies, waits for them, and re-layouts  10.4 us
  transfers between devices with their start and end apart: 26, of which 13 were waited for; matrix products, arithmetic and copies ran while one was open for 8% of the time, Pallas kernels for 21%

profile of v8, /device:TPU:0, one launch (start us, length us, event | category | flops | bytes accessed | tf_op | source)
XLA Modules:
  0.0 285.7 jit_solution(14849589123946171824)
XLA Ops:
  6.5 2.1 bitcast_select_fusion
  8.6 3.0 %collective-permute-start = (bf16[160,1280]{1,0:T(8,128)(2,1)}, bf16[160,1280]{1,0:T(8,128)(2,1)S(1)}, u32[]{:S(2)}, u32[]{:S(2)}) collective-permute-start(bf16[160,1280]{1,0:T(8,128)(2,1)} %bitcast_select_fusion), channel_id=1, source_target_pairs={{0,1},{1,0},{2,3},{3,2},{4,5},{5,4},{6,7},{7,6},{8,9},{9,8},{10,11... | collective-permute-start | bytes 1228808 | tf_op jit(solution)/shard_map/ppermute | solution.py:308
  11.6 2.6 collective-permute-start.1
  14.2 2.2 sort.17
  16.5 1.3 fusion.11
  17.8 1.9 compare_convert_fusion
  19.7 0.7 gather_fusion.1
  20.4 1.4 gather_fusion
  22.2 3.5 %fusion.3 = bf16[320,2048]{1,0:T(8,128)(2,1)S(1)} fusion(bf16[2048,320]{0,1:T(8,128)(2,1)S(1)} %copy-done, s32[2048]{0:T(1024)S(1)} %add.115), kind=kOutput, calls=%fused_computation.6 | convolution fusion | flops 2689204224 | bytes 2629632 | tf_op jit(solution)/shard_map/dot_general | solution.py:326
  25.7 0.1 pad_maximum_fusion
  25.9 1.2 copy.18
  27.1 3.7 %all-to-all-start = ((bf16[8,336,256]{2,1,0:T(8,128)(2,1)}), bf16[8,336,256]{2,1,0:T(8,128)(2,1)S(1)}, u32[]{:S(2)}, u32[]{:S(2)}) async-start(bf16[8,336,256]{2,1,0:T(8,128)(2,1)} %bitcast.35), calls=%async_computation | async-start | bytes 2752512 | tf_op jit(solution)/shard_map/all_to_all | solution.py:334
  30.8 0.2 reduce-scatter.2.cloned.1.call-start
  31.0 1.5 collective-permute-done.1
  32.5 0.4 collective-permute-start.2
  32.9 9.8 %collective-permute-done.2 = bf16[160,1280]{1,0:T(8,128)(2,1)S(1)} collective-permute-done((bf16[160,1280]{1,0:T(8,128)(2,1)S(1)}, bf16[160,1280]{1,0:T(8,128)(2,1)S(1)}, u32[]{:S(2)}, u32[]{:S(2)}) %collective-permute-start.2) | collective-permute-done | bytes 409632 | tf_op jit(solution)/shard_map/ppermute | solution.py:308
  42.7 1.2 pad_maximum_fusion.1
  43.9 1.7 collective-permute-start.3
  45.6 1.5 collective-permute-start.4
  47.1 3.1 %all-to-all-done = bf16[8,336,256]{2,1,0:T(8,128)(2,1)S(1)} async-done(((bf16[8,336,256]{2,1,0:T(8,128)(2,1)}), bf16[8,336,256]{2,1,0:T(8,128)(2,1)S(1)}, u32[]{:S(2)}, u32[]{:S(2)}) %all-to-all-start) | async-done | bytes 1376288 | tf_op jit(solution)/shard_map/all_to_all | solution.py:334
  50.3 1.0 copy-done.10
  51.3 0.4 collective-permute-start.5
  51.8 0.3 collective-permute-start.6
  52.2 25.1 %collective-permute-done.5.refs_1_ = bf16[4,320,256]{2,1,0:T(8,128)(2,1)S(1)} collective-permute-done((bf16[4,320,256]{2,1,0:T(8,128)(2,1)S(1)}, bf16[4,320,256]{2,1,0:T(8,128)(2,1)S(1)}, u32[]{:S(2)}, u32[]{:S(2)}) %collective-permute-start.5) | collective-permute-done | bytes 655392 | tf_op jit(solution)/shard_map/ppermute | solution.py:308
  77.3 0.8 copy-done.3
  78.2 1.5 collective-permute-done.6.refs_2_
  79.7 1.6 constant_dynamic-update-slice_fusion.1
  81.3 1.4 constant_dynamic-update-slice_fusion.refs_6_
  82.8 1.6 slice.34
  84.4 1.2 slice.35
  85.6 1.4 collective-permute-start.8
  87.1 2.5 collective-permute-start.9
  89.6 11.8 %collective-permute-done.8 = bf16[240,1280]{1,0:T(8,128)(2,1)S(1)} collective-permute-done((bf16[240,1280]{1,0:T(8,128)(2,1)S(1)}, bf16[240,1280]{1,0:T(8,128)(2,1)S(1)}, u32[]{:S(2)}, u32[]{:S(2)}) %collective-permute-start.8) | collective-permute-done | bytes 614432 | tf_op jit(solution)/shard_map/ppermute | solution.py:302
  101.4 2.0 collective-permute-done.9
  103.5 0.7 copy-done.7
  104.2 1.2 copy-done.16
  105.5 1.7 collective-permute-start.15
  107.2 1.7 collective-permute-start.16
  108.9 0.2 broadcast_in_dim.47.refs_10_
  109.2 1.8 collective-permute-start.12
  111.0 0.3 collective-permute-start.13
  111.3 1.1 copy-done.4
  112.4 1.1 copy-done.6
  113.5 1.1 copy-done.8
  114.6 29.4 %attend.2.refs_12_ = bf16[4,8,64,1280]{3,2,1,0:T(8,128)(2,1)} custom-call(s32[6]{0:T(128)S(1)} %pad_add_fusion.3.info, bf16[4,320,256]{2,1,0:T(8,128)(2,1)S(1)} %get-tuple-element.64.refs_0_, bf16[4,320,256]{2,1,0:T(8,128)(2,1)S(1)} %copy-done.4, bf16[4,320,256]{2,1,0:T(8,128)(2,1)S(1)} %copy-done.6, bf16[4,320,256]{2,1,0:T(8,128)(2,1)S(1)} %copy-done.8, ...), custom_call_target="tpu_custom_call" | custom-call | flops 16777216000 | bytes 14680064 | tf_op jit(solution)/shard_map/attend/pallas_call | solution.py:148
  144.1 1.7 collective-permute-start.14
  145.8 18.0 %collective-permute-done.15.refs_2_ = bf16[640,2048]{1,0:T(8,128)(2,1)} collective-permute-done((bf16[640,2048]{1,0:T(8,128)(2,1)}, bf16[640,2048]{1,0:T(8,128)(2,1)}, u32[]{:S(2)}, u32[]{:S(2)}) %collective-permute-start.15) | collective-permute-done | bytes 2621472 | tf_op jit(solution)/shard_map/ppermute | solution.py:302
  163.8 1.5 collective-permute-done.16.refs_3_
  165.3 1.4 slice.36
  166.8 1.4 slice.37
  168.2 0.6 collective-permute-start.21
  168.8 1.7 collective-permute-start.17
  170.4 0.3 collective-permute-start.18
  170.7 29.4 %attend.3 = bf16[4,8,64,1280]{3,2,1,0:T(8,128)(2,1)} custom-call(s32[6]{0:T(128)S(1)} %pad_add_fusion.1.info, bf16[4,320,256]{2,1,0:T(8,128)(2,1)S(1)} %get-tuple-element.49.refs_0_, bf16[4,320,256]{2,1,0:T(8,128)(2,1)S(1)} %collective-permute-done.12.refs_1_, ...), custom_call_target="tpu_custom_call", output_to_operand_aliasing={{}: (13, {})} | custom-call | flops 16777216000 | bytes 14680064 | tf_op jit(solution)/shard_map/attend/pallas_call | solution.py:148
  200.2 0.8 collective-permute-done.18.refs_5_
  200.9 0.5 collective-permute-start.23
  201.5 2.4 collective-permute-done.22.refs_9_
  204.0 1.9 collective-permute-done.23.refs_10_
  205.8 1.5 copy-done.18
  207.4 25.1 %project.1 = bf16[512,2176]{1,0:T(8,128)(2,1)} custom-call(s32[2]{0:T(128)S(1)} %pad_add_fusion.info, bf16[4,512,1280]{2,1,0:T(8,128)(2,1)} %bitcast.42, bf16[640,2048]{1,0:T(8,128)(2,1)} %refs_1_.1, bf16[640,2048]{1,0:T(8,128)(2,1)} %collective-permute-done.15.refs_2_, bf16[640,2048]{1,0:T(8,128)(2,1)} %collective-permute-done.16.refs_3_, ...), custom_call_target="tpu_custom_call" | custom-call | flops 15032385536 | bytes 37748736 | tf_op jit(solution)/shard_map/project/pallas_call | solution.py:249
  232.5 1.0 slice.40
  233.8 42.9 %reduce-scatter.2.cloned.1.call-done = bf16[128,2176]{1,0:T(8,128)(2,1)} async-done(((bf16[512,2176]{1,0:T(8,128)(2,1)}), bf16[128,2176]{1,0:T(8,128)(2,1)}) %reduce-scatter.2.cloned.1.call-update) | async-done | bytes 557072 | tf_op jit(solution)/shard_map/reduce_scatter | solution.py:496
  276.6 1.1 convert_element_type.31
  277.9 1.0 fusion.5
  (80 shorter events, 1.8 us)
Async XLA Ops:
  6.5 15.7 %copy-start = (bf16[2048,320]{0,1:T(8,128)(2,1)S(1)}, bf16[2048,320]{0,1:T(8,128)(2,1)}, u32[]{:S(2)}) copy-start(bf16[2048,320]{0,1:T(8,128)(2,1)} %param.13) | copy-start | bytes 3932164
  8.6 22.4 %collective-permute-start = (bf16[160,1280]{1,0:T(8,128)(2,1)}, bf16[160,1280]{1,0:T(8,128)(2,1)S(1)}, u32[]{:S(2)}, u32[]{:S(2)}) collective-permute-start(bf16[160,1280]{1,0:T(8,128)(2,1)} %bitcast_select_fusion), channel_id=1, source_target_pairs={{0,1},{1,0},{2,3},{3,2},{4,5},{5,4},{6,7},{7,6},{8,9},{9,8},{10,11... | collective-permute-start | bytes 1228808 | tf_op jit(solution)/shard_map/ppermute | solution.py:308
  11.6 20.9 %collective-permute-start.1 = (bf16[160,1280]{1,0:T(8,128)(2,1)}, bf16[160,1280]{1,0:T(8,128)(2,1)S(1)}, u32[]{:S(2)}, u32[]{:S(2)}) collective-permute-start(bf16[160,1280]{1,0:T(8,128)(2,1)} %bitcast_select_fusion), channel_id=1, source_target_pairs={{0,2},{1,3},{2,0},{3,1},{4,6},{5,7},{6,4},{7,5},{8,10},{9,11},{10,... | collective-permute-start | bytes 1228808 | tf_op jit(solution)/shard_map/ppermute | solution.py:308
  27.1 23.2 %all-to-all-start = ((bf16[8,336,256]{2,1,0:T(8,128)(2,1)}), bf16[8,336,256]{2,1,0:T(8,128)(2,1)S(1)}, u32[]{:S(2)}, u32[]{:S(2)}) async-start(bf16[8,336,256]{2,1,0:T(8,128)(2,1)} %bitcast.35), calls=%async_computation | async-start | bytes 2752512 | tf_op jit(solution)/shard_map/all_to_all | solution.py:334
  30.8 245.9 %reduce-scatter.2.cloned.1.call-start = ((), (), s32[]{:S(2)}) async-start(), calls=%async_computation.2 | async-start | bytes 2785280 | tf_op jit(solution)/shard_map/reduce_scatter | solution.py:496
  32.5 10.2 %collective-permute-start.2 = (bf16[160,1280]{1,0:T(8,128)(2,1)S(1)}, bf16[160,1280]{1,0:T(8,128)(2,1)S(1)}, u32[]{:S(2)}, u32[]{:S(2)}) collective-permute-start(bf16[160,1280]{1,0:T(8,128)(2,1)S(1)} %collective-permute-done.1), channel_id=1, source_target_pairs={{0,1},{1,0},{2,3},{3,2},{4,5},{5,4},{6,7},{7,6},{8,9},{9,8},{10,11... | collective-permute-start | bytes 1228808 | tf_op jit(solution)/shard_map/ppermute | solution.py:308
  42.7 2.9 %copy-start.11 = (bf16[160,1280]{1,0:T(8,128)(2,1)}, bf16[160,1280]{1,0:T(8,128)(2,1)S(1)}, u32[]{:S(2)}) copy-start(bf16[160,1280]{1,0:T(8,128)(2,1)S(1)} %collective-permute-done.2) | copy-start | bytes 1228804
  43.9 35.7 %collective-permute-start.3 = (bf16[480,1280]{1,0:T(8,128)(2,1)}, bf16[480,1280]{1,0:T(8,128)(2,1)}, u32[]{:S(2)}, u32[]{:S(2)}) collective-permute-start(bf16[480,1280]{1,0:T(8,128)(2,1)} %pad_maximum_fusion.1), channel_id=1, source_target_pairs={{0,8},{4,12},{8,0},{12,4},{16,24},{20,28},{24,16},{28,20},{1,9},{5... | collective-permute-start | bytes 3686408 | tf_op jit(solution)/shard_map/ppermute | solution.py:302
  45.6 34.0 %collective-permute-start.4 = (bf16[480,1280]{1,0:T(8,128)(2,1)}, bf16[480,1280]{1,0:T(8,128)(2,1)}, u32[]{:S(2)}, u32[]{:S(2)}) collective-permute-start(bf16[480,1280]{1,0:T(8,128)(2,1)} %pad_maximum_fusion.1), channel_id=1, source_target_pairs={{0,16},{4,20},{8,24},{12,28},{16,0},{20,4},{24,8},{28,12},{1,17},{... | collective-permute-start | bytes 3686408 | tf_op jit(solution)/shard_map/ppermute | solution.py:302
  50.2 1.1 copy-start.10
  50.2 2.0 copy-start.12
  51.3 26.0 %collective-permute-start.5 = (bf16[4,320,256]{2,1,0:T(8,128)(2,1)S(1)}, bf16[4,320,256]{2,1,0:T(8,128)(2,1)S(1)}, u32[]{:S(2)}, u32[]{:S(2)}) collective-permute-start(bf16[4,320,256]{2,1,0:T(8,128)(2,1)S(1)} %get-tuple-element.64.refs_0_), channel_id=1, source_target_pairs={{0,1},{1,0},{2,3},{3,2},{4,5},{5,4},{6,7},{7,6},{8,9},{9,8},{10,11... | collective-permute-start | bytes 1966088 | tf_op jit(solution)/shard_map/ppermute | solution.py:308
  51.8 27.9 %collective-permute-start.6 = (bf16[4,320,256]{2,1,0:T(8,128)(2,1)S(1)}, bf16[4,320,256]{2,1,0:T(8,128)(2,1)S(1)}, u32[]{:S(2)}, u32[]{:S(2)}) collective-permute-start(bf16[4,320,256]{2,1,0:T(8,128)(2,1)S(1)} %get-tuple-element.64.refs_0_), channel_id=1, source_target_pairs={{0,2},{1,3},{2,0},{3,1},{4,6},{5,7},{6,4},{7,5},{8,10},{9,11},{10,... | collective-permute-start | bytes 1966088 | tf_op jit(solution)/shard_map/ppermute | solution.py:308
  77.3 0.8 copy-start.3
  79.7 4.7 %copy-start.5 = (bf16[4,320,256]{2,1,0:T(8,128)(2,1)}, bf16[4,320,256]{2,1,0:T(8,128)(2,1)S(1)}, u32[]{:S(2)}) copy-start(bf16[4,320,256]{2,1,0:T(8,128)(2,1)S(1)} %collective-permute-done.6.refs_2_) | copy-start | bytes 1966084
  82.6 20.9 %copy-start.13 = (bf16[1440,1280]{1,0:T(8,128)(2,1)}, bf16[1440,1280]{1,0:T(8,128)(2,1)S(1)}, u32[]{:S(2)}) copy-start(bf16[1440,1280]{1,0:T(8,128)(2,1)S(1)} %constant_dynamic-update-slice_fusion.refs_6_) | copy-start | bytes 11059204
  82.7 26.2 %copy-start.15 = (f32[1280]{0:T(1024)S(1)}, f32[1280]{0:T(1024)}, u32[]{:S(2)}) copy-start(f32[1280]{0:T(1024)} %param.19) | copy-start | bytes 15364
  82.7 20.7 %collective-permute-start.10 = (bf16[1440,1280]{1,0:T(8,128)(2,1)S(1)}, bf16[1440,1280]{1,0:T(8,128)(2,1)S(1)}, u32[]{:S(2)}, u32[]{:S(2)}) collective-permute-start(bf16[1440,1280]{1,0:T(8,128)(2,1)S(1)} %constant_dynamic-update-slice_fusion.refs_6_), channel_id=1, source_target_pairs={{0,4},{4,0},{8,12},{12,8},{16,20},{20,16},{24,28},{28,24},{1,5},{5... | collective-permute-start | bytes 11059208 | tf_op jit(solution)/shard_map/ppermute | solution.py:302
  82.7 20.6 %collective-permute-start.7 = (bf16[4,320,256]{2,1,0:T(8,128)(2,1)S(1)}, bf16[4,320,256]{2,1,0:T(8,128)(2,1)S(1)}, u32[]{:S(2)}, u32[]{:S(2)}) collective-permute-start(bf16[4,320,256]{2,1,0:T(8,128)(2,1)S(1)} %collective-permute-done.6.refs_2_), channel_id=1, source_target_pairs={{0,1},{1,0},{2,3},{3,2},{4,5},{5,4},{6,7},{7,6},{8,9},{9,8},{10,11... | collective-permute-start | bytes 1966088 | tf_op jit(solution)/shard_map/ppermute | solution.py:308
  84.4 24.7 %copy-start.14 = (f32[1280]{0:T(1024)S(1)}, f32[1280]{0:T(1024)}, u32[]{:S(2)}) copy-start(f32[1280]{0:T(1024)} %param.20) | copy-start | bytes 15364
  84.4 26.9 %copy-start.2 = (bf16[320,1280]{1,0:T(8,128)(2,1)S(1)}, bf16[320,1280]{1,0:T(8,128)(2,1)}, u32[]{:S(2)}) copy-start(bf16[320,1280]{1,0:T(8,128)(2,1)} %refs_5_.3) | copy-start | bytes 2457604
  85.6 15.8 %collective-permute-start.8 = (bf16[240,1280]{1,0:T(8,128)(2,1)S(1)}, bf16[240,1280]{1,0:T(8,128)(2,1)S(1)}, u32[]{:S(2)}, u32[]{:S(2)}) collective-permute-start(bf16[240,1280]{1,0:T(8,128)(2,1)S(1)} %slice.34), channel_id=1, source_target_pairs={{0,16},{4,20},{8,24},{12,28},{16,0},{20,4},{24,8},{28,12},{1,17},{... | collective-permute-start | bytes 1843208 | tf_op jit(solution)/shard_map/ppermute | solution.py:302
  87.1 16.3 %collective-permute-start.9 = (bf16[240,1280]{1,0:T(8,128)(2,1)S(1)}, bf16[240,1280]{1,0:T(8,128)(2,1)S(1)}, u32[]{:S(2)}, u32[]{:S(2)}) collective-permute-start(bf16[240,1280]{1,0:T(8,128)(2,1)S(1)} %slice.35), channel_id=1, source_target_pairs={{0,8},{4,12},{8,0},{12,4},{16,24},{20,28},{24,16},{28,20},{1,9},{5... | collective-permute-start | bytes 1843208 | tf_op jit(solution)/shard_map/ppermute | solution.py:302
  103.4 0.8 copy-start.7
  103.4 2.1 copy-start.16
  104.2 5.0 %collective-permute-start.11 = (bf16[480,1280]{1,0:T(8,128)(2,1)S(1)}, bf16[480,1280]{1,0:T(8,128)(2,1)}, u32[]{:S(2)}, u32[]{:S(2)}) collective-permute-start(bf16[480,1280]{1,0:T(8,128)(2,1)S(1)} %constant_dynamic-update-slice_fusion.5.refs_8_), channel_id=1, source_target_pairs={{0,4},{4,0},{8,12},{12,8},{16,20},{20,16},{24,28},{28,24},{1,5},{5... | collective-permute-start | bytes 3686408 | tf_op jit(solution)/shard_map/ppermute | solution.py:302
  105.5 58.4 %collective-permute-start.15 = (bf16[640,2048]{1,0:T(8,128)(2,1)}, bf16[640,2048]{1,0:T(8,128)(2,1)}, u32[]{:S(2)}, u32[]{:S(2)}) collective-permute-start(bf16[640,2048]{1,0:T(8,128)(2,1)} %refs_1_.1), channel_id=1, source_target_pairs={{0,8},{4,12},{8,0},{12,4},{16,24},{20,28},{24,16},{28,20},{1,9},{5... | collective-permute-start | bytes 7864328 | tf_op jit(solution)/shard_map/ppermute | solution.py:302
  107.2 58.1 %collective-permute-start.16 = (bf16[640,2048]{1,0:T(8,128)(2,1)}, bf16[640,2048]{1,0:T(8,128)(2,1)}, u32[]{:S(2)}, u32[]{:S(2)}) collective-permute-start(bf16[640,2048]{1,0:T(8,128)(2,1)} %refs_1_.1), channel_id=1, source_target_pairs={{0,16},{4,20},{8,24},{12,28},{16,0},{20,4},{24,8},{28,12},{1,17},{... | collective-permute-start | bytes 7864328 | tf_op jit(solution)/shard_map/ppermute | solution.py:302
  109.2 34.8 %collective-permute-start.12 = (bf16[4,320,256]{2,1,0:T(8,128)(2,1)S(1)}, bf16[4,320,256]{2,1,0:T(8,128)(2,1)S(1)}, u32[]{:S(2)}, u32[]{:S(2)}) collective-permute-start(bf16[4,320,256]{2,1,0:T(8,128)(2,1)S(1)} %get-tuple-element.49.refs_0_), channel_id=1, source_target_pairs={{0,1},{1,0},{2,3},{3,2},{4,5},{5,4},{6,7},{7,6},{8,9},{9,8},{10,11... | collective-permute-start | bytes 1966088 | tf_op jit(solution)/shard_map/ppermute | solution.py:308
  111.0 33.0 %collective-permute-start.13 = (bf16[4,320,256]{2,1,0:T(8,128)(2,1)S(1)}, bf16[4,320,256]{2,1,0:T(8,128)(2,1)S(1)}, u32[]{:S(2)}, u32[]{:S(2)}) collective-permute-start(bf16[4,320,256]{2,1,0:T(8,128)(2,1)S(1)} %get-tuple-element.49.refs_0_), channel_id=1, source_target_pairs={{0,2},{1,3},{2,0},{3,1},{4,6},{5,7},{6,4},{7,5},{8,10},{9,11},{10,... | collective-permute-start | bytes 1966088 | tf_op jit(solution)/shard_map/ppermute | solution.py:308
  111.3 1.1 copy-start.4
  112.4 1.1 copy-start.6
  113.5 1.1 copy-start.8
  144.1 21.2 %collective-permute-start.14 = (bf16[4,320,256]{2,1,0:T(8,128)(2,1)S(1)}, bf16[4,320,256]{2,1,0:T(8,128)(2,1)S(1)}, u32[]{:S(2)}, u32[]{:S(2)}) collective-permute-start(bf16[4,320,256]{2,1,0:T(8,128)(2,1)S(1)} %collective-permute-done.13.refs_2_), channel_id=1, source_target_pairs={{0,1},{1,0},{2,3},{3,2},{4,5},{5,4},{6,7},{7,6},{8,9},{9,8},{10,11... | collective-permute-start | bytes 1966088 | tf_op jit(solution)/shard_map/ppermute | solution.py:308
  145.7 55.8 %collective-permute-start.19 = (bf16[640,2048]{1,0:T(8,128)(2,1)}, bf16[640,2048]{1,0:T(8,128)(2,1)S(1)}, u32[]{:S(2)}, u32[]{:S(2)}) collective-permute-start(bf16[640,2048]{1,0:T(8,128)(2,1)} %refs_1_.1), channel_id=1, source_target_pairs={{0,4},{4,0},{8,12},{12,8},{16,20},{20,16},{24,28},{28,24},{1,5},{5... | collective-permute-start | bytes 7864328 | tf_op jit(solution)/shard_map/ppermute | solution.py:302
  166.7 39.1 %collective-permute-start.20 = (bf16[640,2048]{1,0:T(8,128)(2,1)}, bf16[640,2048]{1,0:T(8,128)(2,1)S(1)}, u32[]{:S(2)}, u32[]{:S(2)}) collective-permute-start(bf16[640,2048]{1,0:T(8,128)(2,1)} %collective-permute-done.15.refs_2_), channel_id=1, source_target_pairs={{0,4},{4,0},{8,12},{12,8},{16,20},{20,16},{24,28},{28,24},{1,5},{5... | collective-permute-start | bytes 7864328 | tf_op jit(solution)/shard_map/ppermute | solution.py:302
  168.2 39.2 %copy-start.9 = (f32[2048]{0:T(1024)S(1)}, f32[2048]{0:T(1024)}, u32[]{:S(2)}) copy-start(f32[2048]{0:T(1024)} %param.22) | copy-start | bytes 24580
  168.2 37.6 %collective-permute-start.21 = (bf16[640,2048]{1,0:T(8,128)(2,1)}, bf16[640,2048]{1,0:T(8,128)(2,1)}, u32[]{:S(2)}, u32[]{:S(2)}) collective-permute-start(bf16[640,2048]{1,0:T(8,128)(2,1)} %collective-permute-done.16.refs_3_), channel_id=1, source_target_pairs={{0,4},{4,0},{8,12},{12,8},{16,20},{20,16},{24,28},{28,24},{1,5},{5... | collective-permute-start | bytes 7864328 | tf_op jit(solution)/shard_map/ppermute | solution.py:302
  168.8 31.4 %collective-permute-start.17 = (bf16[320,2048]{1,0:T(8,128)(2,1)S(1)}, bf16[320,2048]{1,0:T(8,128)(2,1)S(1)}, u32[]{:S(2)}, u32[]{:S(2)}) collective-permute-start(bf16[320,2048]{1,0:T(8,128)(2,1)S(1)} %slice.36), channel_id=1, source_target_pairs={{0,16},{4,20},{8,24},{12,28},{16,0},{20,4},{24,8},{28,12},{1,17},{... | collective-permute-start | bytes 3932168 | tf_op jit(solution)/shard_map/ppermute | solution.py:302
  170.4 30.5 %collective-permute-start.18 = (bf16[320,2048]{1,0:T(8,128)(2,1)S(1)}, bf16[320,2048]{1,0:T(8,128)(2,1)S(1)}, u32[]{:S(2)}, u32[]{:S(2)}) collective-permute-start(bf16[320,2048]{1,0:T(8,128)(2,1)S(1)} %slice.37), channel_id=1, source_target_pairs={{0,8},{4,12},{8,0},{12,4},{16,24},{20,28},{24,16},{28,20},{1,9},{5... | collective-permute-start | bytes 3932168 | tf_op jit(solution)/shard_map/ppermute | solution.py:302
  200.9 3.0 %collective-permute-start.22 = (bf16[320,2048]{1,0:T(8,128)(2,1)S(1)}, bf16[320,2048]{1,0:T(8,128)(2,1)S(1)}, u32[]{:S(2)}, u32[]{:S(2)}) collective-permute-start(bf16[320,2048]{1,0:T(8,128)(2,1)S(1)} %collective-permute-done.17.refs_4_), channel_id=1, source_target_pairs={{0,4},{4,0},{8,12},{12,8},{16,20},{20,16},{24,28},{28,24},{1,5},{5... | collective-permute-start | bytes 3932168 | tf_op jit(solution)/shard_map/ppermute | solution.py:302
  200.9 4.9 %collective-permute-start.23 = (bf16[320,2048]{1,0:T(8,128)(2,1)S(1)}, bf16[320,2048]{1,0:T(8,128)(2,1)S(1)}, u32[]{:S(2)}, u32[]{:S(2)}) collective-permute-start(bf16[320,2048]{1,0:T(8,128)(2,1)S(1)} %collective-permute-done.18.refs_5_), channel_id=1, source_target_pairs={{0,4},{4,0},{8,12},{12,8},{16,20},{20,16},{24,28},{28,24},{1,5},{5... | collective-permute-start | bytes 3932168 | tf_op jit(solution)/shard_map/ppermute | solution.py:302
  201.5 4.3 %copy-start.17 = (bf16[640,2048]{1,0:T(8,128)(2,1)}, bf16[640,2048]{1,0:T(8,128)(2,1)S(1)}, u32[]{:S(2)}) copy-start(bf16[640,2048]{1,0:T(8,128)(2,1)S(1)} %collective-permute-done.19.refs_6_) | copy-start | bytes 7864324
  205.8 1.5 copy-start.18
  232.4 46.4 %copy-start.1 = (bf16[2048,320]{0,1:T(8,128)(2,1)S(1)}, bf16[2048,320]{0,1:T(8,128)(2,1)}, u32[]{:S(2)}) copy-start(bf16[2048,320]{0,1:T(8,128)(2,1)} %param.13) | copy-start | bytes 3932164
Sparse Core Ops, SparseCore 0:
  232.6 44.0 reduce-scatter.1

commit v9 on v6

--- a/solution.py
+++ b/solution.py
@@ -369,7 +369,9 @@
         def sides_of_tp(x):
             return lax.optimization_barrier((tp_xor(x, 1), tp_xor(x, 2)))
 
-        by1, by2 = sides_of_tp(mine)
+        quarter = w_merge.shape[0] // 4
+        early = xor(w_merge[:quarter], 2), xor(w_merge[:quarter], 4)
+        (by1, by2), early = lax.optimization_barrier((sides_of_tp(mine), early))
         others = jnp.concatenate([by1, by2, tp_xor(by2, 1)])
         vit_sides = sides(tie(others, full))
         near = sides_of_tp(full[:mid])
@@ -377,7 +379,7 @@
         far = tp_xor(near[1], 1)
         far, vit_corners = lax.optimization_barrier((far, corners(*vit_sides)))
         vit_weights = [wq_t, w_proj] + with_cores([jnp.concatenate([others, *vit_sides, *vit_corners])])
-        merge_sides = sides(tie(w_merge, vit_sides))
+        merge_sides = sides(tie(w_merge[quarter:], vit_sides))
         q_rows, p_rows = wq_t.shape[0], w_proj.shape[0]
         vit_parts = []
         for n, (d, lo, hi) in enumerate(parts(others.shape[0])):
@@ -482,6 +484,7 @@
         merged, by2 = lax.optimization_barrier((merged, by2))
         far, merge_sides = lax.optimization_barrier((tp_xor(by2, 1), merge_sides))
         merged = encode(mid, [full[mid:], by1, by2, far], merged)
+        merge_sides = [jnp.concatenate(pair) for pair in zip(early, merge_sides)]
         merge_corners = corners(*merge_sides)
         merged, merge_corners = lax.optimization_barrier((merged, merge_corners))
         merge_weights = with_cores([w_merge, *merge_sides, *merge_corners])

time: 284 us -> 282 us (level)
  waiting for transfers between devices: 118 us -> 107 us
  local copies, waits for them, and re-layouts: 27 us -> 32 us
  starting transfers between devices: 26.9 us -> 31.6 us
    ppermute x14 -> x16, waiting for transfers between devices: 35.3 us -> 18 us  [xor(): return lax.ppermute(x, 'seq', [(i, i ^ d) for i in range(seq_count)])]
    slice x0 -> x2, local copies, waits for them, and re-layouts: none -> 5 us  [the longest x1 3.03 us: shards(): merge_sides = sides(tie(w_merge[quarter:], vit_sides))]
    ppermute x9, waiting for transfers between devices: 37.9 us -> 42.8 us  [tp_xor(): return lax.ppermute(x, 'tp', [(i, i ^ d) for i in range(tp)])]
    ppermute x14 -> x16, starting transfers between devices: 13.8 us -> 18.6 us  [xor(): return lax.ppermute(x, 'seq', [(i, i ^ d) for i in range(seq_count)])]
    unnamed x36 -> x38, local copies, waits for them, and re-layouts: 14.7 us -> 16.2 us
  transfers between devices with their start and end apart: 25 -> 27, of which waited for: 15 -> 14; matrix products, arithmetic and copies ran while one was open for 10% -> 13% of each run, Pallas kernels for 21% -> 21%
where the time goes in v9:
time: 282 us
  waiting for transfers between devices  107 us (38%)
  Pallas kernels  84 us (30%)
  local copies, waits for them, and re-layouts  32 us (11%)
  starting transfers between devices  31.6 us (11%)
  between operations  13.7 us (5%)
  other arithmetic  9.64 us (3%)
  matrix products  3.45 us (1%)
    pallas_call x2, Pallas kernels, attend(): pl.pallas_call(functools.partial(attend_kernel, tp, moves, len(weights),...  59 us
    reduce_scatter x1, waiting for transfers between devices, shards(): lax.psum_scatter(partial_value, 'tp', scatter_dimension=0, tiled=True)  43.4 us
    ppermute x9, waiting for transfers between devices, tp_xor(): return lax.ppermute(x, 'tp', [(i, i ^ d) for i in range(tp)])  42.8 us
    pallas_call x1, Pallas kernels, project(): pl.pallas_call(functools.partial(project_kernel, moves, position, len(wei...  25 us
    ppermute x16, starting transfers between devices, xor(): return lax.ppermute(x, 'seq', [(i, i ^ d) for i in range(seq_count)])  18.6 us
    ppermute x16, waiting for transfers between devices, xor(): return lax.ppermute(x, 'seq', [(i, i ^ d) for i in range(seq_count)])  18 us
    unnamed x38, local copies, waits for them, and re-layouts  16.2 us
    ppermute x9, starting transfers between devices, tp_xor(): return lax.ppermute(x, 'tp', [(i, i ^ d) for i in range(tp)])  9.21 us
  transfers between devices with their start and end apart: 27, of which 14 were waited for; matrix products, arithmetic and copies ran while one was open for 13% of the time, Pallas kernels for 21%

profile of v9, /device:TPU:0, one launch (start us, length us, event | category | flops | bytes accessed | tf_op | source)
XLA Modules:
  0.0 281.8 jit_solution(12733386016562476139)
XLA Ops:
  6.5 2.1 bitcast_select_fusion
  8.6 3.0 %collective-permute-start = (bf16[160,1280]{1,0:T(8,128)(2,1)}, bf16[160,1280]{1,0:T(8,128)(2,1)S(1)}, u32[]{:S(2)}, u32[]{:S(2)}) collective-permute-start(bf16[160,1280]{1,0:T(8,128)(2,1)} %bitcast_select_fusion), channel_id=1, source_target_pairs={{0,1},{1,0},{2,3},{3,2},{4,5},{5,4},{6,7},{7,6},{8,9},{9,8},{10,11... | collective-permute-start | bytes 1228808 | tf_op jit(solution)/shard_map/ppermute | solution.py:308
  11.7 2.6 collective-permute-start.1
  14.2 2.0 slice.40
  16.2 1.5 collective-permute-start.2
  17.7 1.5 collective-permute-start.3
  19.2 2.3 sort.17
  21.6 1.4 fusion.11
  23.0 0.7 gather_fusion
  23.7 1.3 compare_convert_fusion
  25.0 0.7 gather_fusion.1
  26.0 3.5 %fusion.3 = bf16[320,2048]{1,0:T(8,128)(2,1)S(1)} fusion(bf16[2048,320]{0,1:T(8,128)(2,1)S(1)} %copy-done, s32[2048]{0:T(1024)S(1)} %add.115), kind=kOutput, calls=%fused_computation.6 | convolution fusion | flops 2689204224 | bytes 2629632 | tf_op jit(solution)/shard_map/dot_general | solution.py:326
  29.7 1.2 copy.18
  30.9 3.6 %all-to-all-start = ((bf16[8,336,256]{2,1,0:T(8,128)(2,1)}), bf16[8,336,256]{2,1,0:T(8,128)(2,1)S(1)}, u32[]{:S(2)}, u32[]{:S(2)}) async-start(bf16[8,336,256]{2,1,0:T(8,128)(2,1)} %bitcast.35), calls=%async_computation | async-start | bytes 2752512 | tf_op jit(solution)/shard_map/all_to_all | solution.py:334
  34.8 0.5 collective-permute-start.4
  35.3 11.1 %collective-permute-done.4 = bf16[160,1280]{1,0:T(8,128)(2,1)S(1)} collective-permute-done((bf16[160,1280]{1,0:T(8,128)(2,1)S(1)}, bf16[160,1280]{1,0:T(8,128)(2,1)S(1)}, u32[]{:S(2)}, u32[]{:S(2)}) %collective-permute-start.4) | collective-permute-done | bytes 409632 | tf_op jit(solution)/shard_map/ppermute | solution.py:308
  46.4 1.2 pad_maximum_fusion.1
  47.5 1.7 collective-permute-start.5
  49.2 1.5 collective-permute-start.6
  50.7 3.1 %all-to-all-done = bf16[8,336,256]{2,1,0:T(8,128)(2,1)S(1)} async-done(((bf16[8,336,256]{2,1,0:T(8,128)(2,1)}), bf16[8,336,256]{2,1,0:T(8,128)(2,1)S(1)}, u32[]{:S(2)}, u32[]{:S(2)}) %all-to-all-start) | async-done | bytes 1376288 | tf_op jit(solution)/shard_map/all_to_all | solution.py:334
  53.9 1.0 copy-done.7
  55.0 0.5 collective-permute-start.7
  55.8 1.8 constant_dynamic-update-slice_fusion.6
  57.6 1.8 constant_dynamic-update-slice_fusion.5
  59.4 21.5 %collective-permute-done.7.refs_1_ = bf16[4,320,256]{2,1,0:T(8,128)(2,1)S(1)} collective-permute-done((bf16[4,320,256]{2,1,0:T(8,128)(2,1)S(1)}, bf16[4,320,256]{2,1,0:T(8,128)(2,1)S(1)}, u32[]{:S(2)}, u32[]{:S(2)}) %collective-permute-start.7) | collective-permute-done | bytes 655392 | tf_op jit(solution)/shard_map/ppermute | solution.py:308
  80.9 2.4 collective-permute-done.8.refs_2_
  83.3 1.1 slice.42
  84.5 1.5 collective-permute-start.10
  86.0 1.1 slice.43
  87.1 2.6 collective-permute-start.11
  89.7 0.8 constant_dynamic-update-slice_fusion.4
  90.4 2.5 constant_dynamic-update-slice_fusion.3
  92.9 2.4 constant_dynamic-update-slice_fusion.2
  95.3 1.6 collective-permute-done.10
  96.9 5.5 %collective-permute-done.11 = bf16[240,1280]{1,0:T(8,128)(2,1)S(1)} collective-permute-done((bf16[240,1280]{1,0:T(8,128)(2,1)S(1)}, bf16[240,1280]{1,0:T(8,128)(2,1)S(1)}, u32[]{:S(2)}, u32[]{:S(2)}) %collective-permute-start.11) | collective-permute-done | bytes 614432 | tf_op jit(solution)/shard_map/ppermute | solution.py:302
  102.4 0.8 copy-done.3
  103.2 0.9 constant_dynamic-update-slice_fusion.1
  104.1 0.9 constant_dynamic-update-slice_fusion.refs_6_
  105.0 0.5 collective-permute-start.20
  105.5 3.0 %slice.44 = bf16[480,2048]{1,0:T(8,128)(2,1)} slice(bf16[640,2048]{1,0:T(8,128)(2,1)} %refs_1_.1), slice={[160:640], [0:2048]} | slice | bytes 3932160 | tf_op jit(solution)/shard_map/slice | solution.py:382
  108.8 1.7 collective-permute-start.16
  110.6 1.7 collective-permute-start.17
  112.3 1.2 collective-permute-done.12.refs_7_
  113.5 1.7 collective-permute-start.13
  115.2 0.5 collective-permute-start.14
  115.8 1.1 copy-done.4
  116.9 29.5 %attend.2.refs_10_ = bf16[4,8,64,1280]{3,2,1,0:T(8,128)(2,1)} custom-call(s32[6]{0:T(128)S(1)} %pad_add_fusion.3.info, bf16[4,320,256]{2,1,0:T(8,128)(2,1)S(1)} %get-tuple-element.70.refs_0_, bf16[4,320,256]{2,1,0:T(8,128)(2,1)S(1)} %collective-permute-done.7.refs_1_, bf16[4,320,256]{2,1,0:T(8,128)(2,1)S(1)} %collective-permute-done.8.refs_2_, ...), custom_call_target="tpu_custom_call" | custom-call | flops 16777216000 | bytes 14680064 | tf_op jit(solution)/shard_map/attend/pallas_call | solution.py:148
  146.8 1.1 constant_dynamic-update-slice_fusion.8
  147.9 2.0 constant_dynamic-update-slice_fusion.10
  149.9 3.9 %collective-permute-done.16 = bf16[480,2048]{1,0:T(8,128)(2,1)S(1)} collective-permute-done((bf16[480,2048]{1,0:T(8,128)(2,1)}, bf16[480,2048]{1,0:T(8,128)(2,1)S(1)}, u32[]{:S(2)}, u32[]{:S(2)}) %collective-permute-start.16) | collective-permute-done | bytes 1966112 | tf_op jit(solution)/shard_map/ppermute | solution.py:302
  153.8 1.5 collective-permute-done.17
  155.3 7.4 %collective-permute-done.15.refs_3_ = bf16[4,320,256]{2,1,0:T(8,128)(2,1)S(1)} collective-permute-done((bf16[4,320,256]{2,1,0:T(8,128)(2,1)S(1)}, bf16[4,320,256]{2,1,0:T(8,128)(2,1)S(1)}, u32[]{:S(2)}, u32[]{:S(2)}) %collective-permute-start.15) | collective-permute-done | bytes 655392 | tf_op jit(solution)/shard_map/ppermute | solution.py:308
  163.1 1.8 collective-permute-start.18
  165.1 1.8 collective-permute-start.19
  166.9 1.4 constant_dynamic-update-slice_fusion.9.refs_3_
  168.3 29.5 %attend.3 = bf16[4,8,64,1280]{3,2,1,0:T(8,128)(2,1)} custom-call(s32[6]{0:T(128)S(1)} %pad_add_fusion.1.info, bf16[4,320,256]{2,1,0:T(8,128)(2,1)S(1)} %get-tuple-element.53.refs_0_, bf16[4,320,256]{2,1,0:T(8,128)(2,1)S(1)} %collective-permute-done.13.refs_1_, ...), custom_call_target="tpu_custom_call", output_to_operand_aliasing={{}: (11, {})} | custom-call | flops 16777216000 | bytes 14680064 | tf_op jit(solution)/shard_map/attend/pallas_call | solution.py:148
  197.8 0.6 collective-permute-start.23
  198.5 2.5 collective-permute-done.23.refs_9_
  201.0 1.9 collective-permute-done.24.refs_10_
  202.9 25.0 %project.1 = bf16[512,2176]{1,0:T(8,128)(2,1)} custom-call(s32[2]{0:T(128)S(1)} %pad_add_fusion.info, bf16[4,512,1280]{2,1,0:T(8,128)(2,1)} %bitcast.42, bf16[640,2048]{1,0:T(8,128)(2,1)} %refs_1_.1, bf16[640,2048]{1,0:T(8,128)(2,1)} %copy-done.12, bf16[640,2048]{1,0:T(8,128)(2,1)} %constant_dynamic-update-slice_fusion.9.refs_3_, ...), custom_call_target="tpu_custom_call" | custom-call | flops 15032385536 | bytes 37748736 | tf_op jit(solution)/shard_map/project/pallas_call | solution.py:249
  228.0 1.0 slice.49
  229.3 43.4 %reduce-scatter.2.cloned.1.call-done = bf16[128,2176]{1,0:T(8,128)(2,1)} async-done(((bf16[512,2176]{1,0:T(8,128)(2,1)}), bf16[128,2176]{1,0:T(8,128)(2,1)}) %reduce-scatter.2.cloned.1.call-update) | async-done | bytes 557072 | tf_op jit(solution)/shard_map/reduce_scatter | solution.py:497
  272.7 1.1 convert_element_type.31
  273.9 1.0 fusion.5
  (80 shorter events, 3.3 us)
Async XLA Ops:
  6.5 19.4 %copy-start = (bf16[2048,320]{0,1:T(8,128)(2,1)S(1)}, bf16[2048,320]{0,1:T(8,128)(2,1)}, u32[]{:S(2)}) copy-start(bf16[2048,320]{0,1:T(8,128)(2,1)} %param.13) | copy-start | bytes 3932164
  6.5 16.4 %copy-start.6 = (s32[1,32]{1,0:T(1,128)S(1)}, s32[1,32]{1,0:T(1,128)}, u32[]{:S(2)}) copy-start(s32[1,32]{1,0:T(1,128)} %param.15) | copy-start | bytes 388
  8.6 26.1 %collective-permute-start = (bf16[160,1280]{1,0:T(8,128)(2,1)}, bf16[160,1280]{1,0:T(8,128)(2,1)S(1)}, u32[]{:S(2)}, u32[]{:S(2)}) collective-permute-start(bf16[160,1280]{1,0:T(8,128)(2,1)} %bitcast_select_fusion), channel_id=1, source_target_pairs={{0,1},{1,0},{2,3},{3,2},{4,5},{5,4},{6,7},{7,6},{8,9},{9,8},{10,11... | collective-permute-start | bytes 1228808 | tf_op jit(solution)/shard_map/ppermute | solution.py:308
  11.7 23.1 %collective-permute-start.1 = (bf16[160,1280]{1,0:T(8,128)(2,1)}, bf16[160,1280]{1,0:T(8,128)(2,1)S(1)}, u32[]{:S(2)}, u32[]{:S(2)}) collective-permute-start(bf16[160,1280]{1,0:T(8,128)(2,1)} %bitcast_select_fusion), channel_id=1, source_target_pairs={{0,2},{1,3},{2,0},{3,1},{4,6},{5,7},{6,4},{7,5},{8,10},{9,11},{10,... | collective-permute-start | bytes 1228808 | tf_op jit(solution)/shard_map/ppermute | solution.py:308
  16.2 18.5 %collective-permute-start.2 = (bf16[160,2048]{1,0:T(8,128)(2,1)}, bf16[160,2048]{1,0:T(8,128)(2,1)}, u32[]{:S(2)}, u32[]{:S(2)}) collective-permute-start(bf16[160,2048]{1,0:T(8,128)(2,1)} %slice.40), channel_id=1, source_target_pairs={{0,8},{4,12},{8,0},{12,4},{16,24},{20,28},{24,16},{28,20},{1,9},{5... | collective-permute-start | bytes 1966088 | tf_op jit(solution)/shard_map/ppermute | solution.py:302
  17.7 17.1 %collective-permute-start.3 = (bf16[160,2048]{1,0:T(8,128)(2,1)}, bf16[160,2048]{1,0:T(8,128)(2,1)}, u32[]{:S(2)}, u32[]{:S(2)}) collective-permute-start(bf16[160,2048]{1,0:T(8,128)(2,1)} %slice.40), channel_id=1, source_target_pairs={{0,16},{4,20},{8,24},{12,28},{16,0},{20,4},{24,8},{28,12},{1,17},{... | collective-permute-start | bytes 1966088 | tf_op jit(solution)/shard_map/ppermute | solution.py:302
  30.9 22.9 %all-to-all-start = ((bf16[8,336,256]{2,1,0:T(8,128)(2,1)}), bf16[8,336,256]{2,1,0:T(8,128)(2,1)S(1)}, u32[]{:S(2)}, u32[]{:S(2)}) async-start(bf16[8,336,256]{2,1,0:T(8,128)(2,1)} %bitcast.35), calls=%async_computation | async-start | bytes 2752512 | tf_op jit(solution)/shard_map/all_to_all | solution.py:334
  34.5 238.2 %reduce-scatter.2.cloned.1.call-start = ((), (), s32[]{:S(2)}) async-start(), calls=%async_computation.2 | async-start | bytes 2785280 | tf_op jit(solution)/shard_map/reduce_scatter | solution.py:497
  34.7 20.3 %copy-start.8 = (bf16[160,1280]{1,0:T(8,128)(2,1)}, bf16[160,1280]{1,0:T(8,128)(2,1)S(1)}, u32[]{:S(2)}) copy-start(bf16[160,1280]{1,0:T(8,128)(2,1)S(1)} %collective-permute-done) | copy-start | bytes 1228804
  34.7 20.2 %copy-start.9 = (bf16[160,1280]{1,0:T(8,128)(2,1)}, bf16[160,1280]{1,0:T(8,128)(2,1)S(1)}, u32[]{:S(2)}) copy-start(bf16[160,1280]{1,0:T(8,128)(2,1)S(1)} %collective-permute-done.1) | copy-start | bytes 1228804
  34.8 11.6 %collective-permute-start.4 = (bf16[160,1280]{1,0:T(8,128)(2,1)S(1)}, bf16[160,1280]{1,0:T(8,128)(2,1)S(1)}, u32[]{:S(2)}, u32[]{:S(2)}) collective-permute-start(bf16[160,1280]{1,0:T(8,128)(2,1)S(1)} %collective-permute-done.1), channel_id=1, source_target_pairs={{0,1},{1,0},{2,3},{3,2},{4,5},{5,4},{6,7},{7,6},{8,9},{9,8},{10,11... | collective-permute-start | bytes 1228808 | tf_op jit(solution)/shard_map/ppermute | solution.py:308
  46.4 4.3 %copy-start.10 = (bf16[160,1280]{1,0:T(8,128)(2,1)}, bf16[160,1280]{1,0:T(8,128)(2,1)S(1)}, u32[]{:S(2)}) copy-start(bf16[160,1280]{1,0:T(8,128)(2,1)S(1)} %collective-permute-done.4) | copy-start | bytes 1228804
  47.5 35.8 %collective-permute-start.5 = (bf16[480,1280]{1,0:T(8,128)(2,1)}, bf16[480,1280]{1,0:T(8,128)(2,1)}, u32[]{:S(2)}, u32[]{:S(2)}) collective-permute-start(bf16[480,1280]{1,0:T(8,128)(2,1)} %pad_maximum_fusion.1), channel_id=1, source_target_pairs={{0,8},{4,12},{8,0},{12,4},{16,24},{20,28},{24,16},{28,20},{1,9},{5... | collective-permute-start | bytes 3686408 | tf_op jit(solution)/shard_map/ppermute | solution.py:302
  49.2 34.1 %collective-permute-start.6 = (bf16[480,1280]{1,0:T(8,128)(2,1)}, bf16[480,1280]{1,0:T(8,128)(2,1)}, u32[]{:S(2)}, u32[]{:S(2)}) collective-permute-start(bf16[480,1280]{1,0:T(8,128)(2,1)} %pad_maximum_fusion.1), channel_id=1, source_target_pairs={{0,16},{4,20},{8,24},{12,28},{16,0},{20,4},{24,8},{28,12},{1,17},{... | collective-permute-start | bytes 3686408 | tf_op jit(solution)/shard_map/ppermute | solution.py:302
  53.8 1.1 copy-start.7
  55.0 34.7 %copy-start.11 = (bf16[160,1280]{1,0:T(8,128)(2,1)S(1)}, bf16[160,1280]{1,0:T(8,128)(2,1)}, u32[]{:S(2)}) copy-start(bf16[160,1280]{1,0:T(8,128)(2,1)} %copy-done.10) | copy-start | bytes 1228804
  55.0 25.9 %collective-permute-start.7 = (bf16[4,320,256]{2,1,0:T(8,128)(2,1)S(1)}, bf16[4,320,256]{2,1,0:T(8,128)(2,1)S(1)}, u32[]{:S(2)}, u32[]{:S(2)}) collective-permute-start(bf16[4,320,256]{2,1,0:T(8,128)(2,1)S(1)} %get-tuple-element.70.refs_0_), channel_id=1, source_target_pairs={{0,1},{1,0},{2,3},{3,2},{4,5},{5,4},{6,7},{7,6},{8,9},{9,8},{10,11... | collective-permute-start | bytes 1966088 | tf_op jit(solution)/shard_map/ppermute | solution.py:308
  55.4 27.9 %collective-permute-start.8 = (bf16[4,320,256]{2,1,0:T(8,128)(2,1)S(1)}, bf16[4,320,256]{2,1,0:T(8,128)(2,1)S(1)}, u32[]{:S(2)}, u32[]{:S(2)}) collective-permute-start(bf16[4,320,256]{2,1,0:T(8,128)(2,1)S(1)} %get-tuple-element.70.refs_0_), channel_id=1, source_target_pairs={{0,2},{1,3},{2,0},{3,1},{4,6},{5,7},{6,4},{7,5},{8,10},{9,11},{10,... | collective-permute-start | bytes 1966088 | tf_op jit(solution)/shard_map/ppermute | solution.py:308
  83.3 19.1 %collective-permute-start.9 = (bf16[4,320,256]{2,1,0:T(8,128)(2,1)S(1)}, bf16[4,320,256]{2,1,0:T(8,128)(2,1)S(1)}, u32[]{:S(2)}, u32[]{:S(2)}) collective-permute-start(bf16[4,320,256]{2,1,0:T(8,128)(2,1)S(1)} %collective-permute-done.8.refs_2_), channel_id=1, source_target_pairs={{0,1},{1,0},{2,3},{3,2},{4,5},{5,4},{6,7},{7,6},{8,9},{9,8},{10,11... | collective-permute-start | bytes 1966088 | tf_op jit(solution)/shard_map/ppermute | solution.py:308
  84.5 12.4 %collective-permute-start.10 = (bf16[240,1280]{1,0:T(8,128)(2,1)S(1)}, bf16[240,1280]{1,0:T(8,128)(2,1)S(1)}, u32[]{:S(2)}, u32[]{:S(2)}) collective-permute-start(bf16[240,1280]{1,0:T(8,128)(2,1)S(1)} %slice.42), channel_id=1, source_target_pairs={{0,16},{4,20},{8,24},{12,28},{16,0},{20,4},{24,8},{28,12},{1,17},{... | collective-permute-start | bytes 1843208 | tf_op jit(solution)/shard_map/ppermute | solution.py:302
  87.1 15.3 %collective-permute-start.11 = (bf16[240,1280]{1,0:T(8,128)(2,1)S(1)}, bf16[240,1280]{1,0:T(8,128)(2,1)S(1)}, u32[]{:S(2)}, u32[]{:S(2)}) collective-permute-start(bf16[240,1280]{1,0:T(8,128)(2,1)S(1)} %slice.43), channel_id=1, source_target_pairs={{0,8},{4,12},{8,0},{12,4},{16,24},{20,28},{24,16},{28,20},{1,9},{5... | collective-permute-start | bytes 1843208 | tf_op jit(solution)/shard_map/ppermute | solution.py:302
  102.4 0.8 copy-start.3
  104.1 4.4 %copy-start.14 = (f32[1280]{0:T(1024)S(1)}, f32[1280]{0:T(1024)}, u32[]{:S(2)}) copy-start(f32[1280]{0:T(1024)} %param.19) | copy-start | bytes 15364
  104.1 4.6 %copy-start.13 = (f32[1280]{0:T(1024)S(1)}, f32[1280]{0:T(1024)}, u32[]{:S(2)}) copy-start(f32[1280]{0:T(1024)} %param.20) | copy-start | bytes 15364
  104.1 11.7 %copy-start.2 = (bf16[320,1280]{1,0:T(8,128)(2,1)S(1)}, bf16[320,1280]{1,0:T(8,128)(2,1)}, u32[]{:S(2)}) copy-start(bf16[320,1280]{1,0:T(8,128)(2,1)} %refs_5_.3) | copy-start | bytes 2457604
  105.0 8.5 %collective-permute-start.12 = (bf16[1920,1280]{1,0:T(8,128)(2,1)}, bf16[1920,1280]{1,0:T(8,128)(2,1)}, u32[]{:S(2)}, u32[]{:S(2)}) collective-permute-start(bf16[1920,1280]{1,0:T(8,128)(2,1)} %constant_dynamic-update-slice_fusion.refs_6_), channel_id=1, source_target_pairs={{0,4},{4,0},{8,12},{12,8},{16,20},{20,16},{24,28},{28,24},{1,5},{5... | collective-permute-start | bytes 14745608 | tf_op jit(solution)/shard_map/ppermute | solution.py:302
  105.0 93.5 %collective-permute-start.20 = (bf16[640,2048]{1,0:T(8,128)(2,1)}, bf16[640,2048]{1,0:T(8,128)(2,1)}, u32[]{:S(2)}, u32[]{:S(2)}) collective-permute-start(bf16[640,2048]{1,0:T(8,128)(2,1)} %refs_1_.1), channel_id=1, source_target_pairs={{0,4},{4,0},{8,12},{12,8},{16,20},{20,16},{24,28},{28,24},{1,5},{5... | collective-permute-start | bytes 7864328 | tf_op jit(solution)/shard_map/ppermute | solution.py:302
  108.8 44.9 %collective-permute-start.16 = (bf16[480,2048]{1,0:T(8,128)(2,1)}, bf16[480,2048]{1,0:T(8,128)(2,1)S(1)}, u32[]{:S(2)}, u32[]{:S(2)}) collective-permute-start(bf16[480,2048]{1,0:T(8,128)(2,1)} %slice.44), channel_id=1, source_target_pairs={{0,8},{4,12},{8,0},{12,4},{16,24},{20,28},{24,16},{28,20},{1,9},{5... | collective-permute-start | bytes 5898248 | tf_op jit(solution)/shard_map/ppermute | solution.py:302
  110.6 44.7 %collective-permute-start.17 = (bf16[480,2048]{1,0:T(8,128)(2,1)}, bf16[480,2048]{1,0:T(8,128)(2,1)S(1)}, u32[]{:S(2)}, u32[]{:S(2)}) collective-permute-start(bf16[480,2048]{1,0:T(8,128)(2,1)} %slice.44), channel_id=1, source_target_pairs={{0,16},{4,20},{8,24},{12,28},{16,0},{20,4},{24,8},{28,12},{1,17},{... | collective-permute-start | bytes 5898248 | tf_op jit(solution)/shard_map/ppermute | solution.py:302
  113.5 32.9 %collective-permute-start.13 = (bf16[4,320,256]{2,1,0:T(8,128)(2,1)S(1)}, bf16[4,320,256]{2,1,0:T(8,128)(2,1)S(1)}, u32[]{:S(2)}, u32[]{:S(2)}) collective-permute-start(bf16[4,320,256]{2,1,0:T(8,128)(2,1)S(1)} %get-tuple-element.53.refs_0_), channel_id=1, source_target_pairs={{0,1},{1,0},{2,3},{3,2},{4,5},{5,4},{6,7},{7,6},{8,9},{9,8},{10,11... | collective-permute-start | bytes 1966088 | tf_op jit(solution)/shard_map/ppermute | solution.py:308
  115.2 31.5 %collective-permute-start.14 = (bf16[4,320,256]{2,1,0:T(8,128)(2,1)S(1)}, bf16[4,320,256]{2,1,0:T(8,128)(2,1)S(1)}, u32[]{:S(2)}, u32[]{:S(2)}) collective-permute-start(bf16[4,320,256]{2,1,0:T(8,128)(2,1)S(1)} %get-tuple-element.53.refs_0_), channel_id=1, source_target_pairs={{0,2},{1,3},{2,0},{3,1},{4,6},{5,7},{6,4},{7,5},{8,10},{9,11},{10,... | collective-permute-start | bytes 1966088 | tf_op jit(solution)/shard_map/ppermute | solution.py:308
  115.8 1.1 copy-start.4
  146.7 15.9 %collective-permute-start.15 = (bf16[4,320,256]{2,1,0:T(8,128)(2,1)S(1)}, bf16[4,320,256]{2,1,0:T(8,128)(2,1)S(1)}, u32[]{:S(2)}, u32[]{:S(2)}) collective-permute-start(bf16[4,320,256]{2,1,0:T(8,128)(2,1)S(1)} %collective-permute-done.14.refs_2_), channel_id=1, source_target_pairs={{0,1},{1,0},{2,3},{3,2},{4,5},{5,4},{6,7},{7,6},{8,9},{9,8},{10,11... | collective-permute-start | bytes 1966088 | tf_op jit(solution)/shard_map/ppermute | solution.py:308
  162.9 2.2 copy-start.12
  163.0 39.9 %collective-permute-start.21 = (bf16[640,2048]{1,0:T(8,128)(2,1)S(1)}, bf16[640,2048]{1,0:T(8,128)(2,1)}, u32[]{:S(2)}, u32[]{:S(2)}) collective-permute-start(bf16[640,2048]{1,0:T(8,128)(2,1)S(1)} %constant_dynamic-update-slice_fusion.7.refs_2_), channel_id=1, source_target_pairs={{0,4},{4,0},{8,12},{12,8},{16,20},{20,16},{24,28},{28,24},{1,5},{5... | collective-permute-start | bytes 7864328 | tf_op jit(solution)/shard_map/ppermute | solution.py:302
  163.1 34.6 %collective-permute-start.18 = (bf16[320,2048]{1,0:T(8,128)(2,1)S(1)}, bf16[320,2048]{1,0:T(8,128)(2,1)S(1)}, u32[]{:S(2)}, u32[]{:S(2)}) collective-permute-start(bf16[320,2048]{1,0:T(8,128)(2,1)S(1)} %slice.59), channel_id=1, source_target_pairs={{0,16},{4,20},{8,24},{12,28},{16,0},{20,4},{24,8},{28,12},{1,17},{... | collective-permute-start | bytes 3932168 | tf_op jit(solution)/shard_map/ppermute | solution.py:302
  165.1 32.7 %collective-permute-start.19 = (bf16[320,2048]{1,0:T(8,128)(2,1)S(1)}, bf16[320,2048]{1,0:T(8,128)(2,1)S(1)}, u32[]{:S(2)}, u32[]{:S(2)}) collective-permute-start(bf16[320,2048]{1,0:T(8,128)(2,1)S(1)} %slice.46), channel_id=1, source_target_pairs={{0,8},{4,12},{8,0},{12,4},{16,24},{20,28},{24,16},{28,20},{1,9},{5... | collective-permute-start | bytes 3932168 | tf_op jit(solution)/shard_map/ppermute | solution.py:302
  168.2 34.6 %copy-start.5 = (f32[2048]{0:T(1024)S(1)}, f32[2048]{0:T(1024)}, u32[]{:S(2)}) copy-start(f32[2048]{0:T(1024)} %param.22) | copy-start | bytes 24580
  168.2 34.6 %collective-permute-start.22 = (bf16[640,2048]{1,0:T(8,128)(2,1)}, bf16[640,2048]{1,0:T(8,128)(2,1)}, u32[]{:S(2)}, u32[]{:S(2)}) collective-permute-start(bf16[640,2048]{1,0:T(8,128)(2,1)} %constant_dynamic-update-slice_fusion.9.refs_3_), channel_id=1, source_target_pairs={{0,4},{4,0},{8,12},{12,8},{16,20},{20,16},{24,28},{28,24},{1,5},{5... | collective-permute-start | bytes 7864328 | tf_op jit(solution)/shard_map/ppermute | solution.py:302
  197.8 3.2 %collective-permute-start.23 = (bf16[320,2048]{1,0:T(8,128)(2,1)S(1)}, bf16[320,2048]{1,0:T(8,128)(2,1)S(1)}, u32[]{:S(2)}, u32[]{:S(2)}) collective-permute-start(bf16[320,2048]{1,0:T(8,128)(2,1)S(1)} %collective-permute-done.18.refs_4_), channel_id=1, source_target_pairs={{0,4},{4,0},{8,12},{12,8},{16,20},{20,16},{24,28},{28,24},{1,5},{5... | collective-permute-start | bytes 3932168 | tf_op jit(solution)/shard_map/ppermute | solution.py:302
  198.3 4.5 %collective-permute-start.24 = (bf16[320,2048]{1,0:T(8,128)(2,1)S(1)}, bf16[320,2048]{1,0:T(8,128)(2,1)S(1)}, u32[]{:S(2)}, u32[]{:S(2)}) collective-permute-start(bf16[320,2048]{1,0:T(8,128)(2,1)S(1)} %collective-permute-done.19.refs_5_), channel_id=1, source_target_pairs={{0,4},{4,0},{8,12},{12,8},{16,20},{20,16},{24,28},{28,24},{1,5},{5... | collective-permute-start | bytes 3932168 | tf_op jit(solution)/shard_map/ppermute | solution.py:302
  227.9 47.0 %copy-start.1 = (bf16[2048,320]{0,1:T(8,128)(2,1)S(1)}, bf16[2048,320]{0,1:T(8,128)(2,1)}, u32[]{:S(2)}) copy-start(bf16[2048,320]{0,1:T(8,128)(2,1)} %param.13) | copy-start | bytes 3932164
Sparse Core Ops, SparseCore 0:
  228.1 44.5 reduce-scatter.1

commit v10 on v9

--- a/solution.py
+++ b/solution.py
@@ -375,11 +375,11 @@
         others = jnp.concatenate([by1, by2, tp_xor(by2, 1)])
         vit_sides = sides(tie(others, full))
         near = sides_of_tp(full[:mid])
-        vit_sides, near = lax.optimization_barrier((vit_sides, near))
+        vit_sides, near, rest = lax.optimization_barrier((vit_sides, near, w_merge[quarter:]))
         far = tp_xor(near[1], 1)
         far, vit_corners = lax.optimization_barrier((far, corners(*vit_sides)))
         vit_weights = [wq_t, w_proj] + with_cores([jnp.concatenate([others, *vit_sides, *vit_corners])])
-        merge_sides = sides(tie(w_merge[quarter:], vit_sides))
+        merge_sides = sides(rest)
         q_rows, p_rows = wq_t.shape[0], w_proj.shape[0]
         vit_parts = []
         for n, (d, lo, hi) in enumerate(parts(others.shape[0])):
@@ -482,10 +482,10 @@
         merged = encode(0, [full[:mid], by1, by2, far], None)
         by1, by2 = sides_of_tp(own)
         merged, by2 = lax.optimization_barrier((merged, by2))
+        merge_sides = [jnp.concatenate(pair) for pair in zip(early, merge_sides)]
+        merge_corners = corners(*merge_sides)
         far, merge_sides = lax.optimization_barrier((tp_xor(by2, 1), merge_sides))
         merged = encode(mid, [full[mid:], by1, by2, far], merged)
-        merge_sides = [jnp.concatenate(pair) for pair in zip(early, merge_sides)]
-        merge_corners = corners(*merge_sides)
         merged, merge_corners = lax.optimization_barrier((merged, merge_corners))
         merge_weights = with_cores([w_merge, *merge_sides, *merge_corners])
     else:

time: 282 us -> 281 us (level)
  local copies, waits for them, and re-layouts: 32 us -> 27.8 us
    unnamed x38 -> x43, local copies, waits for them, and re-layouts: 16.2 us -> 12.3 us
  transfers between devices with their start and end apart: 27 -> 27, of which waited for: 14 -> 15; matrix products, arithmetic and copies ran while one was open for 13% -> 12% of each run, Pallas kernels for 21% -> 21%
where the time goes in v10:
time: 281 us; the launch traced here: 280 us
  waiting for transfers between devices  109 us (39%)
  Pallas kernels  84.1 us (30%)
  starting transfers between devices  30.4 us (11%)
  local copies, waits for them, and re-layouts  27.8 us (10%)
  between operations  13.7 us (5%)
  other arithmetic  11.4 us (4%)
  matrix products  3.45 us (1%)
    pallas_call x2, Pallas kernels, attend(): pl.pallas_call(functools.partial(attend_kernel, tp, moves, len(weights),...  59 us
    reduce_scatter x1, waiting for transfers between devices, shards(): lax.psum_scatter(partial_value, 'tp', scatter_dimension=0, tiled=True)  45.3 us
    ppermute x9, waiting for transfers between devices, tp_xor(): return lax.ppermute(x, 'tp', [(i, i ^ d) for i in range(tp)])  41 us
    pallas_call x1, Pallas kernels, project(): pl.pallas_call(functools.partial(project_kernel, moves, position, len(wei...  25.1 us
    ppermute x16, waiting for transfers between devices, xor(): return lax.ppermute(x, 'seq', [(i, i ^ d) for i in range(seq_count)])  19.6 us
    ppermute x16, starting transfers between devices, xor(): return lax.ppermute(x, 'seq', [(i, i ^ d) for i in range(seq_count)])  17.4 us
    unnamed x43, local copies, waits for them, and re-layouts  12.3 us
    ppermute x9, starting transfers between devices, tp_xor(): return lax.ppermute(x, 'tp', [(i, i ^ d) for i in range(tp)])  9.24 us
  transfers between devices with their start and end apart: 27, of which 15 were waited for; matrix products, arithmetic and copies ran while one was open for 12% of the time, Pallas kernels for 21%

profile of v10, /device:TPU:0, one launch (start us, length us, event | category | flops | bytes accessed | tf_op | source)
XLA Modules:
  0.0 280.0 jit_solution(15711486944450409228)
XLA Ops:
  6.5 2.1 bitcast_select_fusion
  8.6 3.0 %collective-permute-start = (bf16[160,1280]{1,0:T(8,128)(2,1)}, bf16[160,1280]{1,0:T(8,128)(2,1)S(1)}, u32[]{:S(2)}, u32[]{:S(2)}) collective-permute-start(bf16[160,1280]{1,0:T(8,128)(2,1)} %bitcast_select_fusion), channel_id=1, source_target_pairs={{0,1},{1,0},{2,3},{3,2},{4,5},{5,4},{6,7},{7,6},{8,9},{9,8},{10,11... | collective-permute-start | bytes 1228808 | tf_op jit(solution)/shard_map/ppermute | solution.py:308
  11.7 2.6 collective-permute-start.1
  14.2 2.0 slice.40
  16.2 1.5 collective-permute-start.2
  17.7 1.5 collective-permute-start.3
  19.2 2.3 sort.17
  21.5 1.3 fusion.11
  22.9 1.8 compare_convert_fusion
  24.7 0.7 gather_fusion.1
  25.4 0.7 gather_fusion
  26.4 3.5 %fusion.3 = bf16[320,2048]{1,0:T(8,128)(2,1)S(1)} fusion(bf16[2048,320]{0,1:T(8,128)(2,1)S(1)} %copy-done, s32[2048]{0:T(1024)S(1)} %add.115), kind=kOutput, calls=%fused_computation.7 | convolution fusion | flops 2689204224 | bytes 2629632 | tf_op jit(solution)/shard_map/dot_general | solution.py:326
  30.2 1.2 copy.18
  31.3 3.6 %all-to-all-start = ((bf16[8,336,256]{2,1,0:T(8,128)(2,1)}), bf16[8,336,256]{2,1,0:T(8,128)(2,1)S(1)}, u32[]{:S(2)}, u32[]{:S(2)}) async-start(bf16[8,336,256]{2,1,0:T(8,128)(2,1)} %bitcast.35), calls=%async_computation | async-start | bytes 2752512 | tf_op jit(solution)/shard_map/all_to_all | solution.py:334
  35.2 0.5 collective-permute-start.4
  35.7 11.1 %collective-permute-done.4 = bf16[160,1280]{1,0:T(8,128)(2,1)S(1)} collective-permute-done((bf16[160,1280]{1,0:T(8,128)(2,1)S(1)}, bf16[160,1280]{1,0:T(8,128)(2,1)S(1)}, u32[]{:S(2)}, u32[]{:S(2)}) %collective-permute-start.4) | collective-permute-done | bytes 409632 | tf_op jit(solution)/shard_map/ppermute | solution.py:308
  46.8 1.2 pad_maximum_fusion.2
  48.0 1.7 collective-permute-start.5
  49.7 1.5 collective-permute-start.6
  51.2 3.1 %all-to-all-done = bf16[8,336,256]{2,1,0:T(8,128)(2,1)S(1)} async-done(((bf16[8,336,256]{2,1,0:T(8,128)(2,1)}), bf16[8,336,256]{2,1,0:T(8,128)(2,1)S(1)}, u32[]{:S(2)}, u32[]{:S(2)}) %all-to-all-start) | async-done | bytes 1376288 | tf_op jit(solution)/shard_map/all_to_all | solution.py:334
  54.4 1.1 copy-done.7
  55.4 0.4 collective-permute-start.7
  56.2 3.0 %slice.42 = bf16[480,2048]{1,0:T(8,128)(2,1)} slice(bf16[640,2048]{1,0:T(8,128)(2,1)} %refs_1_.1), slice={[160:640], [0:2048]} | slice | bytes 3932160 | tf_op jit(solution)/shard_map/slice | solution.py:378
  59.3 0.8 constant_dynamic-update-slice_fusion.6
  60.1 0.8 constant_dynamic-update-slice_fusion.5
  60.9 20.5 %collective-permute-done.7.refs_1_ = bf16[4,320,256]{2,1,0:T(8,128)(2,1)S(1)} collective-permute-done((bf16[4,320,256]{2,1,0:T(8,128)(2,1)S(1)}, bf16[4,320,256]{2,1,0:T(8,128)(2,1)S(1)}, u32[]{:S(2)}, u32[]{:S(2)}) %collective-permute-start.7) | collective-permute-done | bytes 655392 | tf_op jit(solution)/shard_map/ppermute | solution.py:308
  81.3 2.4 collective-permute-done.8.refs_2_
  83.7 1.1 slice.43
  84.8 1.5 collective-permute-start.10
  86.3 1.1 slice.44
  87.5 2.6 collective-permute-start.11
  90.0 0.8 constant_dynamic-update-slice_fusion.4
  90.8 2.4 constant_dynamic-update-slice_fusion.3
  93.3 2.5 constant_dynamic-update-slice_fusion.2
  95.7 1.6 collective-permute-done.10
  97.3 5.6 %collective-permute-done.11 = bf16[240,1280]{1,0:T(8,128)(2,1)S(1)} collective-permute-done((bf16[240,1280]{1,0:T(8,128)(2,1)S(1)}, bf16[240,1280]{1,0:T(8,128)(2,1)S(1)}, u32[]{:S(2)}, u32[]{:S(2)}) %collective-permute-start.11) | collective-permute-done | bytes 614432 | tf_op jit(solution)/shard_map/ppermute | solution.py:302
  102.8 2.3 collective-permute-done.9.refs_3_
  105.2 0.8 copy-done.3
  106.0 0.9 constant_dynamic-update-slice_fusion.1
  106.9 0.9 constant_dynamic-update-slice_fusion.refs_6_
  107.8 0.5 collective-permute-start.20
  108.7 1.7 collective-permute-start.17
  110.8 5.5 %collective-permute-done.12.refs_7_ = bf16[1920,1280]{1,0:T(8,128)(2,1)} collective-permute-done((bf16[1920,1280]{1,0:T(8,128)(2,1)}, bf16[1920,1280]{1,0:T(8,128)(2,1)}, u32[]{:S(2)}, u32[]{:S(2)}) %collective-permute-start.12) | collective-permute-done | bytes 4915232 | tf_op jit(solution)/shard_map/ppermute | solution.py:302
  116.6 0.5 collective-permute-start.14
  117.2 1.1 copy-done.4
  118.2 29.5 %attend.2.refs_10_ = bf16[4,8,64,1280]{3,2,1,0:T(8,128)(2,1)} custom-call(s32[6]{0:T(128)S(1)} %pad_add_fusion.3.info, bf16[4,320,256]{2,1,0:T(8,128)(2,1)S(1)} %get-tuple-element.70.refs_0_, bf16[4,320,256]{2,1,0:T(8,128)(2,1)S(1)} %collective-permute-done.7.refs_1_, bf16[4,320,256]{2,1,0:T(8,128)(2,1)S(1)} %collective-permute-done.8.refs_2_, ...), custom_call_target="tpu_custom_call" | custom-call | flops 16777216000 | bytes 14680064 | tf_op jit(solution)/shard_map/attend/pallas_call | solution.py:148
  148.1 1.5 collective-permute-start.15
  149.6 1.1 constant_dynamic-update-slice_fusion.8
  150.7 2.5 collective-permute-done.16
  153.7 1.8 collective-permute-start.18
  155.5 1.2 slice.46
  156.7 1.7 collective-permute-start.19
  158.4 1.3 pad_maximum_fusion.refs_3_
  159.6 4.4 %collective-permute-done.15.refs_3_ = bf16[4,320,256]{2,1,0:T(8,128)(2,1)S(1)} collective-permute-done((bf16[4,320,256]{2,1,0:T(8,128)(2,1)S(1)}, bf16[4,320,256]{2,1,0:T(8,128)(2,1)S(1)}, u32[]{:S(2)}, u32[]{:S(2)}) %collective-permute-start.15) | collective-permute-done | bytes 655392 | tf_op jit(solution)/shard_map/ppermute | solution.py:308
  164.1 0.5 collective-permute-start.22
  164.6 29.5 %attend.3 = bf16[4,8,64,1280]{3,2,1,0:T(8,128)(2,1)} custom-call(s32[6]{0:T(128)S(1)} %pad_add_fusion.1.info, bf16[4,320,256]{2,1,0:T(8,128)(2,1)S(1)} %get-tuple-element.53.refs_0_, bf16[4,320,256]{2,1,0:T(8,128)(2,1)S(1)} %collective-permute-done.13.refs_1_, ...), custom_call_target="tpu_custom_call", output_to_operand_aliasing={{}: (11, {})} | custom-call | flops 16777216000 | bytes 14680064 | tf_op jit(solution)/shard_map/attend/pallas_call | solution.py:148
  194.2 0.5 collective-permute-start.24
  194.8 2.4 collective-permute-done.23.refs_9_
  197.2 1.9 collective-permute-done.24.refs_10_
  199.1 25.1 %project.1 = bf16[512,2176]{1,0:T(8,128)(2,1)} custom-call(s32[2]{0:T(128)S(1)} %pad_add_fusion.info, bf16[4,512,1280]{2,1,0:T(8,128)(2,1)} %bitcast.42, bf16[640,2048]{1,0:T(8,128)(2,1)} %refs_1_.1, bf16[640,2048]{1,0:T(8,128)(2,1)} %copy-done.15, bf16[640,2048]{1,0:T(8,128)(2,1)} %copy-done.8, bf16[320,2048]{1,0:T(8,128)(2,1)S(1)} %collective-permute-done.18.refs_4_, ...), custom_call_target="tpu_custom_call" | custom-call | flops 15032385536 | bytes 37748736 | tf_op jit(solution)/shard_map/project/pallas_call | solution.py:249
  224.3 1.0 slice.49
  225.6 45.3 %reduce-scatter.2.cloned.1.call-done = bf16[128,2176]{1,0:T(8,128)(2,1)} async-done(((bf16[512,2176]{1,0:T(8,128)(2,1)}), bf16[128,2176]{1,0:T(8,128)(2,1)}) %reduce-scatter.2.cloned.1.call-update) | async-done | bytes 557072 | tf_op jit(solution)/shard_map/reduce_scatter | solution.py:497
  270.9 1.1 convert_element_type.31
  272.2 1.0 fusion.5
  (85 shorter events, 3.7 us)
Async XLA Ops:
  6.5 19.9 %copy-start = (bf16[2048,320]{0,1:T(8,128)(2,1)S(1)}, bf16[2048,320]{0,1:T(8,128)(2,1)}, u32[]{:S(2)}) copy-start(bf16[2048,320]{0,1:T(8,128)(2,1)} %param.13) | copy-start | bytes 3932164
  6.5 18.9 %copy-start.6 = (s32[1,32]{1,0:T(1,128)S(1)}, s32[1,32]{1,0:T(1,128)}, u32[]{:S(2)}) copy-start(s32[1,32]{1,0:T(1,128)} %param.15) | copy-start | bytes 388
  8.6 26.5 %collective-permute-start = (bf16[160,1280]{1,0:T(8,128)(2,1)}, bf16[160,1280]{1,0:T(8,128)(2,1)S(1)}, u32[]{:S(2)}, u32[]{:S(2)}) collective-permute-start(bf16[160,1280]{1,0:T(8,128)(2,1)} %bitcast_select_fusion), channel_id=1, source_target_pairs={{0,1},{1,0},{2,3},{3,2},{4,5},{5,4},{6,7},{7,6},{8,9},{9,8},{10,11... | collective-permute-start | bytes 1228808 | tf_op jit(solution)/shard_map/ppermute | solution.py:308
  11.7 23.5 %collective-permute-start.1 = (bf16[160,1280]{1,0:T(8,128)(2,1)}, bf16[160,1280]{1,0:T(8,128)(2,1)S(1)}, u32[]{:S(2)}, u32[]{:S(2)}) collective-permute-start(bf16[160,1280]{1,0:T(8,128)(2,1)} %bitcast_select_fusion), channel_id=1, source_target_pairs={{0,2},{1,3},{2,0},{3,1},{4,6},{5,7},{6,4},{7,5},{8,10},{9,11},{10,... | collective-permute-start | bytes 1228808 | tf_op jit(solution)/shard_map/ppermute | solution.py:308
  16.2 19.0 %collective-permute-start.2 = (bf16[160,2048]{1,0:T(8,128)(2,1)}, bf16[160,2048]{1,0:T(8,128)(2,1)}, u32[]{:S(2)}, u32[]{:S(2)}) collective-permute-start(bf16[160,2048]{1,0:T(8,128)(2,1)} %slice.40), channel_id=1, source_target_pairs={{0,8},{4,12},{8,0},{12,4},{16,24},{20,28},{24,16},{28,20},{1,9},{5... | collective-permute-start | bytes 1966088 | tf_op jit(solution)/shard_map/ppermute | solution.py:302
  17.7 17.5 %collective-permute-start.3 = (bf16[160,2048]{1,0:T(8,128)(2,1)}, bf16[160,2048]{1,0:T(8,128)(2,1)}, u32[]{:S(2)}, u32[]{:S(2)}) collective-permute-start(bf16[160,2048]{1,0:T(8,128)(2,1)} %slice.40), channel_id=1, source_target_pairs={{0,16},{4,20},{8,24},{12,28},{16,0},{20,4},{24,8},{28,12},{1,17},{... | collective-permute-start | bytes 1966088 | tf_op jit(solution)/shard_map/ppermute | solution.py:302
  31.3 22.9 %all-to-all-start = ((bf16[8,336,256]{2,1,0:T(8,128)(2,1)}), bf16[8,336,256]{2,1,0:T(8,128)(2,1)S(1)}, u32[]{:S(2)}, u32[]{:S(2)}) async-start(bf16[8,336,256]{2,1,0:T(8,128)(2,1)} %bitcast.35), calls=%async_computation | async-start | bytes 2752512 | tf_op jit(solution)/shard_map/all_to_all | solution.py:334
  34.9 236.0 %reduce-scatter.2.cloned.1.call-start = ((), (), s32[]{:S(2)}) async-start(), calls=%async_computation.2 | async-start | bytes 2785280 | tf_op jit(solution)/shard_map/reduce_scatter | solution.py:497
  35.2 19.2 %copy-start.9 = (bf16[160,1280]{1,0:T(8,128)(2,1)}, bf16[160,1280]{1,0:T(8,128)(2,1)S(1)}, u32[]{:S(2)}) copy-start(bf16[160,1280]{1,0:T(8,128)(2,1)S(1)} %collective-permute-done) | copy-start | bytes 1228804
  35.2 20.3 %copy-start.11 = (bf16[160,1280]{1,0:T(8,128)(2,1)}, bf16[160,1280]{1,0:T(8,128)(2,1)S(1)}, u32[]{:S(2)}) copy-start(bf16[160,1280]{1,0:T(8,128)(2,1)S(1)} %collective-permute-done.1) | copy-start | bytes 1228804
  35.2 11.6 %collective-permute-start.4 = (bf16[160,1280]{1,0:T(8,128)(2,1)S(1)}, bf16[160,1280]{1,0:T(8,128)(2,1)S(1)}, u32[]{:S(2)}, u32[]{:S(2)}) collective-permute-start(bf16[160,1280]{1,0:T(8,128)(2,1)S(1)} %collective-permute-done.1), channel_id=1, source_target_pairs={{0,1},{1,0},{2,3},{3,2},{4,5},{5,4},{6,7},{7,6},{8,9},{9,8},{10,11... | collective-permute-start | bytes 1228808 | tf_op jit(solution)/shard_map/ppermute | solution.py:308
  46.8 4.3 %copy-start.13 = (bf16[160,1280]{1,0:T(8,128)(2,1)}, bf16[160,1280]{1,0:T(8,128)(2,1)S(1)}, u32[]{:S(2)}) copy-start(bf16[160,1280]{1,0:T(8,128)(2,1)S(1)} %collective-permute-done.4) | copy-start | bytes 1228804
  48.0 35.7 %collective-permute-start.5 = (bf16[480,1280]{1,0:T(8,128)(2,1)}, bf16[480,1280]{1,0:T(8,128)(2,1)}, u32[]{:S(2)}, u32[]{:S(2)}) collective-permute-start(bf16[480,1280]{1,0:T(8,128)(2,1)} %pad_maximum_fusion.2), channel_id=1, source_target_pairs={{0,8},{4,12},{8,0},{12,4},{16,24},{20,28},{24,16},{28,20},{1,9},{5... | collective-permute-start | bytes 3686408 | tf_op jit(solution)/shard_map/ppermute | solution.py:302
  49.7 34.0 %collective-permute-start.6 = (bf16[480,1280]{1,0:T(8,128)(2,1)}, bf16[480,1280]{1,0:T(8,128)(2,1)}, u32[]{:S(2)}, u32[]{:S(2)}) collective-permute-start(bf16[480,1280]{1,0:T(8,128)(2,1)} %pad_maximum_fusion.2), channel_id=1, source_target_pairs={{0,16},{4,20},{8,24},{12,28},{16,0},{20,4},{24,8},{28,12},{1,17},{... | collective-permute-start | bytes 3686408 | tf_op jit(solution)/shard_map/ppermute | solution.py:302
  54.3 1.2 copy-start.7
  55.4 3.8 %copy-start.10 = (bf16[160,1280]{1,0:T(8,128)(2,1)S(1)}, bf16[160,1280]{1,0:T(8,128)(2,1)}, u32[]{:S(2)}) copy-start(bf16[160,1280]{1,0:T(8,128)(2,1)} %copy-done.9) | copy-start | bytes 1228804
  55.4 25.9 %collective-permute-start.7 = (bf16[4,320,256]{2,1,0:T(8,128)(2,1)S(1)}, bf16[4,320,256]{2,1,0:T(8,128)(2,1)S(1)}, u32[]{:S(2)}, u32[]{:S(2)}) collective-permute-start(bf16[4,320,256]{2,1,0:T(8,128)(2,1)S(1)} %get-tuple-element.70.refs_0_), channel_id=1, source_target_pairs={{0,1},{1,0},{2,3},{3,2},{4,5},{5,4},{6,7},{7,6},{8,9},{9,8},{10,11... | collective-permute-start | bytes 1966088 | tf_op jit(solution)/shard_map/ppermute | solution.py:308
  55.9 4.2 %copy-start.12 = (bf16[160,1280]{1,0:T(8,128)(2,1)S(1)}, bf16[160,1280]{1,0:T(8,128)(2,1)}, u32[]{:S(2)}) copy-start(bf16[160,1280]{1,0:T(8,128)(2,1)} %copy-done.11) | copy-start | bytes 1228804
  55.9 27.8 %collective-permute-start.8 = (bf16[4,320,256]{2,1,0:T(8,128)(2,1)S(1)}, bf16[4,320,256]{2,1,0:T(8,128)(2,1)S(1)}, u32[]{:S(2)}, u32[]{:S(2)}) collective-permute-start(bf16[4,320,256]{2,1,0:T(8,128)(2,1)S(1)} %get-tuple-element.70.refs_0_), channel_id=1, source_target_pairs={{0,2},{1,3},{2,0},{3,1},{4,6},{5,7},{6,4},{7,5},{8,10},{9,11},{10,... | collective-permute-start | bytes 1966088 | tf_op jit(solution)/shard_map/ppermute | solution.py:308
  59.3 30.8 %copy-start.14 = (bf16[160,1280]{1,0:T(8,128)(2,1)S(1)}, bf16[160,1280]{1,0:T(8,128)(2,1)}, u32[]{:S(2)}) copy-start(bf16[160,1280]{1,0:T(8,128)(2,1)} %copy-done.13) | copy-start | bytes 1228804
  84.8 12.4 %collective-permute-start.10 = (bf16[240,1280]{1,0:T(8,128)(2,1)S(1)}, bf16[240,1280]{1,0:T(8,128)(2,1)S(1)}, u32[]{:S(2)}, u32[]{:S(2)}) collective-permute-start(bf16[240,1280]{1,0:T(8,128)(2,1)S(1)} %slice.43), channel_id=1, source_target_pairs={{0,16},{4,20},{8,24},{12,28},{16,0},{20,4},{24,8},{28,12},{1,17},{... | collective-permute-start | bytes 1843208 | tf_op jit(solution)/shard_map/ppermute | solution.py:302
  87.5 15.4 %collective-permute-start.11 = (bf16[240,1280]{1,0:T(8,128)(2,1)S(1)}, bf16[240,1280]{1,0:T(8,128)(2,1)S(1)}, u32[]{:S(2)}, u32[]{:S(2)}) collective-permute-start(bf16[240,1280]{1,0:T(8,128)(2,1)S(1)} %slice.44), channel_id=1, source_target_pairs={{0,8},{4,12},{8,0},{12,4},{16,24},{20,28},{24,16},{28,20},{1,9},{5... | collective-permute-start | bytes 1843208 | tf_op jit(solution)/shard_map/ppermute | solution.py:302
  90.0 15.2 %collective-permute-start.9 = (bf16[4,320,256]{2,1,0:T(8,128)(2,1)S(1)}, bf16[4,320,256]{2,1,0:T(8,128)(2,1)S(1)}, u32[]{:S(2)}, u32[]{:S(2)}) collective-permute-start(bf16[4,320,256]{2,1,0:T(8,128)(2,1)S(1)} %collective-permute-done.8.refs_2_), channel_id=1, source_target_pairs={{0,1},{1,0},{2,3},{3,2},{4,5},{5,4},{6,7},{7,6},{8,9},{9,8},{10,11... | collective-permute-start | bytes 1966088 | tf_op jit(solution)/shard_map/ppermute | solution.py:308
  93.2 17.2 %copy-start.17 = (f32[1280]{0:T(1024)S(1)}, f32[1280]{0:T(1024)}, u32[]{:S(2)}) copy-start(f32[1280]{0:T(1024)} %param.19) | copy-start | bytes 15364
  93.2 17.5 %copy-start.16 = (f32[1280]{0:T(1024)S(1)}, f32[1280]{0:T(1024)}, u32[]{:S(2)}) copy-start(f32[1280]{0:T(1024)} %param.20) | copy-start | bytes 15364
  93.3 23.9 %copy-start.2 = (bf16[320,1280]{1,0:T(8,128)(2,1)S(1)}, bf16[320,1280]{1,0:T(8,128)(2,1)}, u32[]{:S(2)}) copy-start(bf16[320,1280]{1,0:T(8,128)(2,1)} %refs_5_.3) | copy-start | bytes 2457604
  105.2 0.8 copy-start.3
  107.8 8.5 %collective-permute-start.12 = (bf16[1920,1280]{1,0:T(8,128)(2,1)}, bf16[1920,1280]{1,0:T(8,128)(2,1)}, u32[]{:S(2)}, u32[]{:S(2)}) collective-permute-start(bf16[1920,1280]{1,0:T(8,128)(2,1)} %constant_dynamic-update-slice_fusion.refs_6_), channel_id=1, source_target_pairs={{0,4},{4,0},{8,12},{12,8},{16,20},{20,16},{24,28},{28,24},{1,5},{5... | collective-permute-start | bytes 14745608 | tf_op jit(solution)/shard_map/ppermute | solution.py:302
  107.8 87.0 %collective-permute-start.20 = (bf16[640,2048]{1,0:T(8,128)(2,1)}, bf16[640,2048]{1,0:T(8,128)(2,1)}, u32[]{:S(2)}, u32[]{:S(2)}) collective-permute-start(bf16[640,2048]{1,0:T(8,128)(2,1)} %refs_1_.1), channel_id=1, source_target_pairs={{0,4},{4,0},{8,12},{12,8},{16,20},{20,16},{24,28},{28,24},{1,5},{5... | collective-permute-start | bytes 7864328 | tf_op jit(solution)/shard_map/ppermute | solution.py:302
  108.3 44.9 %collective-permute-start.16 = (bf16[480,2048]{1,0:T(8,128)(2,1)}, bf16[480,2048]{1,0:T(8,128)(2,1)S(1)}, u32[]{:S(2)}, u32[]{:S(2)}) collective-permute-start(bf16[480,2048]{1,0:T(8,128)(2,1)} %slice.42), channel_id=1, source_target_pairs={{0,8},{4,12},{8,0},{12,4},{16,24},{20,28},{24,16},{28,20},{1,9},{5... | collective-permute-start | bytes 5898248 | tf_op jit(solution)/shard_map/ppermute | solution.py:302
  108.7 44.7 %collective-permute-start.17 = (bf16[480,2048]{1,0:T(8,128)(2,1)}, bf16[480,2048]{1,0:T(8,128)(2,1)S(1)}, u32[]{:S(2)}, u32[]{:S(2)}) collective-permute-start(bf16[480,2048]{1,0:T(8,128)(2,1)} %slice.42), channel_id=1, source_target_pairs={{0,16},{4,20},{8,24},{12,28},{16,0},{20,4},{24,8},{28,12},{1,17},{... | collective-permute-start | bytes 5898248 | tf_op jit(solution)/shard_map/ppermute | solution.py:302
  116.3 31.4 %collective-permute-start.13 = (bf16[4,320,256]{2,1,0:T(8,128)(2,1)S(1)}, bf16[4,320,256]{2,1,0:T(8,128)(2,1)S(1)}, u32[]{:S(2)}, u32[]{:S(2)}) collective-permute-start(bf16[4,320,256]{2,1,0:T(8,128)(2,1)S(1)} %get-tuple-element.53.refs_0_), channel_id=1, source_target_pairs={{0,1},{1,0},{2,3},{3,2},{4,5},{5,4},{6,7},{7,6},{8,9},{9,8},{10,11... | collective-permute-start | bytes 1966088 | tf_op jit(solution)/shard_map/ppermute | solution.py:308
  116.6 31.5 %collective-permute-start.14 = (bf16[4,320,256]{2,1,0:T(8,128)(2,1)S(1)}, bf16[4,320,256]{2,1,0:T(8,128)(2,1)S(1)}, u32[]{:S(2)}, u32[]{:S(2)}) collective-permute-start(bf16[4,320,256]{2,1,0:T(8,128)(2,1)S(1)} %get-tuple-element.53.refs_0_), channel_id=1, source_target_pairs={{0,2},{1,3},{2,0},{3,1},{4,6},{5,7},{6,4},{7,5},{8,10},{9,11},{10,... | collective-permute-start | bytes 1966088 | tf_op jit(solution)/shard_map/ppermute | solution.py:308
  117.2 1.1 copy-start.4
  148.1 16.0 %collective-permute-start.15 = (bf16[4,320,256]{2,1,0:T(8,128)(2,1)S(1)}, bf16[4,320,256]{2,1,0:T(8,128)(2,1)S(1)}, u32[]{:S(2)}, u32[]{:S(2)}) collective-permute-start(bf16[4,320,256]{2,1,0:T(8,128)(2,1)S(1)} %collective-permute-done.14.refs_2_), channel_id=1, source_target_pairs={{0,1},{1,0},{2,3},{3,2},{4,5},{5,4},{6,7},{7,6},{8,9},{9,8},{10,11... | collective-permute-start | bytes 1966088 | tf_op jit(solution)/shard_map/ppermute | solution.py:308
  153.6 10.5 %copy-start.15 = (bf16[640,2048]{1,0:T(8,128)(2,1)}, bf16[640,2048]{1,0:T(8,128)(2,1)S(1)}, u32[]{:S(2)}) copy-start(bf16[640,2048]{1,0:T(8,128)(2,1)S(1)} %constant_dynamic-update-slice_fusion.7.refs_2_) | copy-start | bytes 7864324
  153.7 40.4 %collective-permute-start.18 = (bf16[320,2048]{1,0:T(8,128)(2,1)S(1)}, bf16[320,2048]{1,0:T(8,128)(2,1)S(1)}, u32[]{:S(2)}, u32[]{:S(2)}) collective-permute-start(bf16[320,2048]{1,0:T(8,128)(2,1)S(1)} %slice.59), channel_id=1, source_target_pairs={{0,16},{4,20},{8,24},{12,28},{16,0},{20,4},{24,8},{28,12},{1,17},{... | collective-permute-start | bytes 3932168 | tf_op jit(solution)/shard_map/ppermute | solution.py:302
  156.7 37.4 %collective-permute-start.19 = (bf16[320,2048]{1,0:T(8,128)(2,1)}, bf16[320,2048]{1,0:T(8,128)(2,1)S(1)}, u32[]{:S(2)}, u32[]{:S(2)}) collective-permute-start(bf16[320,2048]{1,0:T(8,128)(2,1)} %slice.46), channel_id=1, source_target_pairs={{0,8},{4,12},{8,0},{12,4},{16,24},{20,28},{24,16},{28,20},{1,9},{5... | collective-permute-start | bytes 3932168 | tf_op jit(solution)/shard_map/ppermute | solution.py:302
  159.6 34.5 %copy-start.8 = (bf16[640,2048]{1,0:T(8,128)(2,1)}, bf16[640,2048]{1,0:T(8,128)(2,1)S(1)}, u32[]{:S(2)}) copy-start(bf16[640,2048]{1,0:T(8,128)(2,1)S(1)} %pad_maximum_fusion.refs_3_) | copy-start | bytes 7864324
  159.6 39.5 %copy-start.5 = (f32[2048]{0:T(1024)S(1)}, f32[2048]{0:T(1024)}, u32[]{:S(2)}) copy-start(f32[2048]{0:T(1024)} %param.22) | copy-start | bytes 24580
  164.1 35.0 %collective-permute-start.21 = (bf16[640,2048]{1,0:T(8,128)(2,1)S(1)}, bf16[640,2048]{1,0:T(8,128)(2,1)}, u32[]{:S(2)}, u32[]{:S(2)}) collective-permute-start(bf16[640,2048]{1,0:T(8,128)(2,1)S(1)} %constant_dynamic-update-slice_fusion.7.refs_2_), channel_id=1, source_target_pairs={{0,4},{4,0},{8,12},{12,8},{16,20},{20,16},{24,28},{28,24},{1,5},{5... | collective-permute-start | bytes 7864328 | tf_op jit(solution)/shard_map/ppermute | solution.py:302
  164.1 35.0 %collective-permute-start.22 = (bf16[640,2048]{1,0:T(8,128)(2,1)S(1)}, bf16[640,2048]{1,0:T(8,128)(2,1)}, u32[]{:S(2)}, u32[]{:S(2)}) collective-permute-start(bf16[640,2048]{1,0:T(8,128)(2,1)S(1)} %pad_maximum_fusion.refs_3_), channel_id=1, source_target_pairs={{0,4},{4,0},{8,12},{12,8},{16,20},{20,16},{24,28},{28,24},{1,5},{5... | collective-permute-start | bytes 7864328 | tf_op jit(solution)/shard_map/ppermute | solution.py:302
  194.1 3.1 %collective-permute-start.23 = (bf16[320,2048]{1,0:T(8,128)(2,1)S(1)}, bf16[320,2048]{1,0:T(8,128)(2,1)S(1)}, u32[]{:S(2)}, u32[]{:S(2)}) collective-permute-start(bf16[320,2048]{1,0:T(8,128)(2,1)S(1)} %collective-permute-done.18.refs_4_), channel_id=1, source_target_pairs={{0,4},{4,0},{8,12},{12,8},{16,20},{20,16},{24,28},{28,24},{1,5},{5... | collective-permute-start | bytes 3932168 | tf_op jit(solution)/shard_map/ppermute | solution.py:302
  194.2 4.9 %collective-permute-start.24 = (bf16[320,2048]{1,0:T(8,128)(2,1)S(1)}, bf16[320,2048]{1,0:T(8,128)(2,1)S(1)}, u32[]{:S(2)}, u32[]{:S(2)}) collective-permute-start(bf16[320,2048]{1,0:T(8,128)(2,1)S(1)} %collective-permute-done.19.refs_5_), channel_id=1, source_target_pairs={{0,4},{4,0},{8,12},{12,8},{16,20},{20,16},{24,28},{28,24},{1,5},{5... | collective-permute-start | bytes 3932168 | tf_op jit(solution)/shard_map/ppermute | solution.py:302
  224.2 48.9 %copy-start.1 = (bf16[2048,320]{0,1:T(8,128)(2,1)S(1)}, bf16[2048,320]{0,1:T(8,128)(2,1)}, u32[]{:S(2)}) copy-start(bf16[2048,320]{0,1:T(8,128)(2,1)} %param.13) | copy-start | bytes 3932164
Sparse Core Ops, SparseCore 0:
  224.4 46.4 reduce-scatter.1

commit v11 on v10

--- a/solution.py
+++ b/solution.py
@@ -233,12 +233,14 @@
     load_cache.wait()
     kvw = cache.shape[1]
 
+    span = min(1024, kvw)
+
     def kv_tile(j, carry):
-        spot = pl.ds(pl.multiple_of(j * 256, 256), 256)
+        spot = pl.ds(pl.multiple_of(j * span, span), span)
         out[:, spot] = jnp.dot(scaled[...], cache[:, spot], preferred_element_type=F32).astype(BF)
         return carry
 
-    lax.fori_loop(0, kvw // 256, kv_tile, 0)
+    lax.fori_loop(0, kvw // span, kv_tile, 0)
     out[:, kvw:] = jnp.broadcast_to(total, (rows, 128)).astype(BF)
 
 

time: 281 us -> 279 us (level)
  no operation moved by 1% of the time
where the time goes in v11:
time: 279 us
  waiting for transfers between devices  109 us (39%)
  Pallas kernels  82.9 us (30%)
  starting transfers between devices  30.4 us (11%)
  local copies, waits for them, and re-layouts  27.8 us (10%)
  between operations  13.7 us (5%)
  other arithmetic  11.4 us (4%)
  matrix products  3.45 us (1%)
    pallas_call x2, Pallas kernels, attend(): pl.pallas_call(functools.partial(attend_kernel, tp, moves, len(weights),...  59 us
    reduce_scatter x1, waiting for transfers between devices, shards(): lax.psum_scatter(partial_value, 'tp', scatter_dimension=0, tiled=True)  45.3 us
    ppermute x9, waiting for transfers between devices, tp_xor(): return lax.ppermute(x, 'tp', [(i, i ^ d) for i in range(tp)])  41 us
    pallas_call x1, Pallas kernels, project(): pl.pallas_call(functools.partial(project_kernel, moves, position, len(wei...  23.9 us
    ppermute x16, waiting for transfers between devices, xor(): return lax.ppermute(x, 'seq', [(i, i ^ d) for i in range(seq_count)])  19.6 us
    ppermute x16, starting transfers between devices, xor(): return lax.ppermute(x, 'seq', [(i, i ^ d) for i in range(seq_count)])  17.4 us
    unnamed x43, local copies, waits for them, and re-layouts  12.3 us
    ppermute x9, starting transfers between devices, tp_xor(): return lax.ppermute(x, 'tp', [(i, i ^ d) for i in range(tp)])  9.24 us
  transfers between devices with their start and end apart: 27, of which 15 were waited for; matrix products, arithmetic and copies ran while one was open for 12% of the time, Pallas kernels for 21%

profile of v11, /device:TPU:0, one launch (start us, length us, event | category | flops | bytes accessed | tf_op | source)
XLA Modules:
  0.0 278.8 jit_solution(13302001270285081062)
XLA Ops:
  6.5 2.1 bitcast_select_fusion
  8.6 3.0 %collective-permute-start = (bf16[160,1280]{1,0:T(8,128)(2,1)}, bf16[160,1280]{1,0:T(8,128)(2,1)S(1)}, u32[]{:S(2)}, u32[]{:S(2)}) collective-permute-start(bf16[160,1280]{1,0:T(8,128)(2,1)} %bitcast_select_fusion), channel_id=1, source_target_pairs={{0,1},{1,0},{2,3},{3,2},{4,5},{5,4},{6,7},{7,6},{8,9},{9,8},{10,11... | collective-permute-start | bytes 1228808 | tf_op jit(solution)/shard_map/ppermute | solution.py:310
  11.7 2.6 collective-permute-start.1
  14.2 2.0 slice.40
  16.2 1.5 collective-permute-start.2
  17.7 1.5 collective-permute-start.3
  19.2 2.3 sort.17
  21.5 1.3 fusion.11
  22.9 1.8 compare_convert_fusion
  24.7 0.7 gather_fusion.1
  25.4 0.7 gather_fusion
  26.4 3.5 %fusion.3 = bf16[320,2048]{1,0:T(8,128)(2,1)S(1)} fusion(bf16[2048,320]{0,1:T(8,128)(2,1)S(1)} %copy-done, s32[2048]{0:T(1024)S(1)} %add.115), kind=kOutput, calls=%fused_computation.7 | convolution fusion | flops 2689204224 | bytes 2629632 | tf_op jit(solution)/shard_map/dot_general | solution.py:328
  30.2 1.2 copy.18
  31.3 3.6 %all-to-all-start = ((bf16[8,336,256]{2,1,0:T(8,128)(2,1)}), bf16[8,336,256]{2,1,0:T(8,128)(2,1)S(1)}, u32[]{:S(2)}, u32[]{:S(2)}) async-start(bf16[8,336,256]{2,1,0:T(8,128)(2,1)} %bitcast.35), calls=%async_computation | async-start | bytes 2752512 | tf_op jit(solution)/shard_map/all_to_all | solution.py:336
  35.2 0.5 collective-permute-start.4
  35.7 11.1 %collective-permute-done.4 = bf16[160,1280]{1,0:T(8,128)(2,1)S(1)} collective-permute-done((bf16[160,1280]{1,0:T(8,128)(2,1)S(1)}, bf16[160,1280]{1,0:T(8,128)(2,1)S(1)}, u32[]{:S(2)}, u32[]{:S(2)}) %collective-permute-start.4) | collective-permute-done | bytes 409632 | tf_op jit(solution)/shard_map/ppermute | solution.py:310
  46.8 1.2 pad_maximum_fusion.2
  48.0 1.7 collective-permute-start.5
  49.7 1.5 collective-permute-start.6
  51.2 3.1 %all-to-all-done = bf16[8,336,256]{2,1,0:T(8,128)(2,1)S(1)} async-done(((bf16[8,336,256]{2,1,0:T(8,128)(2,1)}), bf16[8,336,256]{2,1,0:T(8,128)(2,1)S(1)}, u32[]{:S(2)}, u32[]{:S(2)}) %all-to-all-start) | async-done | bytes 1376288 | tf_op jit(solution)/shard_map/all_to_all | solution.py:336
  54.4 1.1 copy-done.7
  55.4 0.4 collective-permute-start.7
  56.2 3.0 %slice.42 = bf16[480,2048]{1,0:T(8,128)(2,1)} slice(bf16[640,2048]{1,0:T(8,128)(2,1)} %refs_1_.1), slice={[160:640], [0:2048]} | slice | bytes 3932160 | tf_op jit(solution)/shard_map/slice | solution.py:380
  59.3 0.8 constant_dynamic-update-slice_fusion.6
  60.1 0.8 constant_dynamic-update-slice_fusion.5
  60.9 20.5 %collective-permute-done.7.refs_1_ = bf16[4,320,256]{2,1,0:T(8,128)(2,1)S(1)} collective-permute-done((bf16[4,320,256]{2,1,0:T(8,128)(2,1)S(1)}, bf16[4,320,256]{2,1,0:T(8,128)(2,1)S(1)}, u32[]{:S(2)}, u32[]{:S(2)}) %collective-permute-start.7) | collective-permute-done | bytes 655392 | tf_op jit(solution)/shard_map/ppermute | solution.py:310
  81.3 2.4 collective-permute-done.8.refs_2_
  83.7 1.1 slice.43
  84.8 1.5 collective-permute-start.10
  86.3 1.1 slice.44
  87.5 2.6 collective-permute-start.11
  90.0 0.8 constant_dynamic-update-slice_fusion.4
  90.8 2.4 constant_dynamic-update-slice_fusion.3
  93.3 2.5 constant_dynamic-update-slice_fusion.2
  95.7 1.6 collective-permute-done.10
  97.3 5.6 %collective-permute-done.11 = bf16[240,1280]{1,0:T(8,128)(2,1)S(1)} collective-permute-done((bf16[240,1280]{1,0:T(8,128)(2,1)S(1)}, bf16[240,1280]{1,0:T(8,128)(2,1)S(1)}, u32[]{:S(2)}, u32[]{:S(2)}) %collective-permute-start.11) | collective-permute-done | bytes 614432 | tf_op jit(solution)/shard_map/ppermute | solution.py:304
  102.8 2.3 collective-permute-done.9.refs_3_
  105.2 0.8 copy-done.3
  106.0 0.9 constant_dynamic-update-slice_fusion.1
  106.9 0.9 constant_dynamic-update-slice_fusion.refs_6_
  107.8 0.5 collective-permute-start.20
  108.7 1.7 collective-permute-start.17
  110.8 5.5 %collective-permute-done.12.refs_7_ = bf16[1920,1280]{1,0:T(8,128)(2,1)} collective-permute-done((bf16[1920,1280]{1,0:T(8,128)(2,1)}, bf16[1920,1280]{1,0:T(8,128)(2,1)}, u32[]{:S(2)}, u32[]{:S(2)}) %collective-permute-start.12) | collective-permute-done | bytes 4915232 | tf_op jit(solution)/shard_map/ppermute | solution.py:304
  116.6 0.5 collective-permute-start.14
  117.2 1.1 copy-done.4
  118.2 29.5 %attend.2.refs_10_ = bf16[4,8,64,1280]{3,2,1,0:T(8,128)(2,1)} custom-call(s32[6]{0:T(128)S(1)} %pad_add_fusion.3.info, bf16[4,320,256]{2,1,0:T(8,128)(2,1)S(1)} %get-tuple-element.70.refs_0_, bf16[4,320,256]{2,1,0:T(8,128)(2,1)S(1)} %collective-permute-done.7.refs_1_, bf16[4,320,256]{2,1,0:T(8,128)(2,1)S(1)} %collective-permute-done.8.refs_2_, ...), custom_call_target="tpu_custom_call" | custom-call | flops 16777216000 | bytes 14680064 | tf_op jit(solution)/shard_map/attend/pallas_call | solution.py:148
  148.1 1.5 collective-permute-start.15
  149.6 1.1 constant_dynamic-update-slice_fusion.8
  150.7 2.5 collective-permute-done.16
  153.7 1.8 collective-permute-start.18
  155.5 1.2 slice.46
  156.7 1.7 collective-permute-start.19
  158.4 1.3 pad_maximum_fusion.refs_3_
  159.6 4.4 %collective-permute-done.15.refs_3_ = bf16[4,320,256]{2,1,0:T(8,128)(2,1)S(1)} collective-permute-done((bf16[4,320,256]{2,1,0:T(8,128)(2,1)S(1)}, bf16[4,320,256]{2,1,0:T(8,128)(2,1)S(1)}, u32[]{:S(2)}, u32[]{:S(2)}) %collective-permute-start.15) | collective-permute-done | bytes 655392 | tf_op jit(solution)/shard_map/ppermute | solution.py:310
  164.1 0.5 collective-permute-start.22
  164.6 29.5 %attend.3 = bf16[4,8,64,1280]{3,2,1,0:T(8,128)(2,1)} custom-call(s32[6]{0:T(128)S(1)} %pad_add_fusion.1.info, bf16[4,320,256]{2,1,0:T(8,128)(2,1)S(1)} %get-tuple-element.53.refs_0_, bf16[4,320,256]{2,1,0:T(8,128)(2,1)S(1)} %collective-permute-done.13.refs_1_, ...), custom_call_target="tpu_custom_call", output_to_operand_aliasing={{}: (11, {})} | custom-call | flops 16777216000 | bytes 14680064 | tf_op jit(solution)/shard_map/attend/pallas_call | solution.py:148
  194.2 0.5 collective-permute-start.24
  194.8 2.4 collective-permute-done.23.refs_9_
  197.2 1.9 collective-permute-done.24.refs_10_
  199.1 23.9 %project.1 = bf16[512,2176]{1,0:T(8,128)(2,1)} custom-call(s32[2]{0:T(128)S(1)} %pad_add_fusion.info, bf16[4,512,1280]{2,1,0:T(8,128)(2,1)} %bitcast.42, bf16[640,2048]{1,0:T(8,128)(2,1)} %refs_1_.1, bf16[640,2048]{1,0:T(8,128)(2,1)} %copy-done.15, bf16[640,2048]{1,0:T(8,128)(2,1)} %copy-done.8, bf16[320,2048]{1,0:T(8,128)(2,1)S(1)} %collective-permute-done.18.refs_4_, ...), custom_call_target="tpu_custom_call" | custom-call | flops 15032385536 | bytes 37748736 | tf_op jit(solution)/shard_map/project/pallas_call | solution.py:251
  223.1 1.0 slice.49
  224.4 45.3 %reduce-scatter.2.cloned.1.call-done = bf16[128,2176]{1,0:T(8,128)(2,1)} async-done(((bf16[512,2176]{1,0:T(8,128)(2,1)}), bf16[128,2176]{1,0:T(8,128)(2,1)}) %reduce-scatter.2.cloned.1.call-update) | async-done | bytes 557072 | tf_op jit(solution)/shard_map/reduce_scatter | solution.py:499
  269.7 1.1 convert_element_type.31
  270.9 1.0 fusion.5
  (85 shorter events, 3.7 us)
Async XLA Ops:
  6.5 19.9 %copy-start = (bf16[2048,320]{0,1:T(8,128)(2,1)S(1)}, bf16[2048,320]{0,1:T(8,128)(2,1)}, u32[]{:S(2)}) copy-start(bf16[2048,320]{0,1:T(8,128)(2,1)} %param.13) | copy-start | bytes 3932164
  6.5 18.9 %copy-start.6 = (s32[1,32]{1,0:T(1,128)S(1)}, s32[1,32]{1,0:T(1,128)}, u32[]{:S(2)}) copy-start(s32[1,32]{1,0:T(1,128)} %param.15) | copy-start | bytes 388
  8.6 26.5 %collective-permute-start = (bf16[160,1280]{1,0:T(8,128)(2,1)}, bf16[160,1280]{1,0:T(8,128)(2,1)S(1)}, u32[]{:S(2)}, u32[]{:S(2)}) collective-permute-start(bf16[160,1280]{1,0:T(8,128)(2,1)} %bitcast_select_fusion), channel_id=1, source_target_pairs={{0,1},{1,0},{2,3},{3,2},{4,5},{5,4},{6,7},{7,6},{8,9},{9,8},{10,11... | collective-permute-start | bytes 1228808 | tf_op jit(solution)/shard_map/ppermute | solution.py:310
  11.7 23.5 %collective-permute-start.1 = (bf16[160,1280]{1,0:T(8,128)(2,1)}, bf16[160,1280]{1,0:T(8,128)(2,1)S(1)}, u32[]{:S(2)}, u32[]{:S(2)}) collective-permute-start(bf16[160,1280]{1,0:T(8,128)(2,1)} %bitcast_select_fusion), channel_id=1, source_target_pairs={{0,2},{1,3},{2,0},{3,1},{4,6},{5,7},{6,4},{7,5},{8,10},{9,11},{10,... | collective-permute-start | bytes 1228808 | tf_op jit(solution)/shard_map/ppermute | solution.py:310
  16.2 19.0 %collective-permute-start.2 = (bf16[160,2048]{1,0:T(8,128)(2,1)}, bf16[160,2048]{1,0:T(8,128)(2,1)}, u32[]{:S(2)}, u32[]{:S(2)}) collective-permute-start(bf16[160,2048]{1,0:T(8,128)(2,1)} %slice.40), channel_id=1, source_target_pairs={{0,8},{4,12},{8,0},{12,4},{16,24},{20,28},{24,16},{28,20},{1,9},{5... | collective-permute-start | bytes 1966088 | tf_op jit(solution)/shard_map/ppermute | solution.py:304
  17.7 17.5 %collective-permute-start.3 = (bf16[160,2048]{1,0:T(8,128)(2,1)}, bf16[160,2048]{1,0:T(8,128)(2,1)}, u32[]{:S(2)}, u32[]{:S(2)}) collective-permute-start(bf16[160,2048]{1,0:T(8,128)(2,1)} %slice.40), channel_id=1, source_target_pairs={{0,16},{4,20},{8,24},{12,28},{16,0},{20,4},{24,8},{28,12},{1,17},{... | collective-permute-start | bytes 1966088 | tf_op jit(solution)/shard_map/ppermute | solution.py:304
  31.3 22.9 %all-to-all-start = ((bf16[8,336,256]{2,1,0:T(8,128)(2,1)}), bf16[8,336,256]{2,1,0:T(8,128)(2,1)S(1)}, u32[]{:S(2)}, u32[]{:S(2)}) async-start(bf16[8,336,256]{2,1,0:T(8,128)(2,1)} %bitcast.35), calls=%async_computation | async-start | bytes 2752512 | tf_op jit(solution)/shard_map/all_to_all | solution.py:336
  34.9 234.8 %reduce-scatter.2.cloned.1.call-start = ((), (), s32[]{:S(2)}) async-start(), calls=%async_computation.2 | async-start | bytes 2785280 | tf_op jit(solution)/shard_map/reduce_scatter | solution.py:499
  35.2 19.2 %copy-start.9 = (bf16[160,1280]{1,0:T(8,128)(2,1)}, bf16[160,1280]{1,0:T(8,128)(2,1)S(1)}, u32[]{:S(2)}) copy-start(bf16[160,1280]{1,0:T(8,128)(2,1)S(1)} %collective-permute-done) | copy-start | bytes 1228804
  35.2 20.3 %copy-start.11 = (bf16[160,1280]{1,0:T(8,128)(2,1)}, bf16[160,1280]{1,0:T(8,128)(2,1)S(1)}, u32[]{:S(2)}) copy-start(bf16[160,1280]{1,0:T(8,128)(2,1)S(1)} %collective-permute-done.1) | copy-start | bytes 1228804
  35.2 11.6 %collective-permute-start.4 = (bf16[160,1280]{1,0:T(8,128)(2,1)S(1)}, bf16[160,1280]{1,0:T(8,128)(2,1)S(1)}, u32[]{:S(2)}, u32[]{:S(2)}) collective-permute-start(bf16[160,1280]{1,0:T(8,128)(2,1)S(1)} %collective-permute-done.1), channel_id=1, source_target_pairs={{0,1},{1,0},{2,3},{3,2},{4,5},{5,4},{6,7},{7,6},{8,9},{9,8},{10,11... | collective-permute-start | bytes 1228808 | tf_op jit(solution)/shard_map/ppermute | solution.py:310
  46.8 4.3 %copy-start.13 = (bf16[160,1280]{1,0:T(8,128)(2,1)}, bf16[160,1280]{1,0:T(8,128)(2,1)S(1)}, u32[]{:S(2)}) copy-start(bf16[160,1280]{1,0:T(8,128)(2,1)S(1)} %collective-permute-done.4) | copy-start | bytes 1228804
  48.0 35.7 %collective-permute-start.5 = (bf16[480,1280]{1,0:T(8,128)(2,1)}, bf16[480,1280]{1,0:T(8,128)(2,1)}, u32[]{:S(2)}, u32[]{:S(2)}) collective-permute-start(bf16[480,1280]{1,0:T(8,128)(2,1)} %pad_maximum_fusion.2), channel_id=1, source_target_pairs={{0,8},{4,12},{8,0},{12,4},{16,24},{20,28},{24,16},{28,20},{1,9},{5... | collective-permute-start | bytes 3686408 | tf_op jit(solution)/shard_map/ppermute | solution.py:304
  49.7 34.0 %collective-permute-start.6 = (bf16[480,1280]{1,0:T(8,128)(2,1)}, bf16[480,1280]{1,0:T(8,128)(2,1)}, u32[]{:S(2)}, u32[]{:S(2)}) collective-permute-start(bf16[480,1280]{1,0:T(8,128)(2,1)} %pad_maximum_fusion.2), channel_id=1, source_target_pairs={{0,16},{4,20},{8,24},{12,28},{16,0},{20,4},{24,8},{28,12},{1,17},{... | collective-permute-start | bytes 3686408 | tf_op jit(solution)/shard_map/ppermute | solution.py:304
  54.3 1.2 copy-start.7
  55.4 3.8 %copy-start.10 = (bf16[160,1280]{1,0:T(8,128)(2,1)S(1)}, bf16[160,1280]{1,0:T(8,128)(2,1)}, u32[]{:S(2)}) copy-start(bf16[160,1280]{1,0:T(8,128)(2,1)} %copy-done.9) | copy-start | bytes 1228804
  55.4 25.9 %collective-permute-start.7 = (bf16[4,320,256]{2,1,0:T(8,128)(2,1)S(1)}, bf16[4,320,256]{2,1,0:T(8,128)(2,1)S(1)}, u32[]{:S(2)}, u32[]{:S(2)}) collective-permute-start(bf16[4,320,256]{2,1,0:T(8,128)(2,1)S(1)} %get-tuple-element.70.refs_0_), channel_id=1, source_target_pairs={{0,1},{1,0},{2,3},{3,2},{4,5},{5,4},{6,7},{7,6},{8,9},{9,8},{10,11... | collective-permute-start | bytes 1966088 | tf_op jit(solution)/shard_map/ppermute | solution.py:310
  55.9 4.2 %copy-start.12 = (bf16[160,1280]{1,0:T(8,128)(2,1)S(1)}, bf16[160,1280]{1,0:T(8,128)(2,1)}, u32[]{:S(2)}) copy-start(bf16[160,1280]{1,0:T(8,128)(2,1)} %copy-done.11) | copy-start | bytes 1228804
  55.9 27.8 %collective-permute-start.8 = (bf16[4,320,256]{2,1,0:T(8,128)(2,1)S(1)}, bf16[4,320,256]{2,1,0:T(8,128)(2,1)S(1)}, u32[]{:S(2)}, u32[]{:S(2)}) collective-permute-start(bf16[4,320,256]{2,1,0:T(8,128)(2,1)S(1)} %get-tuple-element.70.refs_0_), channel_id=1, source_target_pairs={{0,2},{1,3},{2,0},{3,1},{4,6},{5,7},{6,4},{7,5},{8,10},{9,11},{10,... | collective-permute-start | bytes 1966088 | tf_op jit(solution)/shard_map/ppermute | solution.py:310
  59.3 30.8 %copy-start.14 = (bf16[160,1280]{1,0:T(8,128)(2,1)S(1)}, bf16[160,1280]{1,0:T(8,128)(2,1)}, u32[]{:S(2)}) copy-start(bf16[160,1280]{1,0:T(8,128)(2,1)} %copy-done.13) | copy-start | bytes 1228804
  84.8 12.4 %collective-permute-start.10 = (bf16[240,1280]{1,0:T(8,128)(2,1)S(1)}, bf16[240,1280]{1,0:T(8,128)(2,1)S(1)}, u32[]{:S(2)}, u32[]{:S(2)}) collective-permute-start(bf16[240,1280]{1,0:T(8,128)(2,1)S(1)} %slice.43), channel_id=1, source_target_pairs={{0,16},{4,20},{8,24},{12,28},{16,0},{20,4},{24,8},{28,12},{1,17},{... | collective-permute-start | bytes 1843208 | tf_op jit(solution)/shard_map/ppermute | solution.py:304
  87.5 15.4 %collective-permute-start.11 = (bf16[240,1280]{1,0:T(8,128)(2,1)S(1)}, bf16[240,1280]{1,0:T(8,128)(2,1)S(1)}, u32[]{:S(2)}, u32[]{:S(2)}) collective-permute-start(bf16[240,1280]{1,0:T(8,128)(2,1)S(1)} %slice.44), channel_id=1, source_target_pairs={{0,8},{4,12},{8,0},{12,4},{16,24},{20,28},{24,16},{28,20},{1,9},{5... | collective-permute-start | bytes 1843208 | tf_op jit(solution)/shard_map/ppermute | solution.py:304
  90.0 15.2 %collective-permute-start.9 = (bf16[4,320,256]{2,1,0:T(8,128)(2,1)S(1)}, bf16[4,320,256]{2,1,0:T(8,128)(2,1)S(1)}, u32[]{:S(2)}, u32[]{:S(2)}) collective-permute-start(bf16[4,320,256]{2,1,0:T(8,128)(2,1)S(1)} %collective-permute-done.8.refs_2_), channel_id=1, source_target_pairs={{0,1},{1,0},{2,3},{3,2},{4,5},{5,4},{6,7},{7,6},{8,9},{9,8},{10,11... | collective-permute-start | bytes 1966088 | tf_op jit(solution)/shard_map/ppermute | solution.py:310
  93.2 17.2 %copy-start.17 = (f32[1280]{0:T(1024)S(1)}, f32[1280]{0:T(1024)}, u32[]{:S(2)}) copy-start(f32[1280]{0:T(1024)} %param.19) | copy-start | bytes 15364
  93.2 17.5 %copy-start.16 = (f32[1280]{0:T(1024)S(1)}, f32[1280]{0:T(1024)}, u32[]{:S(2)}) copy-start(f32[1280]{0:T(1024)} %param.20) | copy-start | bytes 15364
  93.3 23.9 %copy-start.2 = (bf16[320,1280]{1,0:T(8,128)(2,1)S(1)}, bf16[320,1280]{1,0:T(8,128)(2,1)}, u32[]{:S(2)}) copy-start(bf16[320,1280]{1,0:T(8,128)(2,1)} %refs_5_.3) | copy-start | bytes 2457604
  105.2 0.8 copy-start.3
  107.8 8.5 %collective-permute-start.12 = (bf16[1920,1280]{1,0:T(8,128)(2,1)}, bf16[1920,1280]{1,0:T(8,128)(2,1)}, u32[]{:S(2)}, u32[]{:S(2)}) collective-permute-start(bf16[1920,1280]{1,0:T(8,128)(2,1)} %constant_dynamic-update-slice_fusion.refs_6_), channel_id=1, source_target_pairs={{0,4},{4,0},{8,12},{12,8},{16,20},{20,16},{24,28},{28,24},{1,5},{5... | collective-permute-start | bytes 14745608 | tf_op jit(solution)/shard_map/ppermute | solution.py:304
  107.8 87.0 %collective-permute-start.20 = (bf16[640,2048]{1,0:T(8,128)(2,1)}, bf16[640,2048]{1,0:T(8,128)(2,1)}, u32[]{:S(2)}, u32[]{:S(2)}) collective-permute-start(bf16[640,2048]{1,0:T(8,128)(2,1)} %refs_1_.1), channel_id=1, source_target_pairs={{0,4},{4,0},{8,12},{12,8},{16,20},{20,16},{24,28},{28,24},{1,5},{5... | collective-permute-start | bytes 7864328 | tf_op jit(solution)/shard_map/ppermute | solution.py:304
  108.3 44.9 %collective-permute-start.16 = (bf16[480,2048]{1,0:T(8,128)(2,1)}, bf16[480,2048]{1,0:T(8,128)(2,1)S(1)}, u32[]{:S(2)}, u32[]{:S(2)}) collective-permute-start(bf16[480,2048]{1,0:T(8,128)(2,1)} %slice.42), channel_id=1, source_target_pairs={{0,8},{4,12},{8,0},{12,4},{16,24},{20,28},{24,16},{28,20},{1,9},{5... | collective-permute-start | bytes 5898248 | tf_op jit(solution)/shard_map/ppermute | solution.py:304
  108.7 44.7 %collective-permute-start.17 = (bf16[480,2048]{1,0:T(8,128)(2,1)}, bf16[480,2048]{1,0:T(8,128)(2,1)S(1)}, u32[]{:S(2)}, u32[]{:S(2)}) collective-permute-start(bf16[480,2048]{1,0:T(8,128)(2,1)} %slice.42), channel_id=1, source_target_pairs={{0,16},{4,20},{8,24},{12,28},{16,0},{20,4},{24,8},{28,12},{1,17},{... | collective-permute-start | bytes 5898248 | tf_op jit(solution)/shard_map/ppermute | solution.py:304
  116.3 31.4 %collective-permute-start.13 = (bf16[4,320,256]{2,1,0:T(8,128)(2,1)S(1)}, bf16[4,320,256]{2,1,0:T(8,128)(2,1)S(1)}, u32[]{:S(2)}, u32[]{:S(2)}) collective-permute-start(bf16[4,320,256]{2,1,0:T(8,128)(2,1)S(1)} %get-tuple-element.53.refs_0_), channel_id=1, source_target_pairs={{0,1},{1,0},{2,3},{3,2},{4,5},{5,4},{6,7},{7,6},{8,9},{9,8},{10,11... | collective-permute-start | bytes 1966088 | tf_op jit(solution)/shard_map/ppermute | solution.py:310
  116.6 31.5 %collective-permute-start.14 = (bf16[4,320,256]{2,1,0:T(8,128)(2,1)S(1)}, bf16[4,320,256]{2,1,0:T(8,128)(2,1)S(1)}, u32[]{:S(2)}, u32[]{:S(2)}) collective-permute-start(bf16[4,320,256]{2,1,0:T(8,128)(2,1)S(1)} %get-tuple-element.53.refs_0_), channel_id=1, source_target_pairs={{0,2},{1,3},{2,0},{3,1},{4,6},{5,7},{6,4},{7,5},{8,10},{9,11},{10,... | collective-permute-start | bytes 1966088 | tf_op jit(solution)/shard_map/ppermute | solution.py:310
  117.2 1.1 copy-start.4
  148.1 16.0 %collective-permute-start.15 = (bf16[4,320,256]{2,1,0:T(8,128)(2,1)S(1)}, bf16[4,320,256]{2,1,0:T(8,128)(2,1)S(1)}, u32[]{:S(2)}, u32[]{:S(2)}) collective-permute-start(bf16[4,320,256]{2,1,0:T(8,128)(2,1)S(1)} %collective-permute-done.14.refs_2_), channel_id=1, source_target_pairs={{0,1},{1,0},{2,3},{3,2},{4,5},{5,4},{6,7},{7,6},{8,9},{9,8},{10,11... | collective-permute-start | bytes 1966088 | tf_op jit(solution)/shard_map/ppermute | solution.py:310
  153.6 10.5 %copy-start.15 = (bf16[640,2048]{1,0:T(8,128)(2,1)}, bf16[640,2048]{1,0:T(8,128)(2,1)S(1)}, u32[]{:S(2)}) copy-start(bf16[640,2048]{1,0:T(8,128)(2,1)S(1)} %constant_dynamic-update-slice_fusion.7.refs_2_) | copy-start | bytes 7864324
  153.7 40.4 %collective-permute-start.18 = (bf16[320,2048]{1,0:T(8,128)(2,1)S(1)}, bf16[320,2048]{1,0:T(8,128)(2,1)S(1)}, u32[]{:S(2)}, u32[]{:S(2)}) collective-permute-start(bf16[320,2048]{1,0:T(8,128)(2,1)S(1)} %slice.59), channel_id=1, source_target_pairs={{0,16},{4,20},{8,24},{12,28},{16,0},{20,4},{24,8},{28,12},{1,17},{... | collective-permute-start | bytes 3932168 | tf_op jit(solution)/shard_map/ppermute | solution.py:304
  156.7 37.4 %collective-permute-start.19 = (bf16[320,2048]{1,0:T(8,128)(2,1)}, bf16[320,2048]{1,0:T(8,128)(2,1)S(1)}, u32[]{:S(2)}, u32[]{:S(2)}) collective-permute-start(bf16[320,2048]{1,0:T(8,128)(2,1)} %slice.46), channel_id=1, source_target_pairs={{0,8},{4,12},{8,0},{12,4},{16,24},{20,28},{24,16},{28,20},{1,9},{5... | collective-permute-start | bytes 3932168 | tf_op jit(solution)/shard_map/ppermute | solution.py:304
  159.6 34.5 %copy-start.8 = (bf16[640,2048]{1,0:T(8,128)(2,1)}, bf16[640,2048]{1,0:T(8,128)(2,1)S(1)}, u32[]{:S(2)}) copy-start(bf16[640,2048]{1,0:T(8,128)(2,1)S(1)} %pad_maximum_fusion.refs_3_) | copy-start | bytes 7864324
  159.6 39.5 %copy-start.5 = (f32[2048]{0:T(1024)S(1)}, f32[2048]{0:T(1024)}, u32[]{:S(2)}) copy-start(f32[2048]{0:T(1024)} %param.22) | copy-start | bytes 24580
  164.1 35.0 %collective-permute-start.21 = (bf16[640,2048]{1,0:T(8,128)(2,1)S(1)}, bf16[640,2048]{1,0:T(8,128)(2,1)}, u32[]{:S(2)}, u32[]{:S(2)}) collective-permute-start(bf16[640,2048]{1,0:T(8,128)(2,1)S(1)} %constant_dynamic-update-slice_fusion.7.refs_2_), channel_id=1, source_target_pairs={{0,4},{4,0},{8,12},{12,8},{16,20},{20,16},{24,28},{28,24},{1,5},{5... | collective-permute-start | bytes 7864328 | tf_op jit(solution)/shard_map/ppermute | solution.py:304
  164.1 35.0 %collective-permute-start.22 = (bf16[640,2048]{1,0:T(8,128)(2,1)S(1)}, bf16[640,2048]{1,0:T(8,128)(2,1)}, u32[]{:S(2)}, u32[]{:S(2)}) collective-permute-start(bf16[640,2048]{1,0:T(8,128)(2,1)S(1)} %pad_maximum_fusion.refs_3_), channel_id=1, source_target_pairs={{0,4},{4,0},{8,12},{12,8},{16,20},{20,16},{24,28},{28,24},{1,5},{5... | collective-permute-start | bytes 7864328 | tf_op jit(solution)/shard_map/ppermute | solution.py:304
  194.1 3.1 %collective-permute-start.23 = (bf16[320,2048]{1,0:T(8,128)(2,1)S(1)}, bf16[320,2048]{1,0:T(8,128)(2,1)S(1)}, u32[]{:S(2)}, u32[]{:S(2)}) collective-permute-start(bf16[320,2048]{1,0:T(8,128)(2,1)S(1)} %collective-permute-done.18.refs_4_), channel_id=1, source_target_pairs={{0,4},{4,0},{8,12},{12,8},{16,20},{20,16},{24,28},{28,24},{1,5},{5... | collective-permute-start | bytes 3932168 | tf_op jit(solution)/shard_map/ppermute | solution.py:304
  194.2 4.9 %collective-permute-start.24 = (bf16[320,2048]{1,0:T(8,128)(2,1)S(1)}, bf16[320,2048]{1,0:T(8,128)(2,1)S(1)}, u32[]{:S(2)}, u32[]{:S(2)}) collective-permute-start(bf16[320,2048]{1,0:T(8,128)(2,1)S(1)} %collective-permute-done.19.refs_5_), channel_id=1, source_target_pairs={{0,4},{4,0},{8,12},{12,8},{16,20},{20,16},{24,28},{28,24},{1,5},{5... | collective-permute-start | bytes 3932168 | tf_op jit(solution)/shard_map/ppermute | solution.py:304
  223.0 48.9 %copy-start.1 = (bf16[2048,320]{0,1:T(8,128)(2,1)S(1)}, bf16[2048,320]{0,1:T(8,128)(2,1)}, u32[]{:S(2)}) copy-start(bf16[2048,320]{0,1:T(8,128)(2,1)} %param.13) | copy-start | bytes 3932164
Sparse Core Ops, SparseCore 0:
  223.2 46.4 reduce-scatter.1

commit v12 on v11

--- a/solution.py
+++ b/solution.py
@@ -259,12 +259,12 @@
             out_specs=pl.BlockSpec((rows, kvw + 128), lambda i, s: (0, 0)),
             scratch_shapes=[
                 pltpu.VMEM((MERGE, rows, DV), BF),
-                pltpu.VMEM((3, DV, units // 2), BF),
+                pltpu.VMEM((4, DV, units // 2), BF),
                 pltpu.VMEM((units, kvw), BF),
                 pltpu.VMEM((rows, units // 2), F32),
                 pltpu.VMEM((rows, units), BF),
                 pltpu.SemaphoreType.DMA((MERGE,)),
-                pltpu.SemaphoreType.DMA((3, 4)),
+                pltpu.SemaphoreType.DMA((4, 4)),
                 pltpu.SemaphoreType.DMA,
             ],
         ),

time: 279 us -> 277 us (level)
  no operation moved by 1% of the time
where the time goes in v12:
time: 277 us; the launch traced here: 276 us
  waiting for transfers between devices  109 us (39%)
  Pallas kernels  80.7 us (29%)
  starting transfers between devices  30.4 us (11%)
  local copies, waits for them, and re-layouts  27.8 us (10%)
  between operations  13.7 us (5%)
  other arithmetic  11.4 us (4%)
  matrix products  3.45 us (1%)
    pallas_call x2, Pallas kernels, attend(): pl.pallas_call(functools.partial(attend_kernel, tp, moves, len(weights),...  59.2 us
    reduce_scatter x1, waiting for transfers between devices, shards(): lax.psum_scatter(partial_value, 'tp', scatter_dimension=0, tiled=True)  45.3 us
    ppermute x9, waiting for transfers between devices, tp_xor(): return lax.ppermute(x, 'tp', [(i, i ^ d) for i in range(tp)])  41.2 us
    pallas_call x1, Pallas kernels, project(): pl.pallas_call(functools.partial(project_kernel, moves, position, len(wei...  21.5 us
    ppermute x16, waiting for transfers between devices, xor(): return lax.ppermute(x, 'seq', [(i, i ^ d) for i in range(seq_count)])  19.4 us
    ppermute x16, starting transfers between devices, xor(): return lax.ppermute(x, 'seq', [(i, i ^ d) for i in range(seq_count)])  17.4 us
    unnamed x43, local copies, waits for them, and re-layouts  12.3 us
    ppermute x9, starting transfers between devices, tp_xor(): return lax.ppermute(x, 'tp', [(i, i ^ d) for i in range(tp)])  9.43 us
  transfers between devices with their start and end apart: 27, of which 15 were waited for; matrix products, arithmetic and copies ran while one was open for 12% of the time, Pallas kernels for 21%

profile of v12, /device:TPU:0, one launch (start us, length us, event | category | flops | bytes accessed | tf_op | source)
XLA Modules:
  0.0 276.5 jit_solution(6143224568921882403)
XLA Ops:
  6.5 2.1 bitcast_select_fusion
  8.6 3.0 %collective-permute-start = (bf16[160,1280]{1,0:T(8,128)(2,1)}, bf16[160,1280]{1,0:T(8,128)(2,1)S(1)}, u32[]{:S(2)}, u32[]{:S(2)}) collective-permute-start(bf16[160,1280]{1,0:T(8,128)(2,1)} %bitcast_select_fusion), channel_id=1, source_target_pairs={{0,1},{1,0},{2,3},{3,2},{4,5},{5,4},{6,7},{7,6},{8,9},{9,8},{10,11... | collective-permute-start | bytes 1228808 | tf_op jit(solution)/shard_map/ppermute | solution.py:310
  11.7 2.6 collective-permute-start.1
  14.2 2.0 slice.40
  16.2 1.5 collective-permute-start.2
  17.7 1.5 collective-permute-start.3
  19.2 2.3 sort.17
  21.5 1.3 fusion.11
  22.9 1.8 compare_convert_fusion
  24.7 0.7 gather_fusion.1
  25.4 0.7 gather_fusion
  26.4 3.5 %fusion.3 = bf16[320,2048]{1,0:T(8,128)(2,1)S(1)} fusion(bf16[2048,320]{0,1:T(8,128)(2,1)S(1)} %copy-done, s32[2048]{0:T(1024)S(1)} %add.115), kind=kOutput, calls=%fused_computation.7 | convolution fusion | flops 2689204224 | bytes 2629632 | tf_op jit(solution)/shard_map/dot_general | solution.py:328
  30.2 1.2 copy.18
  31.3 3.6 %all-to-all-start = ((bf16[8,336,256]{2,1,0:T(8,128)(2,1)}), bf16[8,336,256]{2,1,0:T(8,128)(2,1)S(1)}, u32[]{:S(2)}, u32[]{:S(2)}) async-start(bf16[8,336,256]{2,1,0:T(8,128)(2,1)} %bitcast.35), calls=%async_computation | async-start | bytes 2752512 | tf_op jit(solution)/shard_map/all_to_all | solution.py:336
  35.0 0.5 collective-permute-start.4
  35.6 11.3 %collective-permute-done.4 = bf16[160,1280]{1,0:T(8,128)(2,1)S(1)} collective-permute-done((bf16[160,1280]{1,0:T(8,128)(2,1)S(1)}, bf16[160,1280]{1,0:T(8,128)(2,1)S(1)}, u32[]{:S(2)}, u32[]{:S(2)}) %collective-permute-start.4) | collective-permute-done | bytes 409632 | tf_op jit(solution)/shard_map/ppermute | solution.py:310
  46.8 1.2 pad_maximum_fusion.2
  48.0 1.7 collective-permute-start.5
  49.7 1.5 collective-permute-start.6
  51.2 3.1 %all-to-all-done = bf16[8,336,256]{2,1,0:T(8,128)(2,1)S(1)} async-done(((bf16[8,336,256]{2,1,0:T(8,128)(2,1)}), bf16[8,336,256]{2,1,0:T(8,128)(2,1)S(1)}, u32[]{:S(2)}, u32[]{:S(2)}) %all-to-all-start) | async-done | bytes 1376288 | tf_op jit(solution)/shard_map/all_to_all | solution.py:336
  54.4 1.1 copy-done.7
  55.4 0.4 collective-permute-start.7
  56.2 3.0 %slice.42 = bf16[480,2048]{1,0:T(8,128)(2,1)} slice(bf16[640,2048]{1,0:T(8,128)(2,1)} %refs_1_.1), slice={[160:640], [0:2048]} | slice | bytes 3932160 | tf_op jit(solution)/shard_map/slice | solution.py:380
  59.3 0.8 constant_dynamic-update-slice_fusion.6
  60.1 0.8 constant_dynamic-update-slice_fusion.5
  60.9 20.5 %collective-permute-done.7.refs_1_ = bf16[4,320,256]{2,1,0:T(8,128)(2,1)S(1)} collective-permute-done((bf16[4,320,256]{2,1,0:T(8,128)(2,1)S(1)}, bf16[4,320,256]{2,1,0:T(8,128)(2,1)S(1)}, u32[]{:S(2)}, u32[]{:S(2)}) %collective-permute-start.7) | collective-permute-done | bytes 655392 | tf_op jit(solution)/shard_map/ppermute | solution.py:310
  81.3 2.4 collective-permute-done.8.refs_2_
  83.7 1.1 slice.43
  84.8 1.5 collective-permute-start.10
  86.3 1.1 slice.44
  87.5 2.6 collective-permute-start.11
  90.0 0.8 constant_dynamic-update-slice_fusion.4
  90.8 2.4 constant_dynamic-update-slice_fusion.3
  93.3 2.5 constant_dynamic-update-slice_fusion.2
  95.7 1.6 collective-permute-done.10
  97.3 5.6 %collective-permute-done.11 = bf16[240,1280]{1,0:T(8,128)(2,1)S(1)} collective-permute-done((bf16[240,1280]{1,0:T(8,128)(2,1)S(1)}, bf16[240,1280]{1,0:T(8,128)(2,1)S(1)}, u32[]{:S(2)}, u32[]{:S(2)}) %collective-permute-start.11) | collective-permute-done | bytes 614432 | tf_op jit(solution)/shard_map/ppermute | solution.py:304
  102.8 2.3 collective-permute-done.9.refs_3_
  105.2 0.8 copy-done.3
  106.0 0.9 constant_dynamic-update-slice_fusion.1
  106.9 0.9 constant_dynamic-update-slice_fusion.refs_6_
  107.8 0.5 collective-permute-start.20
  108.7 1.7 collective-permute-start.17
  110.8 5.5 %collective-permute-done.12.refs_7_ = bf16[1920,1280]{1,0:T(8,128)(2,1)} collective-permute-done((bf16[1920,1280]{1,0:T(8,128)(2,1)}, bf16[1920,1280]{1,0:T(8,128)(2,1)}, u32[]{:S(2)}, u32[]{:S(2)}) %collective-permute-start.12) | collective-permute-done | bytes 4915232 | tf_op jit(solution)/shard_map/ppermute | solution.py:304
  116.6 0.5 collective-permute-start.14
  117.2 1.1 copy-done.4
  118.2 29.7 %attend.2.refs_10_ = bf16[4,8,64,1280]{3,2,1,0:T(8,128)(2,1)} custom-call(s32[6]{0:T(128)S(1)} %pad_add_fusion.3.info, bf16[4,320,256]{2,1,0:T(8,128)(2,1)S(1)} %get-tuple-element.70.refs_0_, bf16[4,320,256]{2,1,0:T(8,128)(2,1)S(1)} %collective-permute-done.7.refs_1_, bf16[4,320,256]{2,1,0:T(8,128)(2,1)S(1)} %collective-permute-done.8.refs_2_, ...), custom_call_target="tpu_custom_call" | custom-call | flops 16777216000 | bytes 14680064 | tf_op jit(solution)/shard_map/attend/pallas_call | solution.py:148
  148.1 1.7 collective-permute-start.15
  149.8 1.1 constant_dynamic-update-slice_fusion.8
  150.9 2.3 collective-permute-done.16
  153.7 1.8 collective-permute-start.18
  155.5 1.2 slice.46
  156.7 1.7 collective-permute-start.19
  158.4 1.3 pad_maximum_fusion.refs_3_
  159.6 4.6 %collective-permute-done.15.refs_3_ = bf16[4,320,256]{2,1,0:T(8,128)(2,1)S(1)} collective-permute-done((bf16[4,320,256]{2,1,0:T(8,128)(2,1)S(1)}, bf16[4,320,256]{2,1,0:T(8,128)(2,1)S(1)}, u32[]{:S(2)}, u32[]{:S(2)}) %collective-permute-start.15) | collective-permute-done | bytes 655392 | tf_op jit(solution)/shard_map/ppermute | solution.py:310
  164.2 0.5 collective-permute-start.22
  164.8 29.5 %attend.3 = bf16[4,8,64,1280]{3,2,1,0:T(8,128)(2,1)} custom-call(s32[6]{0:T(128)S(1)} %pad_add_fusion.1.info, bf16[4,320,256]{2,1,0:T(8,128)(2,1)S(1)} %get-tuple-element.53.refs_0_, bf16[4,320,256]{2,1,0:T(8,128)(2,1)S(1)} %collective-permute-done.13.refs_1_, ...), custom_call_target="tpu_custom_call", output_to_operand_aliasing={{}: (11, {})} | custom-call | flops 16777216000 | bytes 14680064 | tf_op jit(solution)/shard_map/attend/pallas_call | solution.py:148
  194.4 0.5 collective-permute-start.24
  195.0 2.4 collective-permute-done.23.refs_9_
  197.4 1.9 collective-permute-done.24.refs_10_
  199.3 21.5 %project.1 = bf16[512,2176]{1,0:T(8,128)(2,1)} custom-call(s32[2]{0:T(128)S(1)} %pad_add_fusion.info, bf16[4,512,1280]{2,1,0:T(8,128)(2,1)} %bitcast.42, bf16[640,2048]{1,0:T(8,128)(2,1)} %refs_1_.1, bf16[640,2048]{1,0:T(8,128)(2,1)} %copy-done.15, bf16[640,2048]{1,0:T(8,128)(2,1)} %copy-done.8, bf16[320,2048]{1,0:T(8,128)(2,1)S(1)} %collective-permute-done.18.refs_4_, ...), custom_call_target="tpu_custom_call" | custom-call | flops 15032385536 | bytes 37748736 | tf_op jit(solution)/shard_map/project/pallas_call | solution.py:251
  220.8 1.0 slice.49
  222.1 45.3 %reduce-scatter.2.cloned.1.call-done = bf16[128,2176]{1,0:T(8,128)(2,1)} async-done(((bf16[512,2176]{1,0:T(8,128)(2,1)}), bf16[128,2176]{1,0:T(8,128)(2,1)}) %reduce-scatter.2.cloned.1.call-update) | async-done | bytes 557072 | tf_op jit(solution)/shard_map/reduce_scatter | solution.py:499
  267.4 1.1 convert_element_type.31
  268.7 1.0 fusion.5
  (85 shorter events, 3.4 us)
Async XLA Ops:
  6.5 19.9 %copy-start = (bf16[2048,320]{0,1:T(8,128)(2,1)S(1)}, bf16[2048,320]{0,1:T(8,128)(2,1)}, u32[]{:S(2)}) copy-start(bf16[2048,320]{0,1:T(8,128)(2,1)} %param.13) | copy-start | bytes 3932164
  6.5 18.9 %copy-start.6 = (s32[1,32]{1,0:T(1,128)S(1)}, s32[1,32]{1,0:T(1,128)}, u32[]{:S(2)}) copy-start(s32[1,32]{1,0:T(1,128)} %param.15) | copy-start | bytes 388
  8.6 26.4 %collective-permute-start = (bf16[160,1280]{1,0:T(8,128)(2,1)}, bf16[160,1280]{1,0:T(8,128)(2,1)S(1)}, u32[]{:S(2)}, u32[]{:S(2)}) collective-permute-start(bf16[160,1280]{1,0:T(8,128)(2,1)} %bitcast_select_fusion), channel_id=1, source_target_pairs={{0,1},{1,0},{2,3},{3,2},{4,5},{5,4},{6,7},{7,6},{8,9},{9,8},{10,11... | collective-permute-start | bytes 1228808 | tf_op jit(solution)/shard_map/ppermute | solution.py:310
  11.7 23.3 %collective-permute-start.1 = (bf16[160,1280]{1,0:T(8,128)(2,1)}, bf16[160,1280]{1,0:T(8,128)(2,1)S(1)}, u32[]{:S(2)}, u32[]{:S(2)}) collective-permute-start(bf16[160,1280]{1,0:T(8,128)(2,1)} %bitcast_select_fusion), channel_id=1, source_target_pairs={{0,2},{1,3},{2,0},{3,1},{4,6},{5,7},{6,4},{7,5},{8,10},{9,11},{10,... | collective-permute-start | bytes 1228808 | tf_op jit(solution)/shard_map/ppermute | solution.py:310
  16.2 18.8 %collective-permute-start.2 = (bf16[160,2048]{1,0:T(8,128)(2,1)}, bf16[160,2048]{1,0:T(8,128)(2,1)}, u32[]{:S(2)}, u32[]{:S(2)}) collective-permute-start(bf16[160,2048]{1,0:T(8,128)(2,1)} %slice.40), channel_id=1, source_target_pairs={{0,8},{4,12},{8,0},{12,4},{16,24},{20,28},{24,16},{28,20},{1,9},{5... | collective-permute-start | bytes 1966088 | tf_op jit(solution)/shard_map/ppermute | solution.py:304
  17.7 17.3 %collective-permute-start.3 = (bf16[160,2048]{1,0:T(8,128)(2,1)}, bf16[160,2048]{1,0:T(8,128)(2,1)}, u32[]{:S(2)}, u32[]{:S(2)}) collective-permute-start(bf16[160,2048]{1,0:T(8,128)(2,1)} %slice.40), channel_id=1, source_target_pairs={{0,16},{4,20},{8,24},{12,28},{16,0},{20,4},{24,8},{28,12},{1,17},{... | collective-permute-start | bytes 1966088 | tf_op jit(solution)/shard_map/ppermute | solution.py:304
  31.3 22.9 %all-to-all-start = ((bf16[8,336,256]{2,1,0:T(8,128)(2,1)}), bf16[8,336,256]{2,1,0:T(8,128)(2,1)S(1)}, u32[]{:S(2)}, u32[]{:S(2)}) async-start(bf16[8,336,256]{2,1,0:T(8,128)(2,1)} %bitcast.35), calls=%async_computation | async-start | bytes 2752512 | tf_op jit(solution)/shard_map/all_to_all | solution.py:336
  34.9 232.5 %reduce-scatter.2.cloned.1.call-start = ((), (), s32[]{:S(2)}) async-start(), calls=%async_computation.2 | async-start | bytes 2785280 | tf_op jit(solution)/shard_map/reduce_scatter | solution.py:499
  35.0 19.4 %copy-start.9 = (bf16[160,1280]{1,0:T(8,128)(2,1)}, bf16[160,1280]{1,0:T(8,128)(2,1)S(1)}, u32[]{:S(2)}) copy-start(bf16[160,1280]{1,0:T(8,128)(2,1)S(1)} %collective-permute-done) | copy-start | bytes 1228804
  35.0 20.4 %copy-start.11 = (bf16[160,1280]{1,0:T(8,128)(2,1)}, bf16[160,1280]{1,0:T(8,128)(2,1)S(1)}, u32[]{:S(2)}) copy-start(bf16[160,1280]{1,0:T(8,128)(2,1)S(1)} %collective-permute-done.1) | copy-start | bytes 1228804
  35.0 11.8 %collective-permute-start.4 = (bf16[160,1280]{1,0:T(8,128)(2,1)S(1)}, bf16[160,1280]{1,0:T(8,128)(2,1)S(1)}, u32[]{:S(2)}, u32[]{:S(2)}) collective-permute-start(bf16[160,1280]{1,0:T(8,128)(2,1)S(1)} %collective-permute-done.1), channel_id=1, source_target_pairs={{0,1},{1,0},{2,3},{3,2},{4,5},{5,4},{6,7},{7,6},{8,9},{9,8},{10,11... | collective-permute-start | bytes 1228808 | tf_op jit(solution)/shard_map/ppermute | solution.py:310
  46.8 4.3 %copy-start.13 = (bf16[160,1280]{1,0:T(8,128)(2,1)}, bf16[160,1280]{1,0:T(8,128)(2,1)S(1)}, u32[]{:S(2)}) copy-start(bf16[160,1280]{1,0:T(8,128)(2,1)S(1)} %collective-permute-done.4) | copy-start | bytes 1228804
  48.0 35.7 %collective-permute-start.5 = (bf16[480,1280]{1,0:T(8,128)(2,1)}, bf16[480,1280]{1,0:T(8,128)(2,1)}, u32[]{:S(2)}, u32[]{:S(2)}) collective-permute-start(bf16[480,1280]{1,0:T(8,128)(2,1)} %pad_maximum_fusion.2), channel_id=1, source_target_pairs={{0,8},{4,12},{8,0},{12,4},{16,24},{20,28},{24,16},{28,20},{1,9},{5... | collective-permute-start | bytes 3686408 | tf_op jit(solution)/shard_map/ppermute | solution.py:304
  49.7 34.1 %collective-permute-start.6 = (bf16[480,1280]{1,0:T(8,128)(2,1)}, bf16[480,1280]{1,0:T(8,128)(2,1)}, u32[]{:S(2)}, u32[]{:S(2)}) collective-permute-start(bf16[480,1280]{1,0:T(8,128)(2,1)} %pad_maximum_fusion.2), channel_id=1, source_target_pairs={{0,16},{4,20},{8,24},{12,28},{16,0},{20,4},{24,8},{28,12},{1,17},{... | collective-permute-start | bytes 3686408 | tf_op jit(solution)/shard_map/ppermute | solution.py:304
  54.3 1.2 copy-start.7
  55.4 3.8 %copy-start.10 = (bf16[160,1280]{1,0:T(8,128)(2,1)S(1)}, bf16[160,1280]{1,0:T(8,128)(2,1)}, u32[]{:S(2)}) copy-start(bf16[160,1280]{1,0:T(8,128)(2,1)} %copy-done.9) | copy-start | bytes 1228804
  55.4 25.9 %collective-permute-start.7 = (bf16[4,320,256]{2,1,0:T(8,128)(2,1)S(1)}, bf16[4,320,256]{2,1,0:T(8,128)(2,1)S(1)}, u32[]{:S(2)}, u32[]{:S(2)}) collective-permute-start(bf16[4,320,256]{2,1,0:T(8,128)(2,1)S(1)} %get-tuple-element.70.refs_0_), channel_id=1, source_target_pairs={{0,1},{1,0},{2,3},{3,2},{4,5},{5,4},{6,7},{7,6},{8,9},{9,8},{10,11... | collective-permute-start | bytes 1966088 | tf_op jit(solution)/shard_map/ppermute | solution.py:310
  55.9 4.2 %copy-start.12 = (bf16[160,1280]{1,0:T(8,128)(2,1)S(1)}, bf16[160,1280]{1,0:T(8,128)(2,1)}, u32[]{:S(2)}) copy-start(bf16[160,1280]{1,0:T(8,128)(2,1)} %copy-done.11) | copy-start | bytes 1228804
  55.9 27.8 %collective-permute-start.8 = (bf16[4,320,256]{2,1,0:T(8,128)(2,1)S(1)}, bf16[4,320,256]{2,1,0:T(8,128)(2,1)S(1)}, u32[]{:S(2)}, u32[]{:S(2)}) collective-permute-start(bf16[4,320,256]{2,1,0:T(8,128)(2,1)S(1)} %get-tuple-element.70.refs_0_), channel_id=1, source_target_pairs={{0,2},{1,3},{2,0},{3,1},{4,6},{5,7},{6,4},{7,5},{8,10},{9,11},{10,... | collective-permute-start | bytes 1966088 | tf_op jit(solution)/shard_map/ppermute | solution.py:310
  59.3 30.8 %copy-start.14 = (bf16[160,1280]{1,0:T(8,128)(2,1)S(1)}, bf16[160,1280]{1,0:T(8,128)(2,1)}, u32[]{:S(2)}) copy-start(bf16[160,1280]{1,0:T(8,128)(2,1)} %copy-done.13) | copy-start | bytes 1228804
  84.8 12.4 %collective-permute-start.10 = (bf16[240,1280]{1,0:T(8,128)(2,1)S(1)}, bf16[240,1280]{1,0:T(8,128)(2,1)S(1)}, u32[]{:S(2)}, u32[]{:S(2)}) collective-permute-start(bf16[240,1280]{1,0:T(8,128)(2,1)S(1)} %slice.43), channel_id=1, source_target_pairs={{0,16},{4,20},{8,24},{12,28},{16,0},{20,4},{24,8},{28,12},{1,17},{... | collective-permute-start | bytes 1843208 | tf_op jit(solution)/shard_map/ppermute | solution.py:304
  87.5 15.4 %collective-permute-start.11 = (bf16[240,1280]{1,0:T(8,128)(2,1)S(1)}, bf16[240,1280]{1,0:T(8,128)(2,1)S(1)}, u32[]{:S(2)}, u32[]{:S(2)}) collective-permute-start(bf16[240,1280]{1,0:T(8,128)(2,1)S(1)} %slice.44), channel_id=1, source_target_pairs={{0,8},{4,12},{8,0},{12,4},{16,24},{20,28},{24,16},{28,20},{1,9},{5... | collective-permute-start | bytes 1843208 | tf_op jit(solution)/shard_map/ppermute | solution.py:304
  90.0 15.2 %collective-permute-start.9 = (bf16[4,320,256]{2,1,0:T(8,128)(2,1)S(1)}, bf16[4,320,256]{2,1,0:T(8,128)(2,1)S(1)}, u32[]{:S(2)}, u32[]{:S(2)}) collective-permute-start(bf16[4,320,256]{2,1,0:T(8,128)(2,1)S(1)} %collective-permute-done.8.refs_2_), channel_id=1, source_target_pairs={{0,1},{1,0},{2,3},{3,2},{4,5},{5,4},{6,7},{7,6},{8,9},{9,8},{10,11... | collective-permute-start | bytes 1966088 | tf_op jit(solution)/shard_map/ppermute | solution.py:310
  93.2 17.2 %copy-start.17 = (f32[1280]{0:T(1024)S(1)}, f32[1280]{0:T(1024)}, u32[]{:S(2)}) copy-start(f32[1280]{0:T(1024)} %param.19) | copy-start | bytes 15364
  93.2 17.5 %copy-start.16 = (f32[1280]{0:T(1024)S(1)}, f32[1280]{0:T(1024)}, u32[]{:S(2)}) copy-start(f32[1280]{0:T(1024)} %param.20) | copy-start | bytes 15364
  93.3 23.9 %copy-start.2 = (bf16[320,1280]{1,0:T(8,128)(2,1)S(1)}, bf16[320,1280]{1,0:T(8,128)(2,1)}, u32[]{:S(2)}) copy-start(bf16[320,1280]{1,0:T(8,128)(2,1)} %refs_5_.3) | copy-start | bytes 2457604
  105.2 0.8 copy-start.3
  107.8 8.5 %collective-permute-start.12 = (bf16[1920,1280]{1,0:T(8,128)(2,1)}, bf16[1920,1280]{1,0:T(8,128)(2,1)}, u32[]{:S(2)}, u32[]{:S(2)}) collective-permute-start(bf16[1920,1280]{1,0:T(8,128)(2,1)} %constant_dynamic-update-slice_fusion.refs_6_), channel_id=1, source_target_pairs={{0,4},{4,0},{8,12},{12,8},{16,20},{20,16},{24,28},{28,24},{1,5},{5... | collective-permute-start | bytes 14745608 | tf_op jit(solution)/shard_map/ppermute | solution.py:304
  107.8 87.2 %collective-permute-start.20 = (bf16[640,2048]{1,0:T(8,128)(2,1)}, bf16[640,2048]{1,0:T(8,128)(2,1)}, u32[]{:S(2)}, u32[]{:S(2)}) collective-permute-start(bf16[640,2048]{1,0:T(8,128)(2,1)} %refs_1_.1), channel_id=1, source_target_pairs={{0,4},{4,0},{8,12},{12,8},{16,20},{20,16},{24,28},{28,24},{1,5},{5... | collective-permute-start | bytes 7864328 | tf_op jit(solution)/shard_map/ppermute | solution.py:304
  108.3 44.9 %collective-permute-start.16 = (bf16[480,2048]{1,0:T(8,128)(2,1)}, bf16[480,2048]{1,0:T(8,128)(2,1)S(1)}, u32[]{:S(2)}, u32[]{:S(2)}) collective-permute-start(bf16[480,2048]{1,0:T(8,128)(2,1)} %slice.42), channel_id=1, source_target_pairs={{0,8},{4,12},{8,0},{12,4},{16,24},{20,28},{24,16},{28,20},{1,9},{5... | collective-permute-start | bytes 5898248 | tf_op jit(solution)/shard_map/ppermute | solution.py:304
  108.7 44.7 %collective-permute-start.17 = (bf16[480,2048]{1,0:T(8,128)(2,1)}, bf16[480,2048]{1,0:T(8,128)(2,1)S(1)}, u32[]{:S(2)}, u32[]{:S(2)}) collective-permute-start(bf16[480,2048]{1,0:T(8,128)(2,1)} %slice.42), channel_id=1, source_target_pairs={{0,16},{4,20},{8,24},{12,28},{16,0},{20,4},{24,8},{28,12},{1,17},{... | collective-permute-start | bytes 5898248 | tf_op jit(solution)/shard_map/ppermute | solution.py:304
  116.3 31.6 %collective-permute-start.13 = (bf16[4,320,256]{2,1,0:T(8,128)(2,1)S(1)}, bf16[4,320,256]{2,1,0:T(8,128)(2,1)S(1)}, u32[]{:S(2)}, u32[]{:S(2)}) collective-permute-start(bf16[4,320,256]{2,1,0:T(8,128)(2,1)S(1)} %get-tuple-element.53.refs_0_), channel_id=1, source_target_pairs={{0,1},{1,0},{2,3},{3,2},{4,5},{5,4},{6,7},{7,6},{8,9},{9,8},{10,11... | collective-permute-start | bytes 1966088 | tf_op jit(solution)/shard_map/ppermute | solution.py:310
  116.6 31.5 %collective-permute-start.14 = (bf16[4,320,256]{2,1,0:T(8,128)(2,1)S(1)}, bf16[4,320,256]{2,1,0:T(8,128)(2,1)S(1)}, u32[]{:S(2)}, u32[]{:S(2)}) collective-permute-start(bf16[4,320,256]{2,1,0:T(8,128)(2,1)S(1)} %get-tuple-element.53.refs_0_), channel_id=1, source_target_pairs={{0,2},{1,3},{2,0},{3,1},{4,6},{5,7},{6,4},{7,5},{8,10},{9,11},{10,... | collective-permute-start | bytes 1966088 | tf_op jit(solution)/shard_map/ppermute | solution.py:310
  117.2 1.1 copy-start.4
  148.1 16.2 %collective-permute-start.15 = (bf16[4,320,256]{2,1,0:T(8,128)(2,1)S(1)}, bf16[4,320,256]{2,1,0:T(8,128)(2,1)S(1)}, u32[]{:S(2)}, u32[]{:S(2)}) collective-permute-start(bf16[4,320,256]{2,1,0:T(8,128)(2,1)S(1)} %collective-permute-done.14.refs_2_), channel_id=1, source_target_pairs={{0,1},{1,0},{2,3},{3,2},{4,5},{5,4},{6,7},{7,6},{8,9},{9,8},{10,11... | collective-permute-start | bytes 1966088 | tf_op jit(solution)/shard_map/ppermute | solution.py:310
  153.6 10.7 %copy-start.15 = (bf16[640,2048]{1,0:T(8,128)(2,1)}, bf16[640,2048]{1,0:T(8,128)(2,1)S(1)}, u32[]{:S(2)}) copy-start(bf16[640,2048]{1,0:T(8,128)(2,1)S(1)} %constant_dynamic-update-slice_fusion.7.refs_2_) | copy-start | bytes 7864324
  153.7 40.6 %collective-permute-start.18 = (bf16[320,2048]{1,0:T(8,128)(2,1)S(1)}, bf16[320,2048]{1,0:T(8,128)(2,1)S(1)}, u32[]{:S(2)}, u32[]{:S(2)}) collective-permute-start(bf16[320,2048]{1,0:T(8,128)(2,1)S(1)} %slice.59), channel_id=1, source_target_pairs={{0,16},{4,20},{8,24},{12,28},{16,0},{20,4},{24,8},{28,12},{1,17},{... | collective-permute-start | bytes 3932168 | tf_op jit(solution)/shard_map/ppermute | solution.py:304
  156.7 37.6 %collective-permute-start.19 = (bf16[320,2048]{1,0:T(8,128)(2,1)}, bf16[320,2048]{1,0:T(8,128)(2,1)S(1)}, u32[]{:S(2)}, u32[]{:S(2)}) collective-permute-start(bf16[320,2048]{1,0:T(8,128)(2,1)} %slice.46), channel_id=1, source_target_pairs={{0,8},{4,12},{8,0},{12,4},{16,24},{20,28},{24,16},{28,20},{1,9},{5... | collective-permute-start | bytes 3932168 | tf_op jit(solution)/shard_map/ppermute | solution.py:304
  159.6 34.6 %copy-start.8 = (bf16[640,2048]{1,0:T(8,128)(2,1)}, bf16[640,2048]{1,0:T(8,128)(2,1)S(1)}, u32[]{:S(2)}) copy-start(bf16[640,2048]{1,0:T(8,128)(2,1)S(1)} %pad_maximum_fusion.refs_3_) | copy-start | bytes 7864324
  159.6 39.7 %copy-start.5 = (f32[2048]{0:T(1024)S(1)}, f32[2048]{0:T(1024)}, u32[]{:S(2)}) copy-start(f32[2048]{0:T(1024)} %param.22) | copy-start | bytes 24580
  164.2 35.0 %collective-permute-start.21 = (bf16[640,2048]{1,0:T(8,128)(2,1)S(1)}, bf16[640,2048]{1,0:T(8,128)(2,1)}, u32[]{:S(2)}, u32[]{:S(2)}) collective-permute-start(bf16[640,2048]{1,0:T(8,128)(2,1)S(1)} %constant_dynamic-update-slice_fusion.7.refs_2_), channel_id=1, source_target_pairs={{0,4},{4,0},{8,12},{12,8},{16,20},{20,16},{24,28},{28,24},{1,5},{5... | collective-permute-start | bytes 7864328 | tf_op jit(solution)/shard_map/ppermute | solution.py:304
  164.2 35.0 %collective-permute-start.22 = (bf16[640,2048]{1,0:T(8,128)(2,1)S(1)}, bf16[640,2048]{1,0:T(8,128)(2,1)}, u32[]{:S(2)}, u32[]{:S(2)}) collective-permute-start(bf16[640,2048]{1,0:T(8,128)(2,1)S(1)} %pad_maximum_fusion.refs_3_), channel_id=1, source_target_pairs={{0,4},{4,0},{8,12},{12,8},{16,20},{20,16},{24,28},{28,24},{1,5},{5... | collective-permute-start | bytes 7864328 | tf_op jit(solution)/shard_map/ppermute | solution.py:304
  194.3 3.1 %collective-permute-start.23 = (bf16[320,2048]{1,0:T(8,128)(2,1)S(1)}, bf16[320,2048]{1,0:T(8,128)(2,1)S(1)}, u32[]{:S(2)}, u32[]{:S(2)}) collective-permute-start(bf16[320,2048]{1,0:T(8,128)(2,1)S(1)} %collective-permute-done.18.refs_4_), channel_id=1, source_target_pairs={{0,4},{4,0},{8,12},{12,8},{16,20},{20,16},{24,28},{28,24},{1,5},{5... | collective-permute-start | bytes 3932168 | tf_op jit(solution)/shard_map/ppermute | solution.py:304
  194.4 4.9 %collective-permute-start.24 = (bf16[320,2048]{1,0:T(8,128)(2,1)S(1)}, bf16[320,2048]{1,0:T(8,128)(2,1)S(1)}, u32[]{:S(2)}, u32[]{:S(2)}) collective-permute-start(bf16[320,2048]{1,0:T(8,128)(2,1)S(1)} %collective-permute-done.19.refs_5_), channel_id=1, source_target_pairs={{0,4},{4,0},{8,12},{12,8},{16,20},{20,16},{24,28},{28,24},{1,5},{5... | collective-permute-start | bytes 3932168 | tf_op jit(solution)/shard_map/ppermute | solution.py:304
  220.8 48.9 %copy-start.1 = (bf16[2048,320]{0,1:T(8,128)(2,1)S(1)}, bf16[2048,320]{0,1:T(8,128)(2,1)}, u32[]{:S(2)}) copy-start(bf16[2048,320]{0,1:T(8,128)(2,1)} %param.13) | copy-start | bytes 3932164
Sparse Core Ops, SparseCore 0:
  220.9 46.4 reduce-scatter.1
